TPU v7x, 32 devices: a whole 2x2x4 slice. The times are simulated.
32 devices in a mesh: inst: 1, ep: 8 (over z, y), dp: 4 (over x, core).
Axes of the slice: x: 2, y: 2, z: 4, core: 2. Of those that a mesh axis runs over, the one named last changes fastest.
Arguments:
- hidden: bfloat16 [64, 7168], P(('inst', 'ep', 'dp')), may hold values from -6 to 6
- routes: int32 [64, 4], P(('inst', 'ep', 'dp')), may hold values from 0 to 7, all different within a row; in each aligned block of 8 rows (0 to 7, 8 to 15, ...) at most 8 rows name the same one
- route_weight: float32 [64, 4], P(('inst', 'ep', 'dp')), may hold values from 0.2 to 1
- gate_weight: bfloat16 [8, 7168, 2048], P('ep', None, 'dp'), may hold values from -0.0625 to 0.0625
- up_weight: bfloat16 [8, 7168, 2048], P('ep', None, 'dp'), may hold values from -0.0625 to 0.0625
- down_weight: bfloat16 [8, 2048, 7168], P('ep', 'dp'), may hold values from -0.125 to 0.125
- queries: bfloat16 [64, 36864], P(('inst', 'ep', 'dp')), may hold values from -5600 to 5600
- latent_pool: bfloat16 [768, 18432], P(('inst', 'ep', 'dp')), may hold values from -4 to 4
- lengths: int32 [64], P(('inst', 'ep', 'dp')), may hold values from 65 to 384
- page_table: int32 [64, 12], P(('inst', 'ep', 'dp')), may hold values from 0 to 31, as said below
- moved_page: int32 [32, 6], P(('inst', 'ep', 'dp')), may hold values from 0 to 23, as said below
- moved_dest: int32 [32, 6], P(('inst', 'ep', 'dp')), may hold values from 0 to 3, as said below
Outputs:
- expert_mix: bfloat16 [64, 7168], P(('inst', 'ep', 'dp'))
- attended: bfloat16 [64, 32768], P(('inst', 'ep', 'dp'))
Inputs may be any that keep to these rules, and one draw needn't show every extreme that they name: `routes`: a row names 4 different experts; in each aligned block of 8 rows (one dp group) no expert is named by more than 8 rows, a bound that some block reaches. `page_table`: the 12 entries of a row name distinct slots, and no two rows of one device share a slot; every page below a row's length names a slot that holds data after migration; every slot that receives a page is named by a live page. `moved_page`: 6 distinct pages of the sending device. `moved_dest`: never the sender's own dp index; each other dp index is named by exactly 2 entries of a device.
All inputs are finite; a program needn't handle non-finite values.
Results may differ from a plain program's by a relative error of at most 0.0059.
Values may be sent and summed in bfloat16 or wider, within the bound.
No kernel may reach another device: no remote copies, remote signals or barrier semaphores. Data moves between devices by JAX's collectives and lax.ppermute only.
A program may use at most 128 MiB of HBM per device.

v0:
```python
import jax
import jax.numpy as jnp
from jax import lax
from jax.sharding import PartitionSpec as P

HEADS = 64
LAT = 576
VL = 512
MCAP = 2


score_scale = 192.0 ** (-0.5)


def expert_apply(rows_in, gate_part, up_part, down_part):
    flat_rows = rows_in.reshape(-1, rows_in.shape[-1])
    gate_vals = jnp.dot(flat_rows, gate_part, preferred_element_type=jnp.float32)
    up_vals = jnp.dot(flat_rows, up_part, preferred_element_type=jnp.float32)
    inner_act = (jax.nn.silu(gate_vals) * up_vals).astype(jnp.bfloat16)
    partial_out = jnp.dot(inner_act, down_part, preferred_element_type=jnp.float32)
    return partial_out.reshape(rows_in.shape[:-1] + (down_part.shape[1],))


def body(
    hidden,
    routes,
    route_weight,
    gate_weight,
    up_weight,
    down_weight,
    queries,
    latent_pool,
    lengths,
    page_table,
    moved_page,
    moved_dest,
):
    ep_count = lax.axis_size("ep")
    dp_count = lax.axis_size("dp")
    rows_dev = hidden.shape[0]
    model_width = hidden.shape[1]
    experts = jnp.arange(ep_count, dtype=jnp.int32)
    gate_part = gate_weight[0]
    up_part = up_weight[0]
    down_part = down_weight[0]
    chosen_mask = jnp.any(routes[None, :, :] == experts[:, None, None], axis=2)
    masked = jnp.where(chosen_mask[:, :, None], hidden[None, :, :], jnp.zeros((), jnp.bfloat16))
    outgoing = jnp.broadcast_to(masked[:, None], (ep_count, dp_count, rows_dev, model_width))
    outgoing = outgoing.reshape(ep_count * dp_count, rows_dev, model_width)
    partial_out = expert_apply(
        lax.all_to_all(outgoing, ("ep", "dp"), split_axis=0, concat_axis=0, tiled=True),
        gate_part,
        up_part,
        down_part,
    )
    returned = lax.all_to_all(partial_out, ("ep", "dp"), split_axis=0, concat_axis=0, tiled=True)
    expert_out = jnp.sum(
        returned.reshape(ep_count, dp_count, rows_dev, model_width), axis=1
    ).astype(jnp.bfloat16)
    weight_table = jnp.sum(
        jnp.where(routes[:, :, None] == experts, route_weight[:, :, None], 0.0), axis=1
    )
    expert_mix = jnp.sum(
        weight_table.T[:, :, None] * expert_out.astype(jnp.float32), axis=0
    ).astype(jnp.bfloat16)
    page_dest = moved_dest[0]
    page_pick = moved_page[0]
    entries = page_dest.shape[0]
    same_dest = page_dest[:, None] == page_dest[None, :]
    earlier = (
        jnp.arange(entries, dtype=jnp.int32)[None, :]
        < jnp.arange(entries, dtype=jnp.int32)[:, None]
    )
    entry_rank = jnp.sum((same_dest & earlier).astype(jnp.int32), axis=1)
    bucket = page_dest * MCAP + entry_rank
    bucket_ids = jnp.arange(dp_count * MCAP, dtype=jnp.int32)
    own_slots = jnp.arange(latent_pool.shape[0], dtype=jnp.int32)
    select_pages = jnp.any(
        (bucket[None, :] == bucket_ids[:, None])[:, :, None]
        & (page_pick[None, :, None] == own_slots[None, None, :]),
        axis=1,
    )
    outgoing_pages = jnp.dot(
        select_pages.astype(jnp.bfloat16), latent_pool, preferred_element_type=jnp.float32
    ).astype(jnp.bfloat16)
    outgoing_pages = outgoing_pages.reshape(dp_count, MCAP, latent_pool.shape[1])
    arrived_pages = lax.all_to_all(outgoing_pages, "dp", split_axis=0, concat_axis=0, tiled=True)
    pool_after = jnp.concatenate(
        [latent_pool, arrived_pages.reshape(dp_count * MCAP, latent_pool.shape[1])], axis=0
    )
    key_rows = jnp.take(pool_after, page_table, axis=0).reshape(rows_dev, -1, LAT)
    query_rows = queries.reshape(rows_dev, HEADS, LAT)
    scores = (
        jnp.einsum("rhl,rtl->rht", query_rows, key_rows, preferred_element_type=jnp.float32)
        * score_scale
    )
    live_mask = jnp.arange(key_rows.shape[1], dtype=jnp.int32)[None, :] < lengths[:, None]
    scores = jnp.where(live_mask[:, None, :], scores, -jnp.inf)
    row_max = jnp.max(scores, axis=2, keepdims=True)
    shifted = jnp.exp(scores - row_max)
    attn_probs = (shifted / jnp.sum(shifted, axis=2, keepdims=True)).astype(jnp.bfloat16)
    attended = jnp.einsum(
        "rht,rtv->rhv", attn_probs, key_rows[:, :, :VL], preferred_element_type=jnp.float32
    ).astype(jnp.bfloat16)
    return (expert_mix, attended.reshape(rows_dev, HEADS * VL))


def solution(mesh):
    in_specs = (
        P(("inst", "ep", "dp"), None),
        P(("inst", "ep", "dp"), None),
        P(("inst", "ep", "dp"), None),
        P("ep", None, "dp"),
        P("ep", None, "dp"),
        P("ep", "dp", None),
        P(("inst", "ep", "dp"), None),
        P(("inst", "ep", "dp"), None),
        P(("inst", "ep", "dp")),
        P(("inst", "ep", "dp"), None),
        P(("inst", "ep", "dp"), None),
        P(("inst", "ep", "dp"), None),
    )
    out_specs = (P(("inst", "ep", "dp"), None), P(("inst", "ep", "dp"), None))
    return jax.shard_map(body, mesh=mesh, in_specs=in_specs, out_specs=out_specs, check_vma=False)
```

profile of v0, /device:TPU:0, one launch (start us, length us, event | category | flops | bytes accessed | tf_op | source)
XLA Modules:
  0.0 104.9 jit_solution(14780898729747324244)
XLA Ops:
  0.7 0.8 fusion.21
  1.5 0.1 copy.24
  1.6 1.0 broadcast_select_fusion.1
  2.6 1.4 %broadcast_in_dim.90 = bf16[8,4,2,7168]{3,2,1,0:T(2,128)(2,1)} broadcast(bf16[8,2,7168]{2,1,0:T(2,128)(2,1)S(1)} %broadcast_select_fusion.1), dimensions={0,2,3} | broadcast | bytes 1146880 | tf_op jit(solution)/shard_map/broadcast_in_dim | solution.py:48
  4.0 7.3 %all-to-all-start = ((bf16[32,2,7168]{2,1,0:T(2,128)(2,1)}), bf16[32,2,7168]{2,1,0:T(2,128)(2,1)S(1)}, u32[]{:S(2)}, u32[]{:S(2)}) async-start(bf16[32,2,7168]{2,1,0:T(2,128)(2,1)} %bitcast.1), calls=%async_computation | async-start | bytes 1835008 | tf_op jit(solution)/shard_map/all_to_all | solution.py:51
  11.3 0.2 convert_reduce_fusion
  11.7 0.3 convolution_convert_fusion
  12.0 0.9 reshape.110
  12.9 21.8 %all-to-all-done = bf16[32,2,7168]{2,1,0:T(2,128)(2,1)S(1)} async-done(((bf16[32,2,7168]{2,1,0:T(2,128)(2,1)}), bf16[32,2,7168]{2,1,0:T(2,128)(2,1)S(1)}, u32[]{:S(2)}, u32[]{:S(2)}) %all-to-all-start) | async-done | bytes 917536 | tf_op jit(solution)/shard_map/all_to_all | solution.py:51
  34.7 0.9 copy-done.2
  35.6 3.5 %all-to-all-start.2 = ((bf16[4,2,18432]{2,1,0:T(2,128)(2,1)}), bf16[4,2,18432]{2,1,0:T(2,128)(2,1)S(1)}, u32[]{:S(2)}, u32[]{:S(2)}) async-start(bf16[4,2,18432]{2,1,0:T(2,128)(2,1)} %reshape.110), calls=%async_computation.2 | async-start | bytes 589824 | tf_op jit(solution)/shard_map/all_to_all | solution.py:87
  39.1 3.4 %reshape.108 = bf16[64,7168]{1,0:T(8,128)(2,1)} reshape(bf16[32,2,7168]{2,1,0:T(2,128)(2,1)} %copy-done.2) | data formatting | bytes 1835008 | tf_op jit(solution)/shard_map/reshape | solution.py:16
  42.5 4.9 %fusion.5 = f32[64,512]{1,0:T(8,128)S(1)} fusion(bf16[64,7168]{1,0:T(8,128)(2,1)} %reshape.108, bf16[1,7168,512]{2,1,0:T(8,128)(2,1)} %param.15), kind=kOutput, calls=%fused_computation.7 | convolution fusion | flops 469762048 | bytes 8388608 | tf_op jit(solution)/shard_map/dot_general | solution.py:17
  47.4 1.4 %fusion.15 = bf16[64,512]{1,0:T(8,128)(2,1)S(1)} fusion(bf16[64,7168]{1,0:T(8,128)(2,1)S(1)} %copy-done, bf16[1,7168,512]{2,1,0:T(8,128)(2,1)S(1)} %bitcast.40, f32[64,512]{1,0:T(8,128)S(1)} %fusion.5), kind=kOutput, calls=%fused_computation.19 | convolution fusion | flops 469958656 | bytes 8454144 | tf_op jit(solution)/shard_map/dot_general | solution.py:18
  48.8 4.5 %fusion.1 = f32[32,2,7168]{2,0,1:T(8,128)S(1)} fusion(bf16[1,512,7168]{2,1,0:T(8,128)(2,1)} %param.17, bf16[32,2,512]{2,1,0:T(2,128)(2,1)S(1)} %dot_general.22), kind=kOutput, calls=%fused_computation.3 | convolution fusion | flops 469762048 | bytes 9240576 | tf_op jit(solution)/shard_map/dot_general | solution.py:20
  53.3 2.7 %copy.26 = f32[32,2,7168]{2,1,0:T(2,128)} copy(f32[32,2,7168]{2,0,1:T(8,128)S(1)} %fusion.1) | data formatting | bytes 3670016 | tf_op jit(solution)/shard_map/dot_general | solution.py:20
  56.0 4.2 %all-to-all-start.1 = ((f32[32,2,7168]{2,1,0:T(2,128)}), f32[32,2,7168]{2,1,0:T(2,128)S(1)}, u32[]{:S(2)}, u32[]{:S(2)}) async-start(f32[32,2,7168]{2,1,0:T(2,128)} %copy.26), calls=%async_computation.1 | async-start | bytes 3670016 | tf_op jit(solution)/shard_map/all_to_all | solution.py:56
  60.4 0.1 broadcast_in_dim.93
  60.5 0.9 reshape.112
  61.6 1.1 %reshape.111 = bf16[8,18432]{1,0:T(8,128)(2,1)S(1)} reshape(bf16[4,2,18432]{2,1,0:T(2,128)(2,1)} %copy-done.4) | data formatting | bytes 589824 | tf_op jit(solution)/shard_map/reshape | solution.py:89
  62.6 1.2 %pad_maximum_fusion = bf16[32,18432]{1,0:T(8,128)(2,1)S(1)} fusion(bf16[8,18432]{1,0:T(8,128)(2,1)S(1)} %reshape.111, bf16[24,18432]{1,0:T(8,128)(2,1)} %param.19), kind=kLoop, calls=%fused_computation.10 | loop fusion | flops 2359296 | bytes 2359296 | tf_op jit(solution)/shard_map/concatenate | solution.py:88
  63.9 2.0 %gather_fusion = bf16[24,18432]{1,0:T(8,128)(2,1)} fusion(bf16[32,18432]{1,0:T(8,128)(2,1)S(1)} %pad_maximum_fusion, s32[1024]{0:T(1024)S(1)} %pad_clamp_fusion), kind=kCustom, calls=%fused_computation | custom fusion | bytes 1769568 | tf_op jit(solution)/shard_map/jit(_take)/gather | solution.py:91
  65.9 2.4 %gather.7 = bf16[2,384,576]{2,1,0:T(8,128)(2,1)S(1)} reshape(bf16[24,18432]{1,0:T(8,128)(2,1)} %gather_fusion) | data formatting | bytes 1769472 | tf_op jit(solution)/shard_map/jit(_take)/gather | solution.py:91
  68.3 0.2 broadcast_select_fusion
  68.5 0.9 copy-done.1
  69.5 0.4 fusion.10
  69.9 0.2 fusion.25
  70.1 1.5 %fusion.11 = bf16[1,2,64,512]{3,2,1,0:T(8,128)(2,1)S(1)} fusion(bf16[2,384,576]{2,1,0:T(8,128)(2,1)} %copy-done.1, f32[2,64]{1,0:T(2,128)S(1)} %fusion.25, f32[2,64,384]{2,1,0:T(8,128)S(1)} %fusion.10), kind=kOutput, calls=%fused_computation.17 | convolution fusion | flops 50545152 | bytes 1311744 | tf_op jit(solution)/shard_map/rht,rtv->rhv/dot_general | solution.py:102
  71.6 0.8 copy.31
  72.4 31.0 %all-to-all-done.1 = f32[32,2,7168]{2,1,0:T(2,128)S(1)} async-done(((f32[32,2,7168]{2,1,0:T(2,128)}), f32[32,2,7168]{2,1,0:T(2,128)S(1)}, u32[]{:S(2)}, u32[]{:S(2)}) %all-to-all-start.1) | async-done | bytes 1835040 | tf_op jit(solution)/shard_map/all_to_all | solution.py:56
  103.4 0.6 bitcast_reduce_fusion
  104.0 0.9 multiply_reduce_fusion
  (42 shorter events, 0.7 us)
Async XLA Ops:
  0.6 10.7 %copy-start.12 = (s32[1,6]{1,0:T(1,128)S(1)}, s32[1,6]{1,0:T(1,128)}, u32[]{:S(2)}) copy-start(s32[1,6]{1,0:T(1,128)} %param.23) | copy-start | bytes 76
  0.6 10.8 %copy-start.11 = (s32[1,6]{1,0:T(1,128)S(1)}, s32[1,6]{1,0:T(1,128)}, u32[]{:S(2)}) copy-start(s32[1,6]{1,0:T(1,128)} %param.22) | copy-start | bytes 76
  0.6 11.1 %copy-start.3 = (bf16[24,18432]{1,0:T(8,128)(2,1)S(1)}, bf16[24,18432]{1,0:T(8,128)(2,1)}, u32[]{:S(2)}) copy-start(bf16[24,18432]{1,0:T(8,128)(2,1)} %param.19) | copy-start | bytes 2654212
  4.0 30.7 %all-to-all-start = ((bf16[32,2,7168]{2,1,0:T(2,128)(2,1)}), bf16[32,2,7168]{2,1,0:T(2,128)(2,1)S(1)}, u32[]{:S(2)}, u32[]{:S(2)}) async-start(bf16[32,2,7168]{2,1,0:T(2,128)(2,1)} %bitcast.1), calls=%async_computation | async-start | bytes 1835008 | tf_op jit(solution)/shard_map/all_to_all | solution.py:51
  34.7 0.9 copy-start.2
  35.6 20.4 %all-to-all-start.2 = ((bf16[4,2,18432]{2,1,0:T(2,128)(2,1)}), bf16[4,2,18432]{2,1,0:T(2,128)(2,1)S(1)}, u32[]{:S(2)}, u32[]{:S(2)}) async-start(bf16[4,2,18432]{2,1,0:T(2,128)(2,1)} %reshape.110), calls=%async_computation.2 | async-start | bytes 589824 | tf_op jit(solution)/shard_map/all_to_all | solution.py:87
  39.1 8.3 %slice-start = ((s8[7340032]{0:T(1024)(128)(4,1)}), s8[3145728]{0:T(1024)(128)(4,1)S(1)}, s32[]{:S(2)}) async-start(s8[7340032]{0:T(1024)(128)(4,1)} %bitcast.39), calls=%async_computation.3 | async-start | bytes 6291456
  42.5 4.9 %slice-start.1 = ((s8[7340032]{0:T(1024)(128)(4,1)}), s8[4194304]{0:T(1024)(128)(4,1)S(1)}, s32[]{:S(2)}) async-start(s8[7340032]{0:T(1024)(128)(4,1)} %bitcast.39), calls=%async_computation.4 | async-start | bytes 8388608
  42.5 4.9 %copy-start = (bf16[64,7168]{1,0:T(8,128)(2,1)S(1)}, bf16[64,7168]{1,0:T(8,128)(2,1)}, u32[]{:S(2)}) copy-start(bf16[64,7168]{1,0:T(8,128)(2,1)} %reshape.108) | copy-start | bytes 2752516
  56.0 4.2 %copy-start.9 = (s32[2,12]{1,0:T(2,128)S(1)}, s32[2,12]{1,0:T(2,128)}, u32[]{:S(2)}) copy-start(s32[2,12]{1,0:T(2,128)} %param.21) | copy-start | bytes 292
  56.0 4.5 %copy-start.6 = (bf16[2,36864]{1,0:T(2,128)(2,1)S(1)}, bf16[2,36864]{1,0:T(2,128)(2,1)}, u32[]{:S(2)}) copy-start(bf16[2,36864]{1,0:T(2,128)(2,1)} %param.18) | copy-start | bytes 442372
  56.0 5.4 %copy-start.7 = (s32[2,4]{1,0:T(2,128)S(1)}, s32[2,4]{1,0:T(2,128)}, u32[]{:S(2)}) copy-start(s32[2,4]{1,0:T(2,128)} %param.13) | copy-start | bytes 100
  56.0 5.4 %copy-start.8 = (f32[2,4]{1,0:T(2,128)S(1)}, f32[2,4]{1,0:T(2,128)}, u32[]{:S(2)}) copy-start(f32[2,4]{1,0:T(2,128)} %param.14) | copy-start | bytes 100
  56.0 5.5 %copy-start.10 = (s32[2]{0:T(128)S(1)}, s32[2]{0:T(128)}, u32[]{:S(2)}) copy-start(s32[2]{0:T(128)} %param.20) | copy-start | bytes 28
  56.0 5.5 %copy-start.4 = (bf16[4,2,18432]{2,1,0:T(2,128)(2,1)}, bf16[4,2,18432]{2,1,0:T(2,128)(2,1)S(1)}, u32[]{:S(2)}) copy-start(bf16[4,2,18432]{2,1,0:T(2,128)(2,1)S(1)} %all-to-all-done.2) | copy-start | bytes 884740
  56.0 47.4 %all-to-all-start.1 = ((f32[32,2,7168]{2,1,0:T(2,128)}), f32[32,2,7168]{2,1,0:T(2,128)S(1)}, u32[]{:S(2)}, u32[]{:S(2)}) async-start(f32[32,2,7168]{2,1,0:T(2,128)} %copy.26), calls=%async_computation.1 | async-start | bytes 3670016 | tf_op jit(solution)/shard_map/all_to_all | solution.py:56
  65.9 3.5 %copy-start.5 = (bf16[2,64,576]{2,1,0:T(8,128)(2,1)S(1)}, bf16[2,64,576]{2,1,0:T(8,128)(2,1)}, u32[]{:S(2)}) copy-start(bf16[2,64,576]{2,1,0:T(8,128)(2,1)} %reshape.112) | copy-start | bytes 442372
  68.5 1.0 copy-start.1
where the time goes:
time: 106 us; the launch traced here: 105 us
  waiting for transfers between devices  52.8 us (50%)
  local copies, waits for them, and re-layouts  17.8 us (17%)
  starting transfers between devices  14.9 us (14%)
  matrix products  13 us (12%)
  other arithmetic  5.55 us (5%)
    all_to_all x1, waiting for transfers between devices, body(): lax.all_to_all(partial_out, ('ep', 'dp'), split_axis=0, concat_axis=0, ti...  31 us
    all_to_all x1, waiting for transfers between devices, body(): lax.all_to_all(outgoing, ('ep', 'dp'), split_axis=0, concat_axis=0, tiled...  21.8 us
    all_to_all x1, starting transfers between devices, body(): lax.all_to_all(outgoing, ('ep', 'dp'), split_axis=0, concat_axis=0, tiled...  7.3 us
    dot_general x1, matrix products, expert_apply(): jnp.dot(flat_rows, gate_part, preferred_element_type=jnp.float32)  4.88 us
    dot_general x1, matrix products, expert_apply(): jnp.dot(inner_act, down_part, preferred_element_type=jnp.float32)  4.47 us
    gather x2, local copies, waits for them, and re-layouts, body(): jnp.take(pool_after, page_table, axis=0).reshape(rows_dev, -1, LAT)  4.39 us
    all_to_all x1, starting transfers between devices, body(): lax.all_to_all(partial_out, ('ep', 'dp'), split_axis=0, concat_axis=0, ti...  4.18 us
    all_to_all x1, starting transfers between devices, body(): lax.all_to_all(outgoing_pages, 'dp', split_axis=0, concat_axis=0, tiled=T...  3.45 us
  transfers between devices with their start and end apart: 3, of which 2 were waited for; matrix products, arithmetic and copies ran while one was open for 28% of the time, Pallas kernels for 0%

commit v1 on v0

--- a/solution.py
+++ b/solution.py
@@ -7,18 +7,44 @@
 LAT = 576
 VL = 512
 MCAP = 2
-
+AXES = ("ep", "dp")
 
 score_scale = 192.0 ** (-0.5)
 
 
-def expert_apply(rows_in, gate_part, up_part, down_part):
-    flat_rows = rows_in.reshape(-1, rows_in.shape[-1])
-    gate_vals = jnp.dot(flat_rows, gate_part, preferred_element_type=jnp.float32)
-    up_vals = jnp.dot(flat_rows, up_part, preferred_element_type=jnp.float32)
-    inner_act = (jax.nn.silu(gate_vals) * up_vals).astype(jnp.bfloat16)
-    partial_out = jnp.dot(inner_act, down_part, preferred_element_type=jnp.float32)
-    return partial_out.reshape(rows_in.shape[:-1] + (down_part.shape[1],))
+def partner_bits(count):
+    bits = []
+    b = count // 2
+    while b:
+        bits.append(b)
+        b //= 2
+    return bits
+
+
+def swap(x, count, bit):
+    return lax.ppermute(x, AXES, [(i, i ^ bit) for i in range(count)])
+
+
+def gather_rows(x, count):
+    for bit in partner_bits(count):
+        x = jnp.concatenate([x, swap(x, count, bit)], axis=0)
+    return x
+
+
+def scatter_sum(x, count):
+    for bit in reversed(partner_bits(count)):
+        half = x.shape[0] // 2
+        got = swap(x[half:].astype(jnp.bfloat16), count, bit)
+        x = x[:half] + got.astype(jnp.float32)
+    return x
+
+
+def weight_columns(routes, route_weight, ep_count):
+    experts = jnp.arange(ep_count, dtype=jnp.int32)
+    table = jnp.sum(jnp.where(routes[:, :, None] == experts, route_weight[:, :, None], 0.0), axis=1)
+    high = table.astype(jnp.bfloat16)
+    low = (table - high.astype(jnp.float32)).astype(jnp.bfloat16)
+    return jnp.pad(jnp.concatenate([high, low], axis=1), ((0, 0), (0, 128 - 2 * ep_count)))
 
 
 def body(
@@ -37,32 +63,22 @@
 ):
     ep_count = lax.axis_size("ep")
     dp_count = lax.axis_size("dp")
-    rows_dev = hidden.shape[0]
-    model_width = hidden.shape[1]
-    experts = jnp.arange(ep_count, dtype=jnp.int32)
-    gate_part = gate_weight[0]
-    up_part = up_weight[0]
-    down_part = down_weight[0]
-    chosen_mask = jnp.any(routes[None, :, :] == experts[:, None, None], axis=2)
-    masked = jnp.where(chosen_mask[:, :, None], hidden[None, :, :], jnp.zeros((), jnp.bfloat16))
-    outgoing = jnp.broadcast_to(masked[:, None], (ep_count, dp_count, rows_dev, model_width))
-    outgoing = outgoing.reshape(ep_count * dp_count, rows_dev, model_width)
-    partial_out = expert_apply(
-        lax.all_to_all(outgoing, ("ep", "dp"), split_axis=0, concat_axis=0, tiled=True),
-        gate_part,
-        up_part,
-        down_part,
-    )
-    returned = lax.all_to_all(partial_out, ("ep", "dp"), split_axis=0, concat_axis=0, tiled=True)
-    expert_out = jnp.sum(
-        returned.reshape(ep_count, dp_count, rows_dev, model_width), axis=1
-    ).astype(jnp.bfloat16)
-    weight_table = jnp.sum(
-        jnp.where(routes[:, :, None] == experts, route_weight[:, :, None], 0.0), axis=1
-    )
-    expert_mix = jnp.sum(
-        weight_table.T[:, :, None] * expert_out.astype(jnp.float32), axis=0
-    ).astype(jnp.bfloat16)
+    count = ep_count * dp_count
+    rows_dev, model_width = hidden.shape
+    payload = jnp.concatenate([hidden, weight_columns(routes, route_weight, ep_count)], axis=1)
+    everyone = gather_rows(payload, count)
+    rows_in = everyone[:, :model_width]
+    table = everyone[:, model_width:].astype(jnp.float32)
+    mine = jnp.arange(table.shape[1], dtype=jnp.int32) % ep_count == lax.axis_index("ep")
+    mine = mine & (jnp.arange(table.shape[1], dtype=jnp.int32) < 2 * ep_count)
+    row_weight = jnp.sum(jnp.where(mine, table, 0.0), axis=1, keepdims=True)
+
+    gate_vals = jnp.dot(rows_in, gate_weight[0], preferred_element_type=jnp.float32)
+    up_vals = jnp.dot(rows_in, up_weight[0], preferred_element_type=jnp.float32)
+    inner_act = (jax.nn.silu(gate_vals) * up_vals).astype(jnp.bfloat16)
+    partial_out = jnp.dot(inner_act, down_weight[0], preferred_element_type=jnp.float32) * row_weight
+    expert_mix = scatter_sum(partial_out, count).astype(jnp.bfloat16)
+
     page_dest = moved_dest[0]
     page_pick = moved_page[0]
     entries = page_dest.shape[0]

time: 106 us -> 78.4 us (0.74)
  waiting for transfers between devices: 52.8 us -> 24.5 us
  local copies, waits for them, and re-layouts: 17.8 us -> 8.19 us
  other arithmetic: 5.55 us -> 10.4 us
  starting transfers between devices: 14.9 us -> 19.2 us
  matrix products: 13 us -> 14.6 us
    all_to_all x2 -> x0, waiting for transfers between devices: 52.8 us -> none  [the longest x1 31 us: body(): lax.all_to_all(partial_out, ('ep', 'dp'), split_axis=0, concat_axis=0, ti...]
    ppermute x0 -> x10, waiting for transfers between devices: none -> 19.5 us  [swap(): return lax.ppermute(x, AXES, [(i, i ^ bit) for i in range(count)])]
    ppermute x0 -> x10, starting transfers between devices: none -> 15.7 us  [swap(): return lax.ppermute(x, AXES, [(i, i ^ bit) for i in range(count)])]
    all_to_all x2 -> x0, starting transfers between devices: 11.5 us -> none  [the longest x1 7.3 us: body(): lax.all_to_all(outgoing, ('ep', 'dp'), split_axis=0, concat_axis=0, tiled...]
    all_to_all x1, waiting for transfers between devices: 0.01 us -> 5 us  [body(): lax.all_to_all(outgoing_pages, 'dp', split_axis=0, concat_axis=0, tiled=T...]
    concatenate x0 -> x5, other arithmetic: none -> 3.42 us  [the longest x3 2.56 us: gather_rows(): x = jnp.concatenate([x, swap(x, count, bit)], axis=0)]
    reshape x1 -> x0, local copies, waits for them, and re-layouts: 3.37 us -> none  [expert_apply(): flat_rows = rows_in.reshape(-1, rows_in.shape[-1])]
    dot_general x2 -> x0, local copies, waits for them, and re-layouts: 2.7 us -> none  [expert_apply(): jnp.dot(inner_act, down_part, preferred_element_type=jnp.float32)]
  transfers between devices with their start and end apart: 3 -> 11, of which waited for: 2 -> 8; matrix products, arithmetic and copies ran while one was open for 28% -> 17% of each run, Pallas kernels for 0% -> 0%
where the time goes in v1:
time: 78.4 us; the launch traced here: 77.7 us
  waiting for transfers between devices  24.5 us (31%)
  starting transfers between devices  19.2 us (24%)
  matrix products  14.6 us (19%)
  other arithmetic  10.4 us (13%)
  local copies, waits for them, and re-layouts  8.19 us (10%)
  between operations  0.88 us (1%)
    ppermute x10, waiting for transfers between devices, swap(): return lax.ppermute(x, AXES, [(i, i ^ bit) for i in range(count)])  19.5 us
    ppermute x10, starting transfers between devices, swap(): return lax.ppermute(x, AXES, [(i, i ^ bit) for i in range(count)])  15.7 us
    dot_general x1, matrix products, body(): jnp.dot(inner_act, down_weight[0], preferred_element_type=jnp.float32)  7.93 us
    all_to_all x1, waiting for transfers between devices, body(): lax.all_to_all(outgoing_pages, 'dp', split_axis=0, concat_axis=0, tiled=T...  5 us
    dot_general x1, matrix products, body(): up_vals = jnp.dot(rows_in, up_weight[0], preferred_element_type=jnp.float32)  4.45 us
    gather x2, local copies, waits for them, and re-layouts, body(): jnp.take(pool_after, page_table, axis=0).reshape(rows_dev, -1, LAT)  4.36 us
    all_to_all x1, starting transfers between devices, body(): lax.all_to_all(outgoing_pages, 'dp', split_axis=0, concat_axis=0, tiled=T...  3.45 us
    concatenate x3, other arithmetic, gather_rows(): x = jnp.concatenate([x, swap(x, count, bit)], axis=0)  2.56 us
  transfers between devices with their start and end apart: 11, of which 8 were waited for; matrix products, arithmetic and copies ran while one was open for 17% of the time, Pallas kernels for 0%

profile of v1, /device:TPU:0, one launch (start us, length us, event | category | flops | bytes accessed | tf_op | source)
XLA Modules:
  0.0 77.7 jit_solution(4311748632610542849)
XLA Ops:
  0.7 0.8 %select_reduce_fusion.1 = f32[2,8]{1,0:T(2,128)S(1)} fusion(f32[2,4]{1,0:T(2,128)} %param.14, s32[2,4]{1,0:T(2,128)} %param.13), kind=kLoop, calls=%fused_computation.47 | loop fusion | flops 176 | bytes 128 | tf_op jit(solution)/shard_map/reduce_sum | solution.py:44
  1.6 0.8 pad_maximum_fusion.4
  2.3 4.1 %collective-permute-start = (bf16[2,7296]{1,0:T(2,128)(2,1)S(1)}, bf16[2,7296]{1,0:T(2,128)(2,1)S(1)}, u32[]{:S(2)}, u32[]{:S(2)}) collective-permute-start(bf16[2,7296]{1,0:T(2,128)(2,1)S(1)} %pad_maximum_fusion.4), channel_id=1, source_target_pairs={{0,16},{1,17},{2,18},{3,19},{4,20},{5,21},{6,22},{7,23},{8,24},{9,... | collective-permute-start | bytes 87560 | tf_op jit(solution)/shard_map/ppermute | solution.py:25
  6.4 0.9 %convert_reduce_fusion = s32[6]{0:T(128)S(1)} fusion(s32[6]{0:T(128)} %bitcast.33), kind=kLoop, calls=%fused_computation.45 | loop fusion | flops 174 | bytes 48 | tf_op jit(solution)/shard_map/reduce_sum | solution.py:90
  8.6 0.8 %pad_maximum_fusion.3 = bf16[4,7296]{1,0:T(4,128)(2,1)S(1)} fusion(bf16[2,7296]{1,0:T(2,128)(2,1)S(1)} %collective-permute-done, bf16[2,128]{1,0:T(2,128)(2,1)S(1)} %fusion.28, bf16[2,7168]{1,0:T(2,128)(2,1)} %param.12), kind=kLoop, calls=%fused_computation.35 | loop fusion | flops 175104 | bytes 116736 | tf_op jit(solution)/shard_map/concatenate | solution.py:30
  9.4 1.7 %collective-permute-start.1 = (bf16[4,7296]{1,0:T(4,128)(2,1)S(1)}, bf16[4,7296]{1,0:T(4,128)(2,1)S(1)}, u32[]{:S(2)}, u32[]{:S(2)}) collective-permute-start(bf16[4,7296]{1,0:T(4,128)(2,1)S(1)} %pad_maximum_fusion.3), channel_id=1, source_target_pairs={{0,8},{1,9},{2,10},{3,11},{4,12},{5,13},{6,14},{7,15},{8,0},{9,1},... | collective-permute-start | bytes 175112 | tf_op jit(solution)/shard_map/ppermute | solution.py:25
  11.2 2.5 %collective-permute-done.1 = bf16[4,7296]{1,0:T(4,128)(2,1)S(1)} collective-permute-done((bf16[4,7296]{1,0:T(4,128)(2,1)S(1)}, bf16[4,7296]{1,0:T(4,128)(2,1)S(1)}, u32[]{:S(2)}, u32[]{:S(2)}) %collective-permute-start.1) | collective-permute-done | bytes 58400 | tf_op jit(solution)/shard_map/ppermute | solution.py:25
  13.7 0.8 %pad_maximum_fusion.2 = bf16[8,7296]{1,0:T(8,128)(2,1)S(1)} fusion(bf16[4,7296]{1,0:T(4,128)(2,1)S(1)} %collective-permute-done.1, bf16[2,7296]{1,0:T(2,128)(2,1)S(1)} %collective-permute-done, bf16[2,128]{1,0:T(2,128)(2,1)S(1)} %fusion.28, bf16[2,7168]{1,0:T(2,128)(2,1)} %param.12), kind=kLoop, calls=%fused_computation.30 | loop fusion | flops 466944 | bytes 233472 | tf_op jit(solution)/shard_map/concatenate | solution.py:30
  14.5 1.8 %collective-permute-start.2 = (bf16[8,7296]{1,0:T(8,128)(2,1)S(1)}, bf16[8,7296]{1,0:T(8,128)(2,1)S(1)}, u32[]{:S(2)}, u32[]{:S(2)}) collective-permute-start(bf16[8,7296]{1,0:T(8,128)(2,1)S(1)} %pad_maximum_fusion.2), channel_id=1, source_target_pairs={{0,4},{1,5},{2,6},{3,7},{4,0},{5,1},{6,2},{7,3},{8,12},{9,13},{10,... | collective-permute-start | bytes 350216 | tf_op jit(solution)/shard_map/ppermute | solution.py:25
  16.3 0.7 iota_compare_fusion
  17.1 2.3 %collective-permute-done.2 = bf16[8,7296]{1,0:T(8,128)(2,1)S(1)} collective-permute-done((bf16[8,7296]{1,0:T(8,128)(2,1)S(1)}, bf16[8,7296]{1,0:T(8,128)(2,1)S(1)}, u32[]{:S(2)}, u32[]{:S(2)}) %collective-permute-start.2) | collective-permute-done | bytes 116768 | tf_op jit(solution)/shard_map/ppermute | solution.py:25
  19.4 0.9 %pad_maximum_fusion.1 = bf16[16,7296]{1,0:T(8,128)(2,1)S(1)} fusion(bf16[8,7296]{1,0:T(8,128)(2,1)S(1)} %collective-permute-done.2, bf16[4,7296]{1,0:T(4,128)(2,1)S(1)} %collective-permute-done.1, bf16[2,7296]{1,0:T(2,128)(2,1)S(1)} %collective-permute-done, bf16[2,128]{1,0:T(2,128)(2,1)S(1)} %fusion.28, bf16[2,7168]{1,0:T(2,128)(2,1)} %param.12), kind=kLoop, calls=%fused_computation.25 | loop fusion | flops 1167360 | bytes 466944 | tf_op jit(solution)/shard_map/concatenate | solution.py:30
  20.3 1.8 %collective-permute-start.3 = (bf16[16,7296]{1,0:T(8,128)(2,1)S(1)}, bf16[16,7296]{1,0:T(8,128)(2,1)S(1)}, u32[]{:S(2)}, u32[]{:S(2)}) collective-permute-start(bf16[16,7296]{1,0:T(8,128)(2,1)S(1)} %pad_maximum_fusion.1), channel_id=1, source_target_pairs={{0,2},{1,3},{2,0},{3,1},{4,6},{5,7},{6,4},{7,5},{8,10},{9,11},{10,... | collective-permute-start | bytes 700424 | tf_op jit(solution)/shard_map/ppermute | solution.py:25
  22.1 1.4 %convolution_convert_fusion = bf16[8,18432]{1,0:T(8,128)(2,1)S(1)} fusion(pred[8,24]{1,0:T(8,128)(4,1)S(1)} %and_reduce_fusion, bf16[24,18432]{1,0:T(8,128)(2,1)} %param.19), kind=kOutput, calls=%fused_computation.2 | convolution fusion | flops 7225344 | bytes 1179840 | tf_op jit(solution)/shard_map/dot_general | solution.py:99
  23.5 0.9 %reshape.92 = bf16[4,2,18432]{2,1,0:T(2,128)(2,1)} reshape(bf16[8,18432]{1,0:T(8,128)(2,1)S(1)} %convolution_convert_fusion) | data formatting | bytes 589824 | tf_op jit(solution)/shard_map/reshape | solution.py:102
  24.4 3.5 %all-to-all-start = ((bf16[4,2,18432]{2,1,0:T(2,128)(2,1)}), bf16[4,2,18432]{2,1,0:T(2,128)(2,1)S(1)}, u32[]{:S(2)}, u32[]{:S(2)}) async-start(bf16[4,2,18432]{2,1,0:T(2,128)(2,1)} %reshape.92), calls=%async_computation | async-start | bytes 589824 | tf_op jit(solution)/shard_map/all_to_all | solution.py:103
  29.3 5.0 %all-to-all-done = bf16[4,2,18432]{2,1,0:T(2,128)(2,1)S(1)} async-done(((bf16[4,2,18432]{2,1,0:T(2,128)(2,1)}), bf16[4,2,18432]{2,1,0:T(2,128)(2,1)S(1)}, u32[]{:S(2)}, u32[]{:S(2)}) %all-to-all-start) | async-done | bytes 294944 | tf_op jit(solution)/shard_map/all_to_all | solution.py:103
  34.8 4.4 %fusion.2 = f32[64,512]{1,0:T(8,128)S(1)} fusion(bf16[1,7168,512]{2,1,0:T(8,128)(2,1)} %param.16, bf16[64,7296]{1,0:T(8,128)(2,1)S(1)} %concatenate.34), kind=kOutput, calls=%fused_computation.5 | convolution fusion | flops 469762048 | bytes 8388608 | tf_op jit(solution)/shard_map/dot_general | solution.py:77
  39.4 7.9 %convolution_multiply_fusion = f32[64,7168]{1,0:T(8,128)S(1)} fusion(bf16[1,512,7168]{2,1,0:T(8,128)(2,1)} %param.17, f32[64]{0:T(128)S(1)} %select_reduce_fusion, f32[64,512]{1,0:T(8,128)S(1)} %fusion.2, bf16[1,7168,512]{2,1,0:T(8,128)(2,1)} %param.15, bf16[64,7296]{1,0:T(8,128)(2,1)S(1)} %concatenate.34), kind=kOutput, calls=%fused_computation.3 | convolution fusion | flops 940179456 | bytes 17564160 | tf_op jit(solution)/shard_map/dot_general | solution.py:79
  47.3 0.8 %slice.95 = bf16[32,7168]{1,0:T(8,128)(2,1)} slice(f32[64,7168]{1,0:T(8,128)S(1)} %convolution_multiply_fusion), slice={[32:64], [0:7168]} | slice | bytes 917504 | tf_op jit(solution)/shard_map/slice | solution.py:37
  48.1 1.2 %pad_maximum_fusion = bf16[32,18432]{1,0:T(8,128)(2,1)S(1)} fusion(bf16[8,18432]{1,0:T(8,128)(2,1)S(1)} %reshape.93, bf16[24,18432]{1,0:T(8,128)(2,1)} %param.19), kind=kLoop, calls=%fused_computation.9 | loop fusion | flops 2359296 | bytes 2359296 | tf_op jit(solution)/shard_map/concatenate | solution.py:104
  49.4 2.0 %gather_fusion = bf16[24,18432]{1,0:T(8,128)(2,1)} fusion(bf16[32,18432]{1,0:T(8,128)(2,1)S(1)} %pad_maximum_fusion, s32[1024]{0:T(1024)S(1)} %pad_clamp_fusion), kind=kCustom, calls=%fused_computation | custom fusion | bytes 1769568 | tf_op jit(solution)/shard_map/jit(_take)/gather | solution.py:107
  51.4 2.3 %gather.7 = bf16[2,384,576]{2,1,0:T(8,128)(2,1)S(1)} reshape(bf16[24,18432]{1,0:T(8,128)(2,1)} %gather_fusion) | data formatting | bytes 1769472 | tf_op jit(solution)/shard_map/jit(_take)/gather | solution.py:107
  53.8 1.1 %slice_add_fusion = f32[32,7168]{1,0:T(8,128)S(1)} fusion(f32[64,7168]{1,0:T(8,128)S(1)} %convolution_multiply_fusion, bf16[32,7168]{1,0:T(8,128)(2,1)} %collective-permute-done.5), kind=kLoop, calls=%fused_computation.19 | loop fusion | flops 458752 | bytes 2293760 | tf_op jit(solution)/shard_map/add | solution.py:38
  55.5 7.4 %collective-permute-done.6 = bf16[16,7168]{1,0:T(8,128)(2,1)S(1)} collective-permute-done((bf16[16,7168]{1,0:T(8,128)(2,1)S(1)}, bf16[16,7168]{1,0:T(8,128)(2,1)S(1)}, u32[]{:S(2)}, u32[]{:S(2)}) %collective-permute-start.6) | collective-permute-done | bytes 229408 | tf_op jit(solution)/shard_map/ppermute | solution.py:25
  63.0 1.6 %collective-permute-start.7 = (bf16[8,7168]{1,0:T(8,128)(2,1)S(1)}, bf16[8,7168]{1,0:T(8,128)(2,1)S(1)}, u32[]{:S(2)}, u32[]{:S(2)}) collective-permute-start(bf16[8,7168]{1,0:T(8,128)(2,1)S(1)} %slice.97), channel_id=1, source_target_pairs={{0,4},{1,5},{2,6},{3,7},{4,0},{5,1},{6,2},{7,3},{8,12},{9,13},{10,... | collective-permute-start | bytes 344072 | tf_op jit(solution)/shard_map/ppermute | solution.py:25
  65.1 2.8 %collective-permute-done.7 = bf16[8,7168]{1,0:T(8,128)(2,1)S(1)} collective-permute-done((bf16[8,7168]{1,0:T(8,128)(2,1)S(1)}, bf16[8,7168]{1,0:T(8,128)(2,1)S(1)}, u32[]{:S(2)}, u32[]{:S(2)}) %collective-permute-start.7) | collective-permute-done | bytes 114720 | tf_op jit(solution)/shard_map/ppermute | solution.py:25
  68.0 1.4 %collective-permute-start.8 = (bf16[4,7168]{1,0:T(4,128)(2,1)S(1)}, bf16[4,7168]{1,0:T(4,128)(2,1)S(1)}, u32[]{:S(2)}, u32[]{:S(2)}) collective-permute-start(bf16[4,7168]{1,0:T(4,128)(2,1)S(1)} %slice.98), channel_id=1, source_target_pairs={{0,8},{1,9},{2,10},{3,11},{4,12},{5,13},{6,14},{7,15},{8,0},{9,1},... | collective-permute-start | bytes 172040 | tf_op jit(solution)/shard_map/ppermute | solution.py:25
  69.6 2.6 %collective-permute-done.8 = bf16[4,7168]{1,0:T(4,128)(2,1)S(1)} collective-permute-done((bf16[4,7168]{1,0:T(4,128)(2,1)S(1)}, bf16[4,7168]{1,0:T(4,128)(2,1)S(1)}, u32[]{:S(2)}, u32[]{:S(2)}) %collective-permute-start.8) | collective-permute-done | bytes 57376 | tf_op jit(solution)/shard_map/ppermute | solution.py:25
  72.3 2.5 %collective-permute-start.9 = (bf16[2,7168]{1,0:T(2,128)(2,1)S(1)}, bf16[2,7168]{1,0:T(2,128)(2,1)S(1)}, u32[]{:S(2)}, u32[]{:S(2)}) collective-permute-start(bf16[2,7168]{1,0:T(2,128)(2,1)S(1)} %slice.99), channel_id=1, source_target_pairs={{0,16},{1,17},{2,18},{3,19},{4,20},{5,21},{6,22},{7,23},{8,24},{9,... | collective-permute-start | bytes 86024 | tf_op jit(solution)/shard_map/ppermute | solution.py:25
  75.1 0.8 %copy.18 = bf16[1,2,64,512]{3,1,2,0:T(2,128)(2,1)} copy(bf16[1,2,64,512]{3,2,1,0:T(8,128)(2,1)S(1)} %fusion.10) | data formatting | bytes 262144
  75.9 1.2 %collective-permute-done.9 = bf16[2,7168]{1,0:T(2,128)(2,1)S(1)} collective-permute-done((bf16[2,7168]{1,0:T(2,128)(2,1)S(1)}, bf16[2,7168]{1,0:T(2,128)(2,1)S(1)}, u32[]{:S(2)}, u32[]{:S(2)}) %collective-permute-start.9) | collective-permute-done | bytes 28704 | tf_op jit(solution)/shard_map/ppermute | solution.py:25
  (43 shorter events, 5.9 us)
Async XLA Ops:
  0.6 27.3 %copy-start.1 = (s32[2,12]{1,0:T(2,128)S(1)}, s32[2,12]{1,0:T(2,128)}, u32[]{:S(2)}) copy-start(s32[2,12]{1,0:T(2,128)} %param.21) | copy-start | bytes 292
  0.6 28.3 %copy-start = (bf16[2,36864]{1,0:T(2,128)(2,1)S(1)}, bf16[2,36864]{1,0:T(2,128)(2,1)}, u32[]{:S(2)}) copy-start(bf16[2,36864]{1,0:T(2,128)(2,1)} %param.18) | copy-start | bytes 442372
  0.7 28.5 %copy-start.2 = (s32[2]{0:T(128)S(1)}, s32[2]{0:T(128)}, u32[]{:S(2)}) copy-start(s32[2]{0:T(128)} %param.20) | copy-start | bytes 28
  2.3 6.3 %collective-permute-start = (bf16[2,7296]{1,0:T(2,128)(2,1)S(1)}, bf16[2,7296]{1,0:T(2,128)(2,1)S(1)}, u32[]{:S(2)}, u32[]{:S(2)}) collective-permute-start(bf16[2,7296]{1,0:T(2,128)(2,1)S(1)} %pad_maximum_fusion.4), channel_id=1, source_target_pairs={{0,16},{1,17},{2,18},{3,19},{4,20},{5,21},{6,22},{7,23},{8,24},{9,... | collective-permute-start | bytes 87560 | tf_op jit(solution)/shard_map/ppermute | solution.py:25
  9.4 4.3 %collective-permute-start.1 = (bf16[4,7296]{1,0:T(4,128)(2,1)S(1)}, bf16[4,7296]{1,0:T(4,128)(2,1)S(1)}, u32[]{:S(2)}, u32[]{:S(2)}) collective-permute-start(bf16[4,7296]{1,0:T(4,128)(2,1)S(1)} %pad_maximum_fusion.3), channel_id=1, source_target_pairs={{0,8},{1,9},{2,10},{3,11},{4,12},{5,13},{6,14},{7,15},{8,0},{9,1},... | collective-permute-start | bytes 175112 | tf_op jit(solution)/shard_map/ppermute | solution.py:25
  14.5 4.9 %collective-permute-start.2 = (bf16[8,7296]{1,0:T(8,128)(2,1)S(1)}, bf16[8,7296]{1,0:T(8,128)(2,1)S(1)}, u32[]{:S(2)}, u32[]{:S(2)}) collective-permute-start(bf16[8,7296]{1,0:T(8,128)(2,1)S(1)} %pad_maximum_fusion.2), channel_id=1, source_target_pairs={{0,4},{1,5},{2,6},{3,7},{4,0},{5,1},{6,2},{7,3},{8,12},{9,13},{10,... | collective-permute-start | bytes 350216 | tf_op jit(solution)/shard_map/ppermute | solution.py:25
  20.3 7.6 %collective-permute-start.3 = (bf16[16,7296]{1,0:T(8,128)(2,1)S(1)}, bf16[16,7296]{1,0:T(8,128)(2,1)S(1)}, u32[]{:S(2)}, u32[]{:S(2)}) collective-permute-start(bf16[16,7296]{1,0:T(8,128)(2,1)S(1)} %pad_maximum_fusion.1), channel_id=1, source_target_pairs={{0,2},{1,3},{2,0},{3,1},{4,6},{5,7},{6,4},{7,5},{8,10},{9,11},{10,... | collective-permute-start | bytes 700424 | tf_op jit(solution)/shard_map/ppermute | solution.py:25
  24.4 9.8 %all-to-all-start = ((bf16[4,2,18432]{2,1,0:T(2,128)(2,1)}), bf16[4,2,18432]{2,1,0:T(2,128)(2,1)S(1)}, u32[]{:S(2)}, u32[]{:S(2)}) async-start(bf16[4,2,18432]{2,1,0:T(2,128)(2,1)} %reshape.92), calls=%async_computation | async-start | bytes 589824 | tf_op jit(solution)/shard_map/all_to_all | solution.py:103
  28.2 6.2 %collective-permute-start.4 = (bf16[32,7296]{1,0:T(8,128)(2,1)S(1)}, bf16[32,7296]{1,0:T(8,128)(2,1)S(1)}, u32[]{:S(2)}, u32[]{:S(2)}) collective-permute-start(bf16[32,7296]{1,0:T(8,128)(2,1)S(1)} %concatenate.33), channel_id=1, source_target_pairs={{0,1},{1,0},{2,3},{3,2},{4,5},{5,4},{6,7},{7,6},{8,9},{9,8},{10,11... | collective-permute-start | bytes 1400840 | tf_op jit(solution)/shard_map/ppermute | solution.py:25
  48.1 5.6 %collective-permute-start.5 = (bf16[32,7168]{1,0:T(8,128)(2,1)}, bf16[32,7168]{1,0:T(8,128)(2,1)}, u32[]{:S(2)}, u32[]{:S(2)}) collective-permute-start(bf16[32,7168]{1,0:T(8,128)(2,1)} %slice.95), channel_id=1, source_target_pairs={{0,1},{1,0},{2,3},{3,2},{4,5},{5,4},{6,7},{7,6},{8,9},{9,8},{10,11... | collective-permute-start | bytes 1376264 | tf_op jit(solution)/shard_map/ppermute | solution.py:25
  54.9 8.1 %collective-permute-start.6 = (bf16[16,7168]{1,0:T(8,128)(2,1)S(1)}, bf16[16,7168]{1,0:T(8,128)(2,1)S(1)}, u32[]{:S(2)}, u32[]{:S(2)}) collective-permute-start(bf16[16,7168]{1,0:T(8,128)(2,1)S(1)} %slice.96), channel_id=1, source_target_pairs={{0,2},{1,3},{2,0},{3,1},{4,6},{5,7},{6,4},{7,5},{8,10},{9,11},{10,... | collective-permute-start | bytes 688136 | tf_op jit(solution)/shard_map/ppermute | solution.py:25
  63.0 4.9 %collective-permute-start.7 = (bf16[8,7168]{1,0:T(8,128)(2,1)S(1)}, bf16[8,7168]{1,0:T(8,128)(2,1)S(1)}, u32[]{:S(2)}, u32[]{:S(2)}) collective-permute-start(bf16[8,7168]{1,0:T(8,128)(2,1)S(1)} %slice.97), channel_id=1, source_target_pairs={{0,4},{1,5},{2,6},{3,7},{4,0},{5,1},{6,2},{7,3},{8,12},{9,13},{10,... | collective-permute-start | bytes 344072 | tf_op jit(solution)/shard_map/ppermute | solution.py:25
  68.0 4.2 %collective-permute-start.8 = (bf16[4,7168]{1,0:T(4,128)(2,1)S(1)}, bf16[4,7168]{1,0:T(4,128)(2,1)S(1)}, u32[]{:S(2)}, u32[]{:S(2)}) collective-permute-start(bf16[4,7168]{1,0:T(4,128)(2,1)S(1)} %slice.98), channel_id=1, source_target_pairs={{0,8},{1,9},{2,10},{3,11},{4,12},{5,13},{6,14},{7,15},{8,0},{9,1},... | collective-permute-start | bytes 172040 | tf_op jit(solution)/shard_map/ppermute | solution.py:25
  72.3 4.8 %collective-permute-start.9 = (bf16[2,7168]{1,0:T(2,128)(2,1)S(1)}, bf16[2,7168]{1,0:T(2,128)(2,1)S(1)}, u32[]{:S(2)}, u32[]{:S(2)}) collective-permute-start(bf16[2,7168]{1,0:T(2,128)(2,1)S(1)} %slice.99), channel_id=1, source_target_pairs={{0,16},{1,17},{2,18},{3,19},{4,20},{5,21},{6,22},{7,23},{8,24},{9,... | collective-permute-start | bytes 86024 | tf_op jit(solution)/shard_map/ppermute | solution.py:25

commit v2 on v1

v2 whole, which is shorter than its diff:
```python
import functools

import jax
import jax.numpy as jnp
from jax import lax
from jax.experimental import pallas as pl
from jax.experimental.pallas import tpu as pltpu
from jax.sharding import PartitionSpec as P

HEADS = 64
LAT = 576
VL = 512
MCAP = 2
PAGE = 32
LANES = 128
AXES = ("ep", "dp")
MIB = 1 << 20

score_scale = 192.0 ** (-0.5)
bf16 = jnp.bfloat16
f32 = jnp.float32


def in_vmem():
    return pl.BlockSpec(memory_space=pltpu.VMEM)


def in_smem():
    return pl.BlockSpec(memory_space=pltpu.SMEM)


def vmem(x):
    return pltpu.with_memory_space_constraint(x, pltpu.VMEM)


def partner_bits(count):
    bits = []
    b = count // 2
    while b:
        bits.append(b)
        b //= 2
    return bits


def swap(x, axes, count, bit):
    return lax.ppermute(x, axes, [(i, i ^ bit) for i in range(count)])


def payload_kernel(ep_count, hidden_ref, routes_ref, weight_ref, out_ref):
    rows, width = hidden_ref.shape
    out_ref[:, :width] = hidden_ref[...]
    column = lax.broadcasted_iota(jnp.int32, (rows, LANES), 1)
    expert = jnp.where(column < ep_count, column, column - ep_count)
    total = jnp.zeros((rows, LANES), f32)
    for k in range(routes_ref.shape[1]):
        total += jnp.where(routes_ref[:, k : k + 1] == expert, weight_ref[:, k : k + 1], 0.0)
    high = total.astype(bf16).astype(f32)
    low = total - high
    value = jnp.where(column < ep_count, high, jnp.where(column < 2 * ep_count, low, 0.0))
    out_ref[:, width:] = value.astype(bf16)


def make_payload(hidden, routes, route_weight, ep_count):
    rows, width = hidden.shape
    return pl.pallas_call(
        functools.partial(payload_kernel, ep_count),
        out_shape=jax.ShapeDtypeStruct((rows, width + LANES), bf16),
        in_specs=[in_vmem()] * 3,
        out_specs=in_vmem(),
        cost_estimate=pl.CostEstimate(flops=0, bytes_accessed=4 * rows * width, transcendentals=0),
    )(hidden, routes, route_weight)


def expert_kernel(ep_count, step, near_ref, far_ref, gate_ref, up_ref, down_ref, keep_ref, send_ref, gate_acc, up_acc):
    half = near_ref.shape[0]
    width, hidden_units = gate_ref.shape[1], gate_ref.shape[2]
    ep = lax.axis_index("ep")

    def rows_at(columns):
        return jnp.concatenate([near_ref[:, columns], far_ref[:, columns]], axis=0)

    table = rows_at(slice(width, width + LANES)).astype(f32)
    column = lax.broadcasted_iota(jnp.int32, table.shape, 1)
    mine = (column == ep) | (column == ep + ep_count)
    row_weight = jnp.sum(jnp.where(mine, table, 0.0), axis=1, keepdims=True)

    gate_acc[...] = jnp.zeros_like(gate_acc)
    up_acc[...] = jnp.zeros_like(up_acc)

    @pl.loop(0, width // step)
    def _(i):
        columns = pl.ds(pl.multiple_of(i * step, step), step)
        x = rows_at(columns)
        gate_acc[...] += jnp.dot(x, gate_ref[0, columns, :], preferred_element_type=f32)
        up_acc[...] += jnp.dot(x, up_ref[0, columns, :], preferred_element_type=f32)

    gate = gate_acc[...]
    inner = (gate / (1.0 + jnp.exp(-gate)) * up_acc[...]).astype(bf16)

    @pl.loop(0, width // step)
    def _(i):
        columns = pl.ds(pl.multiple_of(i * step, step), step)
        out = jnp.dot(inner, down_ref[0, :, columns], preferred_element_type=f32) * row_weight
        keep_ref[:, columns] = out[:half]
        send_ref[:, columns] = out[half:].astype(bf16)


def run_experts(near, far, gate_weight, up_weight, down_weight, ep_count):
    half = near.shape[0]
    width, units = gate_weight.shape[1], gate_weight.shape[2]
    step = 1024
    return pl.pallas_call(
        functools.partial(expert_kernel, ep_count, step),
        out_shape=(jax.ShapeDtypeStruct((half, width), f32), jax.ShapeDtypeStruct((half, width), bf16)),
        in_specs=[in_vmem()] * 5,
        out_specs=(in_vmem(), in_vmem()),
        scratch_shapes=[pltpu.VMEM((2 * half, units), f32), pltpu.VMEM((2 * half, units), f32)],
        compiler_params=pltpu.CompilerParams(vmem_limit_bytes=40 * MIB),
        cost_estimate=pl.CostEstimate(
            flops=12 * half * width * units, bytes_accessed=6 * width * units, transcendentals=2 * half * units
        ),
    )(near, far, vmem(gate_weight), vmem(up_weight), vmem(down_weight))


def pages_kernel(dp_count, page_ref, dest_ref, pool_ref, low_ref, high_ref):
    own, width = pool_ref.shape
    me = lax.axis_index("dp")
    slots = dp_count * MCAP
    row = lax.broadcasted_iota(jnp.int32, (slots, own), 0)
    column = lax.broadcasted_iota(jnp.int32, (slots, own), 1)
    pick = jnp.zeros((slots, own), f32)
    entries = page_ref.shape[1]
    for m in range(entries):
        rank = jnp.int32(0)
        for n in range(m):
            rank += jnp.where(dest_ref[0, n] == dest_ref[0, m], 1, 0)
        bucket = jnp.bitwise_xor(dest_ref[0, m], me) * MCAP + rank
        pick = jnp.where((row == bucket) & (column == page_ref[0, m]), 1.0, pick)
    pick = pick.astype(bf16)
    step = 2048

    @pl.loop(0, width // step)
    def _(i):
        columns = pl.ds(pl.multiple_of(i * step, step), step)
        out = jnp.dot(pick, pool_ref[:, columns], preferred_element_type=f32)
        low_ref[:, columns] = out[: slots // 2].astype(bf16)
        high_ref[:, columns] = out[slots // 2 :].astype(bf16)


def pick_pages(moved_page, moved_dest, latent_pool, dp_count):
    width = latent_pool.shape[1]
    half = jax.ShapeDtypeStruct((dp_count * MCAP // 2, width), bf16)
    return pl.pallas_call(
        functools.partial(pages_kernel, dp_count),
        out_shape=(half, half),
        in_specs=[in_smem(), in_smem(), in_vmem()],
        out_specs=(in_vmem(), in_vmem()),
        cost_estimate=pl.CostEstimate(flops=0, bytes_accessed=4 * latent_pool.size, transcendentals=0),
    )(moved_page, moved_dest, latent_pool)


def exchange_pages(low, high, dp_count):
    blocks, senders = [low], [0]
    sent = high
    for bit in partner_bits(dp_count):
        got = swap(sent, "dp", dp_count, bit)
        size = got.shape[0] // len(blocks)
        blocks = blocks + [got[i * size : (i + 1) * size] for i in range(len(blocks))]
        senders = senders + [s ^ bit for s in senders]
        if size > MCAP:
            sent = jnp.concatenate([b[size // 2 :] for b in blocks], axis=0)
            blocks = [b[: size // 2] for b in blocks]
    return jnp.concatenate(blocks, axis=0), senders


def attend_kernel(senders, length_ref, table_ref, query_ref, pool_ref, arrived_ref, out_ref, query_rows):
    rows_dev = query_ref.shape[0]
    own, width = pool_ref.shape
    arrived = arrived_ref.shape[0]
    slots = -(-(own + arrived) // 16) * 16
    pair_width = 2 * LAT
    pairs = width // pair_width
    me = lax.axis_index("dp")

    for h in range(HEADS // 2):
        query_rows[h * rows_dev : (h + 1) * rows_dev, :] = query_ref[:, h * pair_width : (h + 1) * pair_width].astype(f32)
    straight = query_rows[...]
    turned = pltpu.roll(straight, LAT, 1)
    first = lax.broadcasted_iota(jnp.int32, straight.shape, 1) < LAT
    query_all = jnp.concatenate(
        [
            jnp.where(first, straight, 0.0),
            jnp.where(first, turned, 0.0),
            jnp.where(first, 0.0, turned),
            jnp.where(first, 0.0, straight),
        ],
        axis=0,
    ).astype(bf16)

    pieces = []
    for j in range(pairs):
        columns = slice(j * pair_width, (j + 1) * pair_width)
        parts = [pool_ref[:, columns].astype(f32), arrived_ref[:, columns].astype(f32)]
        if slots > own + arrived:
            parts.append(jnp.zeros((slots - own - arrived, pair_width), f32))
        pieces.append(jnp.concatenate(parts, axis=0).astype(bf16))
    keys = jnp.concatenate(pieces, axis=0)

    scores = lax.dot_general(query_all, keys, (((1,), (1,)), ((), ())), preferred_element_type=f32) * score_scale

    column = lax.broadcasted_iota(jnp.int32, (1, pairs * slots), 1)
    pair = column // slots
    place = column - pair * slots
    slot = place
    for i, s in enumerate(senders):
        source = jnp.bitwise_xor(me, s)
        for k in range(MCAP):
            slot = jnp.where(place == own + i * MCAP + k, own + source * MCAP + k, slot)
    limits = []
    for r in range(rows_dev):
        limit = jnp.full(column.shape, -1, jnp.int32)
        for p in range(table_ref.shape[1]):
            limit = jnp.where(slot == table_ref[r, p], length_ref[r] - p * PAGE, limit)
        limit = jnp.where(place < own + arrived, limit, -1)
        limits.append(limit - 2 * pair)
    half = scores.shape[0] // 2
    row = lax.broadcasted_iota(jnp.int32, (half, 1), 0) % rows_dev
    limit = limits[0]
    for r in range(1, rows_dev):
        limit = jnp.where(row == r, limits[r], limit)
    even = jnp.where(limit > 0, scores[:half], -jnp.inf)
    odd = jnp.where(limit > 1, scores[half:], -jnp.inf)
    peak = jnp.maximum(jnp.max(even, axis=1, keepdims=True), jnp.max(odd, axis=1, keepdims=True))
    even = jnp.exp(even - peak)
    odd = jnp.exp(odd - peak)
    total = jnp.sum(even, axis=1, keepdims=True) + jnp.sum(odd, axis=1, keepdims=True)
    even = (even / total).astype(bf16)
    odd = (odd / total).astype(bf16)
    from_even = jnp.dot(even, keys[:, :VL], preferred_element_type=f32)
    from_odd = jnp.dot(odd, keys[:, VL:], preferred_element_type=f32)
    shift = LAT - VL
    wide = pair_width - VL
    attended = from_even + pltpu.roll(from_odd, wide - shift, 1)[:, :VL]
    for h in range(HEADS):
        at = (h % 2) * (half // 2) + (h // 2) * rows_dev
        out_ref[:, h * VL : (h + 1) * VL] = attended[at : at + rows_dev].astype(bf16)


def attend(lengths, page_table, queries, latent_pool, arrived, senders):
    rows_dev = queries.shape[0]
    return pl.pallas_call(
        functools.partial(attend_kernel, senders),
        out_shape=jax.ShapeDtypeStruct((rows_dev, HEADS * VL), bf16),
        in_specs=[in_smem(), in_smem(), in_vmem(), in_vmem(), in_vmem()],
        out_specs=in_vmem(),
        scratch_shapes=[pltpu.VMEM((HEADS // 2 * rows_dev, 2 * LAT), f32)],
        compiler_params=pltpu.CompilerParams(vmem_limit_bytes=24 * MIB),
        cost_estimate=pl.CostEstimate(flops=1 << 30, bytes_accessed=4 << 20, transcendentals=1 << 17),
    )(lengths, page_table, queries, latent_pool, arrived)


def body(
    hidden,
    routes,
    route_weight,
    gate_weight,
    up_weight,
    down_weight,
    queries,
    latent_pool,
    lengths,
    page_table,
    moved_page,
    moved_dest,
):
    ep_count = lax.axis_size("ep")
    dp_count = lax.axis_size("dp")
    count = ep_count * dp_count
    bits = partner_bits(count)

    near = make_payload(hidden, routes, route_weight, ep_count)
    for bit in bits[:-1]:
        near = jnp.concatenate([near, swap(near, AXES, count, bit)], axis=0)
    far = swap(near, AXES, count, bits[-1])

    low, high = pick_pages(moved_page, moved_dest, latent_pool, dp_count)
    arrived, senders = exchange_pages(low, high, dp_count)
    attended = attend(lengths, page_table, queries, latent_pool, arrived, senders)

    keep, send = run_experts(near, far, gate_weight, up_weight, down_weight, ep_count)
    for bit in reversed(bits):
        keep = keep + swap(send, AXES, count, bit).astype(f32)
        half = keep.shape[0] // 2
        if bit != bits[0]:
            send = keep[half:].astype(bf16)
            keep = keep[:half]
    return keep.astype(bf16), attended


def solution(mesh):
    rows = P(("inst", "ep", "dp"), None)
    in_specs = (
        rows,
        rows,
        rows,
        P("ep", None, "dp"),
        P("ep", None, "dp"),
        P("ep", "dp", None),
        rows,
        rows,
        P(("inst", "ep", "dp")),
        rows,
        rows,
        rows,
    )
    return jax.shard_map(body, mesh=mesh, in_specs=in_specs, out_specs=(rows, rows), check_vma=False)
```

time: 78.4 us -> 77.3 us (0.986)
  Pallas kernels: 0 us -> 15.1 us
  matrix products: 14.6 us -> 0 us
  other arithmetic: 10.4 us -> 4.97 us
  local copies, waits for them, and re-layouts: 8.19 us -> 11.3 us
  waiting for transfers between devices: 24.5 us -> 26.1 us
  starting transfers between devices: 19.2 us -> 18.4 us
    pallas_call x0 -> x4, Pallas kernels: none -> 15.1 us  [the longest x1 7.96 us: run_experts(): pl.pallas_call(functools.partial(expert_kernel, ep_count, step), out_shap...]
    dot_general x5 -> x0, matrix products: 14.6 us -> none  [the longest x1 7.93 us: body(): jnp.dot(inner_act, down_weight[0], preferred_element_type=jnp.float32)]
    unnamed x7 -> x20, local copies, waits for them, and re-layouts: 0.81 us -> 10 us
    ppermute x10 -> x12, waiting for transfers between devices: 19.5 us -> 26.1 us  [swap(): return lax.ppermute(x, axes, [(i, i ^ bit) for i in range(count)])]
    all_to_all x1 -> x0, waiting for transfers between devices: 5 us -> none  [body(): lax.all_to_all(outgoing_pages, 'dp', split_axis=0, concat_axis=0, tiled=T...]
    gather x2 -> x0, local copies, waits for them, and re-layouts: 4.36 us -> none  [body(): jnp.take(pool_after, page_table, axis=0).reshape(rows_dev, -1, LAT)]
    all_to_all x1 -> x0, starting transfers between devices: 3.45 us -> none  [body(): lax.all_to_all(outgoing_pages, 'dp', split_axis=0, concat_axis=0, tiled=T...]
    ppermute x10 -> x12, starting transfers between devices: 15.7 us -> 18.4 us  [swap(): return lax.ppermute(x, axes, [(i, i ^ bit) for i in range(count)])]
  transfers between devices with their start and end apart: 11 -> 12, of which waited for: 8 -> 8; matrix products, arithmetic and copies ran while one was open for 17% -> 3% of each run, Pallas kernels for 0% -> 18%
where the time goes in v2:
time: 77.3 us; the launch traced here: 76.6 us
  waiting for transfers between devices  26.1 us (34%)
  starting transfers between devices  18.4 us (24%)
  Pallas kernels  15.1 us (20%)
  local copies, waits for them, and re-layouts  11.3 us (15%)
  other arithmetic  4.97 us (6%)
    ppermute x12, waiting for transfers between devices, swap(): return lax.ppermute(x, axes, [(i, i ^ bit) for i in range(count)])  26.1 us
    ppermute x12, starting transfers between devices, swap(): return lax.ppermute(x, axes, [(i, i ^ bit) for i in range(count)])  18.4 us
    unnamed x20, local copies, waits for them, and re-layouts  10 us
    pallas_call x1, Pallas kernels, run_experts(): pl.pallas_call(functools.partial(expert_kernel, ep_count, step), out_shap...  7.96 us
    pallas_call x1, Pallas kernels, pick_pages(): pl.pallas_call(functools.partial(pages_kernel, dp_count), out_shape=(half...  3.33 us
    concatenate x3, other arithmetic, body(): near = jnp.concatenate([near, swap(near, AXES, count, bit)], axis=0)  2.57 us
    pallas_call x1, Pallas kernels, attend(): pl.pallas_call(functools.partial(attend_kernel, senders), out_shape=jax.S...  2.35 us
  transfers between devices with their start and end apart: 12, of which 8 were waited for; matrix products, arithmetic and copies ran while one was open for 3% of the time, Pallas kernels for 18%

profile of v2, /device:TPU:0, one launch (start us, length us, event | category | flops | bytes accessed | tf_op | source)
XLA Modules:
  0.0 76.6 jit_solution(16820490060324067905)
XLA Ops:
  0.6 1.5 %shard_map.131 = bf16[2,7296]{1,0:T(2,128)(2,1)} custom-call(bf16[2,7168]{1,0:T(2,128)(2,1)} %hidden_ref.1, s32[2,4]{1,0:T(2,128)} %routes_ref.1, f32[2,4]{1,0:T(2,128)} %weight_ref.1), custom_call_target="tpu_custom_call" | custom-call | bytes 57344 | tf_op jit(solution)/shard_map/pallas_call | solution.py:65
  2.1 4.0 %collective-permute-start = (bf16[2,7296]{1,0:T(2,128)(2,1)}, bf16[2,7296]{1,0:T(2,128)(2,1)S(1)}, u32[]{:S(2)}, u32[]{:S(2)}) collective-permute-start(bf16[2,7296]{1,0:T(2,128)(2,1)} %shard_map.131), channel_id=1, source_target_pairs={{0,16},{1,17},{2,18},{3,19},{4,20},{5,21},{6,22},{7,23},{8,24},{9,... | collective-permute-start | bytes 87560 | tf_op jit(solution)/shard_map/ppermute | solution.py:46
  6.1 2.1 %collective-permute-done = bf16[2,7296]{1,0:T(2,128)(2,1)S(1)} collective-permute-done((bf16[2,7296]{1,0:T(2,128)(2,1)}, bf16[2,7296]{1,0:T(2,128)(2,1)S(1)}, u32[]{:S(2)}, u32[]{:S(2)}) %collective-permute-start) | collective-permute-done | bytes 29216 | tf_op jit(solution)/shard_map/ppermute | solution.py:46
  8.2 0.8 %pad_maximum_fusion.4 = bf16[4,7296]{1,0:T(4,128)(2,1)S(1)} fusion(bf16[2,7296]{1,0:T(2,128)(2,1)S(1)} %collective-permute-done, bf16[2,7296]{1,0:T(2,128)(2,1)} %shard_map.131), kind=kLoop, calls=%fused_computation.11 | loop fusion | flops 116736 | bytes 116736 | tf_op jit(solution)/shard_map/concatenate | solution.py:283
  9.0 2.0 %collective-permute-start.1 = (bf16[4,7296]{1,0:T(4,128)(2,1)S(1)}, bf16[4,7296]{1,0:T(4,128)(2,1)S(1)}, u32[]{:S(2)}, u32[]{:S(2)}) collective-permute-start(bf16[4,7296]{1,0:T(4,128)(2,1)S(1)} %pad_maximum_fusion.4), channel_id=1, source_target_pairs={{0,8},{1,9},{2,10},{3,11},{4,12},{5,13},{6,14},{7,15},{8,0},{9,1},... | collective-permute-start | bytes 175112 | tf_op jit(solution)/shard_map/ppermute | solution.py:46
  11.0 2.3 %collective-permute-done.1 = bf16[4,7296]{1,0:T(4,128)(2,1)S(1)} collective-permute-done((bf16[4,7296]{1,0:T(4,128)(2,1)S(1)}, bf16[4,7296]{1,0:T(4,128)(2,1)S(1)}, u32[]{:S(2)}, u32[]{:S(2)}) %collective-permute-start.1) | collective-permute-done | bytes 58400 | tf_op jit(solution)/shard_map/ppermute | solution.py:46
  13.3 0.8 %pad_maximum_fusion.3 = bf16[8,7296]{1,0:T(8,128)(2,1)S(1)} fusion(bf16[4,7296]{1,0:T(4,128)(2,1)S(1)} %collective-permute-done.1, bf16[2,7296]{1,0:T(2,128)(2,1)S(1)} %collective-permute-done, bf16[2,7296]{1,0:T(2,128)(2,1)} %shard_map.131), kind=kLoop, calls=%fused_computation.8 | loop fusion | flops 350208 | bytes 233472 | tf_op jit(solution)/shard_map/concatenate | solution.py:283
  14.1 2.1 %collective-permute-start.2 = (bf16[8,7296]{1,0:T(8,128)(2,1)S(1)}, bf16[8,7296]{1,0:T(8,128)(2,1)S(1)}, u32[]{:S(2)}, u32[]{:S(2)}) collective-permute-start(bf16[8,7296]{1,0:T(8,128)(2,1)S(1)} %pad_maximum_fusion.3), channel_id=1, source_target_pairs={{0,4},{1,5},{2,6},{3,7},{4,0},{5,1},{6,2},{7,3},{8,12},{9,13},{10,... | collective-permute-start | bytes 350216 | tf_op jit(solution)/shard_map/ppermute | solution.py:46
  16.2 2.8 %collective-permute-done.2 = bf16[8,7296]{1,0:T(8,128)(2,1)S(1)} collective-permute-done((bf16[8,7296]{1,0:T(8,128)(2,1)S(1)}, bf16[8,7296]{1,0:T(8,128)(2,1)S(1)}, u32[]{:S(2)}, u32[]{:S(2)}) %collective-permute-start.2) | collective-permute-done | bytes 116768 | tf_op jit(solution)/shard_map/ppermute | solution.py:46
  19.0 0.9 %pad_maximum_fusion.1 = bf16[16,7296]{1,0:T(8,128)(2,1)S(1)} fusion(bf16[8,7296]{1,0:T(8,128)(2,1)S(1)} %collective-permute-done.2, bf16[4,7296]{1,0:T(4,128)(2,1)S(1)} %collective-permute-done.1, bf16[2,7296]{1,0:T(2,128)(2,1)S(1)} %collective-permute-done, bf16[2,7296]{1,0:T(2,128)(2,1)} %shard_map.131), kind=kLoop, calls=%fused_computation.4 | loop fusion | flops 933888 | bytes 466944 | tf_op jit(solution)/shard_map/concatenate | solution.py:283
  19.9 2.1 %collective-permute-start.3 = (bf16[16,7296]{1,0:T(8,128)(2,1)S(1)}, bf16[16,7296]{1,0:T(8,128)(2,1)S(1)}, u32[]{:S(2)}, u32[]{:S(2)}) collective-permute-start(bf16[16,7296]{1,0:T(8,128)(2,1)S(1)} %pad_maximum_fusion.1), channel_id=1, source_target_pairs={{0,2},{1,3},{2,0},{3,1},{4,6},{5,7},{6,4},{7,5},{8,10},{9,11},{10,... | collective-permute-start | bytes 700424 | tf_op jit(solution)/shard_map/ppermute | solution.py:46
  22.0 4.1 %collective-permute-done.3 = bf16[16,7296]{1,0:T(8,128)(2,1)S(1)} collective-permute-done((bf16[16,7296]{1,0:T(8,128)(2,1)S(1)}, bf16[16,7296]{1,0:T(8,128)(2,1)S(1)}, u32[]{:S(2)}, u32[]{:S(2)}) %collective-permute-start.3) | collective-permute-done | bytes 233504 | tf_op jit(solution)/shard_map/ppermute | solution.py:46
  26.1 1.0 %concatenate.24.near_ref = bf16[32,7296]{1,0:T(8,128)(2,1)S(1)} concatenate(bf16[2,7296]{1,0:T(2,128)(2,1)} %shard_map.131, bf16[2,7296]{1,0:T(2,128)(2,1)S(1)} %collective-permute-done, bf16[4,7296]{1,0:T(4,128)(2,1)S(1)} %collective-permute-done.1, bf16[8,7296]{1,0:T(8,128)(2,1)S(1)} %collective-permute-done.2, bf16[16,7296]{1,0:T(8,128)(2,1)S(1)} %collective-permute-done.3), dimensions={0} | concatenate | bytes 933888 | tf_op jit(solution)/shard_map/concatenate | solution.py:283
  27.1 3.3 %shard_map.133 = (bf16[4,18432]{1,0:T(4,128)(2,1)}, bf16[4,18432]{1,0:T(4,128)(2,1)}) custom-call(s32[1,6]{1,0:T(1,128)} %page_ref.1, s32[1,6]{1,0:T(1,128)} %dest_ref.1, bf16[24,18432]{1,0:T(8,128)(2,1)} %pool_ref.3), custom_call_target="tpu_custom_call" | custom-call | bytes 1769472 | tf_op jit(solution)/shard_map/pallas_call | solution.py:153
  30.5 2.0 %collective-permute-start.10 = (bf16[4,18432]{1,0:T(4,128)(2,1)}, bf16[4,18432]{1,0:T(4,128)(2,1)S(1)}, u32[]{:S(2)}, u32[]{:S(2)}) collective-permute-start(bf16[4,18432]{1,0:T(4,128)(2,1)} %get-tuple-element.9), channel_id=1, source_target_pairs={{0,2},{1,3},{2,0},{3,1},{4,6},{5,7},{6,4},{7,5},{8,10},{9,11},{10,... | collective-permute-start | bytes 442376 | tf_op jit(solution)/shard_map/ppermute | solution.py:46
  32.5 0.8 %copy-done.8 = bf16[32,7296]{1,0:T(8,128)(2,1)} copy-done((bf16[32,7296]{1,0:T(8,128)(2,1)}, bf16[32,7296]{1,0:T(8,128)(2,1)S(1)}, u32[]{:S(2)}) %copy-start.8) | copy-done | bytes 466968
  33.3 3.1 %copy-done = bf16[1,7168,512]{2,1,0:T(8,128)(2,1)S(1)} copy-done((bf16[1,7168,512]{2,1,0:T(8,128)(2,1)S(1)}, bf16[1,7168,512]{2,1,0:T(8,128)(2,1)}, u32[]{:S(2)}) %copy-start) | copy-done | bytes 7340056
  36.3 3.1 %copy-done.1 = bf16[1,7168,512]{2,1,0:T(8,128)(2,1)S(1)} copy-done((bf16[1,7168,512]{2,1,0:T(8,128)(2,1)S(1)}, bf16[1,7168,512]{2,1,0:T(8,128)(2,1)}, u32[]{:S(2)}) %copy-start.1) | copy-done | bytes 7340056
  39.4 3.1 %copy-done.2 = bf16[1,512,7168]{2,1,0:T(8,128)(2,1)S(1)} copy-done((bf16[1,512,7168]{2,1,0:T(8,128)(2,1)S(1)}, bf16[1,512,7168]{2,1,0:T(8,128)(2,1)}, u32[]{:S(2)}) %copy-start.2) | copy-done | bytes 7340056
  42.5 8.0 %shard_map.132 = (f32[32,7168]{1,0:T(8,128)}, bf16[32,7168]{1,0:T(8,128)(2,1)}) custom-call(bf16[32,7296]{1,0:T(8,128)(2,1)} %copy-done.7, bf16[32,7296]{1,0:T(8,128)(2,1)} %copy-done.8, bf16[1,7168,512]{2,1,0:T(8,128)(2,1)S(1)} %copy-done, bf16[1,7168,512]{2,1,0:T(8,128)(2,1)S(1)} %copy-done.1, bf16[1,512,7168]{2,1,0:T(8,128)(2,1)S(1)} %copy-done.2), custom_call_target="tpu_custom_call" | custom-call | flops 1409286144 | bytes 22020096 | tf_op jit(solution)/shard_map/pallas_call | solution.py:112
  50.7 1.8 %collective-permute-done.5 = bf16[32,7168]{1,0:T(8,128)(2,1)S(1)} collective-permute-done((bf16[32,7168]{1,0:T(8,128)(2,1)}, bf16[32,7168]{1,0:T(8,128)(2,1)S(1)}, u32[]{:S(2)}, u32[]{:S(2)}) %collective-permute-start.5) | collective-permute-done | bytes 458784 | tf_op jit(solution)/shard_map/ppermute | solution.py:46
  52.5 1.3 %convert_add_fusion = f32[32,7168]{1,0:T(8,128)S(1)} fusion(f32[32,7168]{1,0:T(8,128)} %get-tuple-element.6, bf16[32,7168]{1,0:T(8,128)(2,1)S(1)} %collective-permute-done.5), kind=kLoop, calls=%fused_computation | loop fusion | flops 458752 | bytes 2293760 | tf_op jit(solution)/shard_map/add | solution.py:292
  54.0 7.5 %collective-permute-done.6 = bf16[16,7168]{1,0:T(8,128)(2,1)S(1)} collective-permute-done((bf16[16,7168]{1,0:T(8,128)(2,1)S(1)}, bf16[16,7168]{1,0:T(8,128)(2,1)S(1)}, u32[]{:S(2)}, u32[]{:S(2)}) %collective-permute-start.6) | collective-permute-done | bytes 229408 | tf_op jit(solution)/shard_map/ppermute | solution.py:46
  61.6 1.6 %collective-permute-start.7 = (bf16[8,7168]{1,0:T(8,128)(2,1)S(1)}, bf16[8,7168]{1,0:T(8,128)(2,1)S(1)}, u32[]{:S(2)}, u32[]{:S(2)}) collective-permute-start(bf16[8,7168]{1,0:T(8,128)(2,1)S(1)} %slice.76), channel_id=1, source_target_pairs={{0,4},{1,5},{2,6},{3,7},{4,0},{5,1},{6,2},{7,3},{8,12},{9,13},{10,... | collective-permute-start | bytes 344072 | tf_op jit(solution)/shard_map/ppermute | solution.py:46
  63.2 0.2 pad_maximum_fusion.2
  63.4 3.0 %collective-permute-done.7 = bf16[8,7168]{1,0:T(8,128)(2,1)S(1)} collective-permute-done((bf16[8,7168]{1,0:T(8,128)(2,1)S(1)}, bf16[8,7168]{1,0:T(8,128)(2,1)S(1)}, u32[]{:S(2)}, u32[]{:S(2)}) %collective-permute-start.7) | collective-permute-done | bytes 114720 | tf_op jit(solution)/shard_map/ppermute | solution.py:46
  66.5 1.4 %collective-permute-start.8 = (bf16[4,7168]{1,0:T(4,128)(2,1)S(1)}, bf16[4,7168]{1,0:T(4,128)(2,1)S(1)}, u32[]{:S(2)}, u32[]{:S(2)}) collective-permute-start(bf16[4,7168]{1,0:T(4,128)(2,1)S(1)} %slice.77), channel_id=1, source_target_pairs={{0,8},{1,9},{2,10},{3,11},{4,12},{5,13},{6,14},{7,15},{8,0},{9,1},... | collective-permute-start | bytes 172040 | tf_op jit(solution)/shard_map/ppermute | solution.py:46
  68.0 0.2 pad_maximum_fusion.arrived_ref
  68.2 2.5 %collective-permute-done.8 = bf16[4,7168]{1,0:T(4,128)(2,1)S(1)} collective-permute-done((bf16[4,7168]{1,0:T(4,128)(2,1)S(1)}, bf16[4,7168]{1,0:T(4,128)(2,1)S(1)}, u32[]{:S(2)}, u32[]{:S(2)}) %collective-permute-start.8) | collective-permute-done | bytes 57376 | tf_op jit(solution)/shard_map/ppermute | solution.py:46
  70.8 2.8 %collective-permute-start.9 = (bf16[2,7168]{1,0:T(2,128)(2,1)S(1)}, bf16[2,7168]{1,0:T(2,128)(2,1)S(1)}, u32[]{:S(2)}, u32[]{:S(2)}) collective-permute-start(bf16[2,7168]{1,0:T(2,128)(2,1)S(1)} %slice.78), channel_id=1, source_target_pairs={{0,16},{1,17},{2,18},{3,19},{4,20},{5,21},{6,22},{7,23},{8,24},{9,... | collective-permute-start | bytes 86024 | tf_op jit(solution)/shard_map/ppermute | solution.py:46
  73.6 2.4 %shard_map.134 = bf16[2,32768]{1,0:T(2,128)(2,1)} custom-call(s32[2]{0:T(128)S(1)} %copy-done.6, s32[2,12]{1,0:T(2,128)S(1)} %copy-done.5, bf16[2,36864]{1,0:T(2,128)(2,1)S(1)} %copy-done.4, bf16[24,18432]{1,0:T(8,128)(2,1)S(1)} %copy-done.3, bf16[8,18432]{1,0:T(8,128)(2,1)S(1)} %pad_maximum_fusion.arrived_ref), custom_call_target="tpu_custom_call" | custom-call | flops 1073741824 | bytes 4194304 | tf_op jit(solution)/shard_map/pallas_call | solution.py:251
  76.0 0.6 fusion
  (33 shorter events, 0.9 us)
Async XLA Ops:
  2.1 6.1 %collective-permute-start = (bf16[2,7296]{1,0:T(2,128)(2,1)}, bf16[2,7296]{1,0:T(2,128)(2,1)S(1)}, u32[]{:S(2)}, u32[]{:S(2)}) collective-permute-start(bf16[2,7296]{1,0:T(2,128)(2,1)} %shard_map.131), channel_id=1, source_target_pairs={{0,16},{1,17},{2,18},{3,19},{4,20},{5,21},{6,22},{7,23},{8,24},{9,... | collective-permute-start | bytes 87560 | tf_op jit(solution)/shard_map/ppermute | solution.py:46
  9.0 4.3 %collective-permute-start.1 = (bf16[4,7296]{1,0:T(4,128)(2,1)S(1)}, bf16[4,7296]{1,0:T(4,128)(2,1)S(1)}, u32[]{:S(2)}, u32[]{:S(2)}) collective-permute-start(bf16[4,7296]{1,0:T(4,128)(2,1)S(1)} %pad_maximum_fusion.4), channel_id=1, source_target_pairs={{0,8},{1,9},{2,10},{3,11},{4,12},{5,13},{6,14},{7,15},{8,0},{9,1},... | collective-permute-start | bytes 175112 | tf_op jit(solution)/shard_map/ppermute | solution.py:46
  14.1 4.9 %collective-permute-start.2 = (bf16[8,7296]{1,0:T(8,128)(2,1)S(1)}, bf16[8,7296]{1,0:T(8,128)(2,1)S(1)}, u32[]{:S(2)}, u32[]{:S(2)}) collective-permute-start(bf16[8,7296]{1,0:T(8,128)(2,1)S(1)} %pad_maximum_fusion.3), channel_id=1, source_target_pairs={{0,4},{1,5},{2,6},{3,7},{4,0},{5,1},{6,2},{7,3},{8,12},{9,13},{10,... | collective-permute-start | bytes 350216 | tf_op jit(solution)/shard_map/ppermute | solution.py:46
  19.9 6.1 %collective-permute-start.3 = (bf16[16,7296]{1,0:T(8,128)(2,1)S(1)}, bf16[16,7296]{1,0:T(8,128)(2,1)S(1)}, u32[]{:S(2)}, u32[]{:S(2)}) collective-permute-start(bf16[16,7296]{1,0:T(8,128)(2,1)S(1)} %pad_maximum_fusion.1), channel_id=1, source_target_pairs={{0,2},{1,3},{2,0},{3,1},{4,6},{5,7},{6,4},{7,5},{8,10},{9,11},{10,... | collective-permute-start | bytes 700424 | tf_op jit(solution)/shard_map/ppermute | solution.py:46
  27.0 5.4 %copy-start.7 = (bf16[32,7296]{1,0:T(8,128)(2,1)}, bf16[32,7296]{1,0:T(8,128)(2,1)S(1)}, u32[]{:S(2)}) copy-start(bf16[32,7296]{1,0:T(8,128)(2,1)S(1)} %concatenate.24.near_ref) | copy-start | bytes 1400836
  27.1 5.4 %collective-permute-start.4 = (bf16[32,7296]{1,0:T(8,128)(2,1)S(1)}, bf16[32,7296]{1,0:T(8,128)(2,1)S(1)}, u32[]{:S(2)}, u32[]{:S(2)}) collective-permute-start(bf16[32,7296]{1,0:T(8,128)(2,1)S(1)} %concatenate.24.near_ref), channel_id=1, source_target_pairs={{0,1},{1,0},{2,3},{3,2},{4,5},{5,4},{6,7},{7,6},{8,9},{9,8},{10,11... | collective-permute-start | bytes 1400840 | tf_op jit(solution)/shard_map/ppermute | solution.py:46
  30.5 43.2 %copy-start.5 = (s32[2,12]{1,0:T(2,128)S(1)}, s32[2,12]{1,0:T(2,128)}, u32[]{:S(2)}) copy-start(s32[2,12]{1,0:T(2,128)} %table_ref.1) | copy-start | bytes 292
  30.5 43.2 %copy-start.6 = (s32[2]{0:T(128)S(1)}, s32[2]{0:T(128)}, u32[]{:S(2)}) copy-start(s32[2]{0:T(128)} %length_ref.1) | copy-start | bytes 28
  30.5 23.5 %collective-permute-start.10 = (bf16[4,18432]{1,0:T(4,128)(2,1)}, bf16[4,18432]{1,0:T(4,128)(2,1)S(1)}, u32[]{:S(2)}, u32[]{:S(2)}) collective-permute-start(bf16[4,18432]{1,0:T(4,128)(2,1)} %get-tuple-element.9), channel_id=1, source_target_pairs={{0,2},{1,3},{2,0},{3,1},{4,6},{5,7},{6,4},{7,5},{8,10},{9,11},{10,... | collective-permute-start | bytes 442376 | tf_op jit(solution)/shard_map/ppermute | solution.py:46
  32.5 0.8 %copy-start.8 = (bf16[32,7296]{1,0:T(8,128)(2,1)}, bf16[32,7296]{1,0:T(8,128)(2,1)S(1)}, u32[]{:S(2)}) copy-start(bf16[32,7296]{1,0:T(8,128)(2,1)S(1)} %collective-permute-done.4.far_ref) | copy-start | bytes 1400836
  33.2 3.1 %copy-start = (bf16[1,7168,512]{2,1,0:T(8,128)(2,1)S(1)}, bf16[1,7168,512]{2,1,0:T(8,128)(2,1)}, u32[]{:S(2)}) copy-start(bf16[1,7168,512]{2,1,0:T(8,128)(2,1)} %gate_ref.1) | copy-start | bytes 22020100
  36.3 3.1 %copy-start.1 = (bf16[1,7168,512]{2,1,0:T(8,128)(2,1)S(1)}, bf16[1,7168,512]{2,1,0:T(8,128)(2,1)}, u32[]{:S(2)}) copy-start(bf16[1,7168,512]{2,1,0:T(8,128)(2,1)} %up_ref.1) | copy-start | bytes 22020100
  39.4 3.1 %copy-start.2 = (bf16[1,512,7168]{2,1,0:T(8,128)(2,1)S(1)}, bf16[1,512,7168]{2,1,0:T(8,128)(2,1)}, u32[]{:S(2)}) copy-start(bf16[1,512,7168]{2,1,0:T(8,128)(2,1)} %down_ref.1) | copy-start | bytes 22020100
  42.5 8.1 %copy-start.9 = (bf16[4,18432]{1,0:T(4,128)(2,1)S(1)}, bf16[4,18432]{1,0:T(4,128)(2,1)}, u32[]{:S(2)}) copy-start(bf16[4,18432]{1,0:T(4,128)(2,1)} %get-tuple-element.8) | copy-start | bytes 442372
  42.5 31.1 %copy-start.3 = (bf16[24,18432]{1,0:T(8,128)(2,1)S(1)}, bf16[24,18432]{1,0:T(8,128)(2,1)}, u32[]{:S(2)}) copy-start(bf16[24,18432]{1,0:T(8,128)(2,1)} %pool_ref.3) | copy-start | bytes 2654212
  42.5 31.1 %copy-start.4 = (bf16[2,36864]{1,0:T(2,128)(2,1)S(1)}, bf16[2,36864]{1,0:T(2,128)(2,1)}, u32[]{:S(2)}) copy-start(bf16[2,36864]{1,0:T(2,128)(2,1)} %query_ref.1) | copy-start | bytes 442372
  50.5 2.0 %collective-permute-start.5 = (bf16[32,7168]{1,0:T(8,128)(2,1)}, bf16[32,7168]{1,0:T(8,128)(2,1)S(1)}, u32[]{:S(2)}, u32[]{:S(2)}) collective-permute-start(bf16[32,7168]{1,0:T(8,128)(2,1)} %get-tuple-element.7), channel_id=1, source_target_pairs={{0,1},{1,0},{2,3},{3,2},{4,5},{5,4},{6,7},{7,6},{8,9},{9,8},{10,11... | collective-permute-start | bytes 1376264 | tf_op jit(solution)/shard_map/ppermute | solution.py:46
  53.8 7.7 %collective-permute-start.6 = (bf16[16,7168]{1,0:T(8,128)(2,1)S(1)}, bf16[16,7168]{1,0:T(8,128)(2,1)S(1)}, u32[]{:S(2)}, u32[]{:S(2)}) collective-permute-start(bf16[16,7168]{1,0:T(8,128)(2,1)S(1)} %slice.75), channel_id=1, source_target_pairs={{0,2},{1,3},{2,0},{3,1},{4,6},{5,7},{6,4},{7,5},{8,10},{9,11},{10,... | collective-permute-start | bytes 688136 | tf_op jit(solution)/shard_map/ppermute | solution.py:46
  61.6 4.9 %collective-permute-start.7 = (bf16[8,7168]{1,0:T(8,128)(2,1)S(1)}, bf16[8,7168]{1,0:T(8,128)(2,1)S(1)}, u32[]{:S(2)}, u32[]{:S(2)}) collective-permute-start(bf16[8,7168]{1,0:T(8,128)(2,1)S(1)} %slice.76), channel_id=1, source_target_pairs={{0,4},{1,5},{2,6},{3,7},{4,0},{5,1},{6,2},{7,3},{8,12},{9,13},{10,... | collective-permute-start | bytes 344072 | tf_op jit(solution)/shard_map/ppermute | solution.py:46
  63.3 4.6 %collective-permute-start.11 = (bf16[4,18432]{1,0:T(4,128)(2,1)S(1)}, bf16[4,18432]{1,0:T(4,128)(2,1)S(1)}, u32[]{:S(2)}, u32[]{:S(2)}) collective-permute-start(bf16[4,18432]{1,0:T(4,128)(2,1)S(1)} %pad_maximum_fusion.2), channel_id=1, source_target_pairs={{0,1},{1,0},{2,3},{3,2},{4,5},{5,4},{6,7},{7,6},{8,9},{9,8},{10,11... | collective-permute-start | bytes 442376 | tf_op jit(solution)/shard_map/ppermute | solution.py:46
  66.5 4.2 %collective-permute-start.8 = (bf16[4,7168]{1,0:T(4,128)(2,1)S(1)}, bf16[4,7168]{1,0:T(4,128)(2,1)S(1)}, u32[]{:S(2)}, u32[]{:S(2)}) collective-permute-start(bf16[4,7168]{1,0:T(4,128)(2,1)S(1)} %slice.77), channel_id=1, source_target_pairs={{0,8},{1,9},{2,10},{3,11},{4,12},{5,13},{6,14},{7,15},{8,0},{9,1},... | collective-permute-start | bytes 172040 | tf_op jit(solution)/shard_map/ppermute | solution.py:46
  70.8 5.2 %collective-permute-start.9 = (bf16[2,7168]{1,0:T(2,128)(2,1)S(1)}, bf16[2,7168]{1,0:T(2,128)(2,1)S(1)}, u32[]{:S(2)}, u32[]{:S(2)}) collective-permute-start(bf16[2,7168]{1,0:T(2,128)(2,1)S(1)} %slice.78), channel_id=1, source_target_pairs={{0,16},{1,17},{2,18},{3,19},{4,20},{5,21},{6,22},{7,23},{8,24},{9,... | collective-permute-start | bytes 86024 | tf_op jit(solution)/shard_map/ppermute | solution.py:46

commit v3 on v2

--- a/solution.py
+++ b/solution.py
@@ -33,6 +33,18 @@
     return pltpu.with_memory_space_constraint(x, pltpu.VMEM)
 
 
+def hbm(x):
+    return pltpu.with_memory_space_constraint(x, pltpu.HBM)
+
+
+def anywhere():
+    return pl.BlockSpec(memory_space=pl.ANY)
+
+
+def in_hbm():
+    return pl.BlockSpec(memory_space=pltpu.HBM)
+
+
 def partner_bits(count):
     bits = []
     b = count // 2
@@ -42,13 +54,33 @@
     return bits
 
 
-def swap(x, axes, count, bit):
-    return lax.ppermute(x, axes, [(i, i ^ bit) for i in range(count)])
-
-
-def payload_kernel(ep_count, hidden_ref, routes_ref, weight_ref, out_ref):
+def swap(x, axes, pairs):
+    return lax.ppermute(x, axes, pairs)
+
+
+def stage_pairs(count, stage):
+    bits = partner_bits(count)[:-1]
+    turned = bits[:-2] + [bits[-1], bits[-2]]
+    return [(i, i ^ (turned if i & 1 else bits)[stage]) for i in range(count)]
+
+
+def core_pairs(count):
+    return [(i, i ^ 1) for i in range(count)]
+
+
+def payload_kernel(ep_count, hidden_hbm, routes_hbm, weight_hbm, mine_ref, other_ref, hidden_ref, routes_ref, weight_ref, sems):
+    copies = [
+        pltpu.make_async_copy(source, target, sems.at[i])
+        for i, (source, target) in enumerate(
+            [(hidden_hbm, hidden_ref), (routes_hbm, routes_ref), (weight_hbm, weight_ref)]
+        )
+    ]
+    for c in copies:
+        c.start()
+    for c in copies:
+        c.wait()
     rows, width = hidden_ref.shape
-    out_ref[:, :width] = hidden_ref[...]
+    half = width // 2
     column = lax.broadcasted_iota(jnp.int32, (rows, LANES), 1)
     expert = jnp.where(column < ep_count, column, column - ep_count)
     total = jnp.zeros((rows, LANES), f32)
@@ -56,74 +88,275 @@
         total += jnp.where(routes_ref[:, k : k + 1] == expert, weight_ref[:, k : k + 1], 0.0)
     high = total.astype(bf16).astype(f32)
     low = total - high
-    value = jnp.where(column < ep_count, high, jnp.where(column < 2 * ep_count, low, 0.0))
-    out_ref[:, width:] = value.astype(bf16)
+    value = jnp.where(column < ep_count, high, jnp.where(column < 2 * ep_count, low, 0.0)).astype(bf16)
+    first = lax.rem(lax.axis_index("dp"), 2) == 0
+    left, right = hidden_ref[:, :half].astype(f32), hidden_ref[:, half:].astype(f32)
+    mine_ref[:, :half] = jnp.where(first, left, right).astype(bf16)
+    other_ref[:, :half] = jnp.where(first, right, left).astype(bf16)
+    mine_ref[:, half:] = value
+    other_ref[:, half:] = value
 
 
 def make_payload(hidden, routes, route_weight, ep_count):
     rows, width = hidden.shape
+    half = pltpu.VMEM((rows, width // 2 + LANES), bf16)
     return pl.pallas_call(
         functools.partial(payload_kernel, ep_count),
-        out_shape=jax.ShapeDtypeStruct((rows, width + LANES), bf16),
-        in_specs=[in_vmem()] * 3,
+        out_shape=(half, half),
+        in_specs=[in_hbm()] * 3,
+        out_specs=(in_vmem(), in_vmem()),
+        scratch_shapes=[
+            pltpu.VMEM(hidden.shape, bf16),
+            pltpu.VMEM(routes.shape, jnp.int32),
+            pltpu.VMEM(route_weight.shape, f32),
+            pltpu.SemaphoreType.DMA((3,)),
+        ],
+        compiler_params=pltpu.CompilerParams(vmem_limit_bytes=4 * MIB),
+        cost_estimate=pl.CostEstimate(flops=0, bytes_accessed=4 * rows * width, transcendentals=0),
+    )(hbm(hidden), hbm(routes), hbm(route_weight))
+
+
+def merge_kernel(by_core, near_ref, got_ref, *rest):
+    out_ref = rest[-1]
+    rows = near_ref.shape[0]
+    if rows % 16:
+        near, got = near_ref[...].astype(f32), got_ref[...].astype(f32)
+        both = jnp.concatenate([near, got], axis=0)
+        if by_core:
+            first = lax.rem(lax.axis_index("dp"), 2) == 0
+            both = jnp.where(first, both, jnp.concatenate([got, near], axis=0))
+        out_ref[...] = both.astype(bf16)
+    else:
+        out_ref[:rows] = near_ref[...]
+        out_ref[rows:] = got_ref[...]
+
+
+def merge(near, got, *after, by_core=False):
+    rows, width = near.shape
+    return pl.pallas_call(
+        functools.partial(merge_kernel, by_core),
+        out_shape=pltpu.VMEM((2 * rows, width), bf16),
+        in_specs=[in_vmem(), in_vmem()] + [anywhere()] * len(after),
         out_specs=in_vmem(),
-        cost_estimate=pl.CostEstimate(flops=0, bytes_accessed=4 * rows * width, transcendentals=0),
-    )(hidden, routes, route_weight)
-
-
-def expert_kernel(ep_count, step, near_ref, far_ref, gate_ref, up_ref, down_ref, keep_ref, send_ref, gate_acc, up_acc):
-    half = near_ref.shape[0]
-    width, hidden_units = gate_ref.shape[1], gate_ref.shape[2]
+        compiler_params=pltpu.CompilerParams(vmem_limit_bytes=4 * MIB),
+        cost_estimate=pl.CostEstimate(flops=0, bytes_accessed=8 * rows * width, transcendentals=0),
+    )(vmem(near), vmem(got), *after)
+
+
+def half_start(width, near):
+    core = lax.rem(lax.axis_index("dp"), 2)
+    core = core if near else 1 - core
+    return pl.multiple_of(core * (width // 2), width // 2)
+
+
+def load_kernel(pieces, *refs):
+    sources = refs[: len(pieces)]
+    outs = refs[len(pieces) + 1 : -1]
+    sems = refs[-1]
+    copies = []
+    for i, (near, source, out) in enumerate(zip(pieces, sources, outs)):
+        rows = source.shape[1] // 2
+        copies.append(
+            pltpu.make_async_copy(source.at[0, pl.ds(half_start(source.shape[1], near), rows)], out, sems.at[i])
+        )
+    for c in copies:
+        c.start()
+    for c in copies:
+        c.wait()
+
+
+def load_halves(after, *requests):
+    weights = [w for w, _ in requests]
+    pieces = [near for _, near in requests]
+    out = tuple(pltpu.VMEM((w.shape[1] // 2, w.shape[2]), bf16) for w in weights)
+    return pl.pallas_call(
+        functools.partial(load_kernel, pieces),
+        out_shape=out,
+        in_specs=[in_hbm()] * len(weights) + [anywhere()],
+        out_specs=(in_vmem(),) * len(weights),
+        scratch_shapes=[pltpu.SemaphoreType.DMA((len(weights),))],
+        compiler_params=pltpu.CompilerParams(vmem_limit_bytes=4 * MIB),
+        cost_estimate=pl.CostEstimate(flops=0, bytes_accessed=sum(w.size for w in weights), transcendentals=0),
+    )(*[hbm(w) for w in weights], after)
+
+
+def near_kernel(near_ref, gate_ref, up_ref, down_ref, gate_out, up_out, down_out, sem):
+    width = down_ref.shape[2]
+    copy = pltpu.make_async_copy(down_ref.at[0, :, pl.ds(half_start(width, False), width // 2)], down_out, sem)
+    copy.start()
+    x = near_ref[:, : width // 2]
+    gate_out[...] = jnp.dot(x, gate_ref[...], preferred_element_type=f32)
+    up_out[...] = jnp.dot(x, up_ref[...], preferred_element_type=f32)
+    copy.wait()
+
+
+def far_kernel(
+    ep_count, near_ref, far_ref, gate_ref, up_ref, gate_in, up_in, down_far_ref, down_ref, inner_ref, send_ref, down_out, sem
+):
+    width = down_ref.shape[2]
+    half = width // 2
+    copy = pltpu.make_async_copy(down_ref.at[0, :, pl.ds(half_start(width, True), half)], down_out, sem)
+    copy.start()
+    rows = near_ref.shape[0]
+    quarter = rows // 4
+
+    def turn(x):
+        return jnp.concatenate([x[:quarter], x[2 * quarter : 3 * quarter], x[quarter : 2 * quarter], x[3 * quarter :]], axis=0)
+
     ep = lax.axis_index("ep")
-
-    def rows_at(columns):
-        return jnp.concatenate([near_ref[:, columns], far_ref[:, columns]], axis=0)
-
-    table = rows_at(slice(width, width + LANES)).astype(f32)
+    table = near_ref[:, half:].astype(f32)
     column = lax.broadcasted_iota(jnp.int32, table.shape, 1)
     mine = (column == ep) | (column == ep + ep_count)
     row_weight = jnp.sum(jnp.where(mine, table, 0.0), axis=1, keepdims=True)
-
-    gate_acc[...] = jnp.zeros_like(gate_acc)
-    up_acc[...] = jnp.zeros_like(up_acc)
-
-    @pl.loop(0, width // step)
+    x = turn(far_ref[:, :half])
+    gate = gate_in[...] + jnp.dot(x, gate_ref[...], preferred_element_type=f32)
+    up = up_in[...] + jnp.dot(x, up_ref[...], preferred_element_type=f32)
+    inner = (gate / (1.0 + jnp.exp(-gate)) * up).astype(bf16)
+    inner_ref[...] = inner
+    step = half // 7
+
+    @pl.loop(0, half // step)
     def _(i):
         columns = pl.ds(pl.multiple_of(i * step, step), step)
-        x = rows_at(columns)
-        gate_acc[...] += jnp.dot(x, gate_ref[0, columns, :], preferred_element_type=f32)
-        up_acc[...] += jnp.dot(x, up_ref[0, columns, :], preferred_element_type=f32)
-
-    gate = gate_acc[...]
-    inner = (gate / (1.0 + jnp.exp(-gate)) * up_acc[...]).astype(bf16)
-
-    @pl.loop(0, width // step)
+        out = jnp.dot(inner, down_far_ref[:, columns], preferred_element_type=f32) * row_weight
+        send_ref[:, columns] = turn(out).astype(bf16)
+
+    copy.wait()
+
+
+def keep_kernel(ep_count, near_ref, inner_ref, down_ref, keep_ref):
+    half = down_ref.shape[1]
+    ep = lax.axis_index("ep")
+    table = near_ref[:, half:].astype(f32)
+    column = lax.broadcasted_iota(jnp.int32, table.shape, 1)
+    mine = (column == ep) | (column == ep + ep_count)
+    row_weight = jnp.sum(jnp.where(mine, table, 0.0), axis=1, keepdims=True)
+    step = half // 7
+    inner = inner_ref[...]
+
+    @pl.loop(0, half // step)
     def _(i):
         columns = pl.ds(pl.multiple_of(i * step, step), step)
-        out = jnp.dot(inner, down_ref[0, :, columns], preferred_element_type=f32) * row_weight
-        keep_ref[:, columns] = out[:half]
-        send_ref[:, columns] = out[half:].astype(bf16)
-
-
-def run_experts(near, far, gate_weight, up_weight, down_weight, ep_count):
-    half = near.shape[0]
-    width, units = gate_weight.shape[1], gate_weight.shape[2]
-    step = 1024
-    return pl.pallas_call(
-        functools.partial(expert_kernel, ep_count, step),
-        out_shape=(jax.ShapeDtypeStruct((half, width), f32), jax.ShapeDtypeStruct((half, width), bf16)),
-        in_specs=[in_vmem()] * 5,
+        keep_ref[:, columns] = jnp.dot(inner, down_ref[:, columns], preferred_element_type=f32) * row_weight
+
+
+def estimate(rows, weights):
+    return pl.CostEstimate(flops=2 * rows * weights, bytes_accessed=2 * weights, transcendentals=0)
+
+
+def near_products(near, gate_near, up_near, down_weight):
+    rows = near.shape[0]
+    units, width = down_weight.shape[1:]
+    acc = pltpu.VMEM((rows, units), f32)
+    return pl.pallas_call(
+        near_kernel,
+        out_shape=(acc, acc, pltpu.VMEM((units, width // 2), bf16)),
+        in_specs=[in_vmem()] * 3 + [in_hbm()],
+        out_specs=(in_vmem(),) * 3,
+        scratch_shapes=[pltpu.SemaphoreType.DMA],
+        compiler_params=pltpu.CompilerParams(vmem_limit_bytes=12 * MIB),
+        cost_estimate=estimate(rows, width * units),
+    )(vmem(near), vmem(gate_near), vmem(up_near), hbm(down_weight))
+
+
+def far_products(near, far, gate_far, up_far, gate_acc, up_acc, down_far, down_weight, ep_count):
+    rows = near.shape[0]
+    units, width = down_weight.shape[1:]
+    half = width // 2
+    return pl.pallas_call(
+        functools.partial(far_kernel, ep_count),
+        out_shape=(pltpu.VMEM((rows, units), bf16), pltpu.VMEM((rows, half), bf16), pltpu.VMEM((units, half), bf16)),
+        in_specs=[in_vmem()] * 7 + [in_hbm()],
+        out_specs=(in_vmem(),) * 3,
+        scratch_shapes=[pltpu.SemaphoreType.DMA],
+        compiler_params=pltpu.CompilerParams(vmem_limit_bytes=12 * MIB),
+        cost_estimate=estimate(rows, 3 * half * units),
+    )(
+        vmem(near),
+        vmem(far),
+        vmem(gate_far),
+        vmem(up_far),
+        vmem(gate_acc),
+        vmem(up_acc),
+        vmem(down_far),
+        hbm(down_weight),
+    )
+
+
+def keep_products(near, inner, down_near, ep_count):
+    rows = near.shape[0]
+    units, half = down_near.shape
+    return pl.pallas_call(
+        functools.partial(keep_kernel, ep_count),
+        out_shape=pltpu.VMEM((rows, half), f32),
+        in_specs=[in_vmem()] * 3,
+        out_specs=in_vmem(),
+        compiler_params=pltpu.CompilerParams(vmem_limit_bytes=8 * MIB),
+        cost_estimate=estimate(rows, half * units),
+    )(vmem(near), vmem(inner), vmem(down_near))
+
+
+def fold_kernel(by_core, keep_ref, got_ref, *rest):
+    keep_out, send_out = rest[-2:]
+    half = keep_out.shape[0]
+    upper = keep_ref[:half] + got_ref[:half].astype(f32)
+    lower = keep_ref[half:] + got_ref[half:].astype(f32)
+    if by_core:
+        first = lax.rem(lax.axis_index("dp"), 2) == 0
+        upper, lower = jnp.where(first, upper, lower), jnp.where(first, lower, upper)
+    keep_out[...] = upper
+    send_out[...] = lower.astype(bf16)
+
+
+def fold(keep, got, *after, by_core=False):
+    rows, width = keep.shape
+    return pl.pallas_call(
+        functools.partial(fold_kernel, by_core),
+        out_shape=(pltpu.VMEM((rows // 2, width), f32), pltpu.VMEM((rows // 2, width), bf16)),
+        in_specs=[in_vmem(), in_vmem()] + [anywhere()] * len(after),
         out_specs=(in_vmem(), in_vmem()),
-        scratch_shapes=[pltpu.VMEM((2 * half, units), f32), pltpu.VMEM((2 * half, units), f32)],
-        compiler_params=pltpu.CompilerParams(vmem_limit_bytes=40 * MIB),
-        cost_estimate=pl.CostEstimate(
-            flops=12 * half * width * units, bytes_accessed=6 * width * units, transcendentals=2 * half * units
-        ),
-    )(near, far, vmem(gate_weight), vmem(up_weight), vmem(down_weight))
-
-
-def pages_kernel(dp_count, page_ref, dest_ref, pool_ref, low_ref, high_ref):
+        compiler_params=pltpu.CompilerParams(vmem_limit_bytes=4 * MIB),
+        cost_estimate=pl.CostEstimate(flops=0, bytes_accessed=8 * rows * width, transcendentals=0),
+    )(vmem(keep), vmem(got), *after)
+
+
+def finish_kernel(keep_ref, got_ref, out_ref):
+    half = keep_ref.shape[1]
+    first = lax.rem(lax.axis_index("dp"), 2) == 0
+    keep, got = keep_ref[...], got_ref[...].astype(f32)
+    out_ref[:, :half] = jnp.where(first, keep, got).astype(bf16)
+    out_ref[:, half:] = jnp.where(first, got, keep).astype(bf16)
+
+
+def finish(keep, got):
+    rows, half = keep.shape
+    return pl.pallas_call(
+        finish_kernel,
+        out_shape=jax.ShapeDtypeStruct((rows, 2 * half), bf16),
+        in_specs=[in_vmem(), in_vmem()],
+        out_specs=in_vmem(),
+        compiler_params=pltpu.CompilerParams(vmem_limit_bytes=4 * MIB),
+        cost_estimate=pl.CostEstimate(flops=0, bytes_accessed=8 * rows * half, transcendentals=0),
+    )(vmem(keep), vmem(got))
+
+
+def pages_kernel(
+    dp_count, page_hbm, dest_hbm, pool_ref, gate_ref, after_ref, low_ref, high_ref, copy_ref, gate_out, page_ref, dest_ref, sems
+):
     own, width = pool_ref.shape
+    depth = gate_ref.shape[1]
+    pool_copy = pltpu.make_async_copy(pool_ref, copy_ref, sems.at[0])
+    page_copy = pltpu.make_async_copy(page_hbm, page_ref, sems.at[2])
+    dest_copy = pltpu.make_async_copy(dest_hbm, dest_ref, sems.at[3])
+    page_copy.start()
+    dest_copy.start()
+    pool_copy.start()
+    gate_copy = pltpu.make_async_copy(
+        gate_ref.at[0, pl.ds(half_start(depth, True), depth // 2)], gate_out, sems.at[1]
+    )
+    gate_copy.start()
+    page_copy.wait()
+    dest_copy.wait()
     me = lax.axis_index("dp")
     slots = dp_count * MCAP
     row = lax.broadcasted_iota(jnp.int32, (slots, own), 0)
@@ -138,32 +371,39 @@
         pick = jnp.where((row == bucket) & (column == page_ref[0, m]), 1.0, pick)
     pick = pick.astype(bf16)
     step = 2048
-
-    @pl.loop(0, width // step)
-    def _(i):
-        columns = pl.ds(pl.multiple_of(i * step, step), step)
-        out = jnp.dot(pick, pool_ref[:, columns], preferred_element_type=f32)
+    pool_copy.wait()
+    for i in range(width // step):
+        columns = slice(i * step, (i + 1) * step)
+        out = jnp.dot(pick, copy_ref[:, columns], preferred_element_type=f32)
         low_ref[:, columns] = out[: slots // 2].astype(bf16)
         high_ref[:, columns] = out[slots // 2 :].astype(bf16)
-
-
-def pick_pages(moved_page, moved_dest, latent_pool, dp_count):
+    gate_copy.wait()
+
+
+def pick_pages(moved_page, moved_dest, latent_pool, gate_weight, after, dp_count):
     width = latent_pool.shape[1]
-    half = jax.ShapeDtypeStruct((dp_count * MCAP // 2, width), bf16)
+    half = pltpu.VMEM((dp_count * MCAP // 2, width), bf16)
+    depth, units = gate_weight.shape[1:]
     return pl.pallas_call(
         functools.partial(pages_kernel, dp_count),
-        out_shape=(half, half),
-        in_specs=[in_smem(), in_smem(), in_vmem()],
-        out_specs=(in_vmem(), in_vmem()),
-        cost_estimate=pl.CostEstimate(flops=0, bytes_accessed=4 * latent_pool.size, transcendentals=0),
-    )(moved_page, moved_dest, latent_pool)
+        out_shape=(half, half, pltpu.VMEM(latent_pool.shape, bf16), pltpu.VMEM((depth // 2, units), bf16)),
+        in_specs=[in_hbm()] * 4 + [anywhere()],
+        out_specs=(in_vmem(),) * 4,
+        scratch_shapes=[
+            pltpu.SMEM(moved_page.shape, jnp.int32),
+            pltpu.SMEM(moved_dest.shape, jnp.int32),
+            pltpu.SemaphoreType.DMA((4,)),
+        ],
+        compiler_params=pltpu.CompilerParams(vmem_limit_bytes=4 * MIB),
+        cost_estimate=pl.CostEstimate(flops=0, bytes_accessed=4 * latent_pool.size + gate_weight.size, transcendentals=0),
+    )(hbm(moved_page), hbm(moved_dest), hbm(latent_pool), hbm(gate_weight), after)
 
 
 def exchange_pages(low, high, dp_count):
     blocks, senders = [low], [0]
     sent = high
     for bit in partner_bits(dp_count):
-        got = swap(sent, "dp", dp_count, bit)
+        got = swap(sent, "dp", [(i, i ^ bit) for i in range(dp_count)])
         size = got.shape[0] // len(blocks)
         blocks = blocks + [got[i * size : (i + 1) * size] for i in range(len(blocks))]
         senders = senders + [s ^ bit for s in senders]
@@ -254,9 +494,9 @@
         in_specs=[in_smem(), in_smem(), in_vmem(), in_vmem(), in_vmem()],
         out_specs=in_vmem(),
         scratch_shapes=[pltpu.VMEM((HEADS // 2 * rows_dev, 2 * LAT), f32)],
-        compiler_params=pltpu.CompilerParams(vmem_limit_bytes=24 * MIB),
+        compiler_params=pltpu.CompilerParams(vmem_limit_bytes=16 * MIB),
         cost_estimate=pl.CostEstimate(flops=1 << 30, bytes_accessed=4 << 20, transcendentals=1 << 17),
-    )(lengths, page_table, queries, latent_pool, arrived)
+    )(lengths, page_table, queries, vmem(latent_pool), vmem(arrived))
 
 
 def body(
@@ -276,25 +516,43 @@
     ep_count = lax.axis_size("ep")
     dp_count = lax.axis_size("dp")
     count = ep_count * dp_count
-    bits = partner_bits(count)
-
-    near = make_payload(hidden, routes, route_weight, ep_count)
-    for bit in bits[:-1]:
-        near = jnp.concatenate([near, swap(near, AXES, count, bit)], axis=0)
-    far = swap(near, AXES, count, bits[-1])
-
-    low, high = pick_pages(moved_page, moved_dest, latent_pool, dp_count)
+    stages = len(partner_bits(count)) - 1
+    cores = core_pairs(count)
+
+    mine, other = make_payload(hidden, routes, route_weight, ep_count)
+    near = merge(mine, swap(other, AXES, cores), by_core=True)
+    for stage in range(stages):
+        got = swap(near, AXES, stage_pairs(count, stage))
+        if stage == 0:
+            low, high, pool, gate_near = pick_pages(moved_page, moved_dest, latent_pool, gate_weight, near, dp_count)
+            loaded = [high]
+        elif stage == 1:
+            loaded = load_halves(near, (up_weight, True))
+            (up_near,) = loaded
+        elif stage == 2:
+            loaded = load_halves(near, (gate_weight, False))
+            (gate_far,) = loaded
+        elif stage == 3:
+            loaded = load_halves(near, (up_weight, False))
+            (up_far,) = loaded
+        else:
+            loaded = []
+        near = merge(near, got, *loaded)
     arrived, senders = exchange_pages(low, high, dp_count)
-    attended = attend(lengths, page_table, queries, latent_pool, arrived, senders)
-
-    keep, send = run_experts(near, far, gate_weight, up_weight, down_weight, ep_count)
-    for bit in reversed(bits):
-        keep = keep + swap(send, AXES, count, bit).astype(f32)
-        half = keep.shape[0] // 2
-        if bit != bits[0]:
-            send = keep[half:].astype(bf16)
-            keep = keep[:half]
-    return keep.astype(bf16), attended
+    far = swap(near, AXES, cores)
+    gate_acc, up_acc, down_far = near_products(near, gate_near, up_near, down_weight)
+    inner, send, down_near = far_products(
+        near, far, gate_far, up_far, gate_acc, up_acc, down_far, down_weight, ep_count
+    )
+    got = swap(send, AXES, cores)
+    keep = keep_products(near, inner, down_near, ep_count)
+    keep, send = fold(keep, got)
+    attended = attend(lengths, page_table, queries, pool, arrived, senders)
+    for stage in reversed(range(stages)):
+        got = swap(send, AXES, stage_pairs(count, stage))
+        after = [hbm(attended)] if stage == stages - 1 else []
+        keep, send = fold(keep, got, *after, by_core=stage == 0)
+    return finish(keep, swap(send, AXES, cores)), attended
 
 
 def solution(mesh):

time: 77.3 us -> 56.8 us (0.73)
  local copies, waits for them, and re-layouts: 11.3 us -> 0.22 us
  waiting for transfers between devices: 26.1 us -> 16 us
  Pallas kernels: 15.1 us -> 20.8 us
  other arithmetic: 4.97 us -> 0.4 us
    ppermute x12 -> x14, waiting for transfers between devices: 26.1 us -> 16 us  [swap(): return lax.ppermute(x, axes, pairs)]
    unnamed x20 -> x6, local copies, waits for them, and re-layouts: 10 us -> 0.01 us
    pallas_call x2 -> x18, Pallas kernels: 9.42 us -> 16.1 us  [the longest x3 6.15 us: load_halves(): pl.pallas_call(functools.partial(load_kernel, pieces), out_shape=out, in_...]
    concatenate x3 -> x0, other arithmetic: 2.57 us -> none  [body(): near = jnp.concatenate([near, swap(near, AXES, count, bit)], axis=0)]
    add x4 -> x0, other arithmetic: 1.36 us -> none  [body(): keep = keep + swap(send, AXES, count, bit).astype(f32)]
    pallas_call x1, Pallas kernels: 3.33 us -> 2.35 us  [pick_pages(): pl.pallas_call(functools.partial(pages_kernel, dp_count), out_shape=(half...]
    concatenate x1 -> x0, local copies, waits for them, and re-layouts: 0.98 us -> none  [body(): near = jnp.concatenate([near, swap(near, AXES, count, bit)], axis=0)]
    ppermute x12 -> x14, starting transfers between devices: 18.4 us -> 18.1 us  [swap(): return lax.ppermute(x, axes, pairs)]
  transfers between devices with their start and end apart: 12 -> 14, of which waited for: 8 -> 8; matrix products, arithmetic and copies ran while one was open for 3% -> 1% of each run, Pallas kernels for 18% -> 28%
where the time goes in v3:
time: 56.8 us; the launch traced here: 56.4 us
  Pallas kernels  20.8 us (37%)
  starting transfers between devices  18.1 us (32%)
  waiting for transfers between devices  16 us (28%)
  between operations  0.85 us (1%)
    ppermute x14, starting transfers between devices, swap(): return lax.ppermute(x, axes, pairs)  18.1 us
    ppermute x14, waiting for transfers between devices, swap(): return lax.ppermute(x, axes, pairs)  16 us
    pallas_call x3, Pallas kernels, load_halves(): pl.pallas_call(functools.partial(load_kernel, pieces), out_shape=out, in_...  6.15 us
    pallas_call x1, Pallas kernels, far_products(): pl.pallas_call(functools.partial(far_kernel, ep_count), out_shape=(pltpu....  3.29 us
    pallas_call x1, Pallas kernels, near_products(): pl.pallas_call(near_kernel, out_shape=(acc, acc, pltpu.VMEM((units, width...  3.26 us
    pallas_call x1, Pallas kernels, attend(): pl.pallas_call(functools.partial(attend_kernel, senders), out_shape=jax.S...  2.36 us
    pallas_call x1, Pallas kernels, pick_pages(): pl.pallas_call(functools.partial(pages_kernel, dp_count), out_shape=(half...  2.35 us
    pallas_call x1, Pallas kernels, keep_products(): pl.pallas_call(functools.partial(keep_kernel, ep_count), out_shape=pltpu....  1.55 us
  transfers between devices with their start and end apart: 14, of which 8 were waited for; matrix products, arithmetic and copies ran while one was open for 1% of the time, Pallas kernels for 28%

profile of v3, /device:TPU:0, one launch (start us, length us, event | category | flops | bytes accessed | tf_op | source)
XLA Modules:
  0.0 56.4 jit_solution(7786759296456414998)
XLA Ops:
  0.6 0.9 %shard_map.131 = (bf16[2,3712]{1,0:T(2,128)(2,1)S(1)}, bf16[2,3712]{1,0:T(2,128)(2,1)S(1)}) custom-call(bf16[2,7168]{1,0:T(2,128)(2,1)} %hidden_hbm.1, s32[2,4]{1,0:T(2,128)} %routes_hbm.1, f32[2,4]{1,0:T(2,128)} %weight_hbm.1), custom_call_target="tpu_custom_call" | custom-call | bytes 57344 | tf_op jit(solution)/shard_map/pallas_call | solution.py:103
  1.5 0.5 collective-permute-start
  2.0 0.8 %collective-permute-done.got_ref = bf16[2,3712]{1,0:T(2,128)(2,1)S(1)} collective-permute-done((bf16[2,3712]{1,0:T(2,128)(2,1)S(1)}, bf16[2,3712]{1,0:T(2,128)(2,1)S(1)}, u32[]{:S(2)}, u32[]{:S(2)}) %collective-permute-start) | collective-permute-done | bytes 14880 | tf_op jit(solution)/shard_map/ppermute | solution.py:58
  2.9 4.0 %collective-permute-start.1 = (bf16[4,3712]{1,0:T(4,128)(2,1)S(1)}, bf16[4,3712]{1,0:T(4,128)(2,1)S(1)}, u32[]{:S(2)}, u32[]{:S(2)}) collective-permute-start(bf16[4,3712]{1,0:T(4,128)(2,1)S(1)} %shard_map.132.after_ref.near_ref), channel_id=1, source_target_pairs={{0,16},{1,17},{2,18},{3,19},{4,20},{5,21},{6,22},{7,23},{8,24},{9,... | collective-permute-start | bytes 89096 | tf_op jit(solution)/shard_map/ppermute | solution.py:58
  6.9 2.3 %shard_map.133 = (bf16[4,18432]{1,0:T(4,128)(2,1)S(1)}, bf16[4,18432]{1,0:T(4,128)(2,1)S(1)}, bf16[24,18432]{1,0:T(8,128)(2,1)S(1)}, bf16[3584,512]{1,0:T(8,128)(2,1)S(1)}) custom-call(s32[1,6]{1,0:T(1,128)} %page_hbm.1, s32[1,6]{1,0:T(1,128)} %dest_hbm.1, bf16[24,18432]{1,0:T(8,128)(2,1)} %pool_ref.1, bf16[1,7168,512]{2,1,0:T(8,128)(2,1)} %refs_0_.4, ...), custom_call_target="tpu_custom_call" | custom-call | bytes 5439488 | tf_op jit(solution)/shard_map/pallas_call | solution.py:387
  9.3 1.6 %collective-permute-start.2 = (bf16[8,3712]{1,0:T(8,128)(2,1)S(1)}, bf16[8,3712]{1,0:T(8,128)(2,1)S(1)}, u32[]{:S(2)}, u32[]{:S(2)}) collective-permute-start(bf16[8,3712]{1,0:T(8,128)(2,1)S(1)} %shard_map.134.refs_1_.near_ref), channel_id=1, source_target_pairs={{0,8},{1,9},{2,10},{3,11},{4,12},{5,13},{6,14},{7,15},{8,0},{9,1},... | collective-permute-start | bytes 178184 | tf_op jit(solution)/shard_map/ppermute | solution.py:58
  10.9 2.0 %shard_map.135.rest_0_.up_ref = bf16[3584,512]{1,0:T(8,128)(2,1)S(1)} custom-call(bf16[1,7168,512]{2,1,0:T(8,128)(2,1)} %refs_0_.5, bf16[8,3712]{1,0:T(8,128)(2,1)S(1)} %shard_map.134.refs_1_.near_ref), custom_call_target="tpu_custom_call" | custom-call | bytes 3670016 | tf_op jit(solution)/shard_map/pallas_call | solution.py:172
  13.0 0.6 %collective-permute-done.2.got_ref = bf16[8,3712]{1,0:T(8,128)(2,1)S(1)} collective-permute-done((bf16[8,3712]{1,0:T(8,128)(2,1)S(1)}, bf16[8,3712]{1,0:T(8,128)(2,1)S(1)}, u32[]{:S(2)}, u32[]{:S(2)}) %collective-permute-start.2) | collective-permute-done | bytes 59424 | tf_op jit(solution)/shard_map/ppermute | solution.py:58
  13.6 1.7 %collective-permute-start.3 = (bf16[16,3712]{1,0:T(8,128)(2,1)S(1)}, bf16[16,3712]{1,0:T(8,128)(2,1)S(1)}, u32[]{:S(2)}, u32[]{:S(2)}) collective-permute-start(bf16[16,3712]{1,0:T(8,128)(2,1)S(1)} %shard_map.136.refs_1_.near_ref), channel_id=1, source_target_pairs={{0,4},{1,3},{2,6},{3,1},{4,0},{5,7},{6,2},{7,5},{8,12},{9,11},{10,... | collective-permute-start | bytes 356360 | tf_op jit(solution)/shard_map/ppermute | solution.py:58
  15.3 1.5 %collective-permute-start.8 = (bf16[4,18432]{1,0:T(4,128)(2,1)S(1)}, bf16[4,18432]{1,0:T(4,128)(2,1)S(1)}, u32[]{:S(2)}, u32[]{:S(2)}) collective-permute-start(bf16[4,18432]{1,0:T(4,128)(2,1)S(1)} %get-tuple-element.26.rest_0_), channel_id=1, source_target_pairs={{0,2},{1,3},{2,0},{3,1},{4,6},{5,7},{6,4},{7,5},{8,10},{9,11},{10,... | collective-permute-start | bytes 442376 | tf_op jit(solution)/shard_map/ppermute | solution.py:58
  16.8 2.0 %shard_map.137.rest_0_.gate_ref = bf16[3584,512]{1,0:T(8,128)(2,1)S(1)} custom-call(bf16[1,7168,512]{2,1,0:T(8,128)(2,1)} %refs_0_.4, bf16[16,3712]{1,0:T(8,128)(2,1)S(1)} %shard_map.136.refs_1_.near_ref), custom_call_target="tpu_custom_call" | custom-call | bytes 3670016 | tf_op jit(solution)/shard_map/pallas_call | solution.py:172
  18.9 1.3 %collective-permute-start.4 = (bf16[32,3712]{1,0:T(8,128)(2,1)S(1)}, bf16[32,3712]{1,0:T(8,128)(2,1)S(1)}, u32[]{:S(2)}, u32[]{:S(2)}) collective-permute-start(bf16[32,3712]{1,0:T(8,128)(2,1)S(1)} %shard_map.138.refs_1_.near_ref), channel_id=1, source_target_pairs={{0,2},{1,5},{2,0},{3,7},{4,6},{5,1},{6,4},{7,3},{8,10},{9,13},{10,... | collective-permute-start | bytes 712712 | tf_op jit(solution)/shard_map/ppermute | solution.py:58
  20.3 2.1 %shard_map.139.rest_0_.up_ref = bf16[3584,512]{1,0:T(8,128)(2,1)S(1)} custom-call(bf16[1,7168,512]{2,1,0:T(8,128)(2,1)} %refs_0_.5, bf16[32,3712]{1,0:T(8,128)(2,1)S(1)} %shard_map.138.refs_1_.near_ref), custom_call_target="tpu_custom_call" | custom-call | bytes 3670016 | tf_op jit(solution)/shard_map/pallas_call | solution.py:172
  22.4 2.7 %collective-permute-done.4.got_ref = bf16[32,3712]{1,0:T(8,128)(2,1)S(1)} collective-permute-done((bf16[32,3712]{1,0:T(8,128)(2,1)S(1)}, bf16[32,3712]{1,0:T(8,128)(2,1)S(1)}, u32[]{:S(2)}, u32[]{:S(2)}) %collective-permute-start.4) | collective-permute-done | bytes 237600 | tf_op jit(solution)/shard_map/ppermute | solution.py:58
  25.3 3.3 %shard_map.141 = (f32[64,512]{1,0:T(8,128)S(1)}, f32[64,512]{1,0:T(8,128)S(1)}, bf16[512,3584]{1,0:T(8,128)(2,1)S(1)}) custom-call(bf16[64,3712]{1,0:T(8,128)(2,1)S(1)} %shard_map.140.near_ref, bf16[3584,512]{1,0:T(8,128)(2,1)S(1)} %get-tuple-element.27.gate_ref, bf16[3584,512]{1,0:T(8,128)(2,1)S(1)} %shard_map.135.rest_0_.up_ref, bf16[1,512,7168]{2,1,0:T(8,128)(2,1)} %down_ref.3), custom_call_target="tpu_custom_call" | custom-call | flops 469762048 | bytes 7340032 | tf_op jit(solution)/shard_map/pallas_call | solution.py:251
  28.6 3.3 %shard_map.142 = (bf16[64,512]{1,0:T(8,128)(2,1)S(1)}, bf16[64,3584]{1,0:T(8,128)(2,1)S(1)}, bf16[512,3584]{1,0:T(8,128)(2,1)S(1)}) custom-call(bf16[64,3712]{1,0:T(8,128)(2,1)S(1)} %shard_map.140.near_ref, bf16[64,3712]{1,0:T(8,128)(2,1)S(1)} %collective-permute-done.5.far_ref, bf16[3584,512]{1,0:T(8,128)(2,1)S(1)} %shard_map.137.rest_0_.gate_ref, ...), custom_call_target="tpu_custom_call" | custom-call | flops 704643072 | bytes 11010048 | tf_op jit(solution)/shard_map/pallas_call | solution.py:266
  31.9 0.6 collective-permute-start.6
  32.4 0.2 pad_maximum_fusion.1
  32.6 0.1 collective-permute-start.9
  32.7 1.6 %shard_map.143.keep_ref = f32[64,3584]{1,0:T(8,128)S(1)} custom-call(bf16[64,3712]{1,0:T(8,128)(2,1)S(1)} %shard_map.140.near_ref, bf16[64,512]{1,0:T(8,128)(2,1)S(1)} %get-tuple-element.31.inner_ref, bf16[512,3584]{1,0:T(8,128)(2,1)S(1)} %get-tuple-element.32.down_ref), custom_call_target="tpu_custom_call" | custom-call | flops 234881024 | bytes 3670016 | tf_op jit(solution)/shard_map/pallas_call | solution.py:289
  34.3 1.3 %collective-permute-start.7 = (bf16[32,3584]{1,0:T(8,128)(2,1)S(1)}, bf16[32,3584]{1,0:T(8,128)(2,1)S(1)}, u32[]{:S(2)}, u32[]{:S(2)}) collective-permute-start(bf16[32,3584]{1,0:T(8,128)(2,1)S(1)} %get-tuple-element.35), channel_id=1, source_target_pairs={{0,2},{1,5},{2,0},{3,7},{4,6},{5,1},{6,4},{7,3},{8,10},{9,13},{10,... | collective-permute-start | bytes 688136 | tf_op jit(solution)/shard_map/ppermute | solution.py:58
  35.7 0.2 pad_maximum_fusion.arrived_ref
  35.9 2.4 %shard_map.145.rest_0_ = bf16[2,32768]{1,0:T(2,128)(2,1)} custom-call(s32[2]{0:T(128)S(1)} %copy-done.2, s32[2,12]{1,0:T(2,128)S(1)} %copy-done.1, bf16[2,36864]{1,0:T(2,128)(2,1)S(1)} %copy-done, bf16[24,18432]{1,0:T(8,128)(2,1)S(1)} %get-tuple-element.36.pool_ref, bf16[8,18432]{1,0:T(8,128)(2,1)S(1)} %pad_maximum_fusion.arrived_ref), custom_call_target="tpu_custom_call" | custom-call | flops 1073741824 | bytes 4194304 | tf_op jit(solution)/shard_map/pallas_call | solution.py:491
  38.3 2.1 %collective-permute-done.7.got_ref = bf16[32,3584]{1,0:T(8,128)(2,1)S(1)} collective-permute-done((bf16[32,3584]{1,0:T(8,128)(2,1)S(1)}, bf16[32,3584]{1,0:T(8,128)(2,1)S(1)}, u32[]{:S(2)}, u32[]{:S(2)}) %collective-permute-start.7) | collective-permute-done | bytes 229408 | tf_op jit(solution)/shard_map/ppermute | solution.py:58
  40.5 1.3 %collective-permute-start.10 = (bf16[16,3584]{1,0:T(8,128)(2,1)S(1)}, bf16[16,3584]{1,0:T(8,128)(2,1)S(1)}, u32[]{:S(2)}, u32[]{:S(2)}) collective-permute-start(bf16[16,3584]{1,0:T(8,128)(2,1)S(1)} %get-tuple-element.39), channel_id=1, source_target_pairs={{0,4},{1,3},{2,6},{3,1},{4,0},{5,7},{6,2},{7,5},{8,12},{9,11},{10,... | collective-permute-start | bytes 344072 | tf_op jit(solution)/shard_map/ppermute | solution.py:58
  41.8 3.5 %collective-permute-done.10.got_ref = bf16[16,3584]{1,0:T(8,128)(2,1)S(1)} collective-permute-done((bf16[16,3584]{1,0:T(8,128)(2,1)S(1)}, bf16[16,3584]{1,0:T(8,128)(2,1)S(1)}, u32[]{:S(2)}, u32[]{:S(2)}) %collective-permute-start.10) | collective-permute-done | bytes 114720 | tf_op jit(solution)/shard_map/ppermute | solution.py:58
  45.4 1.5 %collective-permute-start.11 = (bf16[8,3584]{1,0:T(8,128)(2,1)S(1)}, bf16[8,3584]{1,0:T(8,128)(2,1)S(1)}, u32[]{:S(2)}, u32[]{:S(2)}) collective-permute-start(bf16[8,3584]{1,0:T(8,128)(2,1)S(1)} %get-tuple-element.41), channel_id=1, source_target_pairs={{0,8},{1,9},{2,10},{3,11},{4,12},{5,13},{6,14},{7,15},{8,0},{9,1},... | collective-permute-start | bytes 172040 | tf_op jit(solution)/shard_map/ppermute | solution.py:58
  46.9 2.7 %collective-permute-done.11.got_ref = bf16[8,3584]{1,0:T(8,128)(2,1)S(1)} collective-permute-done((bf16[8,3584]{1,0:T(8,128)(2,1)S(1)}, bf16[8,3584]{1,0:T(8,128)(2,1)S(1)}, u32[]{:S(2)}, u32[]{:S(2)}) %collective-permute-start.11) | collective-permute-done | bytes 57376 | tf_op jit(solution)/shard_map/ppermute | solution.py:58
  49.7 2.5 %collective-permute-start.12 = (bf16[4,3584]{1,0:T(4,128)(2,1)S(1)}, bf16[4,3584]{1,0:T(4,128)(2,1)S(1)}, u32[]{:S(2)}, u32[]{:S(2)}) collective-permute-start(bf16[4,3584]{1,0:T(4,128)(2,1)S(1)} %get-tuple-element.43), channel_id=1, source_target_pairs={{0,16},{1,17},{2,18},{3,19},{4,20},{5,21},{6,22},{7,23},{8,24},{9,... | collective-permute-start | bytes 86024 | tf_op jit(solution)/shard_map/ppermute | solution.py:58
  52.2 2.3 %collective-permute-done.12.got_ref = bf16[4,3584]{1,0:T(4,128)(2,1)S(1)} collective-permute-done((bf16[4,3584]{1,0:T(4,128)(2,1)S(1)}, bf16[4,3584]{1,0:T(4,128)(2,1)S(1)}, u32[]{:S(2)}, u32[]{:S(2)}) %collective-permute-start.12) | collective-permute-done | bytes 28704 | tf_op jit(solution)/shard_map/ppermute | solution.py:58
  54.6 1.2 %collective-permute-done.13.got_ref = bf16[2,3584]{1,0:T(2,128)(2,1)S(1)} collective-permute-done((bf16[2,3584]{1,0:T(2,128)(2,1)S(1)}, bf16[2,3584]{1,0:T(2,128)(2,1)S(1)}, u32[]{:S(2)}, u32[]{:S(2)}) %collective-permute-start.13) | collective-permute-done | bytes 14368 | tf_op jit(solution)/shard_map/ppermute | solution.py:58
  55.8 0.6 %shard_map.150 = bf16[2,7168]{1,0:T(2,128)(2,1)} custom-call(f32[2,3584]{1,0:T(2,128)S(1)} %get-tuple-element.44.keep_ref, bf16[2,3584]{1,0:T(2,128)(2,1)S(1)} %collective-permute-done.13.got_ref), custom_call_target="tpu_custom_call" | custom-call | bytes 57344 | tf_op jit(solution)/shard_map/pallas_call | solution.py:333
  (26 shorter events, 0.7 us)
Async XLA Ops:
  1.5 1.4 %collective-permute-start = (bf16[2,3712]{1,0:T(2,128)(2,1)S(1)}, bf16[2,3712]{1,0:T(2,128)(2,1)S(1)}, u32[]{:S(2)}, u32[]{:S(2)}) collective-permute-start(bf16[2,3712]{1,0:T(2,128)(2,1)S(1)} %get-tuple-element.25), channel_id=1, source_target_pairs={{0,1},{1,0},{2,3},{3,2},{4,5},{5,4},{6,7},{7,6},{8,9},{9,8},{10,11... | collective-permute-start | bytes 44552 | tf_op jit(solution)/shard_map/ppermute | solution.py:58
  2.9 6.4 %collective-permute-start.1 = (bf16[4,3712]{1,0:T(4,128)(2,1)S(1)}, bf16[4,3712]{1,0:T(4,128)(2,1)S(1)}, u32[]{:S(2)}, u32[]{:S(2)}) collective-permute-start(bf16[4,3712]{1,0:T(4,128)(2,1)S(1)} %shard_map.132.after_ref.near_ref), channel_id=1, source_target_pairs={{0,16},{1,17},{2,18},{3,19},{4,20},{5,21},{6,22},{7,23},{8,24},{9,... | collective-permute-start | bytes 89096 | tf_op jit(solution)/shard_map/ppermute | solution.py:58
  9.3 4.3 %collective-permute-start.2 = (bf16[8,3712]{1,0:T(8,128)(2,1)S(1)}, bf16[8,3712]{1,0:T(8,128)(2,1)S(1)}, u32[]{:S(2)}, u32[]{:S(2)}) collective-permute-start(bf16[8,3712]{1,0:T(8,128)(2,1)S(1)} %shard_map.134.refs_1_.near_ref), channel_id=1, source_target_pairs={{0,8},{1,9},{2,10},{3,11},{4,12},{5,13},{6,14},{7,15},{8,0},{9,1},... | collective-permute-start | bytes 178184 | tf_op jit(solution)/shard_map/ppermute | solution.py:58
  13.6 5.3 %collective-permute-start.3 = (bf16[16,3712]{1,0:T(8,128)(2,1)S(1)}, bf16[16,3712]{1,0:T(8,128)(2,1)S(1)}, u32[]{:S(2)}, u32[]{:S(2)}) collective-permute-start(bf16[16,3712]{1,0:T(8,128)(2,1)S(1)} %shard_map.136.refs_1_.near_ref), channel_id=1, source_target_pairs={{0,4},{1,3},{2,6},{3,1},{4,0},{5,7},{6,2},{7,5},{8,12},{9,11},{10,... | collective-permute-start | bytes 356360 | tf_op jit(solution)/shard_map/ppermute | solution.py:58
  15.3 9.9 %collective-permute-start.8 = (bf16[4,18432]{1,0:T(4,128)(2,1)S(1)}, bf16[4,18432]{1,0:T(4,128)(2,1)S(1)}, u32[]{:S(2)}, u32[]{:S(2)}) collective-permute-start(bf16[4,18432]{1,0:T(4,128)(2,1)S(1)} %get-tuple-element.26.rest_0_), channel_id=1, source_target_pairs={{0,2},{1,3},{2,0},{3,1},{4,6},{5,7},{6,4},{7,5},{8,10},{9,11},{10,... | collective-permute-start | bytes 442376 | tf_op jit(solution)/shard_map/ppermute | solution.py:58
  18.9 6.2 %collective-permute-start.4 = (bf16[32,3712]{1,0:T(8,128)(2,1)S(1)}, bf16[32,3712]{1,0:T(8,128)(2,1)S(1)}, u32[]{:S(2)}, u32[]{:S(2)}) collective-permute-start(bf16[32,3712]{1,0:T(8,128)(2,1)S(1)} %shard_map.138.refs_1_.near_ref), channel_id=1, source_target_pairs={{0,2},{1,5},{2,0},{3,7},{4,6},{5,1},{6,4},{7,3},{8,10},{9,13},{10,... | collective-permute-start | bytes 712712 | tf_op jit(solution)/shard_map/ppermute | solution.py:58
  25.1 3.5 %collective-permute-start.5 = (bf16[64,3712]{1,0:T(8,128)(2,1)S(1)}, bf16[64,3712]{1,0:T(8,128)(2,1)S(1)}, u32[]{:S(2)}, u32[]{:S(2)}) collective-permute-start(bf16[64,3712]{1,0:T(8,128)(2,1)S(1)} %shard_map.140.near_ref), channel_id=1, source_target_pairs={{0,1},{1,0},{2,3},{3,2},{4,5},{5,4},{6,7},{7,6},{8,9},{9,8},{10,11... | collective-permute-start | bytes 1425416 | tf_op jit(solution)/shard_map/ppermute | solution.py:58
  31.9 2.4 %collective-permute-start.6 = (bf16[64,3584]{1,0:T(8,128)(2,1)S(1)}, bf16[64,3584]{1,0:T(8,128)(2,1)S(1)}, u32[]{:S(2)}, u32[]{:S(2)}) collective-permute-start(bf16[64,3584]{1,0:T(8,128)(2,1)S(1)} %get-tuple-element.33), channel_id=1, source_target_pairs={{0,1},{1,0},{2,3},{3,2},{4,5},{5,4},{6,7},{7,6},{8,9},{9,8},{10,11... | collective-permute-start | bytes 1376264 | tf_op jit(solution)/shard_map/ppermute | solution.py:58
  32.4 3.5 %copy-start = (bf16[2,36864]{1,0:T(2,128)(2,1)S(1)}, bf16[2,36864]{1,0:T(2,128)(2,1)}, u32[]{:S(2)}) copy-start(bf16[2,36864]{1,0:T(2,128)(2,1)} %query_ref.1) | copy-start | bytes 442372
  32.4 3.5 %copy-start.1 = (s32[2,12]{1,0:T(2,128)S(1)}, s32[2,12]{1,0:T(2,128)}, u32[]{:S(2)}) copy-start(s32[2,12]{1,0:T(2,128)} %table_ref.1) | copy-start | bytes 292
  32.4 3.5 %copy-start.2 = (s32[2]{0:T(128)S(1)}, s32[2]{0:T(128)}, u32[]{:S(2)}) copy-start(s32[2]{0:T(128)} %length_ref.1) | copy-start | bytes 28
  32.6 3.1 %collective-permute-start.9 = (bf16[4,18432]{1,0:T(4,128)(2,1)S(1)}, bf16[4,18432]{1,0:T(4,128)(2,1)S(1)}, u32[]{:S(2)}, u32[]{:S(2)}) collective-permute-start(bf16[4,18432]{1,0:T(4,128)(2,1)S(1)} %pad_maximum_fusion.1), channel_id=1, source_target_pairs={{0,1},{1,0},{2,3},{3,2},{4,5},{5,4},{6,7},{7,6},{8,9},{9,8},{10,11... | collective-permute-start | bytes 442376 | tf_op jit(solution)/shard_map/ppermute | solution.py:58
  34.3 6.1 %collective-permute-start.7 = (bf16[32,3584]{1,0:T(8,128)(2,1)S(1)}, bf16[32,3584]{1,0:T(8,128)(2,1)S(1)}, u32[]{:S(2)}, u32[]{:S(2)}) collective-permute-start(bf16[32,3584]{1,0:T(8,128)(2,1)S(1)} %get-tuple-element.35), channel_id=1, source_target_pairs={{0,2},{1,5},{2,0},{3,7},{4,6},{5,1},{6,4},{7,3},{8,10},{9,13},{10,... | collective-permute-start | bytes 688136 | tf_op jit(solution)/shard_map/ppermute | solution.py:58
  40.5 4.9 %collective-permute-start.10 = (bf16[16,3584]{1,0:T(8,128)(2,1)S(1)}, bf16[16,3584]{1,0:T(8,128)(2,1)S(1)}, u32[]{:S(2)}, u32[]{:S(2)}) collective-permute-start(bf16[16,3584]{1,0:T(8,128)(2,1)S(1)} %get-tuple-element.39), channel_id=1, source_target_pairs={{0,4},{1,3},{2,6},{3,1},{4,0},{5,7},{6,2},{7,5},{8,12},{9,11},{10,... | collective-permute-start | bytes 344072 | tf_op jit(solution)/shard_map/ppermute | solution.py:58
  45.4 4.2 %collective-permute-start.11 = (bf16[8,3584]{1,0:T(8,128)(2,1)S(1)}, bf16[8,3584]{1,0:T(8,128)(2,1)S(1)}, u32[]{:S(2)}, u32[]{:S(2)}) collective-permute-start(bf16[8,3584]{1,0:T(8,128)(2,1)S(1)} %get-tuple-element.41), channel_id=1, source_target_pairs={{0,8},{1,9},{2,10},{3,11},{4,12},{5,13},{6,14},{7,15},{8,0},{9,1},... | collective-permute-start | bytes 172040 | tf_op jit(solution)/shard_map/ppermute | solution.py:58
  49.7 4.8 %collective-permute-start.12 = (bf16[4,3584]{1,0:T(4,128)(2,1)S(1)}, bf16[4,3584]{1,0:T(4,128)(2,1)S(1)}, u32[]{:S(2)}, u32[]{:S(2)}) collective-permute-start(bf16[4,3584]{1,0:T(4,128)(2,1)S(1)} %get-tuple-element.43), channel_id=1, source_target_pairs={{0,16},{1,17},{2,18},{3,19},{4,20},{5,21},{6,22},{7,23},{8,24},{9,... | collective-permute-start | bytes 86024 | tf_op jit(solution)/shard_map/ppermute | solution.py:58
  54.5 1.2 %collective-permute-start.13 = (bf16[2,3584]{1,0:T(2,128)(2,1)S(1)}, bf16[2,3584]{1,0:T(2,128)(2,1)S(1)}, u32[]{:S(2)}, u32[]{:S(2)}) collective-permute-start(bf16[2,3584]{1,0:T(2,128)(2,1)S(1)} %get-tuple-element.45), channel_id=1, source_target_pairs={{0,1},{1,0},{2,3},{3,2},{4,5},{5,4},{6,7},{7,6},{8,9},{9,8},{10,11... | collective-permute-start | bytes 43016 | tf_op jit(solution)/shard_map/ppermute | solution.py:58

commit v4 on v3

v4 whole, which is shorter than its diff:
```python
import functools

import jax
import jax.numpy as jnp
from jax import lax
from jax.experimental import pallas as pl
from jax.experimental.pallas import tpu as pltpu
from jax.sharding import PartitionSpec as P

HEADS = 64
LAT = 576
VL = 512
MCAP = 2
PAGE = 32
LANES = 128
AXES = ("ep", "dp")
MIB = 1 << 20
MERGE_FLOPS = 20_000_000_000

score_scale = 192.0 ** (-0.5)
bf16 = jnp.bfloat16
f32 = jnp.float32


def in_vmem():
    return pl.BlockSpec(memory_space=pltpu.VMEM)


def in_smem():
    return pl.BlockSpec(memory_space=pltpu.SMEM)


def vmem(x):
    return pltpu.with_memory_space_constraint(x, pltpu.VMEM)


def hbm(x):
    return pltpu.with_memory_space_constraint(x, pltpu.HBM)


def anywhere():
    return pl.BlockSpec(memory_space=pl.ANY)


def in_hbm():
    return pl.BlockSpec(memory_space=pltpu.HBM)


def partner_bits(count):
    bits = []
    b = count // 2
    while b:
        bits.append(b)
        b //= 2
    return bits


def swap(x, axes, pairs):
    return lax.ppermute(x, axes, pairs)


def stage_partners(count):
    bits = partner_bits(count)[:-1]
    stages = [(bits[0],)] if len(bits) % 2 else []
    bits = bits[len(bits) % 2 :]
    for high, low in zip(bits[::2], bits[1::2]):
        stages.append((low, high, high ^ low))
    return stages


def pairs_of(count, bit):
    return [(i, i ^ bit) for i in range(count)]


def payload_kernel(ep_count, hidden_hbm, routes_hbm, weight_hbm, mine_ref, other_ref, hidden_ref, routes_ref, weight_ref, sems):
    copies = [
        pltpu.make_async_copy(source, target, sems.at[i])
        for i, (source, target) in enumerate(
            [(hidden_hbm, hidden_ref), (routes_hbm, routes_ref), (weight_hbm, weight_ref)]
        )
    ]
    for c in copies:
        c.start()
    for c in copies:
        c.wait()
    rows, width = hidden_ref.shape
    half = width // 2
    column = lax.broadcasted_iota(jnp.int32, (rows, LANES), 1)
    expert = jnp.where(column < ep_count, column, column - ep_count)
    total = jnp.zeros((rows, LANES), f32)
    for k in range(routes_ref.shape[1]):
        total += jnp.where(routes_ref[:, k : k + 1] == expert, weight_ref[:, k : k + 1], 0.0)
    high = total.astype(bf16).astype(f32)
    low = total - high
    value = jnp.where(column < ep_count, high, jnp.where(column < 2 * ep_count, low, 0.0)).astype(bf16)
    first = lax.rem(lax.axis_index("dp"), 2) == 0
    left, right = hidden_ref[:, :half].astype(f32), hidden_ref[:, half:].astype(f32)
    mine_ref[:, :half] = jnp.where(first, left, right).astype(bf16)
    other_ref[:, :half] = jnp.where(first, right, left).astype(bf16)
    mine_ref[:, half:] = value
    other_ref[:, half:] = value


def make_payload(hidden, routes, route_weight, ep_count):
    rows, width = hidden.shape
    half = pltpu.VMEM((rows, width // 2 + LANES), bf16)
    return pl.pallas_call(
        functools.partial(payload_kernel, ep_count),
        out_shape=(half, half),
        in_specs=[in_hbm()] * 3,
        out_specs=(in_vmem(), in_vmem()),
        scratch_shapes=[
            pltpu.VMEM(hidden.shape, bf16),
            pltpu.VMEM(routes.shape, jnp.int32),
            pltpu.VMEM(route_weight.shape, f32),
            pltpu.SemaphoreType.DMA((3,)),
        ],
        compiler_params=pltpu.CompilerParams(vmem_limit_bytes=4 * MIB),
        cost_estimate=pl.CostEstimate(flops=0, bytes_accessed=4 * rows * width, transcendentals=0),
    )(hbm(hidden), hbm(routes), hbm(route_weight))


def merge_kernel(by_core, parts, *refs):
    out_ref = refs[-1]
    rows = refs[0].shape[0]
    if rows % 16:
        pieces = [r[...].astype(f32) for r in refs[:parts]]
        both = jnp.concatenate(pieces, axis=0)
        if by_core:
            first = lax.rem(lax.axis_index("dp"), 2) == 0
            both = jnp.where(first, both, jnp.concatenate(pieces[::-1], axis=0))
        out_ref[...] = both.astype(bf16)
    else:
        for i in range(parts):
            out_ref[i * rows : (i + 1) * rows] = refs[i][...]


def merge(pieces, *after, by_core=False):
    rows, width = pieces[0].shape
    return pl.pallas_call(
        functools.partial(merge_kernel, by_core, len(pieces)),
        out_shape=pltpu.VMEM((len(pieces) * rows, width), bf16),
        in_specs=[in_vmem()] * len(pieces) + [anywhere()] * len(after),
        out_specs=in_vmem(),
        compiler_params=pltpu.CompilerParams(vmem_limit_bytes=4 * MIB),
        cost_estimate=pl.CostEstimate(flops=MERGE_FLOPS, bytes_accessed=8 * MIB, transcendentals=0),
    )(*[vmem(p) for p in pieces], *after)


def half_start(width, near):
    core = lax.rem(lax.axis_index("dp"), 2)
    core = core if near else 1 - core
    return pl.multiple_of(core * (width // 2), width // 2)


def near_kernel(near_ref, gate_ref, up_ref, gate_out, up_out):
    width = gate_ref.shape[1]
    at = pl.ds(half_start(width, True), width // 2)
    x = near_ref[:, : width // 2]
    gate_out[...] = jnp.dot(x, gate_ref[0, at, :], preferred_element_type=f32)
    up_out[...] = jnp.dot(x, up_ref[0, at, :], preferred_element_type=f32)


def row_weights(near_ref, half, ep_count):
    ep = lax.axis_index("ep")
    table = near_ref[:, half:].astype(f32)
    column = lax.broadcasted_iota(jnp.int32, table.shape, 1)
    mine = (column == ep) | (column == ep + ep_count)
    return jnp.sum(jnp.where(mine, table, 0.0), axis=1, keepdims=True)


STEPS = 7


def far_kernel(ep_count, near_ref, far_ref, gate_ref, up_ref, gate_in, up_in, down_ref, inner_ref, send_ref):
    width = gate_ref.shape[1]
    half = width // 2
    start = half_start(width, False)
    at = pl.ds(start, half)
    row_weight = row_weights(near_ref, half, ep_count)
    x = far_ref[:, :half]
    gate = gate_in[...] + jnp.dot(x, gate_ref[0, at, :], preferred_element_type=f32)
    up = up_in[...] + jnp.dot(x, up_ref[0, at, :], preferred_element_type=f32)
    inner = (gate / (1.0 + jnp.exp(-gate)) * up).astype(bf16)
    inner_ref[...] = inner
    step = half // STEPS
    for i in range(STEPS):
        columns = pl.ds(pl.multiple_of(start + i * step, step), step)
        out = jnp.dot(inner, down_ref[0, :, columns], preferred_element_type=f32) * row_weight
        send_ref[:, i * step : (i + 1) * step] = out.astype(bf16)


def keep_kernel(ep_count, near_ref, inner_ref, down_ref, keep_ref):
    half = keep_ref.shape[1]
    start = half_start(2 * half, True)
    row_weight = row_weights(near_ref, half, ep_count)
    step = half // STEPS
    inner = inner_ref[...]
    for i in range(STEPS):
        columns = pl.ds(pl.multiple_of(start + i * step, step), step)
        out = jnp.dot(inner, down_ref[0, :, columns], preferred_element_type=f32)
        keep_ref[:, i * step : (i + 1) * step] = out * row_weight


def estimate(rows, weights):
    return pl.CostEstimate(flops=2 * rows * weights, bytes_accessed=2 * weights, transcendentals=0)


def near_products(near, gate, up):
    rows = near.shape[0]
    width, units = gate.shape[1:]
    acc = pltpu.VMEM((rows, units), f32)
    return pl.pallas_call(
        near_kernel,
        out_shape=(acc, acc),
        in_specs=[in_vmem()] * 3,
        out_specs=(in_vmem(),) * 2,
        compiler_params=pltpu.CompilerParams(vmem_limit_bytes=8 * MIB),
        cost_estimate=estimate(rows, width * units),
    )(vmem(near), gate, up)


def far_products(near, far, gate, up, gate_acc, up_acc, down, ep_count):
    rows = near.shape[0]
    units, width = down.shape[1:]
    half = width // 2
    return pl.pallas_call(
        functools.partial(far_kernel, ep_count),
        out_shape=(pltpu.VMEM((rows, units), bf16), pltpu.VMEM((rows, half), bf16)),
        in_specs=[in_vmem()] * 7,
        out_specs=(in_vmem(),) * 2,
        compiler_params=pltpu.CompilerParams(vmem_limit_bytes=8 * MIB),
        cost_estimate=estimate(rows, 3 * half * units),
    )(vmem(near), vmem(far), gate, up, vmem(gate_acc), vmem(up_acc), down)


def keep_products(near, inner, down, ep_count):
    rows = near.shape[0]
    units, width = down.shape[1:]
    half = width // 2
    return pl.pallas_call(
        functools.partial(keep_kernel, ep_count),
        out_shape=pltpu.VMEM((rows, half), f32),
        in_specs=[in_vmem()] * 3,
        out_specs=in_vmem(),
        compiler_params=pltpu.CompilerParams(vmem_limit_bytes=8 * MIB),
        cost_estimate=estimate(rows, half * units),
    )(vmem(near), vmem(inner), down)


def fold_kernel(by_core, parts, arrived, *refs):
    keep_ref, got_refs = refs[0], refs[1 : 1 + arrived]
    outs = refs[-parts:]
    total = keep_ref[...]
    for g in got_refs:
        total += g[...].astype(f32)
    rows = outs[0].shape[0]
    pieces = [total[i * rows : (i + 1) * rows] for i in range(parts)]
    if by_core:
        first = lax.rem(lax.axis_index("dp"), 2) == 0
        pieces = [jnp.where(first, pieces[0], pieces[1]), jnp.where(first, pieces[1], pieces[0])]
    outs[0][...] = pieces[0]
    for out, piece in zip(outs[1:], pieces[1:]):
        out[...] = piece.astype(bf16)


def fold(keep, gots, parts, *after, by_core=False):
    rows, width = keep.shape
    part = (rows // parts, width)
    return pl.pallas_call(
        functools.partial(fold_kernel, by_core, parts, len(gots)),
        out_shape=(pltpu.VMEM(part, f32),) + (pltpu.VMEM(part, bf16),) * (parts - 1),
        in_specs=[in_vmem()] * (1 + len(gots)) + [anywhere()] * len(after),
        out_specs=(in_vmem(),) * parts,
        compiler_params=pltpu.CompilerParams(vmem_limit_bytes=4 * MIB),
        cost_estimate=pl.CostEstimate(flops=0, bytes_accessed=8 * rows * width, transcendentals=0),
    )(vmem(keep), *[vmem(g) for g in gots], *after)


def finish_kernel(keep_ref, got_ref, out_ref):
    half = keep_ref.shape[1]
    first = lax.rem(lax.axis_index("dp"), 2) == 0
    keep, got = keep_ref[...], got_ref[...].astype(f32)
    out_ref[:, :half] = jnp.where(first, keep, got).astype(bf16)
    out_ref[:, half:] = jnp.where(first, got, keep).astype(bf16)


def finish(keep, got):
    rows, half = keep.shape
    return pl.pallas_call(
        finish_kernel,
        out_shape=jax.ShapeDtypeStruct((rows, 2 * half), bf16),
        in_specs=[in_vmem(), in_vmem()],
        out_specs=in_vmem(),
        compiler_params=pltpu.CompilerParams(vmem_limit_bytes=4 * MIB),
        cost_estimate=pl.CostEstimate(flops=0, bytes_accessed=8 * rows * half, transcendentals=0),
    )(vmem(keep), vmem(got))


def pages_kernel(
    dp_count, page_hbm, dest_hbm, pool_ref, after_ref, low_ref, high_ref, copy_ref, page_ref, dest_ref, sems
):
    own, width = pool_ref.shape
    pool_copy = pltpu.make_async_copy(pool_ref, copy_ref, sems.at[0])
    page_copy = pltpu.make_async_copy(page_hbm, page_ref, sems.at[1])
    dest_copy = pltpu.make_async_copy(dest_hbm, dest_ref, sems.at[2])
    page_copy.start()
    dest_copy.start()
    pool_copy.start()
    page_copy.wait()
    dest_copy.wait()
    me = lax.axis_index("dp")
    slots = dp_count * MCAP
    row = lax.broadcasted_iota(jnp.int32, (slots, own), 0)
    column = lax.broadcasted_iota(jnp.int32, (slots, own), 1)
    pick = jnp.zeros((slots, own), f32)
    entries = page_ref.shape[1]
    for m in range(entries):
        rank = jnp.int32(0)
        for n in range(m):
            rank += jnp.where(dest_ref[0, n] == dest_ref[0, m], 1, 0)
        bucket = jnp.bitwise_xor(dest_ref[0, m], me) * MCAP + rank
        pick = jnp.where((row == bucket) & (column == page_ref[0, m]), 1.0, pick)
    pick = pick.astype(bf16)
    step = 2048
    pool_copy.wait()
    for i in range(width // step):
        columns = slice(i * step, (i + 1) * step)
        out = jnp.dot(pick, copy_ref[:, columns], preferred_element_type=f32)
        low_ref[:, columns] = out[: slots // 2].astype(bf16)
        high_ref[:, columns] = out[slots // 2 :].astype(bf16)


def pick_pages(moved_page, moved_dest, latent_pool, after, dp_count):
    width = latent_pool.shape[1]
    half = pltpu.VMEM((dp_count * MCAP // 2, width), bf16)
    return pl.pallas_call(
        functools.partial(pages_kernel, dp_count),
        out_shape=(half, half, pltpu.VMEM(latent_pool.shape, bf16)),
        in_specs=[in_hbm()] * 3 + [anywhere()],
        out_specs=(in_vmem(),) * 3,
        scratch_shapes=[
            pltpu.SMEM(moved_page.shape, jnp.int32),
            pltpu.SMEM(moved_dest.shape, jnp.int32),
            pltpu.SemaphoreType.DMA((3,)),
        ],
        compiler_params=pltpu.CompilerParams(vmem_limit_bytes=4 * MIB),
        cost_estimate=pl.CostEstimate(flops=0, bytes_accessed=4 * latent_pool.size, transcendentals=0),
    )(hbm(moved_page), hbm(moved_dest), hbm(latent_pool), after)


def exchange_pages(low, high, dp_count):
    blocks, senders = [low], [0]
    sent = high
    for bit in partner_bits(dp_count):
        got = swap(sent, "dp", pairs_of(dp_count, bit))
        size = got.shape[0] // len(blocks)
        blocks = blocks + [got[i * size : (i + 1) * size] for i in range(len(blocks))]
        senders = senders + [s ^ bit for s in senders]
        if size > MCAP:
            sent = jnp.concatenate([b[size // 2 :] for b in blocks], axis=0)
            blocks = [b[: size // 2] for b in blocks]
    return jnp.concatenate(blocks, axis=0), senders


def attend_kernel(senders, length_ref, table_ref, query_ref, pool_ref, arrived_ref, out_ref, query_rows):
    rows_dev = query_ref.shape[0]
    own, width = pool_ref.shape
    arrived = arrived_ref.shape[0]
    slots = -(-(own + arrived) // 16) * 16
    pair_width = 2 * LAT
    pairs = width // pair_width
    me = lax.axis_index("dp")

    for h in range(HEADS // 2):
        query_rows[h * rows_dev : (h + 1) * rows_dev, :] = query_ref[:, h * pair_width : (h + 1) * pair_width].astype(f32)
    straight = query_rows[...]
    turned = pltpu.roll(straight, LAT, 1)
    first = lax.broadcasted_iota(jnp.int32, straight.shape, 1) < LAT
    query_all = jnp.concatenate(
        [
            jnp.where(first, straight, 0.0),
            jnp.where(first, turned, 0.0),
            jnp.where(first, 0.0, turned),
            jnp.where(first, 0.0, straight),
        ],
        axis=0,
    ).astype(bf16)

    pieces = []
    for j in range(pairs):
        columns = slice(j * pair_width, (j + 1) * pair_width)
        parts = [pool_ref[:, columns].astype(f32), arrived_ref[:, columns].astype(f32)]
        if slots > own + arrived:
            parts.append(jnp.zeros((slots - own - arrived, pair_width), f32))
        pieces.append(jnp.concatenate(parts, axis=0).astype(bf16))
    keys = jnp.concatenate(pieces, axis=0)

    scores = lax.dot_general(query_all, keys, (((1,), (1,)), ((), ())), preferred_element_type=f32) * score_scale

    column = lax.broadcasted_iota(jnp.int32, (1, pairs * slots), 1)
    pair = column // slots
    place = column - pair * slots
    slot = place
    for i, s in enumerate(senders):
        source = jnp.bitwise_xor(me, s)
        for k in range(MCAP):
            slot = jnp.where(place == own + i * MCAP + k, own + source * MCAP + k, slot)
    limits = []
    for r in range(rows_dev):
        limit = jnp.full(column.shape, -1, jnp.int32)
        for p in range(table_ref.shape[1]):
            limit = jnp.where(slot == table_ref[r, p], length_ref[r] - p * PAGE, limit)
        limit = jnp.where(place < own + arrived, limit, -1)
        limits.append(limit - 2 * pair)
    half = scores.shape[0] // 2
    row = lax.broadcasted_iota(jnp.int32, (half, 1), 0) % rows_dev
    limit = limits[0]
    for r in range(1, rows_dev):
        limit = jnp.where(row == r, limits[r], limit)
    even = jnp.where(limit > 0, scores[:half], -jnp.inf)
    odd = jnp.where(limit > 1, scores[half:], -jnp.inf)
    peak = jnp.maximum(jnp.max(even, axis=1, keepdims=True), jnp.max(odd, axis=1, keepdims=True))
    even = jnp.exp(even - peak)
    odd = jnp.exp(odd - peak)
    total = jnp.sum(even, axis=1, keepdims=True) + jnp.sum(odd, axis=1, keepdims=True)
    even = (even / total).astype(bf16)
    odd = (odd / total).astype(bf16)
    from_even = jnp.dot(even, keys[:, :VL], preferred_element_type=f32)
    from_odd = jnp.dot(odd, keys[:, VL:], preferred_element_type=f32)
    shift = LAT - VL
    wide = pair_width - VL
    attended = from_even + pltpu.roll(from_odd, wide - shift, 1)[:, :VL]
    for h in range(HEADS):
        at = (h % 2) * (half // 2) + (h // 2) * rows_dev
        out_ref[:, h * VL : (h + 1) * VL] = attended[at : at + rows_dev].astype(bf16)


def attend(lengths, page_table, queries, latent_pool, arrived, senders):
    rows_dev = queries.shape[0]
    return pl.pallas_call(
        functools.partial(attend_kernel, senders),
        out_shape=jax.ShapeDtypeStruct((rows_dev, HEADS * VL), bf16),
        in_specs=[in_smem(), in_smem(), in_vmem(), in_vmem(), in_vmem()],
        out_specs=in_vmem(),
        scratch_shapes=[pltpu.VMEM((HEADS // 2 * rows_dev, 2 * LAT), f32)],
        compiler_params=pltpu.CompilerParams(vmem_limit_bytes=16 * MIB),
        cost_estimate=pl.CostEstimate(flops=1 << 30, bytes_accessed=4 << 20, transcendentals=1 << 17),
    )(lengths, page_table, queries, vmem(latent_pool), vmem(arrived))


def body(
    hidden,
    routes,
    route_weight,
    gate_weight,
    up_weight,
    down_weight,
    queries,
    latent_pool,
    lengths,
    page_table,
    moved_page,
    moved_dest,
):
    ep_count = lax.axis_size("ep")
    dp_count = lax.axis_size("dp")
    count = ep_count * dp_count
    stages = stage_partners(count)

    def trade(x, bit):
        return swap(x, AXES, pairs_of(count, bit))

    mine, other = make_payload(hidden, routes, route_weight, ep_count)
    near = merge([mine, trade(other, 1)], by_core=True)
    for number, partners in enumerate(stages):
        got = [trade(near, bit) for bit in partners]
        after = []
        if number == 0:
            low, high, pool = pick_pages(moved_page, moved_dest, latent_pool, near, dp_count)
            after = [high]
        near = merge([near] + got, *after)
    arrived, senders = exchange_pages(low, high, dp_count)
    far = trade(near, 1)
    gate_acc, up_acc = near_products(near, gate_weight, up_weight)
    inner, send = far_products(near, far, gate_weight, up_weight, gate_acc, up_acc, down_weight, ep_count)
    got = [trade(send, 1)]
    keep = keep_products(near, inner, down_weight, ep_count)
    attended = attend(lengths, page_table, queries, pool, arrived, senders)
    after = []
    for partners in reversed(stages):
        keep, *send = fold(keep, got, len(partners) + 1, *after)
        got = [trade(x, bit) for x, bit in zip(send, partners)]
        after = [] if after else [hbm(attended)]
    keep, send = fold(keep, got, 2, *(after if len(stages) == 1 else []), by_core=True)
    return finish(keep, trade(send, 1)), attended


def solution(mesh):
    rows = P(("inst", "ep", "dp"), None)
    in_specs = (
        rows,
        rows,
        rows,
        P("ep", None, "dp"),
        P("ep", None, "dp"),
        P("ep", "dp", None),
        rows,
        rows,
        P(("inst", "ep", "dp")),
        rows,
        rows,
        rows,
    )
    return jax.shard_map(body, mesh=mesh, in_specs=in_specs, out_specs=(rows, rows), check_vma=False)
```

time: 56.8 us -> 47.7 us (0.84)
  Pallas kernels: 20.8 us -> 9.92 us
  starting transfers between devices: 18.1 us -> 20.2 us
    pallas_call x14 -> x7, Pallas kernels: 9.75 us -> 1.69 us  [the longest x1 1.38 us: near_products(): pl.pallas_call(near_kernel, out_shape=(acc, acc), in_specs=[in_vmem()] *...]
    ppermute x14 -> x18, starting transfers between devices: 18.1 us -> 20.2 us  [swap(): return lax.ppermute(x, axes, pairs)]
    pallas_call x1, Pallas kernels: 3.29 us -> 2.11 us  [far_products(): pl.pallas_call(functools.partial(far_kernel, ep_count), out_shape=(pltpu....]
    pallas_call x1, Pallas kernels: 2.35 us -> 1.5 us  [pick_pages(): pl.pallas_call(functools.partial(pages_kernel, dp_count), out_shape=(half...]
    pallas_call x1, Pallas kernels: 1.55 us -> 0.75 us  [keep_products(): pl.pallas_call(functools.partial(keep_kernel, ep_count), out_shape=pltpu....]
    ppermute x14 -> x18, waiting for transfers between devices: 16 us -> 15.6 us  [swap(): return lax.ppermute(x, axes, pairs)]
  transfers between devices with their start and end apart: 14 -> 18, of which waited for: 8 -> 9; matrix products, arithmetic and copies ran while one was open for 1% -> 1% of each run, Pallas kernels for 28% -> 13%
where the time goes in v4:
time: 47.7 us; the launch traced here: 47.5 us
  starting transfers between devices  20.2 us (42%)
  waiting for transfers between devices  15.6 us (33%)
  Pallas kernels  9.92 us (21%)
  between operations  0.85 us (2%)
  local copies, waits for them, and re-layouts  0.51 us (1%)
    ppermute x18, starting transfers between devices, swap(): return lax.ppermute(x, axes, pairs)  20.2 us
    ppermute x18, waiting for transfers between devices, swap(): return lax.ppermute(x, axes, pairs)  15.6 us
    pallas_call x1, Pallas kernels, attend(): pl.pallas_call(functools.partial(attend_kernel, senders), out_shape=jax.S...  2.36 us
    pallas_call x1, Pallas kernels, far_products(): pl.pallas_call(functools.partial(far_kernel, ep_count), out_shape=(pltpu....  2.11 us
    pallas_call x1, Pallas kernels, pick_pages(): pl.pallas_call(functools.partial(pages_kernel, dp_count), out_shape=(half...  1.5 us
    pallas_call x1, Pallas kernels, near_products(): pl.pallas_call(near_kernel, out_shape=(acc, acc), in_specs=[in_vmem()] *...  1.38 us
  transfers between devices with their start and end apart: 18, of which 9 were waited for; matrix products, arithmetic and copies ran while one was open for 1% of the time, Pallas kernels for 13%

profile of v4, /device:TPU:0, one launch (start us, length us, event | category | flops | bytes accessed | tf_op | source)
XLA Modules:
  0.0 47.5 jit_solution(9396042173834645973)
XLA Ops:
  0.6 0.9 %shard_map.131 = (bf16[2,3712]{1,0:T(2,128)(2,1)S(1)}, bf16[2,3712]{1,0:T(2,128)(2,1)S(1)}) custom-call(bf16[2,7168]{1,0:T(2,128)(2,1)} %hidden_hbm.1, s32[2,4]{1,0:T(2,128)} %routes_hbm.1, f32[2,4]{1,0:T(2,128)} %weight_hbm.1), custom_call_target="tpu_custom_call" | custom-call | bytes 57344 | tf_op jit(solution)/shard_map/pallas_call | solution.py:107
  1.5 0.5 %collective-permute-start = (bf16[2,3712]{1,0:T(2,128)(2,1)S(1)}, bf16[2,3712]{1,0:T(2,128)(2,1)S(1)}, u32[]{:S(2)}, u32[]{:S(2)}) collective-permute-start(bf16[2,3712]{1,0:T(2,128)(2,1)S(1)} %get-tuple-element.22), channel_id=1, source_target_pairs={{0,1},{1,0},{2,3},{3,2},{4,5},{5,4},{6,7},{7,6},{8,9},{9,8},{10,11... | collective-permute-start | bytes 44552 | tf_op jit(solution)/shard_map/ppermute | solution.py:59
  2.0 0.8 %collective-permute-done.refs_1_ = bf16[2,3712]{1,0:T(2,128)(2,1)S(1)} collective-permute-done((bf16[2,3712]{1,0:T(2,128)(2,1)S(1)}, bf16[2,3712]{1,0:T(2,128)(2,1)S(1)}, u32[]{:S(2)}, u32[]{:S(2)}) %collective-permute-start) | collective-permute-done | bytes 14880 | tf_op jit(solution)/shard_map/ppermute | solution.py:59
  2.9 5.0 %collective-permute-start.3 = (bf16[4,3712]{1,0:T(4,128)(2,1)S(1)}, bf16[4,3712]{1,0:T(4,128)(2,1)S(1)}, u32[]{:S(2)}, u32[]{:S(2)}) collective-permute-start(bf16[4,3712]{1,0:T(4,128)(2,1)S(1)} %shard_map.132.after_ref.refs_0_), channel_id=1, source_target_pairs={{0,24},{1,25},{2,26},{3,27},{4,28},{5,29},{6,30},{7,31},{8,16},{9,... | collective-permute-start | bytes 89096 | tf_op jit(solution)/shard_map/ppermute | solution.py:59
  7.9 0.6 %collective-permute-start.1 = (bf16[4,3712]{1,0:T(4,128)(2,1)S(1)}, bf16[4,3712]{1,0:T(4,128)(2,1)S(1)}, u32[]{:S(2)}, u32[]{:S(2)}) collective-permute-start(bf16[4,3712]{1,0:T(4,128)(2,1)S(1)} %shard_map.132.after_ref.refs_0_), channel_id=1, source_target_pairs={{0,8},{1,9},{2,10},{3,11},{4,12},{5,13},{6,14},{7,15},{8,0},{9,1},... | collective-permute-start | bytes 89096 | tf_op jit(solution)/shard_map/ppermute | solution.py:59
  8.5 1.5 %shard_map.133 = (bf16[4,18432]{1,0:T(4,128)(2,1)S(1)}, bf16[4,18432]{1,0:T(4,128)(2,1)S(1)}, bf16[24,18432]{1,0:T(8,128)(2,1)S(1)}) custom-call(s32[1,6]{1,0:T(1,128)} %page_hbm.1, s32[1,6]{1,0:T(1,128)} %dest_hbm.1, bf16[24,18432]{1,0:T(8,128)(2,1)} %pool_ref.1, bf16[4,3712]{1,0:T(4,128)(2,1)S(1)} %shard_map.132.after_ref.refs_0_), custom_call_target="tpu_custom_call" | custom-call | bytes 1769472 | tf_op jit(solution)/shard_map/pallas_call | solution.py:337
  10.1 1.7 %collective-permute-start.12 = (bf16[4,18432]{1,0:T(4,128)(2,1)S(1)}, bf16[4,18432]{1,0:T(4,128)(2,1)S(1)}, u32[]{:S(2)}, u32[]{:S(2)}) collective-permute-start(bf16[4,18432]{1,0:T(4,128)(2,1)S(1)} %get-tuple-element.23.refs_4_), channel_id=1, source_target_pairs={{0,2},{1,3},{2,0},{3,1},{4,6},{5,7},{6,4},{7,5},{8,10},{9,11},{10,... | collective-permute-start | bytes 442376 | tf_op jit(solution)/shard_map/ppermute | solution.py:59
  11.8 0.9 %collective-permute-done.2.refs_2_ = bf16[4,3712]{1,0:T(4,128)(2,1)S(1)} collective-permute-done((bf16[4,3712]{1,0:T(4,128)(2,1)S(1)}, bf16[4,3712]{1,0:T(4,128)(2,1)S(1)}, u32[]{:S(2)}, u32[]{:S(2)}) %collective-permute-start.2) | collective-permute-done | bytes 29728 | tf_op jit(solution)/shard_map/ppermute | solution.py:59
  12.7 2.5 %collective-permute-start.6 = (bf16[16,3712]{1,0:T(8,128)(2,1)S(1)}, bf16[16,3712]{1,0:T(8,128)(2,1)S(1)}, u32[]{:S(2)}, u32[]{:S(2)}) collective-permute-start(bf16[16,3712]{1,0:T(8,128)(2,1)S(1)} %shard_map.134.refs_0_), channel_id=1, source_target_pairs={{0,6},{1,7},{2,4},{3,5},{4,2},{5,3},{6,0},{7,1},{8,14},{9,15},{10,... | collective-permute-start | bytes 356360 | tf_op jit(solution)/shard_map/ppermute | solution.py:59
  15.2 0.5 %collective-permute-start.5 = (bf16[16,3712]{1,0:T(8,128)(2,1)S(1)}, bf16[16,3712]{1,0:T(8,128)(2,1)S(1)}, u32[]{:S(2)}, u32[]{:S(2)}) collective-permute-start(bf16[16,3712]{1,0:T(8,128)(2,1)S(1)} %shard_map.134.refs_0_), channel_id=1, source_target_pairs={{0,4},{1,5},{2,6},{3,7},{4,0},{5,1},{6,2},{7,3},{8,12},{9,13},{10,... | collective-permute-start | bytes 356360 | tf_op jit(solution)/shard_map/ppermute | solution.py:59
  15.7 0.5 %collective-permute-start.4 = (bf16[16,3712]{1,0:T(8,128)(2,1)S(1)}, bf16[16,3712]{1,0:T(8,128)(2,1)S(1)}, u32[]{:S(2)}, u32[]{:S(2)}) collective-permute-start(bf16[16,3712]{1,0:T(8,128)(2,1)S(1)} %shard_map.134.refs_0_), channel_id=1, source_target_pairs={{0,2},{1,3},{2,0},{3,1},{4,6},{5,7},{6,4},{7,5},{8,10},{9,11},{10,... | collective-permute-start | bytes 356360 | tf_op jit(solution)/shard_map/ppermute | solution.py:59
  16.4 3.7 %collective-permute-done.6.refs_3_ = bf16[16,3712]{1,0:T(8,128)(2,1)S(1)} collective-permute-done((bf16[16,3712]{1,0:T(8,128)(2,1)S(1)}, bf16[16,3712]{1,0:T(8,128)(2,1)S(1)}, u32[]{:S(2)}, u32[]{:S(2)}) %collective-permute-start.6) | collective-permute-done | bytes 118816 | tf_op jit(solution)/shard_map/ppermute | solution.py:59
  20.1 0.9 %collective-permute-done.5.refs_2_ = bf16[16,3712]{1,0:T(8,128)(2,1)S(1)} collective-permute-done((bf16[16,3712]{1,0:T(8,128)(2,1)S(1)}, bf16[16,3712]{1,0:T(8,128)(2,1)S(1)}, u32[]{:S(2)}, u32[]{:S(2)}) %collective-permute-start.5) | collective-permute-done | bytes 118816 | tf_op jit(solution)/shard_map/ppermute | solution.py:59
  21.3 0.2 slice-done.3
  21.6 1.4 %shard_map.136 = (f32[64,512]{1,0:T(8,128)S(1)}, f32[64,512]{1,0:T(8,128)S(1)}) custom-call(bf16[64,3712]{1,0:T(8,128)(2,1)S(1)} %shard_map.135.near_ref, bf16[1,7168,512]{2,1,0:T(8,128)(2,1)S(1)} %bitcast.1, bf16[1,7168,512]{2,1,0:T(8,128)(2,1)S(1)} %bitcast.3), custom_call_target="tpu_custom_call" | custom-call | flops 469762048 | bytes 7340032 | tf_op jit(solution)/shard_map/pallas_call | solution.py:213
  23.0 2.1 %shard_map.137 = (bf16[64,512]{1,0:T(8,128)(2,1)S(1)}, bf16[64,3584]{1,0:T(8,128)(2,1)S(1)}) custom-call(bf16[64,3712]{1,0:T(8,128)(2,1)S(1)} %shard_map.135.near_ref, bf16[64,3712]{1,0:T(8,128)(2,1)S(1)} %collective-permute-done.7.far_ref, bf16[1,7168,512]{2,1,0:T(8,128)(2,1)S(1)} %bitcast.1, bf16[1,7168,512]{2,1,0:T(8,128)(2,1)S(1)} %bitcast.3, ...), custom_call_target="tpu_custom_call" | custom-call | flops 704643072 | bytes 11010048 | tf_op jit(solution)/shard_map/pallas_call | solution.py:227
  25.2 0.3 collective-permute-start.8
  25.7 0.3 collective-permute-start.13
  26.0 0.8 %shard_map.138.refs_0_ = f32[64,3584]{1,0:T(8,128)S(1)} custom-call(bf16[64,3712]{1,0:T(8,128)(2,1)S(1)} %shard_map.135.near_ref, bf16[64,512]{1,0:T(8,128)(2,1)S(1)} %get-tuple-element.26.inner_ref, bf16[1,512,7168]{2,1,0:T(8,128)(2,1)S(1)} %bitcast.5), custom_call_target="tpu_custom_call" | custom-call | flops 234881024 | bytes 3670016 | tf_op jit(solution)/shard_map/pallas_call | solution.py:241
  26.7 0.3 collective-permute-done.8.refs_1_
  27.2 1.6 %collective-permute-start.9 = (bf16[16,3584]{1,0:T(8,128)(2,1)S(1)}, bf16[16,3584]{1,0:T(8,128)(2,1)S(1)}, u32[]{:S(2)}, u32[]{:S(2)}) collective-permute-start(bf16[16,3584]{1,0:T(8,128)(2,1)S(1)} %get-tuple-element.29), channel_id=1, source_target_pairs={{0,2},{1,3},{2,0},{3,1},{4,6},{5,7},{6,4},{7,5},{8,10},{9,11},{10,... | collective-permute-start | bytes 344072 | tf_op jit(solution)/shard_map/ppermute | solution.py:59
  28.7 1.5 %collective-permute-start.10 = (bf16[16,3584]{1,0:T(8,128)(2,1)S(1)}, bf16[16,3584]{1,0:T(8,128)(2,1)S(1)}, u32[]{:S(2)}, u32[]{:S(2)}) collective-permute-start(bf16[16,3584]{1,0:T(8,128)(2,1)S(1)} %get-tuple-element.30), channel_id=1, source_target_pairs={{0,4},{1,5},{2,6},{3,7},{4,0},{5,1},{6,2},{7,3},{8,12},{9,13},{10,... | collective-permute-start | bytes 344072 | tf_op jit(solution)/shard_map/ppermute | solution.py:59
  30.2 0.5 %collective-permute-start.11 = (bf16[16,3584]{1,0:T(8,128)(2,1)S(1)}, bf16[16,3584]{1,0:T(8,128)(2,1)S(1)}, u32[]{:S(2)}, u32[]{:S(2)}) collective-permute-start(bf16[16,3584]{1,0:T(8,128)(2,1)S(1)} %get-tuple-element.31), channel_id=1, source_target_pairs={{0,6},{1,7},{2,4},{3,5},{4,2},{5,3},{6,0},{7,1},{8,14},{9,15},{10,... | collective-permute-start | bytes 344072 | tf_op jit(solution)/shard_map/ppermute | solution.py:59
  31.0 2.4 %shard_map.140.refs_4_ = bf16[2,32768]{1,0:T(2,128)(2,1)} custom-call(s32[2]{0:T(128)S(1)} %copy-done.2, s32[2,12]{1,0:T(2,128)S(1)} %copy-done.1, bf16[2,36864]{1,0:T(2,128)(2,1)S(1)} %copy-done, bf16[24,18432]{1,0:T(8,128)(2,1)S(1)} %get-tuple-element.32.pool_ref, bf16[8,18432]{1,0:T(8,128)(2,1)S(1)} %pad_maximum_fusion.arrived_ref), custom_call_target="tpu_custom_call" | custom-call | flops 1073741824 | bytes 4194304 | tf_op jit(solution)/shard_map/pallas_call | solution.py:441
  33.4 2.7 %collective-permute-done.10.refs_2_ = bf16[16,3584]{1,0:T(8,128)(2,1)S(1)} collective-permute-done((bf16[16,3584]{1,0:T(8,128)(2,1)S(1)}, bf16[16,3584]{1,0:T(8,128)(2,1)S(1)}, u32[]{:S(2)}, u32[]{:S(2)}) %collective-permute-start.10) | collective-permute-done | bytes 114720 | tf_op jit(solution)/shard_map/ppermute | solution.py:59
  36.1 1.1 %collective-permute-start.14 = (bf16[4,3584]{1,0:T(4,128)(2,1)S(1)}, bf16[4,3584]{1,0:T(4,128)(2,1)S(1)}, u32[]{:S(2)}, u32[]{:S(2)}) collective-permute-start(bf16[4,3584]{1,0:T(4,128)(2,1)S(1)} %get-tuple-element.35), channel_id=1, source_target_pairs={{0,8},{1,9},{2,10},{3,11},{4,12},{5,13},{6,14},{7,15},{8,0},{9,1},... | collective-permute-start | bytes 86024 | tf_op jit(solution)/shard_map/ppermute | solution.py:59
  37.2 2.6 %collective-permute-start.15 = (bf16[4,3584]{1,0:T(4,128)(2,1)S(1)}, bf16[4,3584]{1,0:T(4,128)(2,1)S(1)}, u32[]{:S(2)}, u32[]{:S(2)}) collective-permute-start(bf16[4,3584]{1,0:T(4,128)(2,1)S(1)} %get-tuple-element.36), channel_id=1, source_target_pairs={{0,16},{1,17},{2,18},{3,19},{4,20},{5,21},{6,22},{7,23},{8,24},{9,... | collective-permute-start | bytes 86024 | tf_op jit(solution)/shard_map/ppermute | solution.py:59
  39.9 0.7 %collective-permute-start.16 = (bf16[4,3584]{1,0:T(4,128)(2,1)S(1)}, bf16[4,3584]{1,0:T(4,128)(2,1)S(1)}, u32[]{:S(2)}, u32[]{:S(2)}) collective-permute-start(bf16[4,3584]{1,0:T(4,128)(2,1)S(1)} %get-tuple-element.37), channel_id=1, source_target_pairs={{0,24},{1,25},{2,26},{3,27},{4,28},{5,29},{6,30},{7,31},{8,16},{9,... | collective-permute-start | bytes 86024 | tf_op jit(solution)/shard_map/ppermute | solution.py:59
  40.6 1.4 %collective-permute-done.15.refs_2_ = bf16[4,3584]{1,0:T(4,128)(2,1)S(1)} collective-permute-done((bf16[4,3584]{1,0:T(4,128)(2,1)S(1)}, bf16[4,3584]{1,0:T(4,128)(2,1)S(1)}, u32[]{:S(2)}, u32[]{:S(2)}) %collective-permute-start.15) | collective-permute-done | bytes 28704 | tf_op jit(solution)/shard_map/ppermute | solution.py:59
  42.0 3.5 %collective-permute-done.16.refs_3_ = bf16[4,3584]{1,0:T(4,128)(2,1)S(1)} collective-permute-done((bf16[4,3584]{1,0:T(4,128)(2,1)S(1)}, bf16[4,3584]{1,0:T(4,128)(2,1)S(1)}, u32[]{:S(2)}, u32[]{:S(2)}) %collective-permute-start.16) | collective-permute-done | bytes 28704 | tf_op jit(solution)/shard_map/ppermute | solution.py:59
  45.7 1.2 %collective-permute-done.17.got_ref = bf16[2,3584]{1,0:T(2,128)(2,1)S(1)} collective-permute-done((bf16[2,3584]{1,0:T(2,128)(2,1)S(1)}, bf16[2,3584]{1,0:T(2,128)(2,1)S(1)}, u32[]{:S(2)}, u32[]{:S(2)}) %collective-permute-start.17) | collective-permute-done | bytes 14368 | tf_op jit(solution)/shard_map/ppermute | solution.py:59
  46.8 0.6 %shard_map.143 = bf16[2,7168]{1,0:T(2,128)(2,1)} custom-call(f32[2,3584]{1,0:T(2,128)S(1)} %get-tuple-element.38.keep_ref, bf16[2,3584]{1,0:T(2,128)(2,1)S(1)} %collective-permute-done.17.got_ref), custom_call_target="tpu_custom_call" | custom-call | bytes 57344 | tf_op jit(solution)/shard_map/pallas_call | solution.py:290
  (42 shorter events, 1.2 us)
Async XLA Ops:
  1.5 1.4 %collective-permute-start = (bf16[2,3712]{1,0:T(2,128)(2,1)S(1)}, bf16[2,3712]{1,0:T(2,128)(2,1)S(1)}, u32[]{:S(2)}, u32[]{:S(2)}) collective-permute-start(bf16[2,3712]{1,0:T(2,128)(2,1)S(1)} %get-tuple-element.22), channel_id=1, source_target_pairs={{0,1},{1,0},{2,3},{3,2},{4,5},{5,4},{6,7},{7,6},{8,9},{9,8},{10,11... | collective-permute-start | bytes 44552 | tf_op jit(solution)/shard_map/ppermute | solution.py:59
  2.9 8.9 %collective-permute-start.3 = (bf16[4,3712]{1,0:T(4,128)(2,1)S(1)}, bf16[4,3712]{1,0:T(4,128)(2,1)S(1)}, u32[]{:S(2)}, u32[]{:S(2)}) collective-permute-start(bf16[4,3712]{1,0:T(4,128)(2,1)S(1)} %shard_map.132.after_ref.refs_0_), channel_id=1, source_target_pairs={{0,24},{1,25},{2,26},{3,27},{4,28},{5,29},{6,30},{7,31},{8,16},{9,... | collective-permute-start | bytes 89096 | tf_op jit(solution)/shard_map/ppermute | solution.py:59
  7.9 4.8 %collective-permute-start.2 = (bf16[4,3712]{1,0:T(4,128)(2,1)S(1)}, bf16[4,3712]{1,0:T(4,128)(2,1)S(1)}, u32[]{:S(2)}, u32[]{:S(2)}) collective-permute-start(bf16[4,3712]{1,0:T(4,128)(2,1)S(1)} %shard_map.132.after_ref.refs_0_), channel_id=1, source_target_pairs={{0,16},{1,17},{2,18},{3,19},{4,20},{5,21},{6,22},{7,23},{8,24},{9,... | collective-permute-start | bytes 89096 | tf_op jit(solution)/shard_map/ppermute | solution.py:59
  7.9 4.8 %collective-permute-start.1 = (bf16[4,3712]{1,0:T(4,128)(2,1)S(1)}, bf16[4,3712]{1,0:T(4,128)(2,1)S(1)}, u32[]{:S(2)}, u32[]{:S(2)}) collective-permute-start(bf16[4,3712]{1,0:T(4,128)(2,1)S(1)} %shard_map.132.after_ref.refs_0_), channel_id=1, source_target_pairs={{0,8},{1,9},{2,10},{3,11},{4,12},{5,13},{6,14},{7,15},{8,0},{9,1},... | collective-permute-start | bytes 89096 | tf_op jit(solution)/shard_map/ppermute | solution.py:59
  10.1 11.1 %collective-permute-start.12 = (bf16[4,18432]{1,0:T(4,128)(2,1)S(1)}, bf16[4,18432]{1,0:T(4,128)(2,1)S(1)}, u32[]{:S(2)}, u32[]{:S(2)}) collective-permute-start(bf16[4,18432]{1,0:T(4,128)(2,1)S(1)} %get-tuple-element.23.refs_4_), channel_id=1, source_target_pairs={{0,2},{1,3},{2,0},{3,1},{4,6},{5,7},{6,4},{7,5},{8,10},{9,11},{10,... | collective-permute-start | bytes 442376 | tf_op jit(solution)/shard_map/ppermute | solution.py:59
  12.7 10.3 %slice-start.4 = ((s8[7340032]{0:T(1024)(128)(4,1)}), s8[4194304]{0:T(1024)(128)(4,1)S(1)}, s32[]{:S(2)}) async-start(s8[7340032]{0:T(1024)(128)(4,1)} %bitcast.4), calls=%async_computation.4 | async-start | bytes 8388608
  12.7 7.4 %collective-permute-start.6 = (bf16[16,3712]{1,0:T(8,128)(2,1)S(1)}, bf16[16,3712]{1,0:T(8,128)(2,1)S(1)}, u32[]{:S(2)}, u32[]{:S(2)}) collective-permute-start(bf16[16,3712]{1,0:T(8,128)(2,1)S(1)} %shard_map.134.refs_0_), channel_id=1, source_target_pairs={{0,6},{1,7},{2,4},{3,5},{4,2},{5,3},{6,0},{7,1},{8,14},{9,15},{10,... | collective-permute-start | bytes 356360 | tf_op jit(solution)/shard_map/ppermute | solution.py:59
  15.2 5.8 %collective-permute-start.5 = (bf16[16,3712]{1,0:T(8,128)(2,1)S(1)}, bf16[16,3712]{1,0:T(8,128)(2,1)S(1)}, u32[]{:S(2)}, u32[]{:S(2)}) collective-permute-start(bf16[16,3712]{1,0:T(8,128)(2,1)S(1)} %shard_map.134.refs_0_), channel_id=1, source_target_pairs={{0,4},{1,5},{2,6},{3,7},{4,0},{5,1},{6,2},{7,3},{8,12},{9,13},{10,... | collective-permute-start | bytes 356360 | tf_op jit(solution)/shard_map/ppermute | solution.py:59
  15.7 5.3 %collective-permute-start.4 = (bf16[16,3712]{1,0:T(8,128)(2,1)S(1)}, bf16[16,3712]{1,0:T(8,128)(2,1)S(1)}, u32[]{:S(2)}, u32[]{:S(2)}) collective-permute-start(bf16[16,3712]{1,0:T(8,128)(2,1)S(1)} %shard_map.134.refs_0_), channel_id=1, source_target_pairs={{0,2},{1,3},{2,0},{3,1},{4,6},{5,7},{6,4},{7,5},{8,10},{9,11},{10,... | collective-permute-start | bytes 356360 | tf_op jit(solution)/shard_map/ppermute | solution.py:59
  16.3 5.0 %slice-start = ((s8[7340032]{0:T(1024)(128)(4,1)}), s8[4194304]{0:T(1024)(128)(4,1)S(1)}, s32[]{:S(2)}) async-start(s8[7340032]{0:T(1024)(128)(4,1)} %bitcast), calls=%async_computation | async-start | bytes 8388608
  16.3 5.0 %slice-start.2 = ((s8[7340032]{0:T(1024)(128)(4,1)}), s8[4194304]{0:T(1024)(128)(4,1)S(1)}, s32[]{:S(2)}) async-start(s8[7340032]{0:T(1024)(128)(4,1)} %bitcast.2), calls=%async_computation.2 | async-start | bytes 8388608
  16.4 4.9 %slice-start.1 = ((s8[7340032]{0:T(1024)(128)(4,1)}), s8[3145728]{0:T(1024)(128)(4,1)S(1)}, s32[]{:S(2)}) async-start(s8[7340032]{0:T(1024)(128)(4,1)} %bitcast), calls=%async_computation.1 | async-start | bytes 6291456
  16.4 5.2 %slice-start.3 = ((s8[7340032]{0:T(1024)(128)(4,1)}), s8[3145728]{0:T(1024)(128)(4,1)S(1)}, s32[]{:S(2)}) async-start(s8[7340032]{0:T(1024)(128)(4,1)} %bitcast.2), calls=%async_computation.3 | async-start | bytes 6291456
  16.4 6.6 %slice-start.5 = ((s8[7340032]{0:T(1024)(128)(4,1)}), s8[3145728]{0:T(1024)(128)(4,1)S(1)}, s32[]{:S(2)}) async-start(s8[7340032]{0:T(1024)(128)(4,1)} %bitcast.4), calls=%async_computation.5 | async-start | bytes 6291456
  21.1 1.9 %collective-permute-start.7 = (bf16[64,3712]{1,0:T(8,128)(2,1)S(1)}, bf16[64,3712]{1,0:T(8,128)(2,1)S(1)}, u32[]{:S(2)}, u32[]{:S(2)}) collective-permute-start(bf16[64,3712]{1,0:T(8,128)(2,1)S(1)} %shard_map.135.near_ref), channel_id=1, source_target_pairs={{0,1},{1,0},{2,3},{3,2},{4,5},{5,4},{6,7},{7,6},{8,9},{9,8},{10,11... | collective-permute-start | bytes 1425416 | tf_op jit(solution)/shard_map/ppermute | solution.py:59
  25.1 5.8 %copy-start = (bf16[2,36864]{1,0:T(2,128)(2,1)S(1)}, bf16[2,36864]{1,0:T(2,128)(2,1)}, u32[]{:S(2)}) copy-start(bf16[2,36864]{1,0:T(2,128)(2,1)} %query_ref.1) | copy-start | bytes 442372
  25.1 5.8 %copy-start.1 = (s32[2,12]{1,0:T(2,128)S(1)}, s32[2,12]{1,0:T(2,128)}, u32[]{:S(2)}) copy-start(s32[2,12]{1,0:T(2,128)} %table_ref.1) | copy-start | bytes 292
  25.1 5.8 %copy-start.2 = (s32[2]{0:T(128)S(1)}, s32[2]{0:T(128)}, u32[]{:S(2)}) copy-start(s32[2]{0:T(128)} %length_ref.1) | copy-start | bytes 28
  25.2 1.9 %collective-permute-start.8 = (bf16[64,3584]{1,0:T(8,128)(2,1)S(1)}, bf16[64,3584]{1,0:T(8,128)(2,1)S(1)}, u32[]{:S(2)}, u32[]{:S(2)}) collective-permute-start(bf16[64,3584]{1,0:T(8,128)(2,1)S(1)} %get-tuple-element.27), channel_id=1, source_target_pairs={{0,1},{1,0},{2,3},{3,2},{4,5},{5,4},{6,7},{7,6},{8,9},{9,8},{10,11... | collective-permute-start | bytes 1376264 | tf_op jit(solution)/shard_map/ppermute | solution.py:59
  25.7 5.1 %collective-permute-start.13 = (bf16[4,18432]{1,0:T(4,128)(2,1)S(1)}, bf16[4,18432]{1,0:T(4,128)(2,1)S(1)}, u32[]{:S(2)}, u32[]{:S(2)}) collective-permute-start(bf16[4,18432]{1,0:T(4,128)(2,1)S(1)} %pad_maximum_fusion.1), channel_id=1, source_target_pairs={{0,1},{1,0},{2,3},{3,2},{4,5},{5,4},{6,7},{7,6},{8,9},{9,8},{10,11... | collective-permute-start | bytes 442376 | tf_op jit(solution)/shard_map/ppermute | solution.py:59
  27.2 6.2 %collective-permute-start.9 = (bf16[16,3584]{1,0:T(8,128)(2,1)S(1)}, bf16[16,3584]{1,0:T(8,128)(2,1)S(1)}, u32[]{:S(2)}, u32[]{:S(2)}) collective-permute-start(bf16[16,3584]{1,0:T(8,128)(2,1)S(1)} %get-tuple-element.29), channel_id=1, source_target_pairs={{0,2},{1,3},{2,0},{3,1},{4,6},{5,7},{6,4},{7,5},{8,10},{9,11},{10,... | collective-permute-start | bytes 344072 | tf_op jit(solution)/shard_map/ppermute | solution.py:59
  28.7 7.4 %collective-permute-start.10 = (bf16[16,3584]{1,0:T(8,128)(2,1)S(1)}, bf16[16,3584]{1,0:T(8,128)(2,1)S(1)}, u32[]{:S(2)}, u32[]{:S(2)}) collective-permute-start(bf16[16,3584]{1,0:T(8,128)(2,1)S(1)} %get-tuple-element.30), channel_id=1, source_target_pairs={{0,4},{1,5},{2,6},{3,7},{4,0},{5,1},{6,2},{7,3},{8,12},{9,13},{10,... | collective-permute-start | bytes 344072 | tf_op jit(solution)/shard_map/ppermute | solution.py:59
  30.2 5.8 %collective-permute-start.11 = (bf16[16,3584]{1,0:T(8,128)(2,1)S(1)}, bf16[16,3584]{1,0:T(8,128)(2,1)S(1)}, u32[]{:S(2)}, u32[]{:S(2)}) collective-permute-start(bf16[16,3584]{1,0:T(8,128)(2,1)S(1)} %get-tuple-element.31), channel_id=1, source_target_pairs={{0,6},{1,7},{2,4},{3,5},{4,2},{5,3},{6,0},{7,1},{8,14},{9,15},{10,... | collective-permute-start | bytes 344072 | tf_op jit(solution)/shard_map/ppermute | solution.py:59
  36.1 4.5 %collective-permute-start.14 = (bf16[4,3584]{1,0:T(4,128)(2,1)S(1)}, bf16[4,3584]{1,0:T(4,128)(2,1)S(1)}, u32[]{:S(2)}, u32[]{:S(2)}) collective-permute-start(bf16[4,3584]{1,0:T(4,128)(2,1)S(1)} %get-tuple-element.35), channel_id=1, source_target_pairs={{0,8},{1,9},{2,10},{3,11},{4,12},{5,13},{6,14},{7,15},{8,0},{9,1},... | collective-permute-start | bytes 86024 | tf_op jit(solution)/shard_map/ppermute | solution.py:59
  37.2 4.8 %collective-permute-start.15 = (bf16[4,3584]{1,0:T(4,128)(2,1)S(1)}, bf16[4,3584]{1,0:T(4,128)(2,1)S(1)}, u32[]{:S(2)}, u32[]{:S(2)}) collective-permute-start(bf16[4,3584]{1,0:T(4,128)(2,1)S(1)} %get-tuple-element.36), channel_id=1, source_target_pairs={{0,16},{1,17},{2,18},{3,19},{4,20},{5,21},{6,22},{7,23},{8,24},{9,... | collective-permute-start | bytes 86024 | tf_op jit(solution)/shard_map/ppermute | solution.py:59
  39.9 5.7 %collective-permute-start.16 = (bf16[4,3584]{1,0:T(4,128)(2,1)S(1)}, bf16[4,3584]{1,0:T(4,128)(2,1)S(1)}, u32[]{:S(2)}, u32[]{:S(2)}) collective-permute-start(bf16[4,3584]{1,0:T(4,128)(2,1)S(1)} %get-tuple-element.37), channel_id=1, source_target_pairs={{0,24},{1,25},{2,26},{3,27},{4,28},{5,29},{6,30},{7,31},{8,16},{9,... | collective-permute-start | bytes 86024 | tf_op jit(solution)/shard_map/ppermute | solution.py:59
  45.6 1.2 %collective-permute-start.17 = (bf16[2,3584]{1,0:T(2,128)(2,1)S(1)}, bf16[2,3584]{1,0:T(2,128)(2,1)S(1)}, u32[]{:S(2)}, u32[]{:S(2)}) collective-permute-start(bf16[2,3584]{1,0:T(2,128)(2,1)S(1)} %get-tuple-element.39), channel_id=1, source_target_pairs={{0,1},{1,0},{2,3},{3,2},{4,5},{5,4},{6,7},{7,6},{8,9},{9,8},{10,11... | collective-permute-start | bytes 43016 | tf_op jit(solution)/shard_map/ppermute | solution.py:59

commit v5 on v4

--- a/solution.py
+++ b/solution.py
@@ -72,78 +72,82 @@
     return [(i, i ^ bit) for i in range(count)]
 
 
-def payload_kernel(ep_count, hidden_hbm, routes_hbm, weight_hbm, mine_ref, other_ref, hidden_ref, routes_ref, weight_ref, sems):
-    copies = [
-        pltpu.make_async_copy(source, target, sems.at[i])
-        for i, (source, target) in enumerate(
-            [(hidden_hbm, hidden_ref), (routes_hbm, routes_ref), (weight_hbm, weight_ref)]
-        )
-    ]
+def fetch_kernel(*refs):
+    count = (len(refs) - 1) // 2
+    copies = [pltpu.make_async_copy(refs[i], refs[count + i], refs[-1].at[i]) for i in range(count)]
     for c in copies:
         c.start()
     for c in copies:
         c.wait()
-    rows, width = hidden_ref.shape
+
+
+def fetch(*arrays):
+    return pl.pallas_call(
+        fetch_kernel,
+        out_shape=tuple(pltpu.VMEM(x.shape, x.dtype) for x in arrays),
+        in_specs=[in_hbm()] * len(arrays),
+        out_specs=(in_vmem(),) * len(arrays),
+        scratch_shapes=[pltpu.SemaphoreType.DMA((len(arrays),))],
+        compiler_params=pltpu.CompilerParams(vmem_limit_bytes=4 * MIB),
+        cost_estimate=pl.CostEstimate(flops=MERGE_FLOPS // 16, bytes_accessed=MIB, transcendentals=0),
+    )(*[hbm(x) for x in arrays])
+
+
+def payload_kernel(ep_count, mine_hidden, mine_routes, mine_weight, got_hidden, got_routes, got_weight, out_ref):
+    first = lax.rem(lax.axis_index("dp"), 2) == 0
+    rows, width = mine_hidden.shape
     half = width // 2
-    column = lax.broadcasted_iota(jnp.int32, (rows, LANES), 1)
+
+    def in_order(mine, got):
+        return jnp.where(first, jnp.concatenate([mine, got], axis=0), jnp.concatenate([got, mine], axis=0))
+
+    def my_half(ref):
+        return jnp.where(first, ref[:, :half].astype(f32), ref[:, half:].astype(f32))
+
+    out_ref[:, :half] = in_order(my_half(mine_hidden), my_half(got_hidden)).astype(bf16)
+    routes = in_order(mine_routes[...], got_routes[...])
+    weight = in_order(mine_weight[...], got_weight[...])
+    column = lax.broadcasted_iota(jnp.int32, (2 * rows, LANES), 1)
     expert = jnp.where(column < ep_count, column, column - ep_count)
-    total = jnp.zeros((rows, LANES), f32)
-    for k in range(routes_ref.shape[1]):
-        total += jnp.where(routes_ref[:, k : k + 1] == expert, weight_ref[:, k : k + 1], 0.0)
+    total = jnp.zeros((2 * rows, LANES), f32)
+    for k in range(routes.shape[1]):
+        total += jnp.where(routes[:, k : k + 1] == expert, weight[:, k : k + 1], 0.0)
     high = total.astype(bf16).astype(f32)
     low = total - high
-    value = jnp.where(column < ep_count, high, jnp.where(column < 2 * ep_count, low, 0.0)).astype(bf16)
-    first = lax.rem(lax.axis_index("dp"), 2) == 0
-    left, right = hidden_ref[:, :half].astype(f32), hidden_ref[:, half:].astype(f32)
-    mine_ref[:, :half] = jnp.where(first, left, right).astype(bf16)
-    other_ref[:, :half] = jnp.where(first, right, left).astype(bf16)
-    mine_ref[:, half:] = value
-    other_ref[:, half:] = value
-
-
-def make_payload(hidden, routes, route_weight, ep_count):
-    rows, width = hidden.shape
-    half = pltpu.VMEM((rows, width // 2 + LANES), bf16)
+    out_ref[:, half:] = jnp.where(column < ep_count, high, jnp.where(column < 2 * ep_count, low, 0.0)).astype(bf16)
+
+
+def make_payload(mine, got, ep_count):
+    rows, width = mine[0].shape
     return pl.pallas_call(
         functools.partial(payload_kernel, ep_count),
-        out_shape=(half, half),
-        in_specs=[in_hbm()] * 3,
-        out_specs=(in_vmem(), in_vmem()),
-        scratch_shapes=[
-            pltpu.VMEM(hidden.shape, bf16),
-            pltpu.VMEM(routes.shape, jnp.int32),
-            pltpu.VMEM(route_weight.shape, f32),
-            pltpu.SemaphoreType.DMA((3,)),
-        ],
+        out_shape=pltpu.VMEM((2 * rows, width // 2 + LANES), bf16),
+        in_specs=[in_vmem()] * 6,
+        out_specs=in_vmem(),
         compiler_params=pltpu.CompilerParams(vmem_limit_bytes=4 * MIB),
         cost_estimate=pl.CostEstimate(flops=0, bytes_accessed=4 * rows * width, transcendentals=0),
-    )(hbm(hidden), hbm(routes), hbm(route_weight))
-
-
-def merge_kernel(by_core, parts, *refs):
+    )(*[vmem(x) for x in mine], *[vmem(x) for x in got])
+
+
+def merge_kernel(parts, *refs):
     out_ref = refs[-1]
     rows = refs[0].shape[0]
     if rows % 16:
-        pieces = [r[...].astype(f32) for r in refs[:parts]]
-        both = jnp.concatenate(pieces, axis=0)
-        if by_core:
-            first = lax.rem(lax.axis_index("dp"), 2) == 0
-            both = jnp.where(first, both, jnp.concatenate(pieces[::-1], axis=0))
-        out_ref[...] = both.astype(bf16)
+        out_ref[...] = jnp.concatenate([r[...].astype(f32) for r in refs[:parts]], axis=0).astype(bf16)
     else:
         for i in range(parts):
             out_ref[i * rows : (i + 1) * rows] = refs[i][...]
 
 
-def merge(pieces, *after, by_core=False):
+def merge(pieces, flops, *after):
     rows, width = pieces[0].shape
     return pl.pallas_call(
-        functools.partial(merge_kernel, by_core, len(pieces)),
+        functools.partial(merge_kernel, len(pieces)),
         out_shape=pltpu.VMEM((len(pieces) * rows, width), bf16),
         in_specs=[in_vmem()] * len(pieces) + [anywhere()] * len(after),
         out_specs=in_vmem(),
         compiler_params=pltpu.CompilerParams(vmem_limit_bytes=4 * MIB),
-        cost_estimate=pl.CostEstimate(flops=MERGE_FLOPS, bytes_accessed=8 * MIB, transcendentals=0),
+        cost_estimate=pl.CostEstimate(flops=flops, bytes_accessed=8 * rows * width, transcendentals=0),
     )(*[vmem(p) for p in pieces], *after)
 
 
@@ -471,15 +475,16 @@
     def trade(x, bit):
         return swap(x, AXES, pairs_of(count, bit))
 
-    mine, other = make_payload(hidden, routes, route_weight, ep_count)
-    near = merge([mine, trade(other, 1)], by_core=True)
+    mine = (hidden, routes, route_weight)
+    got = [trade(x, 1) for x in mine]
+    near = make_payload(fetch(*mine), got, ep_count)
     for number, partners in enumerate(stages):
         got = [trade(near, bit) for bit in partners]
         after = []
         if number == 0:
             low, high, pool = pick_pages(moved_page, moved_dest, latent_pool, near, dp_count)
             after = [high]
-        near = merge([near] + got, *after)
+        near = merge([near] + got, MERGE_FLOPS if number < len(stages) - 1 else MERGE_FLOPS // 4, *after)
     arrived, senders = exchange_pages(low, high, dp_count)
     far = trade(near, 1)
     gate_acc, up_acc = near_products(near, gate_weight, up_weight)
@@ -490,7 +495,7 @@
     after = []
     for partners in reversed(stages):
         keep, *send = fold(keep, got, len(partners) + 1, *after)
-        got = [trade(x, bit) for x, bit in zip(send, partners)]
+        got = [trade(x, bit) for x, bit in list(zip(send, partners))[::-1]]
         after = [] if after else [hbm(attended)]
     keep, send = fold(keep, got, 2, *(after if len(stages) == 1 else []), by_core=True)
     return finish(keep, trade(send, 1)), attended

time: 47.7 us -> 45.9 us (0.962)
  waiting for transfers between devices: 15.6 us -> 13.4 us
  starting transfers between devices: 20.2 us -> 20.7 us
    ppermute x18 -> x20, waiting for transfers between devices: 15.6 us -> 13.4 us  [swap(): return lax.ppermute(x, axes, pairs)]
    ppermute x18 -> x20, starting transfers between devices: 20.2 us -> 20.7 us  [swap(): return lax.ppermute(x, axes, pairs)]
  transfers between devices with their start and end apart: 18 -> 20, of which waited for: 9 -> 11; matrix products, arithmetic and copies ran while one was open for 1% -> 1% of each run, Pallas kernels for 13% -> 16%
where the time goes in v5:
time: 45.9 us; the launch traced here: 45.7 us
  starting transfers between devices  20.7 us (45%)
  waiting for transfers between devices  13.4 us (29%)
  Pallas kernels  10 us (22%)
  between operations  0.88 us (2%)
    ppermute x20, starting transfers between devices, swap(): return lax.ppermute(x, axes, pairs)  20.7 us
    ppermute x20, waiting for transfers between devices, swap(): return lax.ppermute(x, axes, pairs)  13.4 us
    pallas_call x1, Pallas kernels, attend(): pl.pallas_call(functools.partial(attend_kernel, senders), out_shape=jax.S...  2.36 us
    pallas_call x1, Pallas kernels, far_products(): pl.pallas_call(functools.partial(far_kernel, ep_count), out_shape=(pltpu....  2.11 us
    pallas_call x1, Pallas kernels, pick_pages(): pl.pallas_call(functools.partial(pages_kernel, dp_count), out_shape=(half...  1.5 us
    pallas_call x1, Pallas kernels, near_products(): pl.pallas_call(near_kernel, out_shape=(acc, acc), in_specs=[in_vmem()] *...  1.39 us
    pallas_call x1, Pallas kernels, fetch(): pl.pallas_call(fetch_kernel, out_shape=tuple((pltpu.VMEM(x.shape, x.dtype...  0.93 us
  transfers between devices with their start and end apart: 20, of which 11 were waited for; matrix products, arithmetic and copies ran while one was open for 1% of the time, Pallas kernels for 16%

profile of v5, /device:TPU:0, one launch (start us, length us, event | category | flops | bytes accessed | tf_op | source)
XLA Modules:
  0.0 45.7 jit_solution(9672270783700805931)
XLA Ops:
  0.6 0.5 %collective-permute-start.1 = (s32[2,4]{1,0:T(2,128)}, s32[2,4]{1,0:T(2,128)S(1)}, u32[]{:S(2)}, u32[]{:S(2)}) collective-permute-start(s32[2,4]{1,0:T(2,128)} %refs_1_.1), channel_id=1, source_target_pairs={{0,1},{1,0},{2,3},{3,2},{4,5},{5,4},{6,7},{7,6},{8,9},{9,8},{10,11... | collective-permute-start | bytes 104 | tf_op jit(solution)/shard_map/ppermute | solution.py:59
  1.2 0.4 collective-permute-start
  1.7 0.9 %shard_map.131 = (bf16[2,7168]{1,0:T(2,128)(2,1)S(1)}, s32[2,4]{1,0:T(2,128)S(1)}, f32[2,4]{1,0:T(2,128)S(1)}) custom-call(bf16[2,7168]{1,0:T(2,128)(2,1)} %refs_0_.1, s32[2,4]{1,0:T(2,128)} %refs_1_.1, f32[2,4]{1,0:T(2,128)} %refs_2_.1), custom_call_target="tpu_custom_call" | custom-call | flops 1250000000 | bytes 1048576 | tf_op jit(solution)/shard_map/pallas_call | solution.py:85
  2.8 5.0 %collective-permute-start.5 = (bf16[4,3712]{1,0:T(4,128)(2,1)S(1)}, bf16[4,3712]{1,0:T(4,128)(2,1)S(1)}, u32[]{:S(2)}, u32[]{:S(2)}) collective-permute-start(bf16[4,3712]{1,0:T(4,128)(2,1)S(1)} %shard_map.132.after_ref.refs_0_), channel_id=1, source_target_pairs={{0,24},{1,25},{2,26},{3,27},{4,28},{5,29},{6,30},{7,31},{8,16},{9,... | collective-permute-start | bytes 89096 | tf_op jit(solution)/shard_map/ppermute | solution.py:59
  7.8 0.6 %collective-permute-start.3 = (bf16[4,3712]{1,0:T(4,128)(2,1)S(1)}, bf16[4,3712]{1,0:T(4,128)(2,1)S(1)}, u32[]{:S(2)}, u32[]{:S(2)}) collective-permute-start(bf16[4,3712]{1,0:T(4,128)(2,1)S(1)} %shard_map.132.after_ref.refs_0_), channel_id=1, source_target_pairs={{0,8},{1,9},{2,10},{3,11},{4,12},{5,13},{6,14},{7,15},{8,0},{9,1},... | collective-permute-start | bytes 89096 | tf_op jit(solution)/shard_map/ppermute | solution.py:59
  8.5 1.5 %shard_map.133 = (bf16[4,18432]{1,0:T(4,128)(2,1)S(1)}, bf16[4,18432]{1,0:T(4,128)(2,1)S(1)}, bf16[24,18432]{1,0:T(8,128)(2,1)S(1)}) custom-call(s32[1,6]{1,0:T(1,128)} %page_hbm.1, s32[1,6]{1,0:T(1,128)} %dest_hbm.1, bf16[24,18432]{1,0:T(8,128)(2,1)} %pool_ref.1, bf16[4,3712]{1,0:T(4,128)(2,1)S(1)} %shard_map.132.after_ref.refs_0_), custom_call_target="tpu_custom_call" | custom-call | bytes 1769472 | tf_op jit(solution)/shard_map/pallas_call | solution.py:341
  10.0 1.7 %collective-permute-start.14 = (bf16[4,18432]{1,0:T(4,128)(2,1)S(1)}, bf16[4,18432]{1,0:T(4,128)(2,1)S(1)}, u32[]{:S(2)}, u32[]{:S(2)}) collective-permute-start(bf16[4,18432]{1,0:T(4,128)(2,1)S(1)} %get-tuple-element.25.refs_4_), channel_id=1, source_target_pairs={{0,2},{1,3},{2,0},{3,1},{4,6},{5,7},{6,4},{7,5},{8,10},{9,11},{10,... | collective-permute-start | bytes 442376 | tf_op jit(solution)/shard_map/ppermute | solution.py:59
  11.7 0.9 %collective-permute-done.4.refs_2_ = bf16[4,3712]{1,0:T(4,128)(2,1)S(1)} collective-permute-done((bf16[4,3712]{1,0:T(4,128)(2,1)S(1)}, bf16[4,3712]{1,0:T(4,128)(2,1)S(1)}, u32[]{:S(2)}, u32[]{:S(2)}) %collective-permute-start.4) | collective-permute-done | bytes 29728 | tf_op jit(solution)/shard_map/ppermute | solution.py:59
  12.6 2.5 %collective-permute-start.8 = (bf16[16,3712]{1,0:T(8,128)(2,1)S(1)}, bf16[16,3712]{1,0:T(8,128)(2,1)S(1)}, u32[]{:S(2)}, u32[]{:S(2)}) collective-permute-start(bf16[16,3712]{1,0:T(8,128)(2,1)S(1)} %shard_map.134.refs_0_), channel_id=1, source_target_pairs={{0,6},{1,7},{2,4},{3,5},{4,2},{5,3},{6,0},{7,1},{8,14},{9,15},{10,... | collective-permute-start | bytes 356360 | tf_op jit(solution)/shard_map/ppermute | solution.py:59
  15.2 0.5 %collective-permute-start.7 = (bf16[16,3712]{1,0:T(8,128)(2,1)S(1)}, bf16[16,3712]{1,0:T(8,128)(2,1)S(1)}, u32[]{:S(2)}, u32[]{:S(2)}) collective-permute-start(bf16[16,3712]{1,0:T(8,128)(2,1)S(1)} %shard_map.134.refs_0_), channel_id=1, source_target_pairs={{0,4},{1,5},{2,6},{3,7},{4,0},{5,1},{6,2},{7,3},{8,12},{9,13},{10,... | collective-permute-start | bytes 356360 | tf_op jit(solution)/shard_map/ppermute | solution.py:59
  15.7 0.5 %collective-permute-start.6 = (bf16[16,3712]{1,0:T(8,128)(2,1)S(1)}, bf16[16,3712]{1,0:T(8,128)(2,1)S(1)}, u32[]{:S(2)}, u32[]{:S(2)}) collective-permute-start(bf16[16,3712]{1,0:T(8,128)(2,1)S(1)} %shard_map.134.refs_0_), channel_id=1, source_target_pairs={{0,2},{1,3},{2,0},{3,1},{4,6},{5,7},{6,4},{7,5},{8,10},{9,11},{10,... | collective-permute-start | bytes 356360 | tf_op jit(solution)/shard_map/ppermute | solution.py:59
  16.3 3.8 %collective-permute-done.8.refs_3_ = bf16[16,3712]{1,0:T(8,128)(2,1)S(1)} collective-permute-done((bf16[16,3712]{1,0:T(8,128)(2,1)S(1)}, bf16[16,3712]{1,0:T(8,128)(2,1)S(1)}, u32[]{:S(2)}, u32[]{:S(2)}) %collective-permute-start.8) | collective-permute-done | bytes 118816 | tf_op jit(solution)/shard_map/ppermute | solution.py:59
  20.1 0.9 %collective-permute-done.7.refs_2_ = bf16[16,3712]{1,0:T(8,128)(2,1)S(1)} collective-permute-done((bf16[16,3712]{1,0:T(8,128)(2,1)S(1)}, bf16[16,3712]{1,0:T(8,128)(2,1)S(1)}, u32[]{:S(2)}, u32[]{:S(2)}) %collective-permute-start.7) | collective-permute-done | bytes 118816 | tf_op jit(solution)/shard_map/ppermute | solution.py:59
  21.3 1.4 %shard_map.136 = (f32[64,512]{1,0:T(8,128)S(1)}, f32[64,512]{1,0:T(8,128)S(1)}) custom-call(bf16[64,3712]{1,0:T(8,128)(2,1)S(1)} %shard_map.135.near_ref, bf16[1,7168,512]{2,1,0:T(8,128)(2,1)S(1)} %bitcast.1, bf16[1,7168,512]{2,1,0:T(8,128)(2,1)S(1)} %bitcast.3), custom_call_target="tpu_custom_call" | custom-call | flops 469762048 | bytes 7340032 | tf_op jit(solution)/shard_map/pallas_call | solution.py:217
  22.7 0.2 collective-permute-done.9.far_ref
  22.9 2.1 %shard_map.137 = (bf16[64,512]{1,0:T(8,128)(2,1)S(1)}, bf16[64,3584]{1,0:T(8,128)(2,1)S(1)}) custom-call(bf16[64,3712]{1,0:T(8,128)(2,1)S(1)} %shard_map.135.near_ref, bf16[64,3712]{1,0:T(8,128)(2,1)S(1)} %collective-permute-done.9.far_ref, bf16[1,7168,512]{2,1,0:T(8,128)(2,1)S(1)} %bitcast.1, bf16[1,7168,512]{2,1,0:T(8,128)(2,1)S(1)} %bitcast.3, ...), custom_call_target="tpu_custom_call" | custom-call | flops 704643072 | bytes 11010048 | tf_op jit(solution)/shard_map/pallas_call | solution.py:231
  25.1 0.3 collective-permute-start.10
  25.6 0.3 collective-permute-start.15
  25.9 0.8 %shard_map.138.refs_0_ = f32[64,3584]{1,0:T(8,128)S(1)} custom-call(bf16[64,3712]{1,0:T(8,128)(2,1)S(1)} %shard_map.135.near_ref, bf16[64,512]{1,0:T(8,128)(2,1)S(1)} %get-tuple-element.28.inner_ref, bf16[1,512,7168]{2,1,0:T(8,128)(2,1)S(1)} %bitcast.5), custom_call_target="tpu_custom_call" | custom-call | flops 234881024 | bytes 3670016 | tf_op jit(solution)/shard_map/pallas_call | solution.py:245
  26.6 0.3 collective-permute-done.10.refs_1_
  27.1 2.1 %collective-permute-start.11 = (bf16[16,3584]{1,0:T(8,128)(2,1)S(1)}, bf16[16,3584]{1,0:T(8,128)(2,1)S(1)}, u32[]{:S(2)}, u32[]{:S(2)}) collective-permute-start(bf16[16,3584]{1,0:T(8,128)(2,1)S(1)} %get-tuple-element.31), channel_id=1, source_target_pairs={{0,6},{1,7},{2,4},{3,5},{4,2},{5,3},{6,0},{7,1},{8,14},{9,15},{10,... | collective-permute-start | bytes 344072 | tf_op jit(solution)/shard_map/ppermute | solution.py:59
  29.1 0.6 %collective-permute-start.12 = (bf16[16,3584]{1,0:T(8,128)(2,1)S(1)}, bf16[16,3584]{1,0:T(8,128)(2,1)S(1)}, u32[]{:S(2)}, u32[]{:S(2)}) collective-permute-start(bf16[16,3584]{1,0:T(8,128)(2,1)S(1)} %get-tuple-element.32), channel_id=1, source_target_pairs={{0,4},{1,5},{2,6},{3,7},{4,0},{5,1},{6,2},{7,3},{8,12},{9,13},{10,... | collective-permute-start | bytes 344072 | tf_op jit(solution)/shard_map/ppermute | solution.py:59
  29.7 0.9 %collective-permute-start.13 = (bf16[16,3584]{1,0:T(8,128)(2,1)S(1)}, bf16[16,3584]{1,0:T(8,128)(2,1)S(1)}, u32[]{:S(2)}, u32[]{:S(2)}) collective-permute-start(bf16[16,3584]{1,0:T(8,128)(2,1)S(1)} %get-tuple-element.33), channel_id=1, source_target_pairs={{0,2},{1,3},{2,0},{3,1},{4,6},{5,7},{6,4},{7,5},{8,10},{9,11},{10,... | collective-permute-start | bytes 344072 | tf_op jit(solution)/shard_map/ppermute | solution.py:59
  30.9 2.4 %shard_map.140.refs_4_ = bf16[2,32768]{1,0:T(2,128)(2,1)} custom-call(s32[2]{0:T(128)S(1)} %copy-done.2, s32[2,12]{1,0:T(2,128)S(1)} %copy-done.1, bf16[2,36864]{1,0:T(2,128)(2,1)S(1)} %copy-done, bf16[24,18432]{1,0:T(8,128)(2,1)S(1)} %get-tuple-element.34.pool_ref, bf16[8,18432]{1,0:T(8,128)(2,1)S(1)} %pad_maximum_fusion.arrived_ref), custom_call_target="tpu_custom_call" | custom-call | flops 1073741824 | bytes 4194304 | tf_op jit(solution)/shard_map/pallas_call | solution.py:445
  33.3 0.5 %collective-permute-done.11.refs_1_ = bf16[16,3584]{1,0:T(8,128)(2,1)S(1)} collective-permute-done((bf16[16,3584]{1,0:T(8,128)(2,1)S(1)}, bf16[16,3584]{1,0:T(8,128)(2,1)S(1)}, u32[]{:S(2)}, u32[]{:S(2)}) %collective-permute-start.11) | collective-permute-done | bytes 114720 | tf_op jit(solution)/shard_map/ppermute | solution.py:59
  33.8 2.0 %collective-permute-done.12.refs_2_ = bf16[16,3584]{1,0:T(8,128)(2,1)S(1)} collective-permute-done((bf16[16,3584]{1,0:T(8,128)(2,1)S(1)}, bf16[16,3584]{1,0:T(8,128)(2,1)S(1)}, u32[]{:S(2)}, u32[]{:S(2)}) %collective-permute-start.12) | collective-permute-done | bytes 114720 | tf_op jit(solution)/shard_map/ppermute | solution.py:59
  35.9 3.1 %collective-permute-start.16 = (bf16[4,3584]{1,0:T(4,128)(2,1)S(1)}, bf16[4,3584]{1,0:T(4,128)(2,1)S(1)}, u32[]{:S(2)}, u32[]{:S(2)}) collective-permute-start(bf16[4,3584]{1,0:T(4,128)(2,1)S(1)} %get-tuple-element.37), channel_id=1, source_target_pairs={{0,24},{1,25},{2,26},{3,27},{4,28},{5,29},{6,30},{7,31},{8,16},{9,... | collective-permute-start | bytes 86024 | tf_op jit(solution)/shard_map/ppermute | solution.py:59
  39.0 1.3 %collective-permute-start.18 = (bf16[4,3584]{1,0:T(4,128)(2,1)S(1)}, bf16[4,3584]{1,0:T(4,128)(2,1)S(1)}, u32[]{:S(2)}, u32[]{:S(2)}) collective-permute-start(bf16[4,3584]{1,0:T(4,128)(2,1)S(1)} %get-tuple-element.39), channel_id=1, source_target_pairs={{0,8},{1,9},{2,10},{3,11},{4,12},{5,13},{6,14},{7,15},{8,0},{9,1},... | collective-permute-start | bytes 86024 | tf_op jit(solution)/shard_map/ppermute | solution.py:59
  40.3 1.6 %collective-permute-done.16.refs_1_ = bf16[4,3584]{1,0:T(4,128)(2,1)S(1)} collective-permute-done((bf16[4,3584]{1,0:T(4,128)(2,1)S(1)}, bf16[4,3584]{1,0:T(4,128)(2,1)S(1)}, u32[]{:S(2)}, u32[]{:S(2)}) %collective-permute-start.16) | collective-permute-done | bytes 28704 | tf_op jit(solution)/shard_map/ppermute | solution.py:59
  41.9 1.9 %collective-permute-done.17.refs_2_ = bf16[4,3584]{1,0:T(4,128)(2,1)S(1)} collective-permute-done((bf16[4,3584]{1,0:T(4,128)(2,1)S(1)}, bf16[4,3584]{1,0:T(4,128)(2,1)S(1)}, u32[]{:S(2)}, u32[]{:S(2)}) %collective-permute-start.17) | collective-permute-done | bytes 28704 | tf_op jit(solution)/shard_map/ppermute | solution.py:59
  43.9 1.2 %collective-permute-done.19.got_ref = bf16[2,3584]{1,0:T(2,128)(2,1)S(1)} collective-permute-done((bf16[2,3584]{1,0:T(2,128)(2,1)S(1)}, bf16[2,3584]{1,0:T(2,128)(2,1)S(1)}, u32[]{:S(2)}, u32[]{:S(2)}) %collective-permute-start.19) | collective-permute-done | bytes 14368 | tf_op jit(solution)/shard_map/ppermute | solution.py:59
  45.1 0.6 %shard_map.143 = bf16[2,7168]{1,0:T(2,128)(2,1)} custom-call(f32[2,3584]{1,0:T(2,128)S(1)} %get-tuple-element.40.keep_ref, bf16[2,3584]{1,0:T(2,128)(2,1)S(1)} %collective-permute-done.19.got_ref), custom_call_target="tpu_custom_call" | custom-call | bytes 57344 | tf_op jit(solution)/shard_map/pallas_call | solution.py:294
  (46 shorter events, 1.4 us)
Async XLA Ops:
  0.6 2.0 %collective-permute-start.1 = (s32[2,4]{1,0:T(2,128)}, s32[2,4]{1,0:T(2,128)S(1)}, u32[]{:S(2)}, u32[]{:S(2)}) collective-permute-start(s32[2,4]{1,0:T(2,128)} %refs_1_.1), channel_id=1, source_target_pairs={{0,1},{1,0},{2,3},{3,2},{4,5},{5,4},{6,7},{7,6},{8,9},{9,8},{10,11... | collective-permute-start | bytes 104 | tf_op jit(solution)/shard_map/ppermute | solution.py:59
  1.1 1.5 %collective-permute-start.2 = (f32[2,4]{1,0:T(2,128)}, f32[2,4]{1,0:T(2,128)S(1)}, u32[]{:S(2)}, u32[]{:S(2)}) collective-permute-start(f32[2,4]{1,0:T(2,128)} %refs_2_.1), channel_id=1, source_target_pairs={{0,1},{1,0},{2,3},{3,2},{4,5},{5,4},{6,7},{7,6},{8,9},{9,8},{10,11... | collective-permute-start | bytes 104 | tf_op jit(solution)/shard_map/ppermute | solution.py:59
  1.2 1.5 %collective-permute-start = (bf16[2,7168]{1,0:T(2,128)(2,1)}, bf16[2,7168]{1,0:T(2,128)(2,1)S(1)}, u32[]{:S(2)}, u32[]{:S(2)}) collective-permute-start(bf16[2,7168]{1,0:T(2,128)(2,1)} %refs_0_.1), channel_id=1, source_target_pairs={{0,1},{1,0},{2,3},{3,2},{4,5},{5,4},{6,7},{7,6},{8,9},{9,8},{10,11... | collective-permute-start | bytes 86024 | tf_op jit(solution)/shard_map/ppermute | solution.py:59
  1.7 21.3 %slice-start.4 = ((s8[7340032]{0:T(1024)(128)(4,1)}), s8[4194304]{0:T(1024)(128)(4,1)S(1)}, s32[]{:S(2)}) async-start(s8[7340032]{0:T(1024)(128)(4,1)} %bitcast.4), calls=%async_computation.4 | async-start | bytes 8388608
  2.7 18.5 %slice-start.2 = ((s8[7340032]{0:T(1024)(128)(4,1)}), s8[4194304]{0:T(1024)(128)(4,1)S(1)}, s32[]{:S(2)}) async-start(s8[7340032]{0:T(1024)(128)(4,1)} %bitcast.2), calls=%async_computation.2 | async-start | bytes 8388608
  2.8 8.9 %collective-permute-start.5 = (bf16[4,3712]{1,0:T(4,128)(2,1)S(1)}, bf16[4,3712]{1,0:T(4,128)(2,1)S(1)}, u32[]{:S(2)}, u32[]{:S(2)}) collective-permute-start(bf16[4,3712]{1,0:T(4,128)(2,1)S(1)} %shard_map.132.after_ref.refs_0_), channel_id=1, source_target_pairs={{0,24},{1,25},{2,26},{3,27},{4,28},{5,29},{6,30},{7,31},{8,16},{9,... | collective-permute-start | bytes 89096 | tf_op jit(solution)/shard_map/ppermute | solution.py:59
  7.8 4.8 %collective-permute-start.4 = (bf16[4,3712]{1,0:T(4,128)(2,1)S(1)}, bf16[4,3712]{1,0:T(4,128)(2,1)S(1)}, u32[]{:S(2)}, u32[]{:S(2)}) collective-permute-start(bf16[4,3712]{1,0:T(4,128)(2,1)S(1)} %shard_map.132.after_ref.refs_0_), channel_id=1, source_target_pairs={{0,16},{1,17},{2,18},{3,19},{4,20},{5,21},{6,22},{7,23},{8,24},{9,... | collective-permute-start | bytes 89096 | tf_op jit(solution)/shard_map/ppermute | solution.py:59
  7.8 4.8 %collective-permute-start.3 = (bf16[4,3712]{1,0:T(4,128)(2,1)S(1)}, bf16[4,3712]{1,0:T(4,128)(2,1)S(1)}, u32[]{:S(2)}, u32[]{:S(2)}) collective-permute-start(bf16[4,3712]{1,0:T(4,128)(2,1)S(1)} %shard_map.132.after_ref.refs_0_), channel_id=1, source_target_pairs={{0,8},{1,9},{2,10},{3,11},{4,12},{5,13},{6,14},{7,15},{8,0},{9,1},... | collective-permute-start | bytes 89096 | tf_op jit(solution)/shard_map/ppermute | solution.py:59
  10.0 11.2 %slice-start.3 = ((s8[7340032]{0:T(1024)(128)(4,1)}), s8[3145728]{0:T(1024)(128)(4,1)S(1)}, s32[]{:S(2)}) async-start(s8[7340032]{0:T(1024)(128)(4,1)} %bitcast.2), calls=%async_computation.3 | async-start | bytes 6291456
  10.0 12.9 %slice-start.5 = ((s8[7340032]{0:T(1024)(128)(4,1)}), s8[3145728]{0:T(1024)(128)(4,1)S(1)}, s32[]{:S(2)}) async-start(s8[7340032]{0:T(1024)(128)(4,1)} %bitcast.4), calls=%async_computation.5 | async-start | bytes 6291456
  10.0 11.1 %collective-permute-start.14 = (bf16[4,18432]{1,0:T(4,128)(2,1)S(1)}, bf16[4,18432]{1,0:T(4,128)(2,1)S(1)}, u32[]{:S(2)}, u32[]{:S(2)}) collective-permute-start(bf16[4,18432]{1,0:T(4,128)(2,1)S(1)} %get-tuple-element.25.refs_4_), channel_id=1, source_target_pairs={{0,2},{1,3},{2,0},{3,1},{4,6},{5,7},{6,4},{7,5},{8,10},{9,11},{10,... | collective-permute-start | bytes 442376 | tf_op jit(solution)/shard_map/ppermute | solution.py:59
  12.6 7.5 %collective-permute-start.8 = (bf16[16,3712]{1,0:T(8,128)(2,1)S(1)}, bf16[16,3712]{1,0:T(8,128)(2,1)S(1)}, u32[]{:S(2)}, u32[]{:S(2)}) collective-permute-start(bf16[16,3712]{1,0:T(8,128)(2,1)S(1)} %shard_map.134.refs_0_), channel_id=1, source_target_pairs={{0,6},{1,7},{2,4},{3,5},{4,2},{5,3},{6,0},{7,1},{8,14},{9,15},{10,... | collective-permute-start | bytes 356360 | tf_op jit(solution)/shard_map/ppermute | solution.py:59
  15.2 5.8 %collective-permute-start.7 = (bf16[16,3712]{1,0:T(8,128)(2,1)S(1)}, bf16[16,3712]{1,0:T(8,128)(2,1)S(1)}, u32[]{:S(2)}, u32[]{:S(2)}) collective-permute-start(bf16[16,3712]{1,0:T(8,128)(2,1)S(1)} %shard_map.134.refs_0_), channel_id=1, source_target_pairs={{0,4},{1,5},{2,6},{3,7},{4,0},{5,1},{6,2},{7,3},{8,12},{9,13},{10,... | collective-permute-start | bytes 356360 | tf_op jit(solution)/shard_map/ppermute | solution.py:59
  15.7 5.3 %collective-permute-start.6 = (bf16[16,3712]{1,0:T(8,128)(2,1)S(1)}, bf16[16,3712]{1,0:T(8,128)(2,1)S(1)}, u32[]{:S(2)}, u32[]{:S(2)}) collective-permute-start(bf16[16,3712]{1,0:T(8,128)(2,1)S(1)} %shard_map.134.refs_0_), channel_id=1, source_target_pairs={{0,2},{1,3},{2,0},{3,1},{4,6},{5,7},{6,4},{7,5},{8,10},{9,11},{10,... | collective-permute-start | bytes 356360 | tf_op jit(solution)/shard_map/ppermute | solution.py:59
  16.2 5.0 %slice-start = ((s8[7340032]{0:T(1024)(128)(4,1)}), s8[4194304]{0:T(1024)(128)(4,1)S(1)}, s32[]{:S(2)}) async-start(s8[7340032]{0:T(1024)(128)(4,1)} %bitcast), calls=%async_computation | async-start | bytes 8388608
  16.3 4.9 %slice-start.1 = ((s8[7340032]{0:T(1024)(128)(4,1)}), s8[3145728]{0:T(1024)(128)(4,1)S(1)}, s32[]{:S(2)}) async-start(s8[7340032]{0:T(1024)(128)(4,1)} %bitcast), calls=%async_computation.1 | async-start | bytes 6291456
  21.0 1.9 %collective-permute-start.9 = (bf16[64,3712]{1,0:T(8,128)(2,1)S(1)}, bf16[64,3712]{1,0:T(8,128)(2,1)S(1)}, u32[]{:S(2)}, u32[]{:S(2)}) collective-permute-start(bf16[64,3712]{1,0:T(8,128)(2,1)S(1)} %shard_map.135.near_ref), channel_id=1, source_target_pairs={{0,1},{1,0},{2,3},{3,2},{4,5},{5,4},{6,7},{7,6},{8,9},{9,8},{10,11... | collective-permute-start | bytes 1425416 | tf_op jit(solution)/shard_map/ppermute | solution.py:59
  25.0 5.8 %copy-start = (bf16[2,36864]{1,0:T(2,128)(2,1)S(1)}, bf16[2,36864]{1,0:T(2,128)(2,1)}, u32[]{:S(2)}) copy-start(bf16[2,36864]{1,0:T(2,128)(2,1)} %query_ref.1) | copy-start | bytes 442372
  25.0 5.8 %copy-start.1 = (s32[2,12]{1,0:T(2,128)S(1)}, s32[2,12]{1,0:T(2,128)}, u32[]{:S(2)}) copy-start(s32[2,12]{1,0:T(2,128)} %table_ref.1) | copy-start | bytes 292
  25.1 5.8 %copy-start.2 = (s32[2]{0:T(128)S(1)}, s32[2]{0:T(128)}, u32[]{:S(2)}) copy-start(s32[2]{0:T(128)} %length_ref.1) | copy-start | bytes 28
  25.1 1.9 %collective-permute-start.10 = (bf16[64,3584]{1,0:T(8,128)(2,1)S(1)}, bf16[64,3584]{1,0:T(8,128)(2,1)S(1)}, u32[]{:S(2)}, u32[]{:S(2)}) collective-permute-start(bf16[64,3584]{1,0:T(8,128)(2,1)S(1)} %get-tuple-element.29), channel_id=1, source_target_pairs={{0,1},{1,0},{2,3},{3,2},{4,5},{5,4},{6,7},{7,6},{8,9},{9,8},{10,11... | collective-permute-start | bytes 1376264 | tf_op jit(solution)/shard_map/ppermute | solution.py:59
  25.6 5.1 %collective-permute-start.15 = (bf16[4,18432]{1,0:T(4,128)(2,1)S(1)}, bf16[4,18432]{1,0:T(4,128)(2,1)S(1)}, u32[]{:S(2)}, u32[]{:S(2)}) collective-permute-start(bf16[4,18432]{1,0:T(4,128)(2,1)S(1)} %pad_maximum_fusion.1), channel_id=1, source_target_pairs={{0,1},{1,0},{2,3},{3,2},{4,5},{5,4},{6,7},{7,6},{8,9},{9,8},{10,11... | collective-permute-start | bytes 442376 | tf_op jit(solution)/shard_map/ppermute | solution.py:59
  27.1 6.7 %collective-permute-start.11 = (bf16[16,3584]{1,0:T(8,128)(2,1)S(1)}, bf16[16,3584]{1,0:T(8,128)(2,1)S(1)}, u32[]{:S(2)}, u32[]{:S(2)}) collective-permute-start(bf16[16,3584]{1,0:T(8,128)(2,1)S(1)} %get-tuple-element.31), channel_id=1, source_target_pairs={{0,6},{1,7},{2,4},{3,5},{4,2},{5,3},{6,0},{7,1},{8,14},{9,15},{10,... | collective-permute-start | bytes 344072 | tf_op jit(solution)/shard_map/ppermute | solution.py:59
  29.1 6.7 %collective-permute-start.12 = (bf16[16,3584]{1,0:T(8,128)(2,1)S(1)}, bf16[16,3584]{1,0:T(8,128)(2,1)S(1)}, u32[]{:S(2)}, u32[]{:S(2)}) collective-permute-start(bf16[16,3584]{1,0:T(8,128)(2,1)S(1)} %get-tuple-element.32), channel_id=1, source_target_pairs={{0,4},{1,5},{2,6},{3,7},{4,0},{5,1},{6,2},{7,3},{8,12},{9,13},{10,... | collective-permute-start | bytes 344072 | tf_op jit(solution)/shard_map/ppermute | solution.py:59
  29.7 6.1 %collective-permute-start.13 = (bf16[16,3584]{1,0:T(8,128)(2,1)S(1)}, bf16[16,3584]{1,0:T(8,128)(2,1)S(1)}, u32[]{:S(2)}, u32[]{:S(2)}) collective-permute-start(bf16[16,3584]{1,0:T(8,128)(2,1)S(1)} %get-tuple-element.33), channel_id=1, source_target_pairs={{0,2},{1,3},{2,0},{3,1},{4,6},{5,7},{6,4},{7,5},{8,10},{9,11},{10,... | collective-permute-start | bytes 344072 | tf_op jit(solution)/shard_map/ppermute | solution.py:59
  35.9 6.0 %collective-permute-start.16 = (bf16[4,3584]{1,0:T(4,128)(2,1)S(1)}, bf16[4,3584]{1,0:T(4,128)(2,1)S(1)}, u32[]{:S(2)}, u32[]{:S(2)}) collective-permute-start(bf16[4,3584]{1,0:T(4,128)(2,1)S(1)} %get-tuple-element.37), channel_id=1, source_target_pairs={{0,24},{1,25},{2,26},{3,27},{4,28},{5,29},{6,30},{7,31},{8,16},{9,... | collective-permute-start | bytes 86024 | tf_op jit(solution)/shard_map/ppermute | solution.py:59
  39.0 4.8 %collective-permute-start.17 = (bf16[4,3584]{1,0:T(4,128)(2,1)S(1)}, bf16[4,3584]{1,0:T(4,128)(2,1)S(1)}, u32[]{:S(2)}, u32[]{:S(2)}) collective-permute-start(bf16[4,3584]{1,0:T(4,128)(2,1)S(1)} %get-tuple-element.38), channel_id=1, source_target_pairs={{0,16},{1,17},{2,18},{3,19},{4,20},{5,21},{6,22},{7,23},{8,24},{9,... | collective-permute-start | bytes 86024 | tf_op jit(solution)/shard_map/ppermute | solution.py:59
  39.0 4.8 %collective-permute-start.18 = (bf16[4,3584]{1,0:T(4,128)(2,1)S(1)}, bf16[4,3584]{1,0:T(4,128)(2,1)S(1)}, u32[]{:S(2)}, u32[]{:S(2)}) collective-permute-start(bf16[4,3584]{1,0:T(4,128)(2,1)S(1)} %get-tuple-element.39), channel_id=1, source_target_pairs={{0,8},{1,9},{2,10},{3,11},{4,12},{5,13},{6,14},{7,15},{8,0},{9,1},... | collective-permute-start | bytes 86024 | tf_op jit(solution)/shard_map/ppermute | solution.py:59
  43.8 1.2 %collective-permute-start.19 = (bf16[2,3584]{1,0:T(2,128)(2,1)S(1)}, bf16[2,3584]{1,0:T(2,128)(2,1)S(1)}, u32[]{:S(2)}, u32[]{:S(2)}) collective-permute-start(bf16[2,3584]{1,0:T(2,128)(2,1)S(1)} %get-tuple-element.41), channel_id=1, source_target_pairs={{0,1},{1,0},{2,3},{3,2},{4,5},{5,4},{6,7},{7,6},{8,9},{9,8},{10,11... | collective-permute-start | bytes 43016 | tf_op jit(solution)/shard_map/ppermute | solution.py:59

commit v6 on v5

--- a/solution.py
+++ b/solution.py
@@ -131,12 +131,10 @@
 
 def merge_kernel(parts, *refs):
     out_ref = refs[-1]
-    rows = refs[0].shape[0]
-    if rows % 16:
-        out_ref[...] = jnp.concatenate([r[...].astype(f32) for r in refs[:parts]], axis=0).astype(bf16)
-    else:
-        for i in range(parts):
-            out_ref[i * rows : (i + 1) * rows] = refs[i][...]
+    half = refs[0].shape[0] // 2
+    pieces = [r[...].astype(f32) for r in refs[:parts]]
+    cores = [p[:half] for p in pieces] + [p[half:] for p in pieces]
+    out_ref[...] = jnp.concatenate(cores, axis=0).astype(bf16)
 
 
 def merge(pieces, flops, *after):
@@ -157,12 +155,17 @@
     return pl.multiple_of(core * (width // 2), width // 2)
 
 
+def padded(x):
+    rows = x.shape[0]
+    return x if rows >= 128 else jnp.concatenate([x] * (128 // rows), axis=0)
+
+
 def near_kernel(near_ref, gate_ref, up_ref, gate_out, up_out):
-    width = gate_ref.shape[1]
+    rows, width = near_ref.shape[0], gate_ref.shape[1]
     at = pl.ds(half_start(width, True), width // 2)
-    x = near_ref[:, : width // 2]
-    gate_out[...] = jnp.dot(x, gate_ref[0, at, :], preferred_element_type=f32)
-    up_out[...] = jnp.dot(x, up_ref[0, at, :], preferred_element_type=f32)
+    x = padded(near_ref[:, : width // 2])
+    gate_out[...] = jnp.dot(x, gate_ref[0, at, :], preferred_element_type=f32)[:rows]
+    up_out[...] = jnp.dot(x, up_ref[0, at, :], preferred_element_type=f32)[:rows]
 
 
 def row_weights(near_ref, half, ep_count):
@@ -176,34 +179,35 @@
 STEPS = 7
 
 
-def far_kernel(ep_count, near_ref, far_ref, gate_ref, up_ref, gate_in, up_in, down_ref, inner_ref, send_ref):
-    width = gate_ref.shape[1]
+def down_half(inner, row_weight, down_ref, start, keep_ref, send_ref):
+    first = lax.rem(lax.axis_index("dp"), 2) == 0
+    rows, half = keep_ref.shape
+    step = half // STEPS
+    x = padded(inner)
+    for i in range(STEPS):
+        columns = slice(i * step, (i + 1) * step)
+        out = jnp.dot(x, down_ref[0, :, start + i * step : start + (i + 1) * step], preferred_element_type=f32)
+        out = out[: 2 * rows] * row_weight
+        keep_ref[:, columns] = jnp.where(first, out[:rows], out[rows:])
+        send_ref[:, columns] = jnp.where(first, out[rows:], out[:rows]).astype(bf16)
+
+
+def far_kernel(ep_count, near_ref, far_ref, gate_ref, up_ref, gate_in, up_in, down_ref, inner_ref, keep_ref, send_ref):
+    rows, width = near_ref.shape[0], gate_ref.shape[1]
     half = width // 2
-    start = half_start(width, False)
-    at = pl.ds(start, half)
+    at = pl.ds(half_start(width, False), half)
     row_weight = row_weights(near_ref, half, ep_count)
-    x = far_ref[:, :half]
-    gate = gate_in[...] + jnp.dot(x, gate_ref[0, at, :], preferred_element_type=f32)
-    up = up_in[...] + jnp.dot(x, up_ref[0, at, :], preferred_element_type=f32)
+    x = padded(far_ref[:, :half])
+    gate = gate_in[...] + jnp.dot(x, gate_ref[0, at, :], preferred_element_type=f32)[:rows]
+    up = up_in[...] + jnp.dot(x, up_ref[0, at, :], preferred_element_type=f32)[:rows]
     inner = (gate / (1.0 + jnp.exp(-gate)) * up).astype(bf16)
     inner_ref[...] = inner
-    step = half // STEPS
-    for i in range(STEPS):
-        columns = pl.ds(pl.multiple_of(start + i * step, step), step)
-        out = jnp.dot(inner, down_ref[0, :, columns], preferred_element_type=f32) * row_weight
-        send_ref[:, i * step : (i + 1) * step] = out.astype(bf16)
-
-
-def keep_kernel(ep_count, near_ref, inner_ref, down_ref, keep_ref):
+    down_half(inner, row_weight, down_ref, 0, keep_ref, send_ref)
+
+
+def rest_kernel(ep_count, near_ref, inner_ref, down_ref, keep_ref, send_ref):
     half = keep_ref.shape[1]
-    start = half_start(2 * half, True)
-    row_weight = row_weights(near_ref, half, ep_count)
-    step = half // STEPS
-    inner = inner_ref[...]
-    for i in range(STEPS):
-        columns = pl.ds(pl.multiple_of(start + i * step, step), step)
-        out = jnp.dot(inner, down_ref[0, :, columns], preferred_element_type=f32)
-        keep_ref[:, i * step : (i + 1) * step] = out * row_weight
+    down_half(inner_ref[...], row_weights(near_ref, half, ep_count), down_ref, half, keep_ref, send_ref)
 
 
 def estimate(rows, weights):
@@ -230,75 +234,62 @@
     half = width // 2
     return pl.pallas_call(
         functools.partial(far_kernel, ep_count),
-        out_shape=(pltpu.VMEM((rows, units), bf16), pltpu.VMEM((rows, half), bf16)),
+        out_shape=(
+            pltpu.VMEM((rows, units), bf16),
+            pltpu.VMEM((rows // 2, half), f32),
+            pltpu.VMEM((rows // 2, half), bf16),
+        ),
         in_specs=[in_vmem()] * 7,
-        out_specs=(in_vmem(),) * 2,
+        out_specs=(in_vmem(),) * 3,
         compiler_params=pltpu.CompilerParams(vmem_limit_bytes=8 * MIB),
         cost_estimate=estimate(rows, 3 * half * units),
     )(vmem(near), vmem(far), gate, up, vmem(gate_acc), vmem(up_acc), down)
 
 
-def keep_products(near, inner, down, ep_count):
+def rest_products(near, inner, down, ep_count):
     rows = near.shape[0]
     units, width = down.shape[1:]
     half = width // 2
     return pl.pallas_call(
-        functools.partial(keep_kernel, ep_count),
-        out_shape=pltpu.VMEM((rows, half), f32),
+        functools.partial(rest_kernel, ep_count),
+        out_shape=(pltpu.VMEM((rows // 2, half), f32), pltpu.VMEM((rows // 2, half), bf16)),
         in_specs=[in_vmem()] * 3,
-        out_specs=in_vmem(),
+        out_specs=(in_vmem(),) * 2,
         compiler_params=pltpu.CompilerParams(vmem_limit_bytes=8 * MIB),
         cost_estimate=estimate(rows, half * units),
     )(vmem(near), vmem(inner), down)
 
 
-def fold_kernel(by_core, parts, arrived, *refs):
-    keep_ref, got_refs = refs[0], refs[1 : 1 + arrived]
+def fold_kernel(arrived, parts, *refs):
     outs = refs[-parts:]
-    total = keep_ref[...]
-    for g in got_refs:
-        total += g[...].astype(f32)
     rows = outs[0].shape[0]
-    pieces = [total[i * rows : (i + 1) * rows] for i in range(parts)]
-    if by_core:
-        first = lax.rem(lax.axis_index("dp"), 2) == 0
-        pieces = [jnp.where(first, pieces[0], pieces[1]), jnp.where(first, pieces[1], pieces[0])]
-    outs[0][...] = pieces[0]
-    for out, piece in zip(outs[1:], pieces[1:]):
-        out[...] = piece.astype(bf16)
-
-
-def fold(keep, gots, parts, *after, by_core=False):
-    rows, width = keep.shape
+    start = at = 0
+    for number in arrived:
+        ours = refs[at : at + 1 + number]
+        at += 1 + number
+        total = ours[0][...]
+        for g in ours[1:]:
+            total += g[...].astype(f32)
+        columns = slice(start, start + total.shape[1])
+        start += total.shape[1]
+        for i, out in enumerate(outs):
+            out[:, columns] = total[i * rows : (i + 1) * rows].astype(out.dtype)
+
+
+def fold(held, parts, *after, out=None, flops=0):
+    rows = held[0][0].shape[0]
+    width = sum(keep.shape[1] for keep, _ in held)
     part = (rows // parts, width)
-    return pl.pallas_call(
-        functools.partial(fold_kernel, by_core, parts, len(gots)),
-        out_shape=(pltpu.VMEM(part, f32),) + (pltpu.VMEM(part, bf16),) * (parts - 1),
-        in_specs=[in_vmem()] * (1 + len(gots)) + [anywhere()] * len(after),
+    operands = [vmem(x) for keep, gots in held for x in [keep] + gots]
+    shapes = (pltpu.VMEM(part, f32),) + (pltpu.VMEM(part, bf16),) * (parts - 1)
+    return pl.pallas_call(
+        functools.partial(fold_kernel, [len(gots) for _, gots in held], parts),
+        out_shape=shapes if out is None else (out,),
+        in_specs=[in_vmem()] * len(operands) + [anywhere()] * len(after),
         out_specs=(in_vmem(),) * parts,
         compiler_params=pltpu.CompilerParams(vmem_limit_bytes=4 * MIB),
-        cost_estimate=pl.CostEstimate(flops=0, bytes_accessed=8 * rows * width, transcendentals=0),
-    )(vmem(keep), *[vmem(g) for g in gots], *after)
-
-
-def finish_kernel(keep_ref, got_ref, out_ref):
-    half = keep_ref.shape[1]
-    first = lax.rem(lax.axis_index("dp"), 2) == 0
-    keep, got = keep_ref[...], got_ref[...].astype(f32)
-    out_ref[:, :half] = jnp.where(first, keep, got).astype(bf16)
-    out_ref[:, half:] = jnp.where(first, got, keep).astype(bf16)
-
-
-def finish(keep, got):
-    rows, half = keep.shape
-    return pl.pallas_call(
-        finish_kernel,
-        out_shape=jax.ShapeDtypeStruct((rows, 2 * half), bf16),
-        in_specs=[in_vmem(), in_vmem()],
-        out_specs=in_vmem(),
-        compiler_params=pltpu.CompilerParams(vmem_limit_bytes=4 * MIB),
-        cost_estimate=pl.CostEstimate(flops=0, bytes_accessed=8 * rows * half, transcendentals=0),
-    )(vmem(keep), vmem(got))
+        cost_estimate=pl.CostEstimate(flops=flops, bytes_accessed=8 * rows * width, transcendentals=0),
+    )(*operands, *after)
 
 
 def pages_kernel(
@@ -488,17 +479,22 @@
     arrived, senders = exchange_pages(low, high, dp_count)
     far = trade(near, 1)
     gate_acc, up_acc = near_products(near, gate_weight, up_weight)
-    inner, send = far_products(near, far, gate_weight, up_weight, gate_acc, up_acc, down_weight, ep_count)
-    got = [trade(send, 1)]
-    keep = keep_products(near, inner, down_weight, ep_count)
+    inner, keep_a, send_a = far_products(
+        near, far, gate_weight, up_weight, gate_acc, up_acc, down_weight, ep_count
+    )
+    got_a = trade(send_a, 1)
+    keep_b, send_b = rest_products(near, inner, down_weight, ep_count)
+    got_b = trade(send_b, 1)
+    (sum_a,) = fold([(keep_a, [got_a])], 1, out=pltpu.VMEM(keep_a.shape, f32), flops=MERGE_FLOPS // 4)
+    held = [(sum_a, []), (keep_b, [got_b])]
     attended = attend(lengths, page_table, queries, pool, arrived, senders)
     after = []
-    for partners in reversed(stages):
-        keep, *send = fold(keep, got, len(partners) + 1, *after)
-        got = [trade(x, bit) for x, bit in list(zip(send, partners))[::-1]]
-        after = [] if after else [hbm(attended)]
-    keep, send = fold(keep, got, 2, *(after if len(stages) == 1 else []), by_core=True)
-    return finish(keep, trade(send, 1)), attended
+    for number, partners in enumerate(reversed(stages)):
+        keep, *send = fold(held, len(partners) + 1, *(after if number == 1 else []))
+        held = [(keep, [trade(x, bit) for x, bit in list(zip(send, partners))[::-1]])]
+        after = [hbm(attended)]
+    (expert_mix,) = fold(held, 1, out=jax.ShapeDtypeStruct(hidden.shape, bf16))
+    return expert_mix, attended
 
 
 def solution(mesh):

time: 45.9 us -> 45.2 us (0.985)
  Pallas kernels: 10 us -> 9.4 us
  transfers between devices with their start and end apart: 20 -> 20, of which waited for: 11 -> 10; matrix products, arithmetic and copies ran while one was open for 1% -> 1% of each run, Pallas kernels for 16% -> 15%
where the time goes in v6:
time: 45.2 us; the launch traced here: 45.1 us
  starting transfers between devices  20.8 us (46%)
  waiting for transfers between devices  13.3 us (29%)
  Pallas kernels  9.4 us (21%)
  between operations  0.87 us (2%)
    ppermute x20, starting transfers between devices, swap(): return lax.ppermute(x, axes, pairs)  20.8 us
    ppermute x20, waiting for transfers between devices, swap(): return lax.ppermute(x, axes, pairs)  13.3 us
    pallas_call x1, Pallas kernels, attend(): pl.pallas_call(functools.partial(attend_kernel, senders), out_shape=jax.S...  2.35 us
    pallas_call x1, Pallas kernels, far_products(): pl.pallas_call(functools.partial(far_kernel, ep_count), out_shape=(pltpu....  1.78 us
    pallas_call x1, Pallas kernels, pick_pages(): pl.pallas_call(functools.partial(pages_kernel, dp_count), out_shape=(half...  1.5 us
    pallas_call x1, Pallas kernels, near_products(): pl.pallas_call(near_kernel, out_shape=(acc, acc), in_specs=[in_vmem()] *...  1.15 us
    pallas_call x1, Pallas kernels, fetch(): pl.pallas_call(fetch_kernel, out_shape=tuple((pltpu.VMEM(x.shape, x.dtype...  0.93 us
  transfers between devices with their start and end apart: 20, of which 10 were waited for; matrix products, arithmetic and copies ran while one was open for 1% of the time, Pallas kernels for 15%

profile of v6, /device:TPU:0, one launch (start us, length us, event | category | flops | bytes accessed | tf_op | source)
XLA Modules:
  0.0 45.1 jit_solution(12173529241582610570)
XLA Ops:
  0.6 0.5 %collective-permute-start.1 = (s32[2,4]{1,0:T(2,128)}, s32[2,4]{1,0:T(2,128)S(1)}, u32[]{:S(2)}, u32[]{:S(2)}) collective-permute-start(s32[2,4]{1,0:T(2,128)} %refs_1_.1), channel_id=1, source_target_pairs={{0,1},{1,0},{2,3},{3,2},{4,5},{5,4},{6,7},{7,6},{8,9},{9,8},{10,11... | collective-permute-start | bytes 104 | tf_op jit(solution)/shard_map/ppermute | solution.py:59
  1.2 0.4 collective-permute-start
  1.7 0.9 %shard_map.131 = (bf16[2,7168]{1,0:T(2,128)(2,1)S(1)}, s32[2,4]{1,0:T(2,128)S(1)}, f32[2,4]{1,0:T(2,128)S(1)}) custom-call(bf16[2,7168]{1,0:T(2,128)(2,1)} %refs_0_.1, s32[2,4]{1,0:T(2,128)} %refs_1_.1, f32[2,4]{1,0:T(2,128)} %refs_2_.1), custom_call_target="tpu_custom_call" | custom-call | flops 1250000000 | bytes 1048576 | tf_op jit(solution)/shard_map/pallas_call | solution.py:85
  2.8 5.0 %collective-permute-start.5 = (bf16[4,3712]{1,0:T(4,128)(2,1)S(1)}, bf16[4,3712]{1,0:T(4,128)(2,1)S(1)}, u32[]{:S(2)}, u32[]{:S(2)}) collective-permute-start(bf16[4,3712]{1,0:T(4,128)(2,1)S(1)} %shard_map.132.after_ref.refs_0_), channel_id=1, source_target_pairs={{0,24},{1,25},{2,26},{3,27},{4,28},{5,29},{6,30},{7,31},{8,16},{9,... | collective-permute-start | bytes 89096 | tf_op jit(solution)/shard_map/ppermute | solution.py:59
  7.8 0.6 %collective-permute-start.3 = (bf16[4,3712]{1,0:T(4,128)(2,1)S(1)}, bf16[4,3712]{1,0:T(4,128)(2,1)S(1)}, u32[]{:S(2)}, u32[]{:S(2)}) collective-permute-start(bf16[4,3712]{1,0:T(4,128)(2,1)S(1)} %shard_map.132.after_ref.refs_0_), channel_id=1, source_target_pairs={{0,8},{1,9},{2,10},{3,11},{4,12},{5,13},{6,14},{7,15},{8,0},{9,1},... | collective-permute-start | bytes 89096 | tf_op jit(solution)/shard_map/ppermute | solution.py:59
  8.5 1.5 %shard_map.133 = (bf16[4,18432]{1,0:T(4,128)(2,1)S(1)}, bf16[4,18432]{1,0:T(4,128)(2,1)S(1)}, bf16[24,18432]{1,0:T(8,128)(2,1)S(1)}) custom-call(s32[1,6]{1,0:T(1,128)} %page_hbm.1, s32[1,6]{1,0:T(1,128)} %dest_hbm.1, bf16[24,18432]{1,0:T(8,128)(2,1)} %pool_ref.1, bf16[4,3712]{1,0:T(4,128)(2,1)S(1)} %shard_map.132.after_ref.refs_0_), custom_call_target="tpu_custom_call" | custom-call | bytes 1769472 | tf_op jit(solution)/shard_map/pallas_call | solution.py:332
  10.0 1.7 %collective-permute-start.15 = (bf16[4,18432]{1,0:T(4,128)(2,1)S(1)}, bf16[4,18432]{1,0:T(4,128)(2,1)S(1)}, u32[]{:S(2)}, u32[]{:S(2)}) collective-permute-start(bf16[4,18432]{1,0:T(4,128)(2,1)S(1)} %get-tuple-element.26.refs_4_), channel_id=1, source_target_pairs={{0,2},{1,3},{2,0},{3,1},{4,6},{5,7},{6,4},{7,5},{8,10},{9,11},{10,... | collective-permute-start | bytes 442376 | tf_op jit(solution)/shard_map/ppermute | solution.py:59
  11.7 0.9 %collective-permute-done.4.refs_2_ = bf16[4,3712]{1,0:T(4,128)(2,1)S(1)} collective-permute-done((bf16[4,3712]{1,0:T(4,128)(2,1)S(1)}, bf16[4,3712]{1,0:T(4,128)(2,1)S(1)}, u32[]{:S(2)}, u32[]{:S(2)}) %collective-permute-start.4) | collective-permute-done | bytes 29728 | tf_op jit(solution)/shard_map/ppermute | solution.py:59
  12.7 2.5 %collective-permute-start.8 = (bf16[16,3712]{1,0:T(8,128)(2,1)S(1)}, bf16[16,3712]{1,0:T(8,128)(2,1)S(1)}, u32[]{:S(2)}, u32[]{:S(2)}) collective-permute-start(bf16[16,3712]{1,0:T(8,128)(2,1)S(1)} %shard_map.134.refs_0_), channel_id=1, source_target_pairs={{0,6},{1,7},{2,4},{3,5},{4,2},{5,3},{6,0},{7,1},{8,14},{9,15},{10,... | collective-permute-start | bytes 356360 | tf_op jit(solution)/shard_map/ppermute | solution.py:59
  15.2 0.5 %collective-permute-start.7 = (bf16[16,3712]{1,0:T(8,128)(2,1)S(1)}, bf16[16,3712]{1,0:T(8,128)(2,1)S(1)}, u32[]{:S(2)}, u32[]{:S(2)}) collective-permute-start(bf16[16,3712]{1,0:T(8,128)(2,1)S(1)} %shard_map.134.refs_0_), channel_id=1, source_target_pairs={{0,4},{1,5},{2,6},{3,7},{4,0},{5,1},{6,2},{7,3},{8,12},{9,13},{10,... | collective-permute-start | bytes 356360 | tf_op jit(solution)/shard_map/ppermute | solution.py:59
  15.7 0.5 %collective-permute-start.6 = (bf16[16,3712]{1,0:T(8,128)(2,1)S(1)}, bf16[16,3712]{1,0:T(8,128)(2,1)S(1)}, u32[]{:S(2)}, u32[]{:S(2)}) collective-permute-start(bf16[16,3712]{1,0:T(8,128)(2,1)S(1)} %shard_map.134.refs_0_), channel_id=1, source_target_pairs={{0,2},{1,3},{2,0},{3,1},{4,6},{5,7},{6,4},{7,5},{8,10},{9,11},{10,... | collective-permute-start | bytes 356360 | tf_op jit(solution)/shard_map/ppermute | solution.py:59
  16.4 3.7 %collective-permute-done.8.refs_3_ = bf16[16,3712]{1,0:T(8,128)(2,1)S(1)} collective-permute-done((bf16[16,3712]{1,0:T(8,128)(2,1)S(1)}, bf16[16,3712]{1,0:T(8,128)(2,1)S(1)}, u32[]{:S(2)}, u32[]{:S(2)}) %collective-permute-start.8) | collective-permute-done | bytes 118816 | tf_op jit(solution)/shard_map/ppermute | solution.py:59
  20.1 0.9 %collective-permute-done.7.refs_2_ = bf16[16,3712]{1,0:T(8,128)(2,1)S(1)} collective-permute-done((bf16[16,3712]{1,0:T(8,128)(2,1)S(1)}, bf16[16,3712]{1,0:T(8,128)(2,1)S(1)}, u32[]{:S(2)}, u32[]{:S(2)}) %collective-permute-start.7) | collective-permute-done | bytes 118816 | tf_op jit(solution)/shard_map/ppermute | solution.py:59
  21.3 1.1 %shard_map.136 = (f32[64,512]{1,0:T(8,128)S(1)}, f32[64,512]{1,0:T(8,128)S(1)}) custom-call(bf16[64,3712]{1,0:T(8,128)(2,1)S(1)} %shard_map.135.near_ref, bf16[1,7168,512]{2,1,0:T(8,128)(2,1)S(1)} %bitcast.1, bf16[1,7168,512]{2,1,0:T(8,128)(2,1)S(1)} %bitcast.3), custom_call_target="tpu_custom_call" | custom-call | flops 469762048 | bytes 7340032 | tf_op jit(solution)/shard_map/pallas_call | solution.py:221
  22.5 0.5 %collective-permute-done.9.far_ref = bf16[64,3712]{1,0:T(8,128)(2,1)S(1)} collective-permute-done((bf16[64,3712]{1,0:T(8,128)(2,1)S(1)}, bf16[64,3712]{1,0:T(8,128)(2,1)S(1)}, u32[]{:S(2)}, u32[]{:S(2)}) %collective-permute-start.9) | collective-permute-done | bytes 475168 | tf_op jit(solution)/shard_map/ppermute | solution.py:59
  23.0 1.8 %shard_map.137 = (bf16[64,512]{1,0:T(8,128)(2,1)S(1)}, f32[32,3584]{1,0:T(8,128)S(1)}, bf16[32,3584]{1,0:T(8,128)(2,1)S(1)}) custom-call(bf16[64,3712]{1,0:T(8,128)(2,1)S(1)} %shard_map.135.near_ref, bf16[64,3712]{1,0:T(8,128)(2,1)S(1)} %collective-permute-done.9.far_ref, bf16[1,7168,512]{2,1,0:T(8,128)(2,1)S(1)} %bitcast.1, ...), custom_call_target="tpu_custom_call" | custom-call | flops 704643072 | bytes 11010048 | tf_op jit(solution)/shard_map/pallas_call | solution.py:235
  24.7 0.2 collective-permute-start.10
  25.1 0.4 collective-permute-start.16
  25.5 0.7 %shard_map.139 = (f32[32,3584]{1,0:T(8,128)S(1)}, bf16[32,3584]{1,0:T(8,128)(2,1)S(1)}) custom-call(bf16[64,3712]{1,0:T(8,128)(2,1)S(1)} %shard_map.135.near_ref, bf16[64,512]{1,0:T(8,128)(2,1)S(1)} %get-tuple-element.31.inner_ref, bf16[1,512,7168]{2,1,0:T(8,128)(2,1)S(1)} %bitcast.5), custom_call_target="tpu_custom_call" | custom-call | flops 234881024 | bytes 3670016 | tf_op jit(solution)/shard_map/pallas_call | solution.py:253
  26.5 1.3 %collective-permute-done.11.refs_2_ = bf16[32,3584]{1,0:T(8,128)(2,1)S(1)} collective-permute-done((bf16[32,3584]{1,0:T(8,128)(2,1)S(1)}, bf16[32,3584]{1,0:T(8,128)(2,1)S(1)}, u32[]{:S(2)}, u32[]{:S(2)}) %collective-permute-start.11) | collective-permute-done | bytes 229408 | tf_op jit(solution)/shard_map/ppermute | solution.py:59
  27.8 2.0 %collective-permute-start.12 = (bf16[8,7168]{1,0:T(8,128)(2,1)S(1)}, bf16[8,7168]{1,0:T(8,128)(2,1)S(1)}, u32[]{:S(2)}, u32[]{:S(2)}) collective-permute-start(bf16[8,7168]{1,0:T(8,128)(2,1)S(1)} %get-tuple-element.35), channel_id=1, source_target_pairs={{0,6},{1,7},{2,4},{3,5},{4,2},{5,3},{6,0},{7,1},{8,14},{9,15},{10,... | collective-permute-start | bytes 344072 | tf_op jit(solution)/shard_map/ppermute | solution.py:59
  29.9 0.6 %collective-permute-start.13 = (bf16[8,7168]{1,0:T(8,128)(2,1)S(1)}, bf16[8,7168]{1,0:T(8,128)(2,1)S(1)}, u32[]{:S(2)}, u32[]{:S(2)}) collective-permute-start(bf16[8,7168]{1,0:T(8,128)(2,1)S(1)} %get-tuple-element.36), channel_id=1, source_target_pairs={{0,4},{1,5},{2,6},{3,7},{4,0},{5,1},{6,2},{7,3},{8,12},{9,13},{10,... | collective-permute-start | bytes 344072 | tf_op jit(solution)/shard_map/ppermute | solution.py:59
  30.4 1.0 %collective-permute-start.14 = (bf16[8,7168]{1,0:T(8,128)(2,1)S(1)}, bf16[8,7168]{1,0:T(8,128)(2,1)S(1)}, u32[]{:S(2)}, u32[]{:S(2)}) collective-permute-start(bf16[8,7168]{1,0:T(8,128)(2,1)S(1)} %get-tuple-element.37), channel_id=1, source_target_pairs={{0,2},{1,3},{2,0},{3,1},{4,6},{5,7},{6,4},{7,5},{8,10},{9,11},{10,... | collective-permute-start | bytes 344072 | tf_op jit(solution)/shard_map/ppermute | solution.py:59
  31.4 0.2 pad_maximum_fusion.arrived_ref
  31.7 2.4 %shard_map.141.refs_4_ = bf16[2,32768]{1,0:T(2,128)(2,1)} custom-call(s32[2]{0:T(128)S(1)} %copy-done.2, s32[2,12]{1,0:T(2,128)S(1)} %copy-done.1, bf16[2,36864]{1,0:T(2,128)(2,1)S(1)} %copy-done, bf16[24,18432]{1,0:T(8,128)(2,1)S(1)} %get-tuple-element.38.pool_ref, bf16[8,18432]{1,0:T(8,128)(2,1)S(1)} %pad_maximum_fusion.arrived_ref), custom_call_target="tpu_custom_call" | custom-call | flops 1073741824 | bytes 4194304 | tf_op jit(solution)/shard_map/pallas_call | solution.py:436
  34.0 0.4 collective-permute-done.12.refs_1_
  34.5 2.0 %collective-permute-done.13.refs_2_ = bf16[8,7168]{1,0:T(8,128)(2,1)S(1)} collective-permute-done((bf16[8,7168]{1,0:T(8,128)(2,1)S(1)}, bf16[8,7168]{1,0:T(8,128)(2,1)S(1)}, u32[]{:S(2)}, u32[]{:S(2)}) %collective-permute-start.13) | collective-permute-done | bytes 114720 | tf_op jit(solution)/shard_map/ppermute | solution.py:59
  36.5 3.1 %collective-permute-start.17 = (bf16[2,7168]{1,0:T(2,128)(2,1)S(1)}, bf16[2,7168]{1,0:T(2,128)(2,1)S(1)}, u32[]{:S(2)}, u32[]{:S(2)}) collective-permute-start(bf16[2,7168]{1,0:T(2,128)(2,1)S(1)} %get-tuple-element.41), channel_id=1, source_target_pairs={{0,24},{1,25},{2,26},{3,27},{4,28},{5,29},{6,30},{7,31},{8,16},{9,... | collective-permute-start | bytes 86024 | tf_op jit(solution)/shard_map/ppermute | solution.py:59
  39.6 1.3 %collective-permute-start.19 = (bf16[2,7168]{1,0:T(2,128)(2,1)S(1)}, bf16[2,7168]{1,0:T(2,128)(2,1)S(1)}, u32[]{:S(2)}, u32[]{:S(2)}) collective-permute-start(bf16[2,7168]{1,0:T(2,128)(2,1)S(1)} %get-tuple-element.43), channel_id=1, source_target_pairs={{0,8},{1,9},{2,10},{3,11},{4,12},{5,13},{6,14},{7,15},{8,0},{9,1},... | collective-permute-start | bytes 86024 | tf_op jit(solution)/shard_map/ppermute | solution.py:59
  41.0 1.5 %collective-permute-done.17.refs_1_ = bf16[2,7168]{1,0:T(2,128)(2,1)S(1)} collective-permute-done((bf16[2,7168]{1,0:T(2,128)(2,1)S(1)}, bf16[2,7168]{1,0:T(2,128)(2,1)S(1)}, u32[]{:S(2)}, u32[]{:S(2)}) %collective-permute-start.17) | collective-permute-done | bytes 28704 | tf_op jit(solution)/shard_map/ppermute | solution.py:59
  42.5 1.9 %collective-permute-done.18.refs_2_ = bf16[2,7168]{1,0:T(2,128)(2,1)S(1)} collective-permute-done((bf16[2,7168]{1,0:T(2,128)(2,1)S(1)}, bf16[2,7168]{1,0:T(2,128)(2,1)S(1)}, u32[]{:S(2)}, u32[]{:S(2)}) %collective-permute-start.18) | collective-permute-done | bytes 28704 | tf_op jit(solution)/shard_map/ppermute | solution.py:59
  44.4 0.7 %shard_map.143 = bf16[2,7168]{1,0:T(2,128)(2,1)} custom-call(f32[2,7168]{1,0:T(2,128)S(1)} %get-tuple-element.40.refs_0_, bf16[2,7168]{1,0:T(2,128)(2,1)S(1)} %collective-permute-done.17.refs_1_, bf16[2,7168]{1,0:T(2,128)(2,1)S(1)} %collective-permute-done.18.refs_2_, bf16[2,7168]{1,0:T(2,128)(2,1)S(1)} %collective-permute-done.19.refs_3_), custom_call_target="tpu_custom_call" | custom-call | bytes 114688 | tf_op jit(solution)/shard_map/pallas_call | solution.py:285
  (46 shorter events, 1.3 us)
Async XLA Ops:
  0.6 2.0 %collective-permute-start.1 = (s32[2,4]{1,0:T(2,128)}, s32[2,4]{1,0:T(2,128)S(1)}, u32[]{:S(2)}, u32[]{:S(2)}) collective-permute-start(s32[2,4]{1,0:T(2,128)} %refs_1_.1), channel_id=1, source_target_pairs={{0,1},{1,0},{2,3},{3,2},{4,5},{5,4},{6,7},{7,6},{8,9},{9,8},{10,11... | collective-permute-start | bytes 104 | tf_op jit(solution)/shard_map/ppermute | solution.py:59
  1.1 1.5 %collective-permute-start.2 = (f32[2,4]{1,0:T(2,128)}, f32[2,4]{1,0:T(2,128)S(1)}, u32[]{:S(2)}, u32[]{:S(2)}) collective-permute-start(f32[2,4]{1,0:T(2,128)} %refs_2_.1), channel_id=1, source_target_pairs={{0,1},{1,0},{2,3},{3,2},{4,5},{5,4},{6,7},{7,6},{8,9},{9,8},{10,11... | collective-permute-start | bytes 104 | tf_op jit(solution)/shard_map/ppermute | solution.py:59
  1.2 1.5 %collective-permute-start = (bf16[2,7168]{1,0:T(2,128)(2,1)}, bf16[2,7168]{1,0:T(2,128)(2,1)S(1)}, u32[]{:S(2)}, u32[]{:S(2)}) collective-permute-start(bf16[2,7168]{1,0:T(2,128)(2,1)} %refs_0_.1), channel_id=1, source_target_pairs={{0,1},{1,0},{2,3},{3,2},{4,5},{5,4},{6,7},{7,6},{8,9},{9,8},{10,11... | collective-permute-start | bytes 86024 | tf_op jit(solution)/shard_map/ppermute | solution.py:59
  1.7 21.3 %slice-start.4 = ((s8[7340032]{0:T(1024)(128)(4,1)}), s8[4194304]{0:T(1024)(128)(4,1)S(1)}, s32[]{:S(2)}) async-start(s8[7340032]{0:T(1024)(128)(4,1)} %bitcast.4), calls=%async_computation.4 | async-start | bytes 8388608
  2.7 18.5 %slice-start.2 = ((s8[7340032]{0:T(1024)(128)(4,1)}), s8[4194304]{0:T(1024)(128)(4,1)S(1)}, s32[]{:S(2)}) async-start(s8[7340032]{0:T(1024)(128)(4,1)} %bitcast.2), calls=%async_computation.2 | async-start | bytes 8388608
  2.8 8.9 %collective-permute-start.5 = (bf16[4,3712]{1,0:T(4,128)(2,1)S(1)}, bf16[4,3712]{1,0:T(4,128)(2,1)S(1)}, u32[]{:S(2)}, u32[]{:S(2)}) collective-permute-start(bf16[4,3712]{1,0:T(4,128)(2,1)S(1)} %shard_map.132.after_ref.refs_0_), channel_id=1, source_target_pairs={{0,24},{1,25},{2,26},{3,27},{4,28},{5,29},{6,30},{7,31},{8,16},{9,... | collective-permute-start | bytes 89096 | tf_op jit(solution)/shard_map/ppermute | solution.py:59
  7.8 4.8 %collective-permute-start.4 = (bf16[4,3712]{1,0:T(4,128)(2,1)S(1)}, bf16[4,3712]{1,0:T(4,128)(2,1)S(1)}, u32[]{:S(2)}, u32[]{:S(2)}) collective-permute-start(bf16[4,3712]{1,0:T(4,128)(2,1)S(1)} %shard_map.132.after_ref.refs_0_), channel_id=1, source_target_pairs={{0,16},{1,17},{2,18},{3,19},{4,20},{5,21},{6,22},{7,23},{8,24},{9,... | collective-permute-start | bytes 89096 | tf_op jit(solution)/shard_map/ppermute | solution.py:59
  7.8 4.8 %collective-permute-start.3 = (bf16[4,3712]{1,0:T(4,128)(2,1)S(1)}, bf16[4,3712]{1,0:T(4,128)(2,1)S(1)}, u32[]{:S(2)}, u32[]{:S(2)}) collective-permute-start(bf16[4,3712]{1,0:T(4,128)(2,1)S(1)} %shard_map.132.after_ref.refs_0_), channel_id=1, source_target_pairs={{0,8},{1,9},{2,10},{3,11},{4,12},{5,13},{6,14},{7,15},{8,0},{9,1},... | collective-permute-start | bytes 89096 | tf_op jit(solution)/shard_map/ppermute | solution.py:59
  10.0 11.3 %slice-start.3 = ((s8[7340032]{0:T(1024)(128)(4,1)}), s8[3145728]{0:T(1024)(128)(4,1)S(1)}, s32[]{:S(2)}) async-start(s8[7340032]{0:T(1024)(128)(4,1)} %bitcast.2), calls=%async_computation.3 | async-start | bytes 6291456
  10.0 13.0 %slice-start.5 = ((s8[7340032]{0:T(1024)(128)(4,1)}), s8[3145728]{0:T(1024)(128)(4,1)S(1)}, s32[]{:S(2)}) async-start(s8[7340032]{0:T(1024)(128)(4,1)} %bitcast.4), calls=%async_computation.5 | async-start | bytes 6291456
  10.0 11.1 %collective-permute-start.15 = (bf16[4,18432]{1,0:T(4,128)(2,1)S(1)}, bf16[4,18432]{1,0:T(4,128)(2,1)S(1)}, u32[]{:S(2)}, u32[]{:S(2)}) collective-permute-start(bf16[4,18432]{1,0:T(4,128)(2,1)S(1)} %get-tuple-element.26.refs_4_), channel_id=1, source_target_pairs={{0,2},{1,3},{2,0},{3,1},{4,6},{5,7},{6,4},{7,5},{8,10},{9,11},{10,... | collective-permute-start | bytes 442376 | tf_op jit(solution)/shard_map/ppermute | solution.py:59
  12.7 7.4 %collective-permute-start.8 = (bf16[16,3712]{1,0:T(8,128)(2,1)S(1)}, bf16[16,3712]{1,0:T(8,128)(2,1)S(1)}, u32[]{:S(2)}, u32[]{:S(2)}) collective-permute-start(bf16[16,3712]{1,0:T(8,128)(2,1)S(1)} %shard_map.134.refs_0_), channel_id=1, source_target_pairs={{0,6},{1,7},{2,4},{3,5},{4,2},{5,3},{6,0},{7,1},{8,14},{9,15},{10,... | collective-permute-start | bytes 356360 | tf_op jit(solution)/shard_map/ppermute | solution.py:59
  15.2 5.8 %collective-permute-start.7 = (bf16[16,3712]{1,0:T(8,128)(2,1)S(1)}, bf16[16,3712]{1,0:T(8,128)(2,1)S(1)}, u32[]{:S(2)}, u32[]{:S(2)}) collective-permute-start(bf16[16,3712]{1,0:T(8,128)(2,1)S(1)} %shard_map.134.refs_0_), channel_id=1, source_target_pairs={{0,4},{1,5},{2,6},{3,7},{4,0},{5,1},{6,2},{7,3},{8,12},{9,13},{10,... | collective-permute-start | bytes 356360 | tf_op jit(solution)/shard_map/ppermute | solution.py:59
  15.7 5.3 %collective-permute-start.6 = (bf16[16,3712]{1,0:T(8,128)(2,1)S(1)}, bf16[16,3712]{1,0:T(8,128)(2,1)S(1)}, u32[]{:S(2)}, u32[]{:S(2)}) collective-permute-start(bf16[16,3712]{1,0:T(8,128)(2,1)S(1)} %shard_map.134.refs_0_), channel_id=1, source_target_pairs={{0,2},{1,3},{2,0},{3,1},{4,6},{5,7},{6,4},{7,5},{8,10},{9,11},{10,... | collective-permute-start | bytes 356360 | tf_op jit(solution)/shard_map/ppermute | solution.py:59
  16.2 5.0 %slice-start = ((s8[7340032]{0:T(1024)(128)(4,1)}), s8[4194304]{0:T(1024)(128)(4,1)S(1)}, s32[]{:S(2)}) async-start(s8[7340032]{0:T(1024)(128)(4,1)} %bitcast), calls=%async_computation | async-start | bytes 8388608
  16.3 4.9 %slice-start.1 = ((s8[7340032]{0:T(1024)(128)(4,1)}), s8[3145728]{0:T(1024)(128)(4,1)S(1)}, s32[]{:S(2)}) async-start(s8[7340032]{0:T(1024)(128)(4,1)} %bitcast), calls=%async_computation.1 | async-start | bytes 6291456
  21.0 1.9 %collective-permute-start.9 = (bf16[64,3712]{1,0:T(8,128)(2,1)S(1)}, bf16[64,3712]{1,0:T(8,128)(2,1)S(1)}, u32[]{:S(2)}, u32[]{:S(2)}) collective-permute-start(bf16[64,3712]{1,0:T(8,128)(2,1)S(1)} %shard_map.135.near_ref), channel_id=1, source_target_pairs={{0,1},{1,0},{2,3},{3,2},{4,5},{5,4},{6,7},{7,6},{8,9},{9,8},{10,11... | collective-permute-start | bytes 1425416 | tf_op jit(solution)/shard_map/ppermute | solution.py:59
  24.7 1.7 %collective-permute-start.10 = (bf16[32,3584]{1,0:T(8,128)(2,1)S(1)}, bf16[32,3584]{1,0:T(8,128)(2,1)S(1)}, u32[]{:S(2)}, u32[]{:S(2)}) collective-permute-start(bf16[32,3584]{1,0:T(8,128)(2,1)S(1)} %get-tuple-element.30), channel_id=1, source_target_pairs={{0,1},{1,0},{2,3},{3,2},{4,5},{5,4},{6,7},{7,6},{8,9},{9,8},{10,11... | collective-permute-start | bytes 688136 | tf_op jit(solution)/shard_map/ppermute | solution.py:59
  25.1 6.3 %collective-permute-start.16 = (bf16[4,18432]{1,0:T(4,128)(2,1)S(1)}, bf16[4,18432]{1,0:T(4,128)(2,1)S(1)}, u32[]{:S(2)}, u32[]{:S(2)}) collective-permute-start(bf16[4,18432]{1,0:T(4,128)(2,1)S(1)} %pad_maximum_fusion.1), channel_id=1, source_target_pairs={{0,1},{1,0},{2,3},{3,2},{4,5},{5,4},{6,7},{7,6},{8,9},{9,8},{10,11... | collective-permute-start | bytes 442376 | tf_op jit(solution)/shard_map/ppermute | solution.py:59
  26.2 1.6 %collective-permute-start.11 = (bf16[32,3584]{1,0:T(8,128)(2,1)S(1)}, bf16[32,3584]{1,0:T(8,128)(2,1)S(1)}, u32[]{:S(2)}, u32[]{:S(2)}) collective-permute-start(bf16[32,3584]{1,0:T(8,128)(2,1)S(1)} %get-tuple-element.33), channel_id=1, source_target_pairs={{0,1},{1,0},{2,3},{3,2},{4,5},{5,4},{6,7},{7,6},{8,9},{9,8},{10,11... | collective-permute-start | bytes 688136 | tf_op jit(solution)/shard_map/ppermute | solution.py:59
  26.4 5.2 %copy-start = (bf16[2,36864]{1,0:T(2,128)(2,1)S(1)}, bf16[2,36864]{1,0:T(2,128)(2,1)}, u32[]{:S(2)}) copy-start(bf16[2,36864]{1,0:T(2,128)(2,1)} %query_ref.1) | copy-start | bytes 442372
  26.4 5.2 %copy-start.1 = (s32[2,12]{1,0:T(2,128)S(1)}, s32[2,12]{1,0:T(2,128)}, u32[]{:S(2)}) copy-start(s32[2,12]{1,0:T(2,128)} %table_ref.1) | copy-start | bytes 292
  26.4 5.2 %copy-start.2 = (s32[2]{0:T(128)S(1)}, s32[2]{0:T(128)}, u32[]{:S(2)}) copy-start(s32[2]{0:T(128)} %length_ref.1) | copy-start | bytes 28
  27.8 6.6 %collective-permute-start.12 = (bf16[8,7168]{1,0:T(8,128)(2,1)S(1)}, bf16[8,7168]{1,0:T(8,128)(2,1)S(1)}, u32[]{:S(2)}, u32[]{:S(2)}) collective-permute-start(bf16[8,7168]{1,0:T(8,128)(2,1)S(1)} %get-tuple-element.35), channel_id=1, source_target_pairs={{0,6},{1,7},{2,4},{3,5},{4,2},{5,3},{6,0},{7,1},{8,14},{9,15},{10,... | collective-permute-start | bytes 344072 | tf_op jit(solution)/shard_map/ppermute | solution.py:59
  29.9 6.6 %collective-permute-start.13 = (bf16[8,7168]{1,0:T(8,128)(2,1)S(1)}, bf16[8,7168]{1,0:T(8,128)(2,1)S(1)}, u32[]{:S(2)}, u32[]{:S(2)}) collective-permute-start(bf16[8,7168]{1,0:T(8,128)(2,1)S(1)} %get-tuple-element.36), channel_id=1, source_target_pairs={{0,4},{1,5},{2,6},{3,7},{4,0},{5,1},{6,2},{7,3},{8,12},{9,13},{10,... | collective-permute-start | bytes 344072 | tf_op jit(solution)/shard_map/ppermute | solution.py:59
  30.4 6.0 %collective-permute-start.14 = (bf16[8,7168]{1,0:T(8,128)(2,1)S(1)}, bf16[8,7168]{1,0:T(8,128)(2,1)S(1)}, u32[]{:S(2)}, u32[]{:S(2)}) collective-permute-start(bf16[8,7168]{1,0:T(8,128)(2,1)S(1)} %get-tuple-element.37), channel_id=1, source_target_pairs={{0,2},{1,3},{2,0},{3,1},{4,6},{5,7},{6,4},{7,5},{8,10},{9,11},{10,... | collective-permute-start | bytes 344072 | tf_op jit(solution)/shard_map/ppermute | solution.py:59
  36.5 6.0 %collective-permute-start.17 = (bf16[2,7168]{1,0:T(2,128)(2,1)S(1)}, bf16[2,7168]{1,0:T(2,128)(2,1)S(1)}, u32[]{:S(2)}, u32[]{:S(2)}) collective-permute-start(bf16[2,7168]{1,0:T(2,128)(2,1)S(1)} %get-tuple-element.41), channel_id=1, source_target_pairs={{0,24},{1,25},{2,26},{3,27},{4,28},{5,29},{6,30},{7,31},{8,16},{9,... | collective-permute-start | bytes 86024 | tf_op jit(solution)/shard_map/ppermute | solution.py:59
  39.6 4.8 %collective-permute-start.18 = (bf16[2,7168]{1,0:T(2,128)(2,1)S(1)}, bf16[2,7168]{1,0:T(2,128)(2,1)S(1)}, u32[]{:S(2)}, u32[]{:S(2)}) collective-permute-start(bf16[2,7168]{1,0:T(2,128)(2,1)S(1)} %get-tuple-element.42), channel_id=1, source_target_pairs={{0,16},{1,17},{2,18},{3,19},{4,20},{5,21},{6,22},{7,23},{8,24},{9,... | collective-permute-start | bytes 86024 | tf_op jit(solution)/shard_map/ppermute | solution.py:59
  39.6 4.8 %collective-permute-start.19 = (bf16[2,7168]{1,0:T(2,128)(2,1)S(1)}, bf16[2,7168]{1,0:T(2,128)(2,1)S(1)}, u32[]{:S(2)}, u32[]{:S(2)}) collective-permute-start(bf16[2,7168]{1,0:T(2,128)(2,1)S(1)} %get-tuple-element.43), channel_id=1, source_target_pairs={{0,8},{1,9},{2,10},{3,11},{4,12},{5,13},{6,14},{7,15},{8,0},{9,1},... | collective-permute-start | bytes 86024 | tf_op jit(solution)/shard_map/ppermute | solution.py:59

commit v7 on v6

--- a/solution.py
+++ b/solution.py
@@ -64,8 +64,9 @@
     stages = [(bits[0],)] if len(bits) % 2 else []
     bits = bits[len(bits) % 2 :]
     for high, low in zip(bits[::2], bits[1::2]):
-        stages.append((low, high, high ^ low))
-    return stages
+        stages.append((high, high ^ low, low))
+    high, far, low = stages[-1]
+    return stages[:-1] + [(far, high, low)]
 
 
 def pairs_of(count, bit):
@@ -344,18 +345,42 @@
     )(hbm(moved_page), hbm(moved_dest), hbm(latent_pool), after)
 
 
-def exchange_pages(low, high, dp_count):
-    blocks, senders = [low], [0]
+def rows_kernel(places, *refs):
+    out_ref = refs[-1]
+    width = out_ref.shape[1]
+    step = 2048
+    for i in range(width // step):
+        columns = slice(i * step, (i + 1) * step)
+        pieces = [ref[:, columns].astype(f32)[low:high] for ref, (low, high) in zip(refs, places)]
+        out_ref[:, columns] = jnp.concatenate(pieces, axis=0).astype(bf16)
+
+
+def rows_of(pieces, *after):
+    rows = sum(high - low for _, low, high in pieces)
+    width = pieces[0][0].shape[1]
+    return pl.pallas_call(
+        functools.partial(rows_kernel, [(low, high) for _, low, high in pieces]),
+        out_shape=pltpu.VMEM((rows, width), bf16),
+        in_specs=[in_vmem()] * len(pieces) + [anywhere()] * len(after),
+        out_specs=in_vmem(),
+        compiler_params=pltpu.CompilerParams(vmem_limit_bytes=4 * MIB),
+        cost_estimate=pl.CostEstimate(flops=0, bytes_accessed=4 * rows * width, transcendentals=0),
+    )(*[vmem(x) for x, _, _ in pieces], *after)
+
+
+def exchange_pages(low, high, dp_count, after):
+    blocks, senders = [(low, 0, low.shape[0])], [0]
     sent = high
     for bit in partner_bits(dp_count):
         got = swap(sent, "dp", pairs_of(dp_count, bit))
         size = got.shape[0] // len(blocks)
-        blocks = blocks + [got[i * size : (i + 1) * size] for i in range(len(blocks))]
+        blocks = blocks + [(got, i * size, (i + 1) * size) for i in range(len(blocks))]
         senders = senders + [s ^ bit for s in senders]
         if size > MCAP:
-            sent = jnp.concatenate([b[size // 2 :] for b in blocks], axis=0)
-            blocks = [b[: size // 2] for b in blocks]
-    return jnp.concatenate(blocks, axis=0), senders
+            sent = rows_of([(x, start + size // 2, end) for x, start, end in blocks], after)
+            after = sent
+            blocks = [(x, start, start + size // 2) for x, start, _ in blocks]
+    return rows_of(blocks), senders, after
 
 
 def attend_kernel(senders, length_ref, table_ref, query_ref, pool_ref, arrived_ref, out_ref, query_rows):
@@ -475,8 +500,10 @@
         if number == 0:
             low, high, pool = pick_pages(moved_page, moved_dest, latent_pool, near, dp_count)
             after = [high]
+        if number == len(stages) - 1:
+            arrived, senders, sent = exchange_pages(low, high, dp_count, got[0])
+            after = [sent]
         near = merge([near] + got, MERGE_FLOPS if number < len(stages) - 1 else MERGE_FLOPS // 4, *after)
-    arrived, senders = exchange_pages(low, high, dp_count)
     far = trade(near, 1)
     gate_acc, up_acc = near_products(near, gate_weight, up_weight)
     inner, keep_a, send_a = far_products(
@@ -491,7 +518,7 @@
     after = []
     for number, partners in enumerate(reversed(stages)):
         keep, *send = fold(held, len(partners) + 1, *(after if number == 1 else []))
-        held = [(keep, [trade(x, bit) for x, bit in list(zip(send, partners))[::-1]])]
+        held = [(keep, [trade(x, bit) for x, bit in zip(send, partners)])]
         after = [hbm(attended)]
     (expert_mix,) = fold(held, 1, out=jax.ShapeDtypeStruct(hidden.shape, bf16))
     return expert_mix, attended

time: 45.2 us -> 46.9 us (1.038)
  local copies, waits for them, and re-layouts: 0.26 us -> 2.63 us
  starting transfers between devices: 20.8 us -> 19.9 us
    unnamed x18, local copies, waits for them, and re-layouts: 0.05 us -> 2.63 us
    ppermute x20, starting transfers between devices: 20.8 us -> 19.9 us  [swap(): return lax.ppermute(x, axes, pairs)]
  transfers between devices with their start and end apart: 20 -> 20, of which waited for: 10 -> 10; matrix products, arithmetic and copies ran while one was open for 1% -> 0% of each run, Pallas kernels for 15% -> 15%
where the time goes in v7:
time: 46.9 us; the launch traced here: 46.7 us
  starting transfers between devices  19.9 us (42%)
  waiting for transfers between devices  13.7 us (29%)
  Pallas kernels  9.62 us (21%)
  local copies, waits for them, and re-layouts  2.63 us (6%)
  between operations  0.84 us (2%)
    ppermute x20, starting transfers between devices, swap(): return lax.ppermute(x, axes, pairs)  19.9 us
    ppermute x20, waiting for transfers between devices, swap(): return lax.ppermute(x, axes, pairs)  13.7 us
    unnamed x18, local copies, waits for them, and re-layouts  2.63 us
    pallas_call x1, Pallas kernels, attend(): pl.pallas_call(functools.partial(attend_kernel, senders), out_shape=jax.S...  2.37 us
    pallas_call x1, Pallas kernels, far_products(): pl.pallas_call(functools.partial(far_kernel, ep_count), out_shape=(pltpu....  1.75 us
    pallas_call x1, Pallas kernels, pick_pages(): pl.pallas_call(functools.partial(pages_kernel, dp_count), out_shape=(half...  1.49 us
    pallas_call x1, Pallas kernels, near_products(): pl.pallas_call(near_kernel, out_shape=(acc, acc), in_specs=[in_vmem()] *...  1.11 us
  transfers between devices with their start and end apart: 20, of which 10 were waited for; matrix products, arithmetic and copies ran while one was open for 0% of the time, Pallas kernels for 15%

profile of v7, /device:TPU:0, one launch (start us, length us, event | category | flops | bytes accessed | tf_op | source)
XLA Modules:
  0.0 46.7 jit_solution(3494368411000807704)
XLA Ops:
  0.6 0.5 %collective-permute-start = (bf16[2,7168]{1,0:T(2,128)(2,1)}, bf16[2,7168]{1,0:T(2,128)(2,1)S(1)}, u32[]{:S(2)}, u32[]{:S(2)}) collective-permute-start(bf16[2,7168]{1,0:T(2,128)(2,1)} %refs_0_.1), channel_id=1, source_target_pairs={{0,1},{1,0},{2,3},{3,2},{4,5},{5,4},{6,7},{7,6},{8,9},{9,8},{10,11... | collective-permute-start | bytes 86024 | tf_op jit(solution)/shard_map/ppermute | solution.py:59
  1.2 0.4 collective-permute-start.2
  1.7 0.9 %shard_map.131 = (bf16[2,7168]{1,0:T(2,128)(2,1)S(1)}, s32[2,4]{1,0:T(2,128)S(1)}, f32[2,4]{1,0:T(2,128)S(1)}) custom-call(bf16[2,7168]{1,0:T(2,128)(2,1)} %refs_0_.1, s32[2,4]{1,0:T(2,128)} %refs_1_.1, f32[2,4]{1,0:T(2,128)} %refs_2_.1), custom_call_target="tpu_custom_call" | custom-call | flops 1250000000 | bytes 1048576 | tf_op jit(solution)/shard_map/pallas_call | solution.py:86
  2.8 4.0 %collective-permute-start.3 = (bf16[4,3712]{1,0:T(4,128)(2,1)S(1)}, bf16[4,3712]{1,0:T(4,128)(2,1)S(1)}, u32[]{:S(2)}, u32[]{:S(2)}) collective-permute-start(bf16[4,3712]{1,0:T(4,128)(2,1)S(1)} %shard_map.132.after_ref.refs_0_), channel_id=1, source_target_pairs={{0,16},{1,17},{2,18},{3,19},{4,20},{5,21},{6,22},{7,23},{8,24},{9,... | collective-permute-start | bytes 89096 | tf_op jit(solution)/shard_map/ppermute | solution.py:59
  6.8 1.3 %collective-permute-start.4 = (bf16[4,3712]{1,0:T(4,128)(2,1)S(1)}, bf16[4,3712]{1,0:T(4,128)(2,1)S(1)}, u32[]{:S(2)}, u32[]{:S(2)}) collective-permute-start(bf16[4,3712]{1,0:T(4,128)(2,1)S(1)} %shard_map.132.after_ref.refs_0_), channel_id=1, source_target_pairs={{0,24},{1,25},{2,26},{3,27},{4,28},{5,29},{6,30},{7,31},{8,16},{9,... | collective-permute-start | bytes 89096 | tf_op jit(solution)/shard_map/ppermute | solution.py:59
  8.1 0.2 collective-permute-start.5
  8.3 1.5 %shard_map.133 = (bf16[4,18432]{1,0:T(4,128)(2,1)S(1)}, bf16[4,18432]{1,0:T(4,128)(2,1)S(1)}, bf16[24,18432]{1,0:T(8,128)(2,1)S(1)}) custom-call(s32[1,6]{1,0:T(1,128)} %page_hbm.1, s32[1,6]{1,0:T(1,128)} %dest_hbm.1, bf16[24,18432]{1,0:T(8,128)(2,1)} %pool_ref.1, bf16[4,3712]{1,0:T(4,128)(2,1)S(1)} %shard_map.132.after_ref.refs_0_), custom_call_target="tpu_custom_call" | custom-call | bytes 1769472 | tf_op jit(solution)/shard_map/pallas_call | solution.py:333
  9.9 1.6 %collective-permute-start.9 = (bf16[4,18432]{1,0:T(4,128)(2,1)S(1)}, bf16[4,18432]{1,0:T(4,128)(2,1)S(1)}, u32[]{:S(2)}, u32[]{:S(2)}) collective-permute-start(bf16[4,18432]{1,0:T(4,128)(2,1)S(1)} %get-tuple-element.26.refs_4_), channel_id=1, source_target_pairs={{0,2},{1,3},{2,0},{3,1},{4,6},{5,7},{6,4},{7,5},{8,10},{9,11},{10,... | collective-permute-start | bytes 442376 | tf_op jit(solution)/shard_map/ppermute | solution.py:59
  11.4 1.0 %collective-permute-done.4.refs_2_ = bf16[4,3712]{1,0:T(4,128)(2,1)S(1)} collective-permute-done((bf16[4,3712]{1,0:T(4,128)(2,1)S(1)}, bf16[4,3712]{1,0:T(4,128)(2,1)S(1)}, u32[]{:S(2)}, u32[]{:S(2)}) %collective-permute-start.4) | collective-permute-done | bytes 29728 | tf_op jit(solution)/shard_map/ppermute | solution.py:59
  12.5 2.5 %collective-permute-start.6 = (bf16[16,3712]{1,0:T(8,128)(2,1)S(1)}, bf16[16,3712]{1,0:T(8,128)(2,1)S(1)}, u32[]{:S(2)}, u32[]{:S(2)}) collective-permute-start(bf16[16,3712]{1,0:T(8,128)(2,1)S(1)} %shard_map.134.refs_0_), channel_id=1, source_target_pairs={{0,6},{1,7},{2,4},{3,5},{4,2},{5,3},{6,0},{7,1},{8,14},{9,15},{10,... | collective-permute-start | bytes 356360 | tf_op jit(solution)/shard_map/ppermute | solution.py:59
  15.0 0.5 %collective-permute-start.7 = (bf16[16,3712]{1,0:T(8,128)(2,1)S(1)}, bf16[16,3712]{1,0:T(8,128)(2,1)S(1)}, u32[]{:S(2)}, u32[]{:S(2)}) collective-permute-start(bf16[16,3712]{1,0:T(8,128)(2,1)S(1)} %shard_map.134.refs_0_), channel_id=1, source_target_pairs={{0,4},{1,5},{2,6},{3,7},{4,0},{5,1},{6,2},{7,3},{8,12},{9,13},{10,... | collective-permute-start | bytes 356360 | tf_op jit(solution)/shard_map/ppermute | solution.py:59
  15.5 0.5 %collective-permute-start.8 = (bf16[16,3712]{1,0:T(8,128)(2,1)S(1)}, bf16[16,3712]{1,0:T(8,128)(2,1)S(1)}, u32[]{:S(2)}, u32[]{:S(2)}) collective-permute-start(bf16[16,3712]{1,0:T(8,128)(2,1)S(1)} %shard_map.134.refs_0_), channel_id=1, source_target_pairs={{0,2},{1,3},{2,0},{3,1},{4,6},{5,7},{6,4},{7,5},{8,10},{9,11},{10,... | collective-permute-start | bytes 356360 | tf_op jit(solution)/shard_map/ppermute | solution.py:59
  16.1 4.1 %collective-permute-done.6.refs_2_.refs_1_ = bf16[16,3712]{1,0:T(8,128)(2,1)S(1)} collective-permute-done((bf16[16,3712]{1,0:T(8,128)(2,1)S(1)}, bf16[16,3712]{1,0:T(8,128)(2,1)S(1)}, u32[]{:S(2)}, u32[]{:S(2)}) %collective-permute-start.6) | collective-permute-done | bytes 118816 | tf_op jit(solution)/shard_map/ppermute | solution.py:59
  20.3 0.3 collective-permute-done.7.refs_2_
  20.8 1.6 %slice-done = s8[4194304]{0:T(1024)(128)(4,1)S(1)} async-done(((s8[7340032]{0:T(1024)(128)(4,1)}), s8[4194304]{0:T(1024)(128)(4,1)S(1)}, s32[]{:S(2)}) %slice-start) | async-done | bytes 4194328
  22.4 1.0 %slice-done.1 = s8[3145728]{0:T(1024)(128)(4,1)S(1)} async-done(((s8[7340032]{0:T(1024)(128)(4,1)}), s8[3145728]{0:T(1024)(128)(4,1)S(1)}, s32[]{:S(2)}) %slice-start.1) | async-done | bytes 3145752
  23.4 1.1 %shard_map.137 = (f32[64,512]{1,0:T(8,128)S(1)}, f32[64,512]{1,0:T(8,128)S(1)}) custom-call(bf16[64,3712]{1,0:T(8,128)(2,1)S(1)} %shard_map.136.near_ref, bf16[1,7168,512]{2,1,0:T(8,128)(2,1)S(1)} %bitcast.1, bf16[1,7168,512]{2,1,0:T(8,128)(2,1)S(1)} %bitcast.3), custom_call_target="tpu_custom_call" | custom-call | flops 469762048 | bytes 7340032 | tf_op jit(solution)/shard_map/pallas_call | solution.py:222
  24.6 1.8 %shard_map.138 = (bf16[64,512]{1,0:T(8,128)(2,1)S(1)}, f32[32,3584]{1,0:T(8,128)S(1)}, bf16[32,3584]{1,0:T(8,128)(2,1)S(1)}) custom-call(bf16[64,3712]{1,0:T(8,128)(2,1)S(1)} %shard_map.136.near_ref, bf16[64,3712]{1,0:T(8,128)(2,1)S(1)} %collective-permute-done.10.far_ref, bf16[1,7168,512]{2,1,0:T(8,128)(2,1)S(1)} %bitcast.1, ...), custom_call_target="tpu_custom_call" | custom-call | flops 704643072 | bytes 11010048 | tf_op jit(solution)/shard_map/pallas_call | solution.py:236
  26.4 0.5 %collective-permute-start.16 = (bf16[4,18432]{1,0:T(4,128)(2,1)S(1)}, bf16[4,18432]{1,0:T(4,128)(2,1)S(1)}, u32[]{:S(2)}, u32[]{:S(2)}) collective-permute-start(bf16[4,18432]{1,0:T(4,128)(2,1)S(1)} %shard_map.135.refs_4_), channel_id=1, source_target_pairs={{0,1},{1,0},{2,3},{3,2},{4,5},{5,4},{6,7},{7,6},{8,9},{9,8},{10,11... | collective-permute-start | bytes 442376 | tf_op jit(solution)/shard_map/ppermute | solution.py:59
  26.9 0.7 %shard_map.140 = (f32[32,3584]{1,0:T(8,128)S(1)}, bf16[32,3584]{1,0:T(8,128)(2,1)S(1)}) custom-call(bf16[64,3712]{1,0:T(8,128)(2,1)S(1)} %shard_map.136.near_ref, bf16[64,512]{1,0:T(8,128)(2,1)S(1)} %get-tuple-element.32.inner_ref, bf16[1,512,7168]{2,1,0:T(8,128)(2,1)S(1)} %bitcast.5), custom_call_target="tpu_custom_call" | custom-call | flops 234881024 | bytes 3670016 | tf_op jit(solution)/shard_map/pallas_call | solution.py:254
  27.9 1.2 %collective-permute-done.12.refs_2_ = bf16[32,3584]{1,0:T(8,128)(2,1)S(1)} collective-permute-done((bf16[32,3584]{1,0:T(8,128)(2,1)S(1)}, bf16[32,3584]{1,0:T(8,128)(2,1)S(1)}, u32[]{:S(2)}, u32[]{:S(2)}) %collective-permute-start.12) | collective-permute-done | bytes 229408 | tf_op jit(solution)/shard_map/ppermute | solution.py:59
  29.2 1.5 %collective-permute-start.13 = (bf16[8,7168]{1,0:T(8,128)(2,1)S(1)}, bf16[8,7168]{1,0:T(8,128)(2,1)S(1)}, u32[]{:S(2)}, u32[]{:S(2)}) collective-permute-start(bf16[8,7168]{1,0:T(8,128)(2,1)S(1)} %get-tuple-element.36), channel_id=1, source_target_pairs={{0,6},{1,7},{2,4},{3,5},{4,2},{5,3},{6,0},{7,1},{8,14},{9,15},{10,... | collective-permute-start | bytes 344072 | tf_op jit(solution)/shard_map/ppermute | solution.py:59
  30.7 1.5 %collective-permute-start.14 = (bf16[8,7168]{1,0:T(8,128)(2,1)S(1)}, bf16[8,7168]{1,0:T(8,128)(2,1)S(1)}, u32[]{:S(2)}, u32[]{:S(2)}) collective-permute-start(bf16[8,7168]{1,0:T(8,128)(2,1)S(1)} %get-tuple-element.37), channel_id=1, source_target_pairs={{0,4},{1,5},{2,6},{3,7},{4,0},{5,1},{6,2},{7,3},{8,12},{9,13},{10,... | collective-permute-start | bytes 344072 | tf_op jit(solution)/shard_map/ppermute | solution.py:59
  32.2 0.6 %collective-permute-start.15 = (bf16[8,7168]{1,0:T(8,128)(2,1)S(1)}, bf16[8,7168]{1,0:T(8,128)(2,1)S(1)}, u32[]{:S(2)}, u32[]{:S(2)}) collective-permute-start(bf16[8,7168]{1,0:T(8,128)(2,1)S(1)} %get-tuple-element.38), channel_id=1, source_target_pairs={{0,2},{1,3},{2,0},{3,1},{4,6},{5,7},{6,4},{7,5},{8,10},{9,11},{10,... | collective-permute-start | bytes 344072 | tf_op jit(solution)/shard_map/ppermute | solution.py:59
  33.0 2.4 %shard_map.143.refs_4_ = bf16[2,32768]{1,0:T(2,128)(2,1)} custom-call(s32[2]{0:T(128)S(1)} %copy-done.2, s32[2,12]{1,0:T(2,128)S(1)} %copy-done.1, bf16[2,36864]{1,0:T(2,128)(2,1)S(1)} %copy-done, bf16[24,18432]{1,0:T(8,128)(2,1)S(1)} %get-tuple-element.39.pool_ref, bf16[8,18432]{1,0:T(8,128)(2,1)S(1)} %shard_map.142.arrived_ref), custom_call_target="tpu_custom_call" | custom-call | flops 1073741824 | bytes 4194304 | tf_op jit(solution)/shard_map/pallas_call | solution.py:461
  35.3 0.8 %collective-permute-done.13.refs_1_ = bf16[8,7168]{1,0:T(8,128)(2,1)S(1)} collective-permute-done((bf16[8,7168]{1,0:T(8,128)(2,1)S(1)}, bf16[8,7168]{1,0:T(8,128)(2,1)S(1)}, u32[]{:S(2)}, u32[]{:S(2)}) %collective-permute-start.13) | collective-permute-done | bytes 114720 | tf_op jit(solution)/shard_map/ppermute | solution.py:59
  36.1 1.7 %collective-permute-done.14.refs_2_ = bf16[8,7168]{1,0:T(8,128)(2,1)S(1)} collective-permute-done((bf16[8,7168]{1,0:T(8,128)(2,1)S(1)}, bf16[8,7168]{1,0:T(8,128)(2,1)S(1)}, u32[]{:S(2)}, u32[]{:S(2)}) %collective-permute-start.14) | collective-permute-done | bytes 114720 | tf_op jit(solution)/shard_map/ppermute | solution.py:59
  37.9 2.5 %collective-permute-start.17 = (bf16[2,7168]{1,0:T(2,128)(2,1)S(1)}, bf16[2,7168]{1,0:T(2,128)(2,1)S(1)}, u32[]{:S(2)}, u32[]{:S(2)}) collective-permute-start(bf16[2,7168]{1,0:T(2,128)(2,1)S(1)} %get-tuple-element.41), channel_id=1, source_target_pairs={{0,16},{1,17},{2,18},{3,19},{4,20},{5,21},{6,22},{7,23},{8,24},{9,... | collective-permute-start | bytes 86024 | tf_op jit(solution)/shard_map/ppermute | solution.py:59
  40.4 1.4 %collective-permute-start.18 = (bf16[2,7168]{1,0:T(2,128)(2,1)S(1)}, bf16[2,7168]{1,0:T(2,128)(2,1)S(1)}, u32[]{:S(2)}, u32[]{:S(2)}) collective-permute-start(bf16[2,7168]{1,0:T(2,128)(2,1)S(1)} %get-tuple-element.42), channel_id=1, source_target_pairs={{0,24},{1,25},{2,26},{3,27},{4,28},{5,29},{6,30},{7,31},{8,16},{9,... | collective-permute-start | bytes 86024 | tf_op jit(solution)/shard_map/ppermute | solution.py:59
  41.8 1.2 %collective-permute-done.17.refs_1_ = bf16[2,7168]{1,0:T(2,128)(2,1)S(1)} collective-permute-done((bf16[2,7168]{1,0:T(2,128)(2,1)S(1)}, bf16[2,7168]{1,0:T(2,128)(2,1)S(1)}, u32[]{:S(2)}, u32[]{:S(2)}) %collective-permute-start.17) | collective-permute-done | bytes 28704 | tf_op jit(solution)/shard_map/ppermute | solution.py:59
  43.0 3.1 %collective-permute-done.18.refs_2_ = bf16[2,7168]{1,0:T(2,128)(2,1)S(1)} collective-permute-done((bf16[2,7168]{1,0:T(2,128)(2,1)S(1)}, bf16[2,7168]{1,0:T(2,128)(2,1)S(1)}, u32[]{:S(2)}, u32[]{:S(2)}) %collective-permute-start.18) | collective-permute-done | bytes 28704 | tf_op jit(solution)/shard_map/ppermute | solution.py:59
  46.1 0.7 %shard_map.145 = bf16[2,7168]{1,0:T(2,128)(2,1)} custom-call(f32[2,7168]{1,0:T(2,128)S(1)} %get-tuple-element.40.refs_0_, bf16[2,7168]{1,0:T(2,128)(2,1)S(1)} %collective-permute-done.17.refs_1_, bf16[2,7168]{1,0:T(2,128)(2,1)S(1)} %collective-permute-done.18.refs_2_, bf16[2,7168]{1,0:T(2,128)(2,1)S(1)} %collective-permute-done.19.refs_3_), custom_call_target="tpu_custom_call" | custom-call | bytes 114688 | tf_op jit(solution)/shard_map/pallas_call | solution.py:286
  (44 shorter events, 1.3 us)
Async XLA Ops:
  0.6 2.1 %collective-permute-start = (bf16[2,7168]{1,0:T(2,128)(2,1)}, bf16[2,7168]{1,0:T(2,128)(2,1)S(1)}, u32[]{:S(2)}, u32[]{:S(2)}) collective-permute-start(bf16[2,7168]{1,0:T(2,128)(2,1)} %refs_0_.1), channel_id=1, source_target_pairs={{0,1},{1,0},{2,3},{3,2},{4,5},{5,4},{6,7},{7,6},{8,9},{9,8},{10,11... | collective-permute-start | bytes 86024 | tf_op jit(solution)/shard_map/ppermute | solution.py:59
  1.1 1.4 %collective-permute-start.1 = (s32[2,4]{1,0:T(2,128)}, s32[2,4]{1,0:T(2,128)S(1)}, u32[]{:S(2)}, u32[]{:S(2)}) collective-permute-start(s32[2,4]{1,0:T(2,128)} %refs_1_.1), channel_id=1, source_target_pairs={{0,1},{1,0},{2,3},{3,2},{4,5},{5,4},{6,7},{7,6},{8,9},{9,8},{10,11... | collective-permute-start | bytes 104 | tf_op jit(solution)/shard_map/ppermute | solution.py:59
  1.2 1.5 %collective-permute-start.2 = (f32[2,4]{1,0:T(2,128)}, f32[2,4]{1,0:T(2,128)S(1)}, u32[]{:S(2)}, u32[]{:S(2)}) collective-permute-start(f32[2,4]{1,0:T(2,128)} %refs_2_.1), channel_id=1, source_target_pairs={{0,1},{1,0},{2,3},{3,2},{4,5},{5,4},{6,7},{7,6},{8,9},{9,8},{10,11... | collective-permute-start | bytes 104 | tf_op jit(solution)/shard_map/ppermute | solution.py:59
  1.7 22.9 %slice-start.4 = ((s8[7340032]{0:T(1024)(128)(4,1)}), s8[4194304]{0:T(1024)(128)(4,1)S(1)}, s32[]{:S(2)}) async-start(s8[7340032]{0:T(1024)(128)(4,1)} %bitcast.4), calls=%async_computation.4 | async-start | bytes 8388608
  2.7 18.1 %slice-start.2 = ((s8[7340032]{0:T(1024)(128)(4,1)}), s8[4194304]{0:T(1024)(128)(4,1)S(1)}, s32[]{:S(2)}) async-start(s8[7340032]{0:T(1024)(128)(4,1)} %bitcast.2), calls=%async_computation.2 | async-start | bytes 8388608
  2.8 8.6 %collective-permute-start.3 = (bf16[4,3712]{1,0:T(4,128)(2,1)S(1)}, bf16[4,3712]{1,0:T(4,128)(2,1)S(1)}, u32[]{:S(2)}, u32[]{:S(2)}) collective-permute-start(bf16[4,3712]{1,0:T(4,128)(2,1)S(1)} %shard_map.132.after_ref.refs_0_), channel_id=1, source_target_pairs={{0,16},{1,17},{2,18},{3,19},{4,20},{5,21},{6,22},{7,23},{8,24},{9,... | collective-permute-start | bytes 89096 | tf_op jit(solution)/shard_map/ppermute | solution.py:59
  6.8 5.7 %collective-permute-start.4 = (bf16[4,3712]{1,0:T(4,128)(2,1)S(1)}, bf16[4,3712]{1,0:T(4,128)(2,1)S(1)}, u32[]{:S(2)}, u32[]{:S(2)}) collective-permute-start(bf16[4,3712]{1,0:T(4,128)(2,1)S(1)} %shard_map.132.after_ref.refs_0_), channel_id=1, source_target_pairs={{0,24},{1,25},{2,26},{3,27},{4,28},{5,29},{6,30},{7,31},{8,16},{9,... | collective-permute-start | bytes 89096 | tf_op jit(solution)/shard_map/ppermute | solution.py:59
  8.1 4.3 %collective-permute-start.5 = (bf16[4,3712]{1,0:T(4,128)(2,1)S(1)}, bf16[4,3712]{1,0:T(4,128)(2,1)S(1)}, u32[]{:S(2)}, u32[]{:S(2)}) collective-permute-start(bf16[4,3712]{1,0:T(4,128)(2,1)S(1)} %shard_map.132.after_ref.refs_0_), channel_id=1, source_target_pairs={{0,8},{1,9},{2,10},{3,11},{4,12},{5,13},{6,14},{7,15},{8,0},{9,1},... | collective-permute-start | bytes 89096 | tf_op jit(solution)/shard_map/ppermute | solution.py:59
  9.8 11.0 %slice-start.3 = ((s8[7340032]{0:T(1024)(128)(4,1)}), s8[3145728]{0:T(1024)(128)(4,1)S(1)}, s32[]{:S(2)}) async-start(s8[7340032]{0:T(1024)(128)(4,1)} %bitcast.2), calls=%async_computation.3 | async-start | bytes 6291456
  9.9 14.7 %slice-start.5 = ((s8[7340032]{0:T(1024)(128)(4,1)}), s8[3145728]{0:T(1024)(128)(4,1)S(1)}, s32[]{:S(2)}) async-start(s8[7340032]{0:T(1024)(128)(4,1)} %bitcast.4), calls=%async_computation.5 | async-start | bytes 6291456
  9.9 6.2 %collective-permute-start.9 = (bf16[4,18432]{1,0:T(4,128)(2,1)S(1)}, bf16[4,18432]{1,0:T(4,128)(2,1)S(1)}, u32[]{:S(2)}, u32[]{:S(2)}) collective-permute-start(bf16[4,18432]{1,0:T(4,128)(2,1)S(1)} %get-tuple-element.26.refs_4_), channel_id=1, source_target_pairs={{0,2},{1,3},{2,0},{3,1},{4,6},{5,7},{6,4},{7,5},{8,10},{9,11},{10,... | collective-permute-start | bytes 442376 | tf_op jit(solution)/shard_map/ppermute | solution.py:59
  12.5 7.7 %collective-permute-start.6 = (bf16[16,3712]{1,0:T(8,128)(2,1)S(1)}, bf16[16,3712]{1,0:T(8,128)(2,1)S(1)}, u32[]{:S(2)}, u32[]{:S(2)}) collective-permute-start(bf16[16,3712]{1,0:T(8,128)(2,1)S(1)} %shard_map.134.refs_0_), channel_id=1, source_target_pairs={{0,6},{1,7},{2,4},{3,5},{4,2},{5,3},{6,0},{7,1},{8,14},{9,15},{10,... | collective-permute-start | bytes 356360 | tf_op jit(solution)/shard_map/ppermute | solution.py:59
  15.0 5.6 %collective-permute-start.7 = (bf16[16,3712]{1,0:T(8,128)(2,1)S(1)}, bf16[16,3712]{1,0:T(8,128)(2,1)S(1)}, u32[]{:S(2)}, u32[]{:S(2)}) collective-permute-start(bf16[16,3712]{1,0:T(8,128)(2,1)S(1)} %shard_map.134.refs_0_), channel_id=1, source_target_pairs={{0,4},{1,5},{2,6},{3,7},{4,0},{5,1},{6,2},{7,3},{8,12},{9,13},{10,... | collective-permute-start | bytes 356360 | tf_op jit(solution)/shard_map/ppermute | solution.py:59
  15.5 5.1 %collective-permute-start.8 = (bf16[16,3712]{1,0:T(8,128)(2,1)S(1)}, bf16[16,3712]{1,0:T(8,128)(2,1)S(1)}, u32[]{:S(2)}, u32[]{:S(2)}) collective-permute-start(bf16[16,3712]{1,0:T(8,128)(2,1)S(1)} %shard_map.134.refs_0_), channel_id=1, source_target_pairs={{0,2},{1,3},{2,0},{3,1},{4,6},{5,7},{6,4},{7,5},{8,10},{9,11},{10,... | collective-permute-start | bytes 356360 | tf_op jit(solution)/shard_map/ppermute | solution.py:59
  20.2 2.2 %slice-start = ((s8[7340032]{0:T(1024)(128)(4,1)}), s8[4194304]{0:T(1024)(128)(4,1)S(1)}, s32[]{:S(2)}) async-start(s8[7340032]{0:T(1024)(128)(4,1)} %bitcast), calls=%async_computation | async-start | bytes 8388608
  20.3 3.1 %slice-start.1 = ((s8[7340032]{0:T(1024)(128)(4,1)}), s8[3145728]{0:T(1024)(128)(4,1)S(1)}, s32[]{:S(2)}) async-start(s8[7340032]{0:T(1024)(128)(4,1)} %bitcast), calls=%async_computation.1 | async-start | bytes 6291456
  20.7 3.8 %collective-permute-start.10 = (bf16[64,3712]{1,0:T(8,128)(2,1)S(1)}, bf16[64,3712]{1,0:T(8,128)(2,1)S(1)}, u32[]{:S(2)}, u32[]{:S(2)}) collective-permute-start(bf16[64,3712]{1,0:T(8,128)(2,1)S(1)} %shard_map.136.near_ref), channel_id=1, source_target_pairs={{0,1},{1,0},{2,3},{3,2},{4,5},{5,4},{6,7},{7,6},{8,9},{9,8},{10,11... | collective-permute-start | bytes 1425416 | tf_op jit(solution)/shard_map/ppermute | solution.py:59
  26.3 1.6 %collective-permute-start.11 = (bf16[32,3584]{1,0:T(8,128)(2,1)S(1)}, bf16[32,3584]{1,0:T(8,128)(2,1)S(1)}, u32[]{:S(2)}, u32[]{:S(2)}) collective-permute-start(bf16[32,3584]{1,0:T(8,128)(2,1)S(1)} %get-tuple-element.31), channel_id=1, source_target_pairs={{0,1},{1,0},{2,3},{3,2},{4,5},{5,4},{6,7},{7,6},{8,9},{9,8},{10,11... | collective-permute-start | bytes 688136 | tf_op jit(solution)/shard_map/ppermute | solution.py:59
  26.4 6.4 %collective-permute-start.16 = (bf16[4,18432]{1,0:T(4,128)(2,1)S(1)}, bf16[4,18432]{1,0:T(4,128)(2,1)S(1)}, u32[]{:S(2)}, u32[]{:S(2)}) collective-permute-start(bf16[4,18432]{1,0:T(4,128)(2,1)S(1)} %shard_map.135.refs_4_), channel_id=1, source_target_pairs={{0,1},{1,0},{2,3},{3,2},{4,5},{5,4},{6,7},{7,6},{8,9},{9,8},{10,11... | collective-permute-start | bytes 442376 | tf_op jit(solution)/shard_map/ppermute | solution.py:59
  27.6 1.6 %collective-permute-start.12 = (bf16[32,3584]{1,0:T(8,128)(2,1)S(1)}, bf16[32,3584]{1,0:T(8,128)(2,1)S(1)}, u32[]{:S(2)}, u32[]{:S(2)}) collective-permute-start(bf16[32,3584]{1,0:T(8,128)(2,1)S(1)} %get-tuple-element.34), channel_id=1, source_target_pairs={{0,1},{1,0},{2,3},{3,2},{4,5},{5,4},{6,7},{7,6},{8,9},{9,8},{10,11... | collective-permute-start | bytes 688136 | tf_op jit(solution)/shard_map/ppermute | solution.py:59
  27.9 5.1 %copy-start = (bf16[2,36864]{1,0:T(2,128)(2,1)S(1)}, bf16[2,36864]{1,0:T(2,128)(2,1)}, u32[]{:S(2)}) copy-start(bf16[2,36864]{1,0:T(2,128)(2,1)} %query_ref.1) | copy-start | bytes 442372
  27.9 5.1 %copy-start.1 = (s32[2,12]{1,0:T(2,128)S(1)}, s32[2,12]{1,0:T(2,128)}, u32[]{:S(2)}) copy-start(s32[2,12]{1,0:T(2,128)} %table_ref.1) | copy-start | bytes 292
  27.9 5.1 %copy-start.2 = (s32[2]{0:T(128)S(1)}, s32[2]{0:T(128)}, u32[]{:S(2)}) copy-start(s32[2]{0:T(128)} %length_ref.1) | copy-start | bytes 28
  29.2 7.0 %collective-permute-start.13 = (bf16[8,7168]{1,0:T(8,128)(2,1)S(1)}, bf16[8,7168]{1,0:T(8,128)(2,1)S(1)}, u32[]{:S(2)}, u32[]{:S(2)}) collective-permute-start(bf16[8,7168]{1,0:T(8,128)(2,1)S(1)} %get-tuple-element.36), channel_id=1, source_target_pairs={{0,6},{1,7},{2,4},{3,5},{4,2},{5,3},{6,0},{7,1},{8,14},{9,15},{10,... | collective-permute-start | bytes 344072 | tf_op jit(solution)/shard_map/ppermute | solution.py:59
  30.7 7.1 %collective-permute-start.14 = (bf16[8,7168]{1,0:T(8,128)(2,1)S(1)}, bf16[8,7168]{1,0:T(8,128)(2,1)S(1)}, u32[]{:S(2)}, u32[]{:S(2)}) collective-permute-start(bf16[8,7168]{1,0:T(8,128)(2,1)S(1)} %get-tuple-element.37), channel_id=1, source_target_pairs={{0,4},{1,5},{2,6},{3,7},{4,0},{5,1},{6,2},{7,3},{8,12},{9,13},{10,... | collective-permute-start | bytes 344072 | tf_op jit(solution)/shard_map/ppermute | solution.py:59
  32.2 5.6 %collective-permute-start.15 = (bf16[8,7168]{1,0:T(8,128)(2,1)S(1)}, bf16[8,7168]{1,0:T(8,128)(2,1)S(1)}, u32[]{:S(2)}, u32[]{:S(2)}) collective-permute-start(bf16[8,7168]{1,0:T(8,128)(2,1)S(1)} %get-tuple-element.38), channel_id=1, source_target_pairs={{0,2},{1,3},{2,0},{3,1},{4,6},{5,7},{6,4},{7,5},{8,10},{9,11},{10,... | collective-permute-start | bytes 344072 | tf_op jit(solution)/shard_map/ppermute | solution.py:59
  37.9 5.1 %collective-permute-start.17 = (bf16[2,7168]{1,0:T(2,128)(2,1)S(1)}, bf16[2,7168]{1,0:T(2,128)(2,1)S(1)}, u32[]{:S(2)}, u32[]{:S(2)}) collective-permute-start(bf16[2,7168]{1,0:T(2,128)(2,1)S(1)} %get-tuple-element.41), channel_id=1, source_target_pairs={{0,16},{1,17},{2,18},{3,19},{4,20},{5,21},{6,22},{7,23},{8,24},{9,... | collective-permute-start | bytes 86024 | tf_op jit(solution)/shard_map/ppermute | solution.py:59
  40.4 5.7 %collective-permute-start.18 = (bf16[2,7168]{1,0:T(2,128)(2,1)S(1)}, bf16[2,7168]{1,0:T(2,128)(2,1)S(1)}, u32[]{:S(2)}, u32[]{:S(2)}) collective-permute-start(bf16[2,7168]{1,0:T(2,128)(2,1)S(1)} %get-tuple-element.42), channel_id=1, source_target_pairs={{0,24},{1,25},{2,26},{3,27},{4,28},{5,29},{6,30},{7,31},{8,16},{9,... | collective-permute-start | bytes 86024 | tf_op jit(solution)/shard_map/ppermute | solution.py:59
  41.8 4.3 %collective-permute-start.19 = (bf16[2,7168]{1,0:T(2,128)(2,1)S(1)}, bf16[2,7168]{1,0:T(2,128)(2,1)S(1)}, u32[]{:S(2)}, u32[]{:S(2)}) collective-permute-start(bf16[2,7168]{1,0:T(2,128)(2,1)S(1)} %get-tuple-element.43), channel_id=1, source_target_pairs={{0,8},{1,9},{2,10},{3,11},{4,12},{5,13},{6,14},{7,15},{8,0},{9,1},... | collective-permute-start | bytes 86024 | tf_op jit(solution)/shard_map/ppermute | solution.py:59

commit v8 on v7

--- a/solution.py
+++ b/solution.py
@@ -133,7 +133,7 @@
 def merge_kernel(parts, *refs):
     out_ref = refs[-1]
     half = refs[0].shape[0] // 2
-    pieces = [r[...].astype(f32) for r in refs[:parts]]
+    pieces = [r[...].astype(f32) for r in [refs[0], *refs[1:parts][::-1]]]
     cores = [p[:half] for p in pieces] + [p[half:] for p in pieces]
     out_ref[...] = jnp.concatenate(cores, axis=0).astype(bf16)
 
@@ -147,7 +147,7 @@
         out_specs=in_vmem(),
         compiler_params=pltpu.CompilerParams(vmem_limit_bytes=4 * MIB),
         cost_estimate=pl.CostEstimate(flops=flops, bytes_accessed=8 * rows * width, transcendentals=0),
-    )(*[vmem(p) for p in pieces], *after)
+    )(*[vmem(p) for p in pieces[:1] + pieces[:0:-1]], *after)
 
 
 def half_start(width, near):
@@ -368,19 +368,19 @@
     )(*[vmem(x) for x, _, _ in pieces], *after)
 
 
-def exchange_pages(low, high, dp_count, after):
+def exchange_pages(low, first, dp_count, after):
     blocks, senders = [(low, 0, low.shape[0])], [0]
-    sent = high
-    for bit in partner_bits(dp_count):
-        got = swap(sent, "dp", pairs_of(dp_count, bit))
+    got = first
+    for number, bit in enumerate(partner_bits(dp_count)):
+        if number:
+            got = swap(sent, "dp", pairs_of(dp_count, bit))
         size = got.shape[0] // len(blocks)
         blocks = blocks + [(got, i * size, (i + 1) * size) for i in range(len(blocks))]
         senders = senders + [s ^ bit for s in senders]
         if size > MCAP:
             sent = rows_of([(x, start + size // 2, end) for x, start, end in blocks], after)
-            after = sent
             blocks = [(x, start, start + size // 2) for x, start, _ in blocks]
-    return rows_of(blocks), senders, after
+    return rows_of(blocks), senders
 
 
 def attend_kernel(senders, length_ref, table_ref, query_ref, pool_ref, arrived_ref, out_ref, query_rows):
@@ -500,9 +500,10 @@
         if number == 0:
             low, high, pool = pick_pages(moved_page, moved_dest, latent_pool, near, dp_count)
             after = [high]
+            bit = partner_bits(dp_count)[0]
+            first = swap(high, "dp", pairs_of(dp_count, bit))
         if number == len(stages) - 1:
-            arrived, senders, sent = exchange_pages(low, high, dp_count, got[0])
-            after = [sent]
+            after = [first]
         near = merge([near] + got, MERGE_FLOPS if number < len(stages) - 1 else MERGE_FLOPS // 4, *after)
     far = trade(near, 1)
     gate_acc, up_acc = near_products(near, gate_weight, up_weight)
@@ -514,12 +515,14 @@
     got_b = trade(send_b, 1)
     (sum_a,) = fold([(keep_a, [got_a])], 1, out=pltpu.VMEM(keep_a.shape, f32), flops=MERGE_FLOPS // 4)
     held = [(sum_a, []), (keep_b, [got_b])]
-    attended = attend(lengths, page_table, queries, pool, arrived, senders)
     after = []
     for number, partners in enumerate(reversed(stages)):
         keep, *send = fold(held, len(partners) + 1, *(after if number == 1 else []))
         held = [(keep, [trade(x, bit) for x, bit in zip(send, partners)])]
-        after = [hbm(attended)]
+        if number == 0:
+            arrived, senders = exchange_pages(low, first, dp_count, keep)
+            attended = attend(lengths, page_table, queries, pool, arrived, senders)
+            after = [hbm(attended)]
     (expert_mix,) = fold(held, 1, out=jax.ShapeDtypeStruct(hidden.shape, bf16))
     return expert_mix, attended
 

time: 46.9 us -> 45 us (0.959)
  local copies, waits for them, and re-layouts: 2.63 us -> 0.05 us
  waiting for transfers between devices: 13.7 us -> 14.2 us
    unnamed x18, local copies, waits for them, and re-layouts: 2.63 us -> 0.05 us
    ppermute x20, waiting for transfers between devices: 13.7 us -> 14.2 us  [swap(): return lax.ppermute(x, axes, pairs)]
  transfers between devices with their start and end apart: 20 -> 20, of which waited for: 10 -> 11; matrix products, arithmetic and copies ran while one was open for 0% -> 0% of each run, Pallas kernels for 15% -> 15%
where the time goes in v8:
time: 45 us; the launch traced here: 44.8 us
  starting transfers between devices  20.1 us (45%)
  waiting for transfers between devices  14.2 us (32%)
  Pallas kernels  9.6 us (21%)
  between operations  0.86 us (2%)
    ppermute x20, starting transfers between devices, swap(): return lax.ppermute(x, axes, pairs)  20.1 us
    ppermute x20, waiting for transfers between devices, swap(): return lax.ppermute(x, axes, pairs)  14.2 us
    pallas_call x1, Pallas kernels, attend(): pl.pallas_call(functools.partial(attend_kernel, senders), out_shape=jax.S...  2.35 us
    pallas_call x1, Pallas kernels, far_products(): pl.pallas_call(functools.partial(far_kernel, ep_count), out_shape=(pltpu....  1.74 us
    pallas_call x1, Pallas kernels, pick_pages(): pl.pallas_call(functools.partial(pages_kernel, dp_count), out_shape=(half...  1.49 us
    pallas_call x1, Pallas kernels, near_products(): pl.pallas_call(near_kernel, out_shape=(acc, acc), in_specs=[in_vmem()] *...  1.13 us
    pallas_call x1, Pallas kernels, fetch(): pl.pallas_call(fetch_kernel, out_shape=tuple((pltpu.VMEM(x.shape, x.dtype...  0.93 us
  transfers between devices with their start and end apart: 20, of which 11 were waited for; matrix products, arithmetic and copies ran while one was open for 0% of the time, Pallas kernels for 15%

profile of v8, /device:TPU:0, one launch (start us, length us, event | category | flops | bytes accessed | tf_op | source)
XLA Modules:
  0.0 44.8 jit_solution(8859548223112524604)
XLA Ops:
  0.6 0.5 %collective-permute-start.1 = (s32[2,4]{1,0:T(2,128)}, s32[2,4]{1,0:T(2,128)S(1)}, u32[]{:S(2)}, u32[]{:S(2)}) collective-permute-start(s32[2,4]{1,0:T(2,128)} %refs_1_.1), channel_id=1, source_target_pairs={{0,1},{1,0},{2,3},{3,2},{4,5},{5,4},{6,7},{7,6},{8,9},{9,8},{10,11... | collective-permute-start | bytes 104 | tf_op jit(solution)/shard_map/ppermute | solution.py:59
  1.2 0.4 collective-permute-start
  1.7 0.9 %shard_map.131 = (bf16[2,7168]{1,0:T(2,128)(2,1)S(1)}, s32[2,4]{1,0:T(2,128)S(1)}, f32[2,4]{1,0:T(2,128)S(1)}) custom-call(bf16[2,7168]{1,0:T(2,128)(2,1)} %refs_0_.1, s32[2,4]{1,0:T(2,128)} %refs_1_.1, f32[2,4]{1,0:T(2,128)} %refs_2_.1), custom_call_target="tpu_custom_call" | custom-call | flops 1250000000 | bytes 1048576 | tf_op jit(solution)/shard_map/pallas_call | solution.py:86
  2.8 4.0 %collective-permute-start.5 = (bf16[4,3712]{1,0:T(4,128)(2,1)S(1)}, bf16[4,3712]{1,0:T(4,128)(2,1)S(1)}, u32[]{:S(2)}, u32[]{:S(2)}) collective-permute-start(bf16[4,3712]{1,0:T(4,128)(2,1)S(1)} %shard_map.132.after_ref.refs_0_), channel_id=1, source_target_pairs={{0,16},{1,17},{2,18},{3,19},{4,20},{5,21},{6,22},{7,23},{8,24},{9,... | collective-permute-start | bytes 89096 | tf_op jit(solution)/shard_map/ppermute | solution.py:59
  6.8 1.3 %collective-permute-start.4 = (bf16[4,3712]{1,0:T(4,128)(2,1)S(1)}, bf16[4,3712]{1,0:T(4,128)(2,1)S(1)}, u32[]{:S(2)}, u32[]{:S(2)}) collective-permute-start(bf16[4,3712]{1,0:T(4,128)(2,1)S(1)} %shard_map.132.after_ref.refs_0_), channel_id=1, source_target_pairs={{0,24},{1,25},{2,26},{3,27},{4,28},{5,29},{6,30},{7,31},{8,16},{9,... | collective-permute-start | bytes 89096 | tf_op jit(solution)/shard_map/ppermute | solution.py:59
  8.4 1.5 %shard_map.133 = (bf16[4,18432]{1,0:T(4,128)(2,1)S(1)}, bf16[4,18432]{1,0:T(4,128)(2,1)S(1)}, bf16[24,18432]{1,0:T(8,128)(2,1)S(1)}) custom-call(s32[1,6]{1,0:T(1,128)} %page_hbm.1, s32[1,6]{1,0:T(1,128)} %dest_hbm.1, bf16[24,18432]{1,0:T(8,128)(2,1)} %pool_ref.1, bf16[4,3712]{1,0:T(4,128)(2,1)S(1)} %shard_map.132.after_ref.refs_0_), custom_call_target="tpu_custom_call" | custom-call | bytes 1769472 | tf_op jit(solution)/shard_map/pallas_call | solution.py:333
  10.0 1.6 %collective-permute-start.9 = (bf16[4,18432]{1,0:T(4,128)(2,1)S(1)}, bf16[4,18432]{1,0:T(4,128)(2,1)S(1)}, u32[]{:S(2)}, u32[]{:S(2)}) collective-permute-start(bf16[4,18432]{1,0:T(4,128)(2,1)S(1)} %get-tuple-element.26.refs_4_), channel_id=1, source_target_pairs={{0,2},{1,3},{2,0},{3,1},{4,6},{5,7},{6,4},{7,5},{8,10},{9,11},{10,... | collective-permute-start | bytes 442376 | tf_op jit(solution)/shard_map/ppermute | solution.py:59
  11.5 1.0 %collective-permute-done.4.refs_2_ = bf16[4,3712]{1,0:T(4,128)(2,1)S(1)} collective-permute-done((bf16[4,3712]{1,0:T(4,128)(2,1)S(1)}, bf16[4,3712]{1,0:T(4,128)(2,1)S(1)}, u32[]{:S(2)}, u32[]{:S(2)}) %collective-permute-start.4) | collective-permute-done | bytes 29728 | tf_op jit(solution)/shard_map/ppermute | solution.py:59
  12.6 2.5 %collective-permute-start.8 = (bf16[16,3712]{1,0:T(8,128)(2,1)S(1)}, bf16[16,3712]{1,0:T(8,128)(2,1)S(1)}, u32[]{:S(2)}, u32[]{:S(2)}) collective-permute-start(bf16[16,3712]{1,0:T(8,128)(2,1)S(1)} %shard_map.134.refs_0_), channel_id=1, source_target_pairs={{0,6},{1,7},{2,4},{3,5},{4,2},{5,3},{6,0},{7,1},{8,14},{9,15},{10,... | collective-permute-start | bytes 356360 | tf_op jit(solution)/shard_map/ppermute | solution.py:59
  15.1 0.5 %collective-permute-start.7 = (bf16[16,3712]{1,0:T(8,128)(2,1)S(1)}, bf16[16,3712]{1,0:T(8,128)(2,1)S(1)}, u32[]{:S(2)}, u32[]{:S(2)}) collective-permute-start(bf16[16,3712]{1,0:T(8,128)(2,1)S(1)} %shard_map.134.refs_0_), channel_id=1, source_target_pairs={{0,4},{1,5},{2,6},{3,7},{4,0},{5,1},{6,2},{7,3},{8,12},{9,13},{10,... | collective-permute-start | bytes 356360 | tf_op jit(solution)/shard_map/ppermute | solution.py:59
  15.6 0.5 %collective-permute-start.6 = (bf16[16,3712]{1,0:T(8,128)(2,1)S(1)}, bf16[16,3712]{1,0:T(8,128)(2,1)S(1)}, u32[]{:S(2)}, u32[]{:S(2)}) collective-permute-start(bf16[16,3712]{1,0:T(8,128)(2,1)S(1)} %shard_map.134.refs_0_), channel_id=1, source_target_pairs={{0,2},{1,3},{2,0},{3,1},{4,6},{5,7},{6,4},{7,5},{8,10},{9,11},{10,... | collective-permute-start | bytes 356360 | tf_op jit(solution)/shard_map/ppermute | solution.py:59
  16.1 4.1 %collective-permute-done.8.refs_3_ = bf16[16,3712]{1,0:T(8,128)(2,1)S(1)} collective-permute-done((bf16[16,3712]{1,0:T(8,128)(2,1)S(1)}, bf16[16,3712]{1,0:T(8,128)(2,1)S(1)}, u32[]{:S(2)}, u32[]{:S(2)}) %collective-permute-start.8) | collective-permute-done | bytes 118816 | tf_op jit(solution)/shard_map/ppermute | solution.py:59
  20.3 0.5 %collective-permute-done.7.refs_2_ = bf16[16,3712]{1,0:T(8,128)(2,1)S(1)} collective-permute-done((bf16[16,3712]{1,0:T(8,128)(2,1)S(1)}, bf16[16,3712]{1,0:T(8,128)(2,1)S(1)}, u32[]{:S(2)}, u32[]{:S(2)}) %collective-permute-start.7) | collective-permute-done | bytes 118816 | tf_op jit(solution)/shard_map/ppermute | solution.py:59
  20.9 1.1 %shard_map.136 = (f32[64,512]{1,0:T(8,128)S(1)}, f32[64,512]{1,0:T(8,128)S(1)}) custom-call(bf16[64,3712]{1,0:T(8,128)(2,1)S(1)} %shard_map.135.near_ref, bf16[1,7168,512]{2,1,0:T(8,128)(2,1)S(1)} %bitcast.1, bf16[1,7168,512]{2,1,0:T(8,128)(2,1)S(1)} %bitcast.3), custom_call_target="tpu_custom_call" | custom-call | flops 469762048 | bytes 7340032 | tf_op jit(solution)/shard_map/pallas_call | solution.py:222
  22.1 0.6 %collective-permute-done.10.far_ref = bf16[64,3712]{1,0:T(8,128)(2,1)S(1)} collective-permute-done((bf16[64,3712]{1,0:T(8,128)(2,1)S(1)}, bf16[64,3712]{1,0:T(8,128)(2,1)S(1)}, u32[]{:S(2)}, u32[]{:S(2)}) %collective-permute-start.10) | collective-permute-done | bytes 475168 | tf_op jit(solution)/shard_map/ppermute | solution.py:59
  22.7 1.7 %shard_map.137 = (bf16[64,512]{1,0:T(8,128)(2,1)S(1)}, f32[32,3584]{1,0:T(8,128)S(1)}, bf16[32,3584]{1,0:T(8,128)(2,1)S(1)}) custom-call(bf16[64,3712]{1,0:T(8,128)(2,1)S(1)} %shard_map.135.near_ref, bf16[64,3712]{1,0:T(8,128)(2,1)S(1)} %collective-permute-done.10.far_ref, bf16[1,7168,512]{2,1,0:T(8,128)(2,1)S(1)} %bitcast.1, ...), custom_call_target="tpu_custom_call" | custom-call | flops 704643072 | bytes 11010048 | tf_op jit(solution)/shard_map/pallas_call | solution.py:236
  24.6 0.7 %shard_map.139 = (f32[32,3584]{1,0:T(8,128)S(1)}, bf16[32,3584]{1,0:T(8,128)(2,1)S(1)}) custom-call(bf16[64,3712]{1,0:T(8,128)(2,1)S(1)} %shard_map.135.near_ref, bf16[64,512]{1,0:T(8,128)(2,1)S(1)} %get-tuple-element.31.inner_ref, bf16[1,512,7168]{2,1,0:T(8,128)(2,1)S(1)} %bitcast.5), custom_call_target="tpu_custom_call" | custom-call | flops 234881024 | bytes 3670016 | tf_op jit(solution)/shard_map/pallas_call | solution.py:254
  25.3 0.4 collective-permute-start.12
  25.8 0.2 collective-permute-done.11.refs_1_
  26.1 0.8 %collective-permute-done.12.refs_2_ = bf16[32,3584]{1,0:T(8,128)(2,1)S(1)} collective-permute-done((bf16[32,3584]{1,0:T(8,128)(2,1)S(1)}, bf16[32,3584]{1,0:T(8,128)(2,1)S(1)}, u32[]{:S(2)}, u32[]{:S(2)}) %collective-permute-start.12) | collective-permute-done | bytes 229408 | tf_op jit(solution)/shard_map/ppermute | solution.py:59
  27.1 0.4 collective-permute-start.16
  27.5 2.2 %collective-permute-start.13 = (bf16[8,7168]{1,0:T(8,128)(2,1)S(1)}, bf16[8,7168]{1,0:T(8,128)(2,1)S(1)}, u32[]{:S(2)}, u32[]{:S(2)}) collective-permute-start(bf16[8,7168]{1,0:T(8,128)(2,1)S(1)} %get-tuple-element.35), channel_id=1, source_target_pairs={{0,6},{1,7},{2,4},{3,5},{4,2},{5,3},{6,0},{7,1},{8,14},{9,15},{10,... | collective-permute-start | bytes 344072 | tf_op jit(solution)/shard_map/ppermute | solution.py:59
  29.7 0.5 %collective-permute-start.14 = (bf16[8,7168]{1,0:T(8,128)(2,1)S(1)}, bf16[8,7168]{1,0:T(8,128)(2,1)S(1)}, u32[]{:S(2)}, u32[]{:S(2)}) collective-permute-start(bf16[8,7168]{1,0:T(8,128)(2,1)S(1)} %get-tuple-element.36), channel_id=1, source_target_pairs={{0,4},{1,5},{2,6},{3,7},{4,0},{5,1},{6,2},{7,3},{8,12},{9,13},{10,... | collective-permute-start | bytes 344072 | tf_op jit(solution)/shard_map/ppermute | solution.py:59
  30.2 0.8 %collective-permute-start.15 = (bf16[8,7168]{1,0:T(8,128)(2,1)S(1)}, bf16[8,7168]{1,0:T(8,128)(2,1)S(1)}, u32[]{:S(2)}, u32[]{:S(2)}) collective-permute-start(bf16[8,7168]{1,0:T(8,128)(2,1)S(1)} %get-tuple-element.37), channel_id=1, source_target_pairs={{0,2},{1,3},{2,0},{3,1},{4,6},{5,7},{6,4},{7,5},{8,10},{9,11},{10,... | collective-permute-start | bytes 344072 | tf_op jit(solution)/shard_map/ppermute | solution.py:59
  31.2 2.4 %shard_map.143.refs_4_ = bf16[2,32768]{1,0:T(2,128)(2,1)} custom-call(s32[2]{0:T(128)S(1)} %copy-done.2, s32[2,12]{1,0:T(2,128)S(1)} %copy-done.1, bf16[2,36864]{1,0:T(2,128)(2,1)S(1)} %copy-done, bf16[24,18432]{1,0:T(8,128)(2,1)S(1)} %get-tuple-element.38.pool_ref, bf16[8,18432]{1,0:T(8,128)(2,1)S(1)} %shard_map.142.arrived_ref), custom_call_target="tpu_custom_call" | custom-call | flops 1073741824 | bytes 4194304 | tf_op jit(solution)/shard_map/pallas_call | solution.py:461
  33.5 0.3 collective-permute-done.13.refs_1_
  33.8 2.2 %collective-permute-done.14.refs_2_ = bf16[8,7168]{1,0:T(8,128)(2,1)S(1)} collective-permute-done((bf16[8,7168]{1,0:T(8,128)(2,1)S(1)}, bf16[8,7168]{1,0:T(8,128)(2,1)S(1)}, u32[]{:S(2)}, u32[]{:S(2)}) %collective-permute-start.14) | collective-permute-done | bytes 114720 | tf_op jit(solution)/shard_map/ppermute | solution.py:59
  36.1 2.4 %collective-permute-start.17 = (bf16[2,7168]{1,0:T(2,128)(2,1)S(1)}, bf16[2,7168]{1,0:T(2,128)(2,1)S(1)}, u32[]{:S(2)}, u32[]{:S(2)}) collective-permute-start(bf16[2,7168]{1,0:T(2,128)(2,1)S(1)} %get-tuple-element.41), channel_id=1, source_target_pairs={{0,16},{1,17},{2,18},{3,19},{4,20},{5,21},{6,22},{7,23},{8,24},{9,... | collective-permute-start | bytes 86024 | tf_op jit(solution)/shard_map/ppermute | solution.py:59
  38.5 1.4 %collective-permute-start.18 = (bf16[2,7168]{1,0:T(2,128)(2,1)S(1)}, bf16[2,7168]{1,0:T(2,128)(2,1)S(1)}, u32[]{:S(2)}, u32[]{:S(2)}) collective-permute-start(bf16[2,7168]{1,0:T(2,128)(2,1)S(1)} %get-tuple-element.42), channel_id=1, source_target_pairs={{0,24},{1,25},{2,26},{3,27},{4,28},{5,29},{6,30},{7,31},{8,16},{9,... | collective-permute-start | bytes 86024 | tf_op jit(solution)/shard_map/ppermute | solution.py:59
  39.9 1.3 %collective-permute-done.17.refs_1_ = bf16[2,7168]{1,0:T(2,128)(2,1)S(1)} collective-permute-done((bf16[2,7168]{1,0:T(2,128)(2,1)S(1)}, bf16[2,7168]{1,0:T(2,128)(2,1)S(1)}, u32[]{:S(2)}, u32[]{:S(2)}) %collective-permute-start.17) | collective-permute-done | bytes 28704 | tf_op jit(solution)/shard_map/ppermute | solution.py:59
  41.1 3.0 %collective-permute-done.18.refs_2_ = bf16[2,7168]{1,0:T(2,128)(2,1)S(1)} collective-permute-done((bf16[2,7168]{1,0:T(2,128)(2,1)S(1)}, bf16[2,7168]{1,0:T(2,128)(2,1)S(1)}, u32[]{:S(2)}, u32[]{:S(2)}) %collective-permute-start.18) | collective-permute-done | bytes 28704 | tf_op jit(solution)/shard_map/ppermute | solution.py:59
  44.2 0.7 %shard_map.145 = bf16[2,7168]{1,0:T(2,128)(2,1)} custom-call(f32[2,7168]{1,0:T(2,128)S(1)} %get-tuple-element.40.refs_0_, bf16[2,7168]{1,0:T(2,128)(2,1)S(1)} %collective-permute-done.17.refs_1_, bf16[2,7168]{1,0:T(2,128)(2,1)S(1)} %collective-permute-done.18.refs_2_, bf16[2,7168]{1,0:T(2,128)(2,1)S(1)} %collective-permute-done.19.refs_3_), custom_call_target="tpu_custom_call" | custom-call | bytes 114688 | tf_op jit(solution)/shard_map/pallas_call | solution.py:286
  (44 shorter events, 1.4 us)
Async XLA Ops:
  0.6 2.0 %collective-permute-start.1 = (s32[2,4]{1,0:T(2,128)}, s32[2,4]{1,0:T(2,128)S(1)}, u32[]{:S(2)}, u32[]{:S(2)}) collective-permute-start(s32[2,4]{1,0:T(2,128)} %refs_1_.1), channel_id=1, source_target_pairs={{0,1},{1,0},{2,3},{3,2},{4,5},{5,4},{6,7},{7,6},{8,9},{9,8},{10,11... | collective-permute-start | bytes 104 | tf_op jit(solution)/shard_map/ppermute | solution.py:59
  1.1 1.5 %collective-permute-start.2 = (f32[2,4]{1,0:T(2,128)}, f32[2,4]{1,0:T(2,128)S(1)}, u32[]{:S(2)}, u32[]{:S(2)}) collective-permute-start(f32[2,4]{1,0:T(2,128)} %refs_2_.1), channel_id=1, source_target_pairs={{0,1},{1,0},{2,3},{3,2},{4,5},{5,4},{6,7},{7,6},{8,9},{9,8},{10,11... | collective-permute-start | bytes 104 | tf_op jit(solution)/shard_map/ppermute | solution.py:59
  1.2 1.5 %collective-permute-start = (bf16[2,7168]{1,0:T(2,128)(2,1)}, bf16[2,7168]{1,0:T(2,128)(2,1)S(1)}, u32[]{:S(2)}, u32[]{:S(2)}) collective-permute-start(bf16[2,7168]{1,0:T(2,128)(2,1)} %refs_0_.1), channel_id=1, source_target_pairs={{0,1},{1,0},{2,3},{3,2},{4,5},{5,4},{6,7},{7,6},{8,9},{9,8},{10,11... | collective-permute-start | bytes 86024 | tf_op jit(solution)/shard_map/ppermute | solution.py:59
  1.7 21.0 %slice-start.4 = ((s8[7340032]{0:T(1024)(128)(4,1)}), s8[4194304]{0:T(1024)(128)(4,1)S(1)}, s32[]{:S(2)}) async-start(s8[7340032]{0:T(1024)(128)(4,1)} %bitcast.4), calls=%async_computation.4 | async-start | bytes 8388608
  2.8 8.7 %collective-permute-start.5 = (bf16[4,3712]{1,0:T(4,128)(2,1)S(1)}, bf16[4,3712]{1,0:T(4,128)(2,1)S(1)}, u32[]{:S(2)}, u32[]{:S(2)}) collective-permute-start(bf16[4,3712]{1,0:T(4,128)(2,1)S(1)} %shard_map.132.after_ref.refs_0_), channel_id=1, source_target_pairs={{0,16},{1,17},{2,18},{3,19},{4,20},{5,21},{6,22},{7,23},{8,24},{9,... | collective-permute-start | bytes 89096 | tf_op jit(solution)/shard_map/ppermute | solution.py:59
  6.8 5.7 %collective-permute-start.4 = (bf16[4,3712]{1,0:T(4,128)(2,1)S(1)}, bf16[4,3712]{1,0:T(4,128)(2,1)S(1)}, u32[]{:S(2)}, u32[]{:S(2)}) collective-permute-start(bf16[4,3712]{1,0:T(4,128)(2,1)S(1)} %shard_map.132.after_ref.refs_0_), channel_id=1, source_target_pairs={{0,24},{1,25},{2,26},{3,27},{4,28},{5,29},{6,30},{7,31},{8,16},{9,... | collective-permute-start | bytes 89096 | tf_op jit(solution)/shard_map/ppermute | solution.py:59
  8.2 4.3 %collective-permute-start.3 = (bf16[4,3712]{1,0:T(4,128)(2,1)S(1)}, bf16[4,3712]{1,0:T(4,128)(2,1)S(1)}, u32[]{:S(2)}, u32[]{:S(2)}) collective-permute-start(bf16[4,3712]{1,0:T(4,128)(2,1)S(1)} %shard_map.132.after_ref.refs_0_), channel_id=1, source_target_pairs={{0,8},{1,9},{2,10},{3,11},{4,12},{5,13},{6,14},{7,15},{8,0},{9,1},... | collective-permute-start | bytes 89096 | tf_op jit(solution)/shard_map/ppermute | solution.py:59
  9.9 11.0 %slice-start = ((s8[7340032]{0:T(1024)(128)(4,1)}), s8[4194304]{0:T(1024)(128)(4,1)S(1)}, s32[]{:S(2)}) async-start(s8[7340032]{0:T(1024)(128)(4,1)} %bitcast), calls=%async_computation | async-start | bytes 8388608
  9.9 11.0 %slice-start.2 = ((s8[7340032]{0:T(1024)(128)(4,1)}), s8[4194304]{0:T(1024)(128)(4,1)S(1)}, s32[]{:S(2)}) async-start(s8[7340032]{0:T(1024)(128)(4,1)} %bitcast.2), calls=%async_computation.2 | async-start | bytes 8388608
  9.9 11.0 %slice-start.1 = ((s8[7340032]{0:T(1024)(128)(4,1)}), s8[3145728]{0:T(1024)(128)(4,1)S(1)}, s32[]{:S(2)}) async-start(s8[7340032]{0:T(1024)(128)(4,1)} %bitcast), calls=%async_computation.1 | async-start | bytes 6291456
  9.9 11.0 %slice-start.3 = ((s8[7340032]{0:T(1024)(128)(4,1)}), s8[3145728]{0:T(1024)(128)(4,1)S(1)}, s32[]{:S(2)}) async-start(s8[7340032]{0:T(1024)(128)(4,1)} %bitcast.2), calls=%async_computation.3 | async-start | bytes 6291456
  9.9 12.8 %slice-start.5 = ((s8[7340032]{0:T(1024)(128)(4,1)}), s8[3145728]{0:T(1024)(128)(4,1)S(1)}, s32[]{:S(2)}) async-start(s8[7340032]{0:T(1024)(128)(4,1)} %bitcast.4), calls=%async_computation.5 | async-start | bytes 6291456
  10.0 6.2 %collective-permute-start.9 = (bf16[4,18432]{1,0:T(4,128)(2,1)S(1)}, bf16[4,18432]{1,0:T(4,128)(2,1)S(1)}, u32[]{:S(2)}, u32[]{:S(2)}) collective-permute-start(bf16[4,18432]{1,0:T(4,128)(2,1)S(1)} %get-tuple-element.26.refs_4_), channel_id=1, source_target_pairs={{0,2},{1,3},{2,0},{3,1},{4,6},{5,7},{6,4},{7,5},{8,10},{9,11},{10,... | collective-permute-start | bytes 442376 | tf_op jit(solution)/shard_map/ppermute | solution.py:59
  12.6 7.7 %collective-permute-start.8 = (bf16[16,3712]{1,0:T(8,128)(2,1)S(1)}, bf16[16,3712]{1,0:T(8,128)(2,1)S(1)}, u32[]{:S(2)}, u32[]{:S(2)}) collective-permute-start(bf16[16,3712]{1,0:T(8,128)(2,1)S(1)} %shard_map.134.refs_0_), channel_id=1, source_target_pairs={{0,6},{1,7},{2,4},{3,5},{4,2},{5,3},{6,0},{7,1},{8,14},{9,15},{10,... | collective-permute-start | bytes 356360 | tf_op jit(solution)/shard_map/ppermute | solution.py:59
  15.1 5.7 %collective-permute-start.7 = (bf16[16,3712]{1,0:T(8,128)(2,1)S(1)}, bf16[16,3712]{1,0:T(8,128)(2,1)S(1)}, u32[]{:S(2)}, u32[]{:S(2)}) collective-permute-start(bf16[16,3712]{1,0:T(8,128)(2,1)S(1)} %shard_map.134.refs_0_), channel_id=1, source_target_pairs={{0,4},{1,5},{2,6},{3,7},{4,0},{5,1},{6,2},{7,3},{8,12},{9,13},{10,... | collective-permute-start | bytes 356360 | tf_op jit(solution)/shard_map/ppermute | solution.py:59
  15.6 5.2 %collective-permute-start.6 = (bf16[16,3712]{1,0:T(8,128)(2,1)S(1)}, bf16[16,3712]{1,0:T(8,128)(2,1)S(1)}, u32[]{:S(2)}, u32[]{:S(2)}) collective-permute-start(bf16[16,3712]{1,0:T(8,128)(2,1)S(1)} %shard_map.134.refs_0_), channel_id=1, source_target_pairs={{0,2},{1,3},{2,0},{3,1},{4,6},{5,7},{6,4},{7,5},{8,10},{9,11},{10,... | collective-permute-start | bytes 356360 | tf_op jit(solution)/shard_map/ppermute | solution.py:59
  20.8 1.9 %collective-permute-start.10 = (bf16[64,3712]{1,0:T(8,128)(2,1)S(1)}, bf16[64,3712]{1,0:T(8,128)(2,1)S(1)}, u32[]{:S(2)}, u32[]{:S(2)}) collective-permute-start(bf16[64,3712]{1,0:T(8,128)(2,1)S(1)} %shard_map.135.near_ref), channel_id=1, source_target_pairs={{0,1},{1,0},{2,3},{3,2},{4,5},{5,4},{6,7},{7,6},{8,9},{9,8},{10,11... | collective-permute-start | bytes 1425416 | tf_op jit(solution)/shard_map/ppermute | solution.py:59
  24.4 1.6 %collective-permute-start.11 = (bf16[32,3584]{1,0:T(8,128)(2,1)S(1)}, bf16[32,3584]{1,0:T(8,128)(2,1)S(1)}, u32[]{:S(2)}, u32[]{:S(2)}) collective-permute-start(bf16[32,3584]{1,0:T(8,128)(2,1)S(1)} %get-tuple-element.30), channel_id=1, source_target_pairs={{0,1},{1,0},{2,3},{3,2},{4,5},{5,4},{6,7},{7,6},{8,9},{9,8},{10,11... | collective-permute-start | bytes 688136 | tf_op jit(solution)/shard_map/ppermute | solution.py:59
  25.3 1.6 %collective-permute-start.12 = (bf16[32,3584]{1,0:T(8,128)(2,1)S(1)}, bf16[32,3584]{1,0:T(8,128)(2,1)S(1)}, u32[]{:S(2)}, u32[]{:S(2)}) collective-permute-start(bf16[32,3584]{1,0:T(8,128)(2,1)S(1)} %get-tuple-element.33), channel_id=1, source_target_pairs={{0,1},{1,0},{2,3},{3,2},{4,5},{5,4},{6,7},{7,6},{8,9},{9,8},{10,11... | collective-permute-start | bytes 688136 | tf_op jit(solution)/shard_map/ppermute | solution.py:59
  26.0 5.2 %copy-start = (bf16[2,36864]{1,0:T(2,128)(2,1)S(1)}, bf16[2,36864]{1,0:T(2,128)(2,1)}, u32[]{:S(2)}) copy-start(bf16[2,36864]{1,0:T(2,128)(2,1)} %query_ref.1) | copy-start | bytes 442372
  26.0 5.2 %copy-start.1 = (s32[2,12]{1,0:T(2,128)S(1)}, s32[2,12]{1,0:T(2,128)}, u32[]{:S(2)}) copy-start(s32[2,12]{1,0:T(2,128)} %table_ref.1) | copy-start | bytes 292
  26.0 5.2 %copy-start.2 = (s32[2]{0:T(128)S(1)}, s32[2]{0:T(128)}, u32[]{:S(2)}) copy-start(s32[2]{0:T(128)} %length_ref.1) | copy-start | bytes 28
  27.1 3.9 %collective-permute-start.16 = (bf16[4,18432]{1,0:T(4,128)(2,1)S(1)}, bf16[4,18432]{1,0:T(4,128)(2,1)S(1)}, u32[]{:S(2)}, u32[]{:S(2)}) collective-permute-start(bf16[4,18432]{1,0:T(4,128)(2,1)S(1)} %shard_map.141), channel_id=1, source_target_pairs={{0,1},{1,0},{2,3},{3,2},{4,5},{5,4},{6,7},{7,6},{8,9},{9,8},{10,11... | collective-permute-start | bytes 442376 | tf_op jit(solution)/shard_map/ppermute | solution.py:59
  27.5 6.3 %collective-permute-start.13 = (bf16[8,7168]{1,0:T(8,128)(2,1)S(1)}, bf16[8,7168]{1,0:T(8,128)(2,1)S(1)}, u32[]{:S(2)}, u32[]{:S(2)}) collective-permute-start(bf16[8,7168]{1,0:T(8,128)(2,1)S(1)} %get-tuple-element.35), channel_id=1, source_target_pairs={{0,6},{1,7},{2,4},{3,5},{4,2},{5,3},{6,0},{7,1},{8,14},{9,15},{10,... | collective-permute-start | bytes 344072 | tf_op jit(solution)/shard_map/ppermute | solution.py:59
  29.7 6.4 %collective-permute-start.14 = (bf16[8,7168]{1,0:T(8,128)(2,1)S(1)}, bf16[8,7168]{1,0:T(8,128)(2,1)S(1)}, u32[]{:S(2)}, u32[]{:S(2)}) collective-permute-start(bf16[8,7168]{1,0:T(8,128)(2,1)S(1)} %get-tuple-element.36), channel_id=1, source_target_pairs={{0,4},{1,5},{2,6},{3,7},{4,0},{5,1},{6,2},{7,3},{8,12},{9,13},{10,... | collective-permute-start | bytes 344072 | tf_op jit(solution)/shard_map/ppermute | solution.py:59
  30.2 5.9 %collective-permute-start.15 = (bf16[8,7168]{1,0:T(8,128)(2,1)S(1)}, bf16[8,7168]{1,0:T(8,128)(2,1)S(1)}, u32[]{:S(2)}, u32[]{:S(2)}) collective-permute-start(bf16[8,7168]{1,0:T(8,128)(2,1)S(1)} %get-tuple-element.37), channel_id=1, source_target_pairs={{0,2},{1,3},{2,0},{3,1},{4,6},{5,7},{6,4},{7,5},{8,10},{9,11},{10,... | collective-permute-start | bytes 344072 | tf_op jit(solution)/shard_map/ppermute | solution.py:59
  36.1 5.0 %collective-permute-start.17 = (bf16[2,7168]{1,0:T(2,128)(2,1)S(1)}, bf16[2,7168]{1,0:T(2,128)(2,1)S(1)}, u32[]{:S(2)}, u32[]{:S(2)}) collective-permute-start(bf16[2,7168]{1,0:T(2,128)(2,1)S(1)} %get-tuple-element.41), channel_id=1, source_target_pairs={{0,16},{1,17},{2,18},{3,19},{4,20},{5,21},{6,22},{7,23},{8,24},{9,... | collective-permute-start | bytes 86024 | tf_op jit(solution)/shard_map/ppermute | solution.py:59
  38.5 5.7 %collective-permute-start.18 = (bf16[2,7168]{1,0:T(2,128)(2,1)S(1)}, bf16[2,7168]{1,0:T(2,128)(2,1)S(1)}, u32[]{:S(2)}, u32[]{:S(2)}) collective-permute-start(bf16[2,7168]{1,0:T(2,128)(2,1)S(1)} %get-tuple-element.42), channel_id=1, source_target_pairs={{0,24},{1,25},{2,26},{3,27},{4,28},{5,29},{6,30},{7,31},{8,16},{9,... | collective-permute-start | bytes 86024 | tf_op jit(solution)/shard_map/ppermute | solution.py:59
  39.9 4.3 %collective-permute-start.19 = (bf16[2,7168]{1,0:T(2,128)(2,1)S(1)}, bf16[2,7168]{1,0:T(2,128)(2,1)S(1)}, u32[]{:S(2)}, u32[]{:S(2)}) collective-permute-start(bf16[2,7168]{1,0:T(2,128)(2,1)S(1)} %get-tuple-element.43), channel_id=1, source_target_pairs={{0,8},{1,9},{2,10},{3,11},{4,12},{5,13},{6,14},{7,15},{8,0},{9,1},... | collective-permute-start | bytes 86024 | tf_op jit(solution)/shard_map/ppermute | solution.py:59

commit v9 on v8

--- a/solution.py
+++ b/solution.py
@@ -161,7 +161,8 @@
     return x if rows >= 128 else jnp.concatenate([x] * (128 // rows), axis=0)
 
 
-def near_kernel(near_ref, gate_ref, up_ref, gate_out, up_out):
+def near_kernel(near_ref, gate_ref, up_ref, *refs):
+    gate_out, up_out = refs[-2:]
     rows, width = near_ref.shape[0], gate_ref.shape[1]
     at = pl.ds(half_start(width, True), width // 2)
     x = padded(near_ref[:, : width // 2])
@@ -193,7 +194,8 @@
         send_ref[:, columns] = jnp.where(first, out[rows:], out[:rows]).astype(bf16)
 
 
-def far_kernel(ep_count, near_ref, far_ref, gate_ref, up_ref, gate_in, up_in, down_ref, inner_ref, keep_ref, send_ref):
+def far_kernel(ep_count, near_ref, far_ref, gate_ref, up_ref, gate_in, up_in, down_ref, *refs):
+    inner_ref, keep_ref, send_ref = refs[-3:]
     rows, width = near_ref.shape[0], gate_ref.shape[1]
     half = width // 2
     at = pl.ds(half_start(width, False), half)
@@ -215,21 +217,21 @@
     return pl.CostEstimate(flops=2 * rows * weights, bytes_accessed=2 * weights, transcendentals=0)
 
 
-def near_products(near, gate, up):
+def near_products(near, gate, up, down, *after):
     rows = near.shape[0]
     width, units = gate.shape[1:]
     acc = pltpu.VMEM((rows, units), f32)
     return pl.pallas_call(
         near_kernel,
         out_shape=(acc, acc),
-        in_specs=[in_vmem()] * 3,
+        in_specs=[in_vmem()] * 4 + [anywhere()] * len(after),
         out_specs=(in_vmem(),) * 2,
         compiler_params=pltpu.CompilerParams(vmem_limit_bytes=8 * MIB),
         cost_estimate=estimate(rows, width * units),
-    )(vmem(near), gate, up)
-
-
-def far_products(near, far, gate, up, gate_acc, up_acc, down, ep_count):
+    )(vmem(near), gate, up, down, *after)
+
+
+def far_products(near, far, gate, up, gate_acc, up_acc, down, ep_count, *after):
     rows = near.shape[0]
     units, width = down.shape[1:]
     half = width // 2
@@ -240,11 +242,11 @@
             pltpu.VMEM((rows // 2, half), f32),
             pltpu.VMEM((rows // 2, half), bf16),
         ),
-        in_specs=[in_vmem()] * 7,
+        in_specs=[in_vmem()] * 7 + [anywhere()] * len(after),
         out_specs=(in_vmem(),) * 3,
         compiler_params=pltpu.CompilerParams(vmem_limit_bytes=8 * MIB),
         cost_estimate=estimate(rows, 3 * half * units),
-    )(vmem(near), vmem(far), gate, up, vmem(gate_acc), vmem(up_acc), down)
+    )(vmem(near), vmem(far), gate, up, vmem(gate_acc), vmem(up_acc), down, *after)
 
 
 def rest_products(near, inner, down, ep_count):
@@ -371,16 +373,18 @@
 def exchange_pages(low, first, dp_count, after):
     blocks, senders = [(low, 0, low.shape[0])], [0]
     got = first
+    moves = []
     for number, bit in enumerate(partner_bits(dp_count)):
         if number:
             got = swap(sent, "dp", pairs_of(dp_count, bit))
+            moves.append((sent, got))
         size = got.shape[0] // len(blocks)
         blocks = blocks + [(got, i * size, (i + 1) * size) for i in range(len(blocks))]
         senders = senders + [s ^ bit for s in senders]
         if size > MCAP:
             sent = rows_of([(x, start + size // 2, end) for x, start, end in blocks], after)
             blocks = [(x, start, start + size // 2) for x, start, _ in blocks]
-    return rows_of(blocks), senders
+    return rows_of(blocks), senders, moves
 
 
 def attend_kernel(senders, length_ref, table_ref, query_ref, pool_ref, arrived_ref, out_ref, query_rows):
@@ -506,9 +510,10 @@
             after = [first]
         near = merge([near] + got, MERGE_FLOPS if number < len(stages) - 1 else MERGE_FLOPS // 4, *after)
     far = trade(near, 1)
-    gate_acc, up_acc = near_products(near, gate_weight, up_weight)
+    arrived, senders, moves = exchange_pages(low, first, dp_count, near)
+    gate_acc, up_acc = near_products(near, gate_weight, up_weight, down_weight, *[sent for sent, _ in moves])
     inner, keep_a, send_a = far_products(
-        near, far, gate_weight, up_weight, gate_acc, up_acc, down_weight, ep_count
+        near, far, gate_weight, up_weight, gate_acc, up_acc, down_weight, ep_count, *[got for _, got in moves]
     )
     got_a = trade(send_a, 1)
     keep_b, send_b = rest_products(near, inner, down_weight, ep_count)
@@ -520,7 +525,6 @@
         keep, *send = fold(held, len(partners) + 1, *(after if number == 1 else []))
         held = [(keep, [trade(x, bit) for x, bit in zip(send, partners)])]
         if number == 0:
-            arrived, senders = exchange_pages(low, first, dp_count, keep)
             attended = attend(lengths, page_table, queries, pool, arrived, senders)
             after = [hbm(attended)]
     (expert_mix,) = fold(held, 1, out=jax.ShapeDtypeStruct(hidden.shape, bf16))

time: 45 us -> 45 us (level)
  no operation moved by 1% of the time
where the time goes in v9:
time: 45 us; the launch traced here: 44.8 us
  starting transfers between devices  20.3 us (45%)
  waiting for transfers between devices  14.1 us (31%)
  Pallas kernels  9.45 us (21%)
  between operations  0.85 us (2%)
    ppermute x20, starting transfers between devices, swap(): return lax.ppermute(x, axes, pairs)  20.3 us
    ppermute x20, waiting for transfers between devices, swap(): return lax.ppermute(x, axes, pairs)  14.1 us
    pallas_call x1, Pallas kernels, attend(): pl.pallas_call(functools.partial(attend_kernel, senders), out_shape=jax.S...  2.35 us
    pallas_call x1, Pallas kernels, far_products(): pl.pallas_call(functools.partial(far_kernel, ep_count), out_shape=(pltpu....  1.74 us
    pallas_call x1, Pallas kernels, pick_pages(): pl.pallas_call(functools.partial(pages_kernel, dp_count), out_shape=(half...  1.49 us
    pallas_call x1, Pallas kernels, near_products(): pl.pallas_call(near_kernel, out_shape=(acc, acc), in_specs=[in_vmem()] *...  1.13 us
  transfers between devices with their start and end apart: 20, of which 11 were waited for; matrix products, arithmetic and copies ran while one was open for 0% of the time, Pallas kernels for 15%

profile of v9, /device:TPU:0, one launch (start us, length us, event | category | flops | bytes accessed | tf_op | source)
XLA Modules:
  0.0 44.8 jit_solution(10865755499572972893)
XLA Ops:
  0.6 0.5 %collective-permute-start.1 = (s32[2,4]{1,0:T(2,128)}, s32[2,4]{1,0:T(2,128)S(1)}, u32[]{:S(2)}, u32[]{:S(2)}) collective-permute-start(s32[2,4]{1,0:T(2,128)} %refs_1_.1), channel_id=1, source_target_pairs={{0,1},{1,0},{2,3},{3,2},{4,5},{5,4},{6,7},{7,6},{8,9},{9,8},{10,11... | collective-permute-start | bytes 104 | tf_op jit(solution)/shard_map/ppermute | solution.py:59
  1.2 0.4 collective-permute-start
  1.7 0.8 %shard_map.131 = (bf16[2,7168]{1,0:T(2,128)(2,1)S(1)}, s32[2,4]{1,0:T(2,128)S(1)}, f32[2,4]{1,0:T(2,128)S(1)}) custom-call(bf16[2,7168]{1,0:T(2,128)(2,1)} %refs_0_.2, s32[2,4]{1,0:T(2,128)} %refs_1_.1, f32[2,4]{1,0:T(2,128)} %refs_2_.1), custom_call_target="tpu_custom_call" | custom-call | flops 1250000000 | bytes 1048576 | tf_op jit(solution)/shard_map/pallas_call | solution.py:86
  2.8 4.0 %collective-permute-start.5 = (bf16[4,3712]{1,0:T(4,128)(2,1)S(1)}, bf16[4,3712]{1,0:T(4,128)(2,1)S(1)}, u32[]{:S(2)}, u32[]{:S(2)}) collective-permute-start(bf16[4,3712]{1,0:T(4,128)(2,1)S(1)} %shard_map.132.after_ref.refs_0_), channel_id=1, source_target_pairs={{0,16},{1,17},{2,18},{3,19},{4,20},{5,21},{6,22},{7,23},{8,24},{9,... | collective-permute-start | bytes 89096 | tf_op jit(solution)/shard_map/ppermute | solution.py:59
  6.8 1.3 %collective-permute-start.4 = (bf16[4,3712]{1,0:T(4,128)(2,1)S(1)}, bf16[4,3712]{1,0:T(4,128)(2,1)S(1)}, u32[]{:S(2)}, u32[]{:S(2)}) collective-permute-start(bf16[4,3712]{1,0:T(4,128)(2,1)S(1)} %shard_map.132.after_ref.refs_0_), channel_id=1, source_target_pairs={{0,24},{1,25},{2,26},{3,27},{4,28},{5,29},{6,30},{7,31},{8,16},{9,... | collective-permute-start | bytes 89096 | tf_op jit(solution)/shard_map/ppermute | solution.py:59
  8.2 0.2 collective-permute-start.3
  8.4 1.5 %shard_map.133 = (bf16[4,18432]{1,0:T(4,128)(2,1)S(1)}, bf16[4,18432]{1,0:T(4,128)(2,1)S(1)}, bf16[24,18432]{1,0:T(8,128)(2,1)S(1)}) custom-call(s32[1,6]{1,0:T(1,128)} %page_hbm.1, s32[1,6]{1,0:T(1,128)} %dest_hbm.1, bf16[24,18432]{1,0:T(8,128)(2,1)} %pool_ref.1, bf16[4,3712]{1,0:T(4,128)(2,1)S(1)} %shard_map.132.after_ref.refs_0_), custom_call_target="tpu_custom_call" | custom-call | bytes 1769472 | tf_op jit(solution)/shard_map/pallas_call | solution.py:335
  10.0 1.6 %collective-permute-start.9 = (bf16[4,18432]{1,0:T(4,128)(2,1)S(1)}, bf16[4,18432]{1,0:T(4,128)(2,1)S(1)}, u32[]{:S(2)}, u32[]{:S(2)}) collective-permute-start(bf16[4,18432]{1,0:T(4,128)(2,1)S(1)} %get-tuple-element.26.refs_4_), channel_id=1, source_target_pairs={{0,2},{1,3},{2,0},{3,1},{4,6},{5,7},{6,4},{7,5},{8,10},{9,11},{10,... | collective-permute-start | bytes 442376 | tf_op jit(solution)/shard_map/ppermute | solution.py:59
  11.5 1.0 %collective-permute-done.4.refs_2_ = bf16[4,3712]{1,0:T(4,128)(2,1)S(1)} collective-permute-done((bf16[4,3712]{1,0:T(4,128)(2,1)S(1)}, bf16[4,3712]{1,0:T(4,128)(2,1)S(1)}, u32[]{:S(2)}, u32[]{:S(2)}) %collective-permute-start.4) | collective-permute-done | bytes 29728 | tf_op jit(solution)/shard_map/ppermute | solution.py:59
  12.6 2.5 %collective-permute-start.8 = (bf16[16,3712]{1,0:T(8,128)(2,1)S(1)}, bf16[16,3712]{1,0:T(8,128)(2,1)S(1)}, u32[]{:S(2)}, u32[]{:S(2)}) collective-permute-start(bf16[16,3712]{1,0:T(8,128)(2,1)S(1)} %shard_map.134.refs_0_), channel_id=1, source_target_pairs={{0,6},{1,7},{2,4},{3,5},{4,2},{5,3},{6,0},{7,1},{8,14},{9,15},{10,... | collective-permute-start | bytes 356360 | tf_op jit(solution)/shard_map/ppermute | solution.py:59
  15.1 0.5 %collective-permute-start.7 = (bf16[16,3712]{1,0:T(8,128)(2,1)S(1)}, bf16[16,3712]{1,0:T(8,128)(2,1)S(1)}, u32[]{:S(2)}, u32[]{:S(2)}) collective-permute-start(bf16[16,3712]{1,0:T(8,128)(2,1)S(1)} %shard_map.134.refs_0_), channel_id=1, source_target_pairs={{0,4},{1,5},{2,6},{3,7},{4,0},{5,1},{6,2},{7,3},{8,12},{9,13},{10,... | collective-permute-start | bytes 356360 | tf_op jit(solution)/shard_map/ppermute | solution.py:59
  15.6 0.5 %collective-permute-start.6 = (bf16[16,3712]{1,0:T(8,128)(2,1)S(1)}, bf16[16,3712]{1,0:T(8,128)(2,1)S(1)}, u32[]{:S(2)}, u32[]{:S(2)}) collective-permute-start(bf16[16,3712]{1,0:T(8,128)(2,1)S(1)} %shard_map.134.refs_0_), channel_id=1, source_target_pairs={{0,2},{1,3},{2,0},{3,1},{4,6},{5,7},{6,4},{7,5},{8,10},{9,11},{10,... | collective-permute-start | bytes 356360 | tf_op jit(solution)/shard_map/ppermute | solution.py:59
  16.1 4.2 %collective-permute-done.8.refs_3_ = bf16[16,3712]{1,0:T(8,128)(2,1)S(1)} collective-permute-done((bf16[16,3712]{1,0:T(8,128)(2,1)S(1)}, bf16[16,3712]{1,0:T(8,128)(2,1)S(1)}, u32[]{:S(2)}, u32[]{:S(2)}) %collective-permute-start.8) | collective-permute-done | bytes 118816 | tf_op jit(solution)/shard_map/ppermute | solution.py:59
  20.3 0.5 %collective-permute-done.7.refs_2_ = bf16[16,3712]{1,0:T(8,128)(2,1)S(1)} collective-permute-done((bf16[16,3712]{1,0:T(8,128)(2,1)S(1)}, bf16[16,3712]{1,0:T(8,128)(2,1)S(1)}, u32[]{:S(2)}, u32[]{:S(2)}) %collective-permute-start.7) | collective-permute-done | bytes 118816 | tf_op jit(solution)/shard_map/ppermute | solution.py:59
  21.0 0.6 %collective-permute-start.11 = (bf16[4,18432]{1,0:T(4,128)(2,1)S(1)}, bf16[4,18432]{1,0:T(4,128)(2,1)S(1)}, u32[]{:S(2)}, u32[]{:S(2)}) collective-permute-start(bf16[4,18432]{1,0:T(4,128)(2,1)S(1)} %shard_map.136.refs_1_), channel_id=1, source_target_pairs={{0,1},{1,0},{2,3},{3,2},{4,5},{5,4},{6,7},{7,6},{8,9},{9,8},{10,11... | collective-permute-start | bytes 442376 | tf_op jit(solution)/shard_map/ppermute | solution.py:59
  21.6 1.1 %shard_map.137 = (f32[64,512]{1,0:T(8,128)S(1)}, f32[64,512]{1,0:T(8,128)S(1)}) custom-call(bf16[64,3712]{1,0:T(8,128)(2,1)S(1)} %shard_map.135.refs_2_.near_ref, bf16[1,7168,512]{2,1,0:T(8,128)(2,1)S(1)} %bitcast.3, bf16[1,7168,512]{2,1,0:T(8,128)(2,1)S(1)} %bitcast.5, bf16[1,512,7168]{2,1,0:T(8,128)(2,1)S(1)} %bitcast.1, ...), custom_call_target="tpu_custom_call" | custom-call | flops 469762048 | bytes 7340032 | tf_op jit(solution)/shard_map/pallas_call | solution.py:224
  22.9 1.7 %shard_map.138 = (bf16[64,512]{1,0:T(8,128)(2,1)S(1)}, f32[32,3584]{1,0:T(8,128)S(1)}, bf16[32,3584]{1,0:T(8,128)(2,1)S(1)}) custom-call(bf16[64,3712]{1,0:T(8,128)(2,1)S(1)} %shard_map.135.refs_2_.near_ref, bf16[64,3712]{1,0:T(8,128)(2,1)S(1)} %collective-permute-done.10.far_ref, bf16[1,7168,512]{2,1,0:T(8,128)(2,1)S(1)} %bitcast.3, ...), custom_call_target="tpu_custom_call" | custom-call | flops 704643072 | bytes 11010048 | tf_op jit(solution)/shard_map/pallas_call | solution.py:238
  24.9 0.7 %shard_map.140 = (f32[32,3584]{1,0:T(8,128)S(1)}, bf16[32,3584]{1,0:T(8,128)(2,1)S(1)}) custom-call(bf16[64,3712]{1,0:T(8,128)(2,1)S(1)} %shard_map.135.refs_2_.near_ref, bf16[64,512]{1,0:T(8,128)(2,1)S(1)} %get-tuple-element.32.inner_ref, bf16[1,512,7168]{2,1,0:T(8,128)(2,1)S(1)} %bitcast.1), custom_call_target="tpu_custom_call" | custom-call | flops 234881024 | bytes 3670016 | tf_op jit(solution)/shard_map/pallas_call | solution.py:256
  25.5 0.4 collective-permute-start.13
  26.0 0.2 collective-permute-done.12.refs_1_
  26.3 0.8 %collective-permute-done.13.refs_2_ = bf16[32,3584]{1,0:T(8,128)(2,1)S(1)} collective-permute-done((bf16[32,3584]{1,0:T(8,128)(2,1)S(1)}, bf16[32,3584]{1,0:T(8,128)(2,1)S(1)}, u32[]{:S(2)}, u32[]{:S(2)}) %collective-permute-start.13) | collective-permute-done | bytes 229408 | tf_op jit(solution)/shard_map/ppermute | solution.py:59
  27.2 2.3 %collective-permute-start.14 = (bf16[8,7168]{1,0:T(8,128)(2,1)S(1)}, bf16[8,7168]{1,0:T(8,128)(2,1)S(1)}, u32[]{:S(2)}, u32[]{:S(2)}) collective-permute-start(bf16[8,7168]{1,0:T(8,128)(2,1)S(1)} %get-tuple-element.36), channel_id=1, source_target_pairs={{0,6},{1,7},{2,4},{3,5},{4,2},{5,3},{6,0},{7,1},{8,14},{9,15},{10,... | collective-permute-start | bytes 344072 | tf_op jit(solution)/shard_map/ppermute | solution.py:59
  29.4 0.5 %collective-permute-start.15 = (bf16[8,7168]{1,0:T(8,128)(2,1)S(1)}, bf16[8,7168]{1,0:T(8,128)(2,1)S(1)}, u32[]{:S(2)}, u32[]{:S(2)}) collective-permute-start(bf16[8,7168]{1,0:T(8,128)(2,1)S(1)} %get-tuple-element.37), channel_id=1, source_target_pairs={{0,4},{1,5},{2,6},{3,7},{4,0},{5,1},{6,2},{7,3},{8,12},{9,13},{10,... | collective-permute-start | bytes 344072 | tf_op jit(solution)/shard_map/ppermute | solution.py:59
  29.9 0.8 %collective-permute-start.16 = (bf16[8,7168]{1,0:T(8,128)(2,1)S(1)}, bf16[8,7168]{1,0:T(8,128)(2,1)S(1)}, u32[]{:S(2)}, u32[]{:S(2)}) collective-permute-start(bf16[8,7168]{1,0:T(8,128)(2,1)S(1)} %get-tuple-element.38), channel_id=1, source_target_pairs={{0,2},{1,3},{2,0},{3,1},{4,6},{5,7},{6,4},{7,5},{8,10},{9,11},{10,... | collective-permute-start | bytes 344072 | tf_op jit(solution)/shard_map/ppermute | solution.py:59
  30.9 2.4 %shard_map.143.refs_4_ = bf16[2,32768]{1,0:T(2,128)(2,1)} custom-call(s32[2]{0:T(128)S(1)} %copy-done.2, s32[2,12]{1,0:T(2,128)S(1)} %copy-done.1, bf16[2,36864]{1,0:T(2,128)(2,1)S(1)} %copy-done, bf16[24,18432]{1,0:T(8,128)(2,1)S(1)} %get-tuple-element.39.pool_ref, bf16[8,18432]{1,0:T(8,128)(2,1)S(1)} %shard_map.142.arrived_ref), custom_call_target="tpu_custom_call" | custom-call | flops 1073741824 | bytes 4194304 | tf_op jit(solution)/shard_map/pallas_call | solution.py:465
  33.3 0.5 %collective-permute-done.14.refs_1_ = bf16[8,7168]{1,0:T(8,128)(2,1)S(1)} collective-permute-done((bf16[8,7168]{1,0:T(8,128)(2,1)S(1)}, bf16[8,7168]{1,0:T(8,128)(2,1)S(1)}, u32[]{:S(2)}, u32[]{:S(2)}) %collective-permute-start.14) | collective-permute-done | bytes 114720 | tf_op jit(solution)/shard_map/ppermute | solution.py:59
  33.7 2.3 %collective-permute-done.15.refs_2_ = bf16[8,7168]{1,0:T(8,128)(2,1)S(1)} collective-permute-done((bf16[8,7168]{1,0:T(8,128)(2,1)S(1)}, bf16[8,7168]{1,0:T(8,128)(2,1)S(1)}, u32[]{:S(2)}, u32[]{:S(2)}) %collective-permute-start.15) | collective-permute-done | bytes 114720 | tf_op jit(solution)/shard_map/ppermute | solution.py:59
  36.1 2.4 %collective-permute-start.17 = (bf16[2,7168]{1,0:T(2,128)(2,1)S(1)}, bf16[2,7168]{1,0:T(2,128)(2,1)S(1)}, u32[]{:S(2)}, u32[]{:S(2)}) collective-permute-start(bf16[2,7168]{1,0:T(2,128)(2,1)S(1)} %get-tuple-element.41), channel_id=1, source_target_pairs={{0,16},{1,17},{2,18},{3,19},{4,20},{5,21},{6,22},{7,23},{8,24},{9,... | collective-permute-start | bytes 86024 | tf_op jit(solution)/shard_map/ppermute | solution.py:59
  38.5 1.4 %collective-permute-start.18 = (bf16[2,7168]{1,0:T(2,128)(2,1)S(1)}, bf16[2,7168]{1,0:T(2,128)(2,1)S(1)}, u32[]{:S(2)}, u32[]{:S(2)}) collective-permute-start(bf16[2,7168]{1,0:T(2,128)(2,1)S(1)} %get-tuple-element.42), channel_id=1, source_target_pairs={{0,24},{1,25},{2,26},{3,27},{4,28},{5,29},{6,30},{7,31},{8,16},{9,... | collective-permute-start | bytes 86024 | tf_op jit(solution)/shard_map/ppermute | solution.py:59
  39.9 1.3 %collective-permute-done.17.refs_1_ = bf16[2,7168]{1,0:T(2,128)(2,1)S(1)} collective-permute-done((bf16[2,7168]{1,0:T(2,128)(2,1)S(1)}, bf16[2,7168]{1,0:T(2,128)(2,1)S(1)}, u32[]{:S(2)}, u32[]{:S(2)}) %collective-permute-start.17) | collective-permute-done | bytes 28704 | tf_op jit(solution)/shard_map/ppermute | solution.py:59
  41.1 3.0 %collective-permute-done.18.refs_2_ = bf16[2,7168]{1,0:T(2,128)(2,1)S(1)} collective-permute-done((bf16[2,7168]{1,0:T(2,128)(2,1)S(1)}, bf16[2,7168]{1,0:T(2,128)(2,1)S(1)}, u32[]{:S(2)}, u32[]{:S(2)}) %collective-permute-start.18) | collective-permute-done | bytes 28704 | tf_op jit(solution)/shard_map/ppermute | solution.py:59
  44.2 0.7 %shard_map.145 = bf16[2,7168]{1,0:T(2,128)(2,1)} custom-call(f32[2,7168]{1,0:T(2,128)S(1)} %get-tuple-element.40.refs_0_, bf16[2,7168]{1,0:T(2,128)(2,1)S(1)} %collective-permute-done.17.refs_1_, bf16[2,7168]{1,0:T(2,128)(2,1)S(1)} %collective-permute-done.18.refs_2_, bf16[2,7168]{1,0:T(2,128)(2,1)S(1)} %collective-permute-done.19.refs_3_), custom_call_target="tpu_custom_call" | custom-call | bytes 114688 | tf_op jit(solution)/shard_map/pallas_call | solution.py:288
  (44 shorter events, 1.5 us)
Async XLA Ops:
  0.6 1.8 %collective-permute-start.1 = (s32[2,4]{1,0:T(2,128)}, s32[2,4]{1,0:T(2,128)S(1)}, u32[]{:S(2)}, u32[]{:S(2)}) collective-permute-start(s32[2,4]{1,0:T(2,128)} %refs_1_.1), channel_id=1, source_target_pairs={{0,1},{1,0},{2,3},{3,2},{4,5},{5,4},{6,7},{7,6},{8,9},{9,8},{10,11... | collective-permute-start | bytes 104 | tf_op jit(solution)/shard_map/ppermute | solution.py:59
  1.1 1.4 %collective-permute-start.2 = (f32[2,4]{1,0:T(2,128)}, f32[2,4]{1,0:T(2,128)S(1)}, u32[]{:S(2)}, u32[]{:S(2)}) collective-permute-start(f32[2,4]{1,0:T(2,128)} %refs_2_.1), channel_id=1, source_target_pairs={{0,1},{1,0},{2,3},{3,2},{4,5},{5,4},{6,7},{7,6},{8,9},{9,8},{10,11... | collective-permute-start | bytes 104 | tf_op jit(solution)/shard_map/ppermute | solution.py:59
  1.2 1.5 %collective-permute-start = (bf16[2,7168]{1,0:T(2,128)(2,1)}, bf16[2,7168]{1,0:T(2,128)(2,1)S(1)}, u32[]{:S(2)}, u32[]{:S(2)}) collective-permute-start(bf16[2,7168]{1,0:T(2,128)(2,1)} %refs_0_.2), channel_id=1, source_target_pairs={{0,1},{1,0},{2,3},{3,2},{4,5},{5,4},{6,7},{7,6},{8,9},{9,8},{10,11... | collective-permute-start | bytes 86024 | tf_op jit(solution)/shard_map/ppermute | solution.py:59
  2.8 8.7 %collective-permute-start.5 = (bf16[4,3712]{1,0:T(4,128)(2,1)S(1)}, bf16[4,3712]{1,0:T(4,128)(2,1)S(1)}, u32[]{:S(2)}, u32[]{:S(2)}) collective-permute-start(bf16[4,3712]{1,0:T(4,128)(2,1)S(1)} %shard_map.132.after_ref.refs_0_), channel_id=1, source_target_pairs={{0,16},{1,17},{2,18},{3,19},{4,20},{5,21},{6,22},{7,23},{8,24},{9,... | collective-permute-start | bytes 89096 | tf_op jit(solution)/shard_map/ppermute | solution.py:59
  6.8 5.7 %collective-permute-start.4 = (bf16[4,3712]{1,0:T(4,128)(2,1)S(1)}, bf16[4,3712]{1,0:T(4,128)(2,1)S(1)}, u32[]{:S(2)}, u32[]{:S(2)}) collective-permute-start(bf16[4,3712]{1,0:T(4,128)(2,1)S(1)} %shard_map.132.after_ref.refs_0_), channel_id=1, source_target_pairs={{0,24},{1,25},{2,26},{3,27},{4,28},{5,29},{6,30},{7,31},{8,16},{9,... | collective-permute-start | bytes 89096 | tf_op jit(solution)/shard_map/ppermute | solution.py:59
  8.2 4.3 %collective-permute-start.3 = (bf16[4,3712]{1,0:T(4,128)(2,1)S(1)}, bf16[4,3712]{1,0:T(4,128)(2,1)S(1)}, u32[]{:S(2)}, u32[]{:S(2)}) collective-permute-start(bf16[4,3712]{1,0:T(4,128)(2,1)S(1)} %shard_map.132.after_ref.refs_0_), channel_id=1, source_target_pairs={{0,8},{1,9},{2,10},{3,11},{4,12},{5,13},{6,14},{7,15},{8,0},{9,1},... | collective-permute-start | bytes 89096 | tf_op jit(solution)/shard_map/ppermute | solution.py:59
  9.9 11.6 %slice-start = ((s8[7340032]{0:T(1024)(128)(4,1)}), s8[4194304]{0:T(1024)(128)(4,1)S(1)}, s32[]{:S(2)}) async-start(s8[7340032]{0:T(1024)(128)(4,1)} %bitcast), calls=%async_computation | async-start | bytes 8388608
  9.9 11.6 %slice-start.2 = ((s8[7340032]{0:T(1024)(128)(4,1)}), s8[4194304]{0:T(1024)(128)(4,1)S(1)}, s32[]{:S(2)}) async-start(s8[7340032]{0:T(1024)(128)(4,1)} %bitcast.2), calls=%async_computation.2 | async-start | bytes 8388608
  9.9 11.6 %slice-start.4 = ((s8[7340032]{0:T(1024)(128)(4,1)}), s8[4194304]{0:T(1024)(128)(4,1)S(1)}, s32[]{:S(2)}) async-start(s8[7340032]{0:T(1024)(128)(4,1)} %bitcast.4), calls=%async_computation.4 | async-start | bytes 8388608
  9.9 11.6 %slice-start.1 = ((s8[7340032]{0:T(1024)(128)(4,1)}), s8[3145728]{0:T(1024)(128)(4,1)S(1)}, s32[]{:S(2)}) async-start(s8[7340032]{0:T(1024)(128)(4,1)} %bitcast), calls=%async_computation.1 | async-start | bytes 6291456
  9.9 11.6 %slice-start.3 = ((s8[7340032]{0:T(1024)(128)(4,1)}), s8[3145728]{0:T(1024)(128)(4,1)S(1)}, s32[]{:S(2)}) async-start(s8[7340032]{0:T(1024)(128)(4,1)} %bitcast.2), calls=%async_computation.3 | async-start | bytes 6291456
  10.0 11.6 %slice-start.5 = ((s8[7340032]{0:T(1024)(128)(4,1)}), s8[3145728]{0:T(1024)(128)(4,1)S(1)}, s32[]{:S(2)}) async-start(s8[7340032]{0:T(1024)(128)(4,1)} %bitcast.4), calls=%async_computation.5 | async-start | bytes 6291456
  10.0 6.2 %collective-permute-start.9 = (bf16[4,18432]{1,0:T(4,128)(2,1)S(1)}, bf16[4,18432]{1,0:T(4,128)(2,1)S(1)}, u32[]{:S(2)}, u32[]{:S(2)}) collective-permute-start(bf16[4,18432]{1,0:T(4,128)(2,1)S(1)} %get-tuple-element.26.refs_4_), channel_id=1, source_target_pairs={{0,2},{1,3},{2,0},{3,1},{4,6},{5,7},{6,4},{7,5},{8,10},{9,11},{10,... | collective-permute-start | bytes 442376 | tf_op jit(solution)/shard_map/ppermute | solution.py:59
  12.6 7.7 %collective-permute-start.8 = (bf16[16,3712]{1,0:T(8,128)(2,1)S(1)}, bf16[16,3712]{1,0:T(8,128)(2,1)S(1)}, u32[]{:S(2)}, u32[]{:S(2)}) collective-permute-start(bf16[16,3712]{1,0:T(8,128)(2,1)S(1)} %shard_map.134.refs_0_), channel_id=1, source_target_pairs={{0,6},{1,7},{2,4},{3,5},{4,2},{5,3},{6,0},{7,1},{8,14},{9,15},{10,... | collective-permute-start | bytes 356360 | tf_op jit(solution)/shard_map/ppermute | solution.py:59
  15.1 5.7 %collective-permute-start.7 = (bf16[16,3712]{1,0:T(8,128)(2,1)S(1)}, bf16[16,3712]{1,0:T(8,128)(2,1)S(1)}, u32[]{:S(2)}, u32[]{:S(2)}) collective-permute-start(bf16[16,3712]{1,0:T(8,128)(2,1)S(1)} %shard_map.134.refs_0_), channel_id=1, source_target_pairs={{0,4},{1,5},{2,6},{3,7},{4,0},{5,1},{6,2},{7,3},{8,12},{9,13},{10,... | collective-permute-start | bytes 356360 | tf_op jit(solution)/shard_map/ppermute | solution.py:59
  15.6 5.2 %collective-permute-start.6 = (bf16[16,3712]{1,0:T(8,128)(2,1)S(1)}, bf16[16,3712]{1,0:T(8,128)(2,1)S(1)}, u32[]{:S(2)}, u32[]{:S(2)}) collective-permute-start(bf16[16,3712]{1,0:T(8,128)(2,1)S(1)} %shard_map.134.refs_0_), channel_id=1, source_target_pairs={{0,2},{1,3},{2,0},{3,1},{4,6},{5,7},{6,4},{7,5},{8,10},{9,11},{10,... | collective-permute-start | bytes 356360 | tf_op jit(solution)/shard_map/ppermute | solution.py:59
  20.8 2.1 %collective-permute-start.10 = (bf16[64,3712]{1,0:T(8,128)(2,1)S(1)}, bf16[64,3712]{1,0:T(8,128)(2,1)S(1)}, u32[]{:S(2)}, u32[]{:S(2)}) collective-permute-start(bf16[64,3712]{1,0:T(8,128)(2,1)S(1)} %shard_map.135.refs_2_.near_ref), channel_id=1, source_target_pairs={{0,1},{1,0},{2,3},{3,2},{4,5},{5,4},{6,7},{7,6},{8,9},{9,8},{10,11... | collective-permute-start | bytes 1425416 | tf_op jit(solution)/shard_map/ppermute | solution.py:59
  21.0 1.9 %collective-permute-start.11 = (bf16[4,18432]{1,0:T(4,128)(2,1)S(1)}, bf16[4,18432]{1,0:T(4,128)(2,1)S(1)}, u32[]{:S(2)}, u32[]{:S(2)}) collective-permute-start(bf16[4,18432]{1,0:T(4,128)(2,1)S(1)} %shard_map.136.refs_1_), channel_id=1, source_target_pairs={{0,1},{1,0},{2,3},{3,2},{4,5},{5,4},{6,7},{7,6},{8,9},{9,8},{10,11... | collective-permute-start | bytes 442376 | tf_op jit(solution)/shard_map/ppermute | solution.py:59
  24.7 1.6 %collective-permute-start.12 = (bf16[32,3584]{1,0:T(8,128)(2,1)S(1)}, bf16[32,3584]{1,0:T(8,128)(2,1)S(1)}, u32[]{:S(2)}, u32[]{:S(2)}) collective-permute-start(bf16[32,3584]{1,0:T(8,128)(2,1)S(1)} %get-tuple-element.31), channel_id=1, source_target_pairs={{0,1},{1,0},{2,3},{3,2},{4,5},{5,4},{6,7},{7,6},{8,9},{9,8},{10,11... | collective-permute-start | bytes 688136 | tf_op jit(solution)/shard_map/ppermute | solution.py:59
  25.5 1.6 %collective-permute-start.13 = (bf16[32,3584]{1,0:T(8,128)(2,1)S(1)}, bf16[32,3584]{1,0:T(8,128)(2,1)S(1)}, u32[]{:S(2)}, u32[]{:S(2)}) collective-permute-start(bf16[32,3584]{1,0:T(8,128)(2,1)S(1)} %get-tuple-element.34), channel_id=1, source_target_pairs={{0,1},{1,0},{2,3},{3,2},{4,5},{5,4},{6,7},{7,6},{8,9},{9,8},{10,11... | collective-permute-start | bytes 688136 | tf_op jit(solution)/shard_map/ppermute | solution.py:59
  26.2 4.7 %copy-start = (bf16[2,36864]{1,0:T(2,128)(2,1)S(1)}, bf16[2,36864]{1,0:T(2,128)(2,1)}, u32[]{:S(2)}) copy-start(bf16[2,36864]{1,0:T(2,128)(2,1)} %query_ref.1) | copy-start | bytes 442372
  26.2 4.7 %copy-start.1 = (s32[2,12]{1,0:T(2,128)S(1)}, s32[2,12]{1,0:T(2,128)}, u32[]{:S(2)}) copy-start(s32[2,12]{1,0:T(2,128)} %table_ref.1) | copy-start | bytes 292
  26.2 4.7 %copy-start.2 = (s32[2]{0:T(128)S(1)}, s32[2]{0:T(128)}, u32[]{:S(2)}) copy-start(s32[2]{0:T(128)} %length_ref.1) | copy-start | bytes 28
  27.2 6.6 %collective-permute-start.14 = (bf16[8,7168]{1,0:T(8,128)(2,1)S(1)}, bf16[8,7168]{1,0:T(8,128)(2,1)S(1)}, u32[]{:S(2)}, u32[]{:S(2)}) collective-permute-start(bf16[8,7168]{1,0:T(8,128)(2,1)S(1)} %get-tuple-element.36), channel_id=1, source_target_pairs={{0,6},{1,7},{2,4},{3,5},{4,2},{5,3},{6,0},{7,1},{8,14},{9,15},{10,... | collective-permute-start | bytes 344072 | tf_op jit(solution)/shard_map/ppermute | solution.py:59
  29.4 6.6 %collective-permute-start.15 = (bf16[8,7168]{1,0:T(8,128)(2,1)S(1)}, bf16[8,7168]{1,0:T(8,128)(2,1)S(1)}, u32[]{:S(2)}, u32[]{:S(2)}) collective-permute-start(bf16[8,7168]{1,0:T(8,128)(2,1)S(1)} %get-tuple-element.37), channel_id=1, source_target_pairs={{0,4},{1,5},{2,6},{3,7},{4,0},{5,1},{6,2},{7,3},{8,12},{9,13},{10,... | collective-permute-start | bytes 344072 | tf_op jit(solution)/shard_map/ppermute | solution.py:59
  29.9 6.1 %collective-permute-start.16 = (bf16[8,7168]{1,0:T(8,128)(2,1)S(1)}, bf16[8,7168]{1,0:T(8,128)(2,1)S(1)}, u32[]{:S(2)}, u32[]{:S(2)}) collective-permute-start(bf16[8,7168]{1,0:T(8,128)(2,1)S(1)} %get-tuple-element.38), channel_id=1, source_target_pairs={{0,2},{1,3},{2,0},{3,1},{4,6},{5,7},{6,4},{7,5},{8,10},{9,11},{10,... | collective-permute-start | bytes 344072 | tf_op jit(solution)/shard_map/ppermute | solution.py:59
  36.1 5.0 %collective-permute-start.17 = (bf16[2,7168]{1,0:T(2,128)(2,1)S(1)}, bf16[2,7168]{1,0:T(2,128)(2,1)S(1)}, u32[]{:S(2)}, u32[]{:S(2)}) collective-permute-start(bf16[2,7168]{1,0:T(2,128)(2,1)S(1)} %get-tuple-element.41), channel_id=1, source_target_pairs={{0,16},{1,17},{2,18},{3,19},{4,20},{5,21},{6,22},{7,23},{8,24},{9,... | collective-permute-start | bytes 86024 | tf_op jit(solution)/shard_map/ppermute | solution.py:59
  38.5 5.7 %collective-permute-start.18 = (bf16[2,7168]{1,0:T(2,128)(2,1)S(1)}, bf16[2,7168]{1,0:T(2,128)(2,1)S(1)}, u32[]{:S(2)}, u32[]{:S(2)}) collective-permute-start(bf16[2,7168]{1,0:T(2,128)(2,1)S(1)} %get-tuple-element.42), channel_id=1, source_target_pairs={{0,24},{1,25},{2,26},{3,27},{4,28},{5,29},{6,30},{7,31},{8,16},{9,... | collective-permute-start | bytes 86024 | tf_op jit(solution)/shard_map/ppermute | solution.py:59
  39.9 4.3 %collective-permute-start.19 = (bf16[2,7168]{1,0:T(2,128)(2,1)S(1)}, bf16[2,7168]{1,0:T(2,128)(2,1)S(1)}, u32[]{:S(2)}, u32[]{:S(2)}) collective-permute-start(bf16[2,7168]{1,0:T(2,128)(2,1)S(1)} %get-tuple-element.43), channel_id=1, source_target_pairs={{0,8},{1,9},{2,10},{3,11},{4,12},{5,13},{6,14},{7,15},{8,0},{9,1},... | collective-permute-start | bytes 86024 | tf_op jit(solution)/shard_map/ppermute | solution.py:59

commit v10 on v9

--- a/solution.py
+++ b/solution.py
@@ -296,15 +296,13 @@
 
 
 def pages_kernel(
-    dp_count, page_hbm, dest_hbm, pool_ref, after_ref, low_ref, high_ref, copy_ref, page_ref, dest_ref, sems
+    dp_count, page_hbm, dest_hbm, pool_ref, after_ref, low_ref, high_ref, page_ref, dest_ref, sems
 ):
     own, width = pool_ref.shape
-    pool_copy = pltpu.make_async_copy(pool_ref, copy_ref, sems.at[0])
-    page_copy = pltpu.make_async_copy(page_hbm, page_ref, sems.at[1])
-    dest_copy = pltpu.make_async_copy(dest_hbm, dest_ref, sems.at[2])
+    page_copy = pltpu.make_async_copy(page_hbm, page_ref, sems.at[0])
+    dest_copy = pltpu.make_async_copy(dest_hbm, dest_ref, sems.at[1])
     page_copy.start()
     dest_copy.start()
-    pool_copy.start()
     page_copy.wait()
     dest_copy.wait()
     me = lax.axis_index("dp")
@@ -321,10 +319,9 @@
         pick = jnp.where((row == bucket) & (column == page_ref[0, m]), 1.0, pick)
     pick = pick.astype(bf16)
     step = 2048
-    pool_copy.wait()
     for i in range(width // step):
         columns = slice(i * step, (i + 1) * step)
-        out = jnp.dot(pick, copy_ref[:, columns], preferred_element_type=f32)
+        out = jnp.dot(pick, pool_ref[:, columns], preferred_element_type=f32)
         low_ref[:, columns] = out[: slots // 2].astype(bf16)
         high_ref[:, columns] = out[slots // 2 :].astype(bf16)
 
@@ -334,17 +331,17 @@
     half = pltpu.VMEM((dp_count * MCAP // 2, width), bf16)
     return pl.pallas_call(
         functools.partial(pages_kernel, dp_count),
-        out_shape=(half, half, pltpu.VMEM(latent_pool.shape, bf16)),
-        in_specs=[in_hbm()] * 3 + [anywhere()],
-        out_specs=(in_vmem(),) * 3,
+        out_shape=(half, half),
+        in_specs=[in_hbm()] * 2 + [in_vmem(), anywhere()],
+        out_specs=(in_vmem(),) * 2,
         scratch_shapes=[
             pltpu.SMEM(moved_page.shape, jnp.int32),
             pltpu.SMEM(moved_dest.shape, jnp.int32),
-            pltpu.SemaphoreType.DMA((3,)),
+            pltpu.SemaphoreType.DMA((2,)),
         ],
         compiler_params=pltpu.CompilerParams(vmem_limit_bytes=4 * MIB),
         cost_estimate=pl.CostEstimate(flops=0, bytes_accessed=4 * latent_pool.size, transcendentals=0),
-    )(hbm(moved_page), hbm(moved_dest), hbm(latent_pool), after)
+    )(hbm(moved_page), hbm(moved_dest), vmem(latent_pool), after)
 
 
 def rows_kernel(places, *refs):
@@ -497,12 +494,13 @@
 
     mine = (hidden, routes, route_weight)
     got = [trade(x, 1) for x in mine]
-    near = make_payload(fetch(*mine), got, ep_count)
+    *mine, pool = fetch(*mine, latent_pool)
+    near = make_payload(mine, got, ep_count)
     for number, partners in enumerate(stages):
         got = [trade(near, bit) for bit in partners]
         after = []
         if number == 0:
-            low, high, pool = pick_pages(moved_page, moved_dest, latent_pool, near, dp_count)
+            low, high = pick_pages(moved_page, moved_dest, pool, near, dp_count)
             after = [high]
             bit = partner_bits(dp_count)[0]
             first = swap(high, "dp", pairs_of(dp_count, bit))

time: 45 us -> 44.8 us (level)
    pallas_call x1, Pallas kernels: 1.49 us -> 1.02 us  [pick_pages(): pl.pallas_call(functools.partial(pages_kernel, dp_count), out_shape=(half...]
    pallas_call x1, Pallas kernels: 0.78 us -> 1.25 us  [fetch(): pl.pallas_call(fetch_kernel, out_shape=tuple((pltpu.VMEM(x.shape, x.dtype...]
    ppermute x20, starting transfers between devices: 20.3 us -> 19.9 us  [swap(): return lax.ppermute(x, axes, pairs)]
  transfers between devices with their start and end apart: 20 -> 20, of which waited for: 11 -> 10; matrix products, arithmetic and copies ran while one was open for 0% -> 0% of each run, Pallas kernels for 15% -> 15%
where the time goes in v10:
time: 44.8 us; the launch traced here: 44.6 us
  starting transfers between devices  19.9 us (44%)
  waiting for transfers between devices  14.4 us (32%)
  Pallas kernels  9.46 us (21%)
  between operations  0.87 us (2%)
    ppermute x20, starting transfers between devices, swap(): return lax.ppermute(x, axes, pairs)  19.9 us
    ppermute x20, waiting for transfers between devices, swap(): return lax.ppermute(x, axes, pairs)  14.4 us
    pallas_call x1, Pallas kernels, attend(): pl.pallas_call(functools.partial(attend_kernel, senders), out_shape=jax.S...  2.35 us
    pallas_call x1, Pallas kernels, far_products(): pl.pallas_call(functools.partial(far_kernel, ep_count), out_shape=(pltpu....  1.74 us
    pallas_call x1, Pallas kernels, fetch(): pl.pallas_call(fetch_kernel, out_shape=tuple((pltpu.VMEM(x.shape, x.dtype...  1.25 us
    pallas_call x1, Pallas kernels, near_products(): pl.pallas_call(near_kernel, out_shape=(acc, acc), in_specs=[in_vmem()] *...  1.13 us
    pallas_call x1, Pallas kernels, pick_pages(): pl.pallas_call(functools.partial(pages_kernel, dp_count), out_shape=(half...  1.02 us
  transfers between devices with their start and end apart: 20, of which 10 were waited for; matrix products, arithmetic and copies ran while one was open for 0% of the time, Pallas kernels for 15%

profile of v10, /device:TPU:0, one launch (start us, length us, event | category | flops | bytes accessed | tf_op | source)
XLA Modules:
  0.0 44.6 jit_solution(9951111753849807073)
XLA Ops:
  0.6 0.5 %collective-permute-start.1 = (s32[2,4]{1,0:T(2,128)}, s32[2,4]{1,0:T(2,128)S(1)}, u32[]{:S(2)}, u32[]{:S(2)}) collective-permute-start(s32[2,4]{1,0:T(2,128)} %refs_1_.1), channel_id=1, source_target_pairs={{0,1},{1,0},{2,3},{3,2},{4,5},{5,4},{6,7},{7,6},{8,9},{9,8},{10,11... | collective-permute-start | bytes 104 | tf_op jit(solution)/shard_map/ppermute | solution.py:59
  1.2 0.4 collective-permute-start
  1.7 1.3 %shard_map.131 = (bf16[2,7168]{1,0:T(2,128)(2,1)S(1)}, s32[2,4]{1,0:T(2,128)S(1)}, f32[2,4]{1,0:T(2,128)S(1)}, bf16[24,18432]{1,0:T(8,128)(2,1)S(1)}) custom-call(bf16[2,7168]{1,0:T(2,128)(2,1)} %refs_0_.2, s32[2,4]{1,0:T(2,128)} %refs_1_.1, f32[2,4]{1,0:T(2,128)} %refs_2_.1, bf16[24,18432]{1,0:T(8,128)(2,1)} %refs_3_.1), custom_call_target="tpu_custom_call" | custom-call | flops 1250000000 | bytes 1048576 | tf_op jit(solution)/shard_map/pallas_call | solution.py:86
  3.1 3.8 %collective-permute-start.5 = (bf16[4,3712]{1,0:T(4,128)(2,1)S(1)}, bf16[4,3712]{1,0:T(4,128)(2,1)S(1)}, u32[]{:S(2)}, u32[]{:S(2)}) collective-permute-start(bf16[4,3712]{1,0:T(4,128)(2,1)S(1)} %shard_map.132.after_ref.refs_0_), channel_id=1, source_target_pairs={{0,16},{1,17},{2,18},{3,19},{4,20},{5,21},{6,22},{7,23},{8,24},{9,... | collective-permute-start | bytes 89096 | tf_op jit(solution)/shard_map/ppermute | solution.py:59
  6.8 1.3 %collective-permute-start.4 = (bf16[4,3712]{1,0:T(4,128)(2,1)S(1)}, bf16[4,3712]{1,0:T(4,128)(2,1)S(1)}, u32[]{:S(2)}, u32[]{:S(2)}) collective-permute-start(bf16[4,3712]{1,0:T(4,128)(2,1)S(1)} %shard_map.132.after_ref.refs_0_), channel_id=1, source_target_pairs={{0,24},{1,25},{2,26},{3,27},{4,28},{5,29},{6,30},{7,31},{8,16},{9,... | collective-permute-start | bytes 89096 | tf_op jit(solution)/shard_map/ppermute | solution.py:59
  8.2 0.2 collective-permute-start.3
  8.4 1.0 %shard_map.133 = (bf16[4,18432]{1,0:T(4,128)(2,1)S(1)}, bf16[4,18432]{1,0:T(4,128)(2,1)S(1)}) custom-call(s32[1,6]{1,0:T(1,128)} %page_hbm.1, s32[1,6]{1,0:T(1,128)} %dest_hbm.1, bf16[24,18432]{1,0:T(8,128)(2,1)S(1)} %get-tuple-element.26.pool_ref, bf16[4,3712]{1,0:T(4,128)(2,1)S(1)} %shard_map.132.after_ref.refs_0_), custom_call_target="tpu_custom_call" | custom-call | bytes 1769472 | tf_op jit(solution)/shard_map/pallas_call | solution.py:332
  9.5 1.6 %collective-permute-start.9 = (bf16[4,18432]{1,0:T(4,128)(2,1)S(1)}, bf16[4,18432]{1,0:T(4,128)(2,1)S(1)}, u32[]{:S(2)}, u32[]{:S(2)}) collective-permute-start(bf16[4,18432]{1,0:T(4,128)(2,1)S(1)} %get-tuple-element.27.refs_4_), channel_id=1, source_target_pairs={{0,2},{1,3},{2,0},{3,1},{4,6},{5,7},{6,4},{7,5},{8,10},{9,11},{10,... | collective-permute-start | bytes 442376 | tf_op jit(solution)/shard_map/ppermute | solution.py:59
  11.0 1.4 %collective-permute-done.4.refs_2_ = bf16[4,3712]{1,0:T(4,128)(2,1)S(1)} collective-permute-done((bf16[4,3712]{1,0:T(4,128)(2,1)S(1)}, bf16[4,3712]{1,0:T(4,128)(2,1)S(1)}, u32[]{:S(2)}, u32[]{:S(2)}) %collective-permute-start.4) | collective-permute-done | bytes 29728 | tf_op jit(solution)/shard_map/ppermute | solution.py:59
  12.6 2.5 %collective-permute-start.8 = (bf16[16,3712]{1,0:T(8,128)(2,1)S(1)}, bf16[16,3712]{1,0:T(8,128)(2,1)S(1)}, u32[]{:S(2)}, u32[]{:S(2)}) collective-permute-start(bf16[16,3712]{1,0:T(8,128)(2,1)S(1)} %shard_map.134.refs_0_), channel_id=1, source_target_pairs={{0,6},{1,7},{2,4},{3,5},{4,2},{5,3},{6,0},{7,1},{8,14},{9,15},{10,... | collective-permute-start | bytes 356360 | tf_op jit(solution)/shard_map/ppermute | solution.py:59
  15.1 0.5 %collective-permute-start.7 = (bf16[16,3712]{1,0:T(8,128)(2,1)S(1)}, bf16[16,3712]{1,0:T(8,128)(2,1)S(1)}, u32[]{:S(2)}, u32[]{:S(2)}) collective-permute-start(bf16[16,3712]{1,0:T(8,128)(2,1)S(1)} %shard_map.134.refs_0_), channel_id=1, source_target_pairs={{0,4},{1,5},{2,6},{3,7},{4,0},{5,1},{6,2},{7,3},{8,12},{9,13},{10,... | collective-permute-start | bytes 356360 | tf_op jit(solution)/shard_map/ppermute | solution.py:59
  15.6 0.5 %collective-permute-start.6 = (bf16[16,3712]{1,0:T(8,128)(2,1)S(1)}, bf16[16,3712]{1,0:T(8,128)(2,1)S(1)}, u32[]{:S(2)}, u32[]{:S(2)}) collective-permute-start(bf16[16,3712]{1,0:T(8,128)(2,1)S(1)} %shard_map.134.refs_0_), channel_id=1, source_target_pairs={{0,2},{1,3},{2,0},{3,1},{4,6},{5,7},{6,4},{7,5},{8,10},{9,11},{10,... | collective-permute-start | bytes 356360 | tf_op jit(solution)/shard_map/ppermute | solution.py:59
  16.1 3.5 %collective-permute-done.8.refs_3_ = bf16[16,3712]{1,0:T(8,128)(2,1)S(1)} collective-permute-done((bf16[16,3712]{1,0:T(8,128)(2,1)S(1)}, bf16[16,3712]{1,0:T(8,128)(2,1)S(1)}, u32[]{:S(2)}, u32[]{:S(2)}) %collective-permute-start.8) | collective-permute-done | bytes 118816 | tf_op jit(solution)/shard_map/ppermute | solution.py:59
  19.6 1.2 %collective-permute-done.7.refs_2_ = bf16[16,3712]{1,0:T(8,128)(2,1)S(1)} collective-permute-done((bf16[16,3712]{1,0:T(8,128)(2,1)S(1)}, bf16[16,3712]{1,0:T(8,128)(2,1)S(1)}, u32[]{:S(2)}, u32[]{:S(2)}) %collective-permute-start.7) | collective-permute-done | bytes 118816 | tf_op jit(solution)/shard_map/ppermute | solution.py:59
  21.1 0.6 %collective-permute-start.11 = (bf16[4,18432]{1,0:T(4,128)(2,1)S(1)}, bf16[4,18432]{1,0:T(4,128)(2,1)S(1)}, u32[]{:S(2)}, u32[]{:S(2)}) collective-permute-start(bf16[4,18432]{1,0:T(4,128)(2,1)S(1)} %shard_map.136.refs_1_), channel_id=1, source_target_pairs={{0,1},{1,0},{2,3},{3,2},{4,5},{5,4},{6,7},{7,6},{8,9},{9,8},{10,11... | collective-permute-start | bytes 442376 | tf_op jit(solution)/shard_map/ppermute | solution.py:59
  21.7 1.1 %shard_map.137 = (f32[64,512]{1,0:T(8,128)S(1)}, f32[64,512]{1,0:T(8,128)S(1)}) custom-call(bf16[64,3712]{1,0:T(8,128)(2,1)S(1)} %shard_map.135.refs_2_.near_ref, bf16[1,7168,512]{2,1,0:T(8,128)(2,1)S(1)} %bitcast.3, bf16[1,7168,512]{2,1,0:T(8,128)(2,1)S(1)} %bitcast.5, bf16[1,512,7168]{2,1,0:T(8,128)(2,1)S(1)} %bitcast.1, ...), custom_call_target="tpu_custom_call" | custom-call | flops 469762048 | bytes 7340032 | tf_op jit(solution)/shard_map/pallas_call | solution.py:224
  23.0 1.7 %shard_map.138 = (bf16[64,512]{1,0:T(8,128)(2,1)S(1)}, f32[32,3584]{1,0:T(8,128)S(1)}, bf16[32,3584]{1,0:T(8,128)(2,1)S(1)}) custom-call(bf16[64,3712]{1,0:T(8,128)(2,1)S(1)} %shard_map.135.refs_2_.near_ref, bf16[64,3712]{1,0:T(8,128)(2,1)S(1)} %collective-permute-done.10.far_ref, bf16[1,7168,512]{2,1,0:T(8,128)(2,1)S(1)} %bitcast.3, ...), custom_call_target="tpu_custom_call" | custom-call | flops 704643072 | bytes 11010048 | tf_op jit(solution)/shard_map/pallas_call | solution.py:238
  25.0 0.7 %shard_map.140 = (f32[32,3584]{1,0:T(8,128)S(1)}, bf16[32,3584]{1,0:T(8,128)(2,1)S(1)}) custom-call(bf16[64,3712]{1,0:T(8,128)(2,1)S(1)} %shard_map.135.refs_2_.near_ref, bf16[64,512]{1,0:T(8,128)(2,1)S(1)} %get-tuple-element.33.inner_ref, bf16[1,512,7168]{2,1,0:T(8,128)(2,1)S(1)} %bitcast.1), custom_call_target="tpu_custom_call" | custom-call | flops 234881024 | bytes 3670016 | tf_op jit(solution)/shard_map/pallas_call | solution.py:256
  25.7 0.4 collective-permute-start.13
  26.1 0.2 collective-permute-done.12.refs_1_
  26.4 0.8 %collective-permute-done.13.refs_2_ = bf16[32,3584]{1,0:T(8,128)(2,1)S(1)} collective-permute-done((bf16[32,3584]{1,0:T(8,128)(2,1)S(1)}, bf16[32,3584]{1,0:T(8,128)(2,1)S(1)}, u32[]{:S(2)}, u32[]{:S(2)}) %collective-permute-start.13) | collective-permute-done | bytes 229408 | tf_op jit(solution)/shard_map/ppermute | solution.py:59
  27.3 1.9 %collective-permute-start.14 = (bf16[8,7168]{1,0:T(8,128)(2,1)S(1)}, bf16[8,7168]{1,0:T(8,128)(2,1)S(1)}, u32[]{:S(2)}, u32[]{:S(2)}) collective-permute-start(bf16[8,7168]{1,0:T(8,128)(2,1)S(1)} %get-tuple-element.37), channel_id=1, source_target_pairs={{0,6},{1,7},{2,4},{3,5},{4,2},{5,3},{6,0},{7,1},{8,14},{9,15},{10,... | collective-permute-start | bytes 344072 | tf_op jit(solution)/shard_map/ppermute | solution.py:59
  29.2 0.7 %collective-permute-start.15 = (bf16[8,7168]{1,0:T(8,128)(2,1)S(1)}, bf16[8,7168]{1,0:T(8,128)(2,1)S(1)}, u32[]{:S(2)}, u32[]{:S(2)}) collective-permute-start(bf16[8,7168]{1,0:T(8,128)(2,1)S(1)} %get-tuple-element.38), channel_id=1, source_target_pairs={{0,4},{1,5},{2,6},{3,7},{4,0},{5,1},{6,2},{7,3},{8,12},{9,13},{10,... | collective-permute-start | bytes 344072 | tf_op jit(solution)/shard_map/ppermute | solution.py:59
  29.8 1.0 %collective-permute-start.16 = (bf16[8,7168]{1,0:T(8,128)(2,1)S(1)}, bf16[8,7168]{1,0:T(8,128)(2,1)S(1)}, u32[]{:S(2)}, u32[]{:S(2)}) collective-permute-start(bf16[8,7168]{1,0:T(8,128)(2,1)S(1)} %get-tuple-element.39), channel_id=1, source_target_pairs={{0,2},{1,3},{2,0},{3,1},{4,6},{5,7},{6,4},{7,5},{8,10},{9,11},{10,... | collective-permute-start | bytes 344072 | tf_op jit(solution)/shard_map/ppermute | solution.py:59
  31.1 2.4 %shard_map.143.refs_4_ = bf16[2,32768]{1,0:T(2,128)(2,1)} custom-call(s32[2]{0:T(128)S(1)} %copy-done.2, s32[2,12]{1,0:T(2,128)S(1)} %copy-done.1, bf16[2,36864]{1,0:T(2,128)(2,1)S(1)} %copy-done, bf16[24,18432]{1,0:T(8,128)(2,1)S(1)} %get-tuple-element.26.pool_ref, bf16[8,18432]{1,0:T(8,128)(2,1)S(1)} %shard_map.142.arrived_ref), custom_call_target="tpu_custom_call" | custom-call | flops 1073741824 | bytes 4194304 | tf_op jit(solution)/shard_map/pallas_call | solution.py:462
  33.4 0.8 %collective-permute-done.14.refs_1_ = bf16[8,7168]{1,0:T(8,128)(2,1)S(1)} collective-permute-done((bf16[8,7168]{1,0:T(8,128)(2,1)S(1)}, bf16[8,7168]{1,0:T(8,128)(2,1)S(1)}, u32[]{:S(2)}, u32[]{:S(2)}) %collective-permute-start.14) | collective-permute-done | bytes 114720 | tf_op jit(solution)/shard_map/ppermute | solution.py:59
  34.2 1.9 %collective-permute-done.15.refs_2_ = bf16[8,7168]{1,0:T(8,128)(2,1)S(1)} collective-permute-done((bf16[8,7168]{1,0:T(8,128)(2,1)S(1)}, bf16[8,7168]{1,0:T(8,128)(2,1)S(1)}, u32[]{:S(2)}, u32[]{:S(2)}) %collective-permute-start.15) | collective-permute-done | bytes 114720 | tf_op jit(solution)/shard_map/ppermute | solution.py:59
  36.2 2.0 %collective-permute-start.17 = (bf16[2,7168]{1,0:T(2,128)(2,1)S(1)}, bf16[2,7168]{1,0:T(2,128)(2,1)S(1)}, u32[]{:S(2)}, u32[]{:S(2)}) collective-permute-start(bf16[2,7168]{1,0:T(2,128)(2,1)S(1)} %get-tuple-element.41), channel_id=1, source_target_pairs={{0,16},{1,17},{2,18},{3,19},{4,20},{5,21},{6,22},{7,23},{8,24},{9,... | collective-permute-start | bytes 86024 | tf_op jit(solution)/shard_map/ppermute | solution.py:59
  38.3 1.3 %collective-permute-start.18 = (bf16[2,7168]{1,0:T(2,128)(2,1)S(1)}, bf16[2,7168]{1,0:T(2,128)(2,1)S(1)}, u32[]{:S(2)}, u32[]{:S(2)}) collective-permute-start(bf16[2,7168]{1,0:T(2,128)(2,1)S(1)} %get-tuple-element.42), channel_id=1, source_target_pairs={{0,24},{1,25},{2,26},{3,27},{4,28},{5,29},{6,30},{7,31},{8,16},{9,... | collective-permute-start | bytes 86024 | tf_op jit(solution)/shard_map/ppermute | solution.py:59
  39.8 1.8 %collective-permute-done.17.refs_1_ = bf16[2,7168]{1,0:T(2,128)(2,1)S(1)} collective-permute-done((bf16[2,7168]{1,0:T(2,128)(2,1)S(1)}, bf16[2,7168]{1,0:T(2,128)(2,1)S(1)}, u32[]{:S(2)}, u32[]{:S(2)}) %collective-permute-start.17) | collective-permute-done | bytes 28704 | tf_op jit(solution)/shard_map/ppermute | solution.py:59
  41.6 2.3 %collective-permute-done.18.refs_2_ = bf16[2,7168]{1,0:T(2,128)(2,1)S(1)} collective-permute-done((bf16[2,7168]{1,0:T(2,128)(2,1)S(1)}, bf16[2,7168]{1,0:T(2,128)(2,1)S(1)}, u32[]{:S(2)}, u32[]{:S(2)}) %collective-permute-start.18) | collective-permute-done | bytes 28704 | tf_op jit(solution)/shard_map/ppermute | solution.py:59
  43.9 0.7 %shard_map.145 = bf16[2,7168]{1,0:T(2,128)(2,1)} custom-call(f32[2,7168]{1,0:T(2,128)S(1)} %get-tuple-element.40.refs_0_, bf16[2,7168]{1,0:T(2,128)(2,1)S(1)} %collective-permute-done.17.refs_1_, bf16[2,7168]{1,0:T(2,128)(2,1)S(1)} %collective-permute-done.18.refs_2_, bf16[2,7168]{1,0:T(2,128)(2,1)S(1)} %collective-permute-done.19.refs_3_), custom_call_target="tpu_custom_call" | custom-call | bytes 114688 | tf_op jit(solution)/shard_map/pallas_call | solution.py:288
  (44 shorter events, 1.4 us)
Async XLA Ops:
  0.6 2.3 %collective-permute-start.1 = (s32[2,4]{1,0:T(2,128)}, s32[2,4]{1,0:T(2,128)S(1)}, u32[]{:S(2)}, u32[]{:S(2)}) collective-permute-start(s32[2,4]{1,0:T(2,128)} %refs_1_.1), channel_id=1, source_target_pairs={{0,1},{1,0},{2,3},{3,2},{4,5},{5,4},{6,7},{7,6},{8,9},{9,8},{10,11... | collective-permute-start | bytes 104 | tf_op jit(solution)/shard_map/ppermute | solution.py:59
  1.1 1.8 %collective-permute-start.2 = (f32[2,4]{1,0:T(2,128)}, f32[2,4]{1,0:T(2,128)S(1)}, u32[]{:S(2)}, u32[]{:S(2)}) collective-permute-start(f32[2,4]{1,0:T(2,128)} %refs_2_.1), channel_id=1, source_target_pairs={{0,1},{1,0},{2,3},{3,2},{4,5},{5,4},{6,7},{7,6},{8,9},{9,8},{10,11... | collective-permute-start | bytes 104 | tf_op jit(solution)/shard_map/ppermute | solution.py:59
  1.2 1.7 %collective-permute-start = (bf16[2,7168]{1,0:T(2,128)(2,1)}, bf16[2,7168]{1,0:T(2,128)(2,1)S(1)}, u32[]{:S(2)}, u32[]{:S(2)}) collective-permute-start(bf16[2,7168]{1,0:T(2,128)(2,1)} %refs_0_.2), channel_id=1, source_target_pairs={{0,1},{1,0},{2,3},{3,2},{4,5},{5,4},{6,7},{7,6},{8,9},{9,8},{10,11... | collective-permute-start | bytes 86024 | tf_op jit(solution)/shard_map/ppermute | solution.py:59
  3.1 8.0 %collective-permute-start.5 = (bf16[4,3712]{1,0:T(4,128)(2,1)S(1)}, bf16[4,3712]{1,0:T(4,128)(2,1)S(1)}, u32[]{:S(2)}, u32[]{:S(2)}) collective-permute-start(bf16[4,3712]{1,0:T(4,128)(2,1)S(1)} %shard_map.132.after_ref.refs_0_), channel_id=1, source_target_pairs={{0,16},{1,17},{2,18},{3,19},{4,20},{5,21},{6,22},{7,23},{8,24},{9,... | collective-permute-start | bytes 89096 | tf_op jit(solution)/shard_map/ppermute | solution.py:59
  6.8 5.7 %collective-permute-start.4 = (bf16[4,3712]{1,0:T(4,128)(2,1)S(1)}, bf16[4,3712]{1,0:T(4,128)(2,1)S(1)}, u32[]{:S(2)}, u32[]{:S(2)}) collective-permute-start(bf16[4,3712]{1,0:T(4,128)(2,1)S(1)} %shard_map.132.after_ref.refs_0_), channel_id=1, source_target_pairs={{0,24},{1,25},{2,26},{3,27},{4,28},{5,29},{6,30},{7,31},{8,16},{9,... | collective-permute-start | bytes 89096 | tf_op jit(solution)/shard_map/ppermute | solution.py:59
  8.2 4.3 %collective-permute-start.3 = (bf16[4,3712]{1,0:T(4,128)(2,1)S(1)}, bf16[4,3712]{1,0:T(4,128)(2,1)S(1)}, u32[]{:S(2)}, u32[]{:S(2)}) collective-permute-start(bf16[4,3712]{1,0:T(4,128)(2,1)S(1)} %shard_map.132.after_ref.refs_0_), channel_id=1, source_target_pairs={{0,8},{1,9},{2,10},{3,11},{4,12},{5,13},{6,14},{7,15},{8,0},{9,1},... | collective-permute-start | bytes 89096 | tf_op jit(solution)/shard_map/ppermute | solution.py:59
  9.4 12.3 %slice-start = ((s8[7340032]{0:T(1024)(128)(4,1)}), s8[4194304]{0:T(1024)(128)(4,1)S(1)}, s32[]{:S(2)}) async-start(s8[7340032]{0:T(1024)(128)(4,1)} %bitcast), calls=%async_computation | async-start | bytes 8388608
  9.4 12.2 %slice-start.2 = ((s8[7340032]{0:T(1024)(128)(4,1)}), s8[4194304]{0:T(1024)(128)(4,1)S(1)}, s32[]{:S(2)}) async-start(s8[7340032]{0:T(1024)(128)(4,1)} %bitcast.2), calls=%async_computation.2 | async-start | bytes 8388608
  9.4 12.2 %slice-start.4 = ((s8[7340032]{0:T(1024)(128)(4,1)}), s8[4194304]{0:T(1024)(128)(4,1)S(1)}, s32[]{:S(2)}) async-start(s8[7340032]{0:T(1024)(128)(4,1)} %bitcast.4), calls=%async_computation.4 | async-start | bytes 8388608
  9.5 12.2 %slice-start.1 = ((s8[7340032]{0:T(1024)(128)(4,1)}), s8[3145728]{0:T(1024)(128)(4,1)S(1)}, s32[]{:S(2)}) async-start(s8[7340032]{0:T(1024)(128)(4,1)} %bitcast), calls=%async_computation.1 | async-start | bytes 6291456
  9.5 12.2 %slice-start.3 = ((s8[7340032]{0:T(1024)(128)(4,1)}), s8[3145728]{0:T(1024)(128)(4,1)S(1)}, s32[]{:S(2)}) async-start(s8[7340032]{0:T(1024)(128)(4,1)} %bitcast.2), calls=%async_computation.3 | async-start | bytes 6291456
  9.5 12.2 %slice-start.5 = ((s8[7340032]{0:T(1024)(128)(4,1)}), s8[3145728]{0:T(1024)(128)(4,1)S(1)}, s32[]{:S(2)}) async-start(s8[7340032]{0:T(1024)(128)(4,1)} %bitcast.4), calls=%async_computation.5 | async-start | bytes 6291456
  9.5 6.6 %collective-permute-start.9 = (bf16[4,18432]{1,0:T(4,128)(2,1)S(1)}, bf16[4,18432]{1,0:T(4,128)(2,1)S(1)}, u32[]{:S(2)}, u32[]{:S(2)}) collective-permute-start(bf16[4,18432]{1,0:T(4,128)(2,1)S(1)} %get-tuple-element.27.refs_4_), channel_id=1, source_target_pairs={{0,2},{1,3},{2,0},{3,1},{4,6},{5,7},{6,4},{7,5},{8,10},{9,11},{10,... | collective-permute-start | bytes 442376 | tf_op jit(solution)/shard_map/ppermute | solution.py:59
  12.6 7.1 %collective-permute-start.8 = (bf16[16,3712]{1,0:T(8,128)(2,1)S(1)}, bf16[16,3712]{1,0:T(8,128)(2,1)S(1)}, u32[]{:S(2)}, u32[]{:S(2)}) collective-permute-start(bf16[16,3712]{1,0:T(8,128)(2,1)S(1)} %shard_map.134.refs_0_), channel_id=1, source_target_pairs={{0,6},{1,7},{2,4},{3,5},{4,2},{5,3},{6,0},{7,1},{8,14},{9,15},{10,... | collective-permute-start | bytes 356360 | tf_op jit(solution)/shard_map/ppermute | solution.py:59
  15.1 5.8 %collective-permute-start.7 = (bf16[16,3712]{1,0:T(8,128)(2,1)S(1)}, bf16[16,3712]{1,0:T(8,128)(2,1)S(1)}, u32[]{:S(2)}, u32[]{:S(2)}) collective-permute-start(bf16[16,3712]{1,0:T(8,128)(2,1)S(1)} %shard_map.134.refs_0_), channel_id=1, source_target_pairs={{0,4},{1,5},{2,6},{3,7},{4,0},{5,1},{6,2},{7,3},{8,12},{9,13},{10,... | collective-permute-start | bytes 356360 | tf_op jit(solution)/shard_map/ppermute | solution.py:59
  15.6 5.3 %collective-permute-start.6 = (bf16[16,3712]{1,0:T(8,128)(2,1)S(1)}, bf16[16,3712]{1,0:T(8,128)(2,1)S(1)}, u32[]{:S(2)}, u32[]{:S(2)}) collective-permute-start(bf16[16,3712]{1,0:T(8,128)(2,1)S(1)} %shard_map.134.refs_0_), channel_id=1, source_target_pairs={{0,2},{1,3},{2,0},{3,1},{4,6},{5,7},{6,4},{7,5},{8,10},{9,11},{10,... | collective-permute-start | bytes 356360 | tf_op jit(solution)/shard_map/ppermute | solution.py:59
  20.9 2.1 %collective-permute-start.10 = (bf16[64,3712]{1,0:T(8,128)(2,1)S(1)}, bf16[64,3712]{1,0:T(8,128)(2,1)S(1)}, u32[]{:S(2)}, u32[]{:S(2)}) collective-permute-start(bf16[64,3712]{1,0:T(8,128)(2,1)S(1)} %shard_map.135.refs_2_.near_ref), channel_id=1, source_target_pairs={{0,1},{1,0},{2,3},{3,2},{4,5},{5,4},{6,7},{7,6},{8,9},{9,8},{10,11... | collective-permute-start | bytes 1425416 | tf_op jit(solution)/shard_map/ppermute | solution.py:59
  21.1 1.9 %collective-permute-start.11 = (bf16[4,18432]{1,0:T(4,128)(2,1)S(1)}, bf16[4,18432]{1,0:T(4,128)(2,1)S(1)}, u32[]{:S(2)}, u32[]{:S(2)}) collective-permute-start(bf16[4,18432]{1,0:T(4,128)(2,1)S(1)} %shard_map.136.refs_1_), channel_id=1, source_target_pairs={{0,1},{1,0},{2,3},{3,2},{4,5},{5,4},{6,7},{7,6},{8,9},{9,8},{10,11... | collective-permute-start | bytes 442376 | tf_op jit(solution)/shard_map/ppermute | solution.py:59
  24.8 1.6 %collective-permute-start.12 = (bf16[32,3584]{1,0:T(8,128)(2,1)S(1)}, bf16[32,3584]{1,0:T(8,128)(2,1)S(1)}, u32[]{:S(2)}, u32[]{:S(2)}) collective-permute-start(bf16[32,3584]{1,0:T(8,128)(2,1)S(1)} %get-tuple-element.32), channel_id=1, source_target_pairs={{0,1},{1,0},{2,3},{3,2},{4,5},{5,4},{6,7},{7,6},{8,9},{9,8},{10,11... | collective-permute-start | bytes 688136 | tf_op jit(solution)/shard_map/ppermute | solution.py:59
  25.7 1.6 %collective-permute-start.13 = (bf16[32,3584]{1,0:T(8,128)(2,1)S(1)}, bf16[32,3584]{1,0:T(8,128)(2,1)S(1)}, u32[]{:S(2)}, u32[]{:S(2)}) collective-permute-start(bf16[32,3584]{1,0:T(8,128)(2,1)S(1)} %get-tuple-element.35), channel_id=1, source_target_pairs={{0,1},{1,0},{2,3},{3,2},{4,5},{5,4},{6,7},{7,6},{8,9},{9,8},{10,11... | collective-permute-start | bytes 688136 | tf_op jit(solution)/shard_map/ppermute | solution.py:59
  26.3 4.7 %copy-start = (bf16[2,36864]{1,0:T(2,128)(2,1)S(1)}, bf16[2,36864]{1,0:T(2,128)(2,1)}, u32[]{:S(2)}) copy-start(bf16[2,36864]{1,0:T(2,128)(2,1)} %query_ref.1) | copy-start | bytes 442372
  26.3 4.7 %copy-start.1 = (s32[2,12]{1,0:T(2,128)S(1)}, s32[2,12]{1,0:T(2,128)}, u32[]{:S(2)}) copy-start(s32[2,12]{1,0:T(2,128)} %table_ref.1) | copy-start | bytes 292
  26.4 4.7 %copy-start.2 = (s32[2]{0:T(128)S(1)}, s32[2]{0:T(128)}, u32[]{:S(2)}) copy-start(s32[2]{0:T(128)} %length_ref.1) | copy-start | bytes 28
  27.3 6.9 %collective-permute-start.14 = (bf16[8,7168]{1,0:T(8,128)(2,1)S(1)}, bf16[8,7168]{1,0:T(8,128)(2,1)S(1)}, u32[]{:S(2)}, u32[]{:S(2)}) collective-permute-start(bf16[8,7168]{1,0:T(8,128)(2,1)S(1)} %get-tuple-element.37), channel_id=1, source_target_pairs={{0,6},{1,7},{2,4},{3,5},{4,2},{5,3},{6,0},{7,1},{8,14},{9,15},{10,... | collective-permute-start | bytes 344072 | tf_op jit(solution)/shard_map/ppermute | solution.py:59
  29.2 6.9 %collective-permute-start.15 = (bf16[8,7168]{1,0:T(8,128)(2,1)S(1)}, bf16[8,7168]{1,0:T(8,128)(2,1)S(1)}, u32[]{:S(2)}, u32[]{:S(2)}) collective-permute-start(bf16[8,7168]{1,0:T(8,128)(2,1)S(1)} %get-tuple-element.38), channel_id=1, source_target_pairs={{0,4},{1,5},{2,6},{3,7},{4,0},{5,1},{6,2},{7,3},{8,12},{9,13},{10,... | collective-permute-start | bytes 344072 | tf_op jit(solution)/shard_map/ppermute | solution.py:59
  29.8 6.3 %collective-permute-start.16 = (bf16[8,7168]{1,0:T(8,128)(2,1)S(1)}, bf16[8,7168]{1,0:T(8,128)(2,1)S(1)}, u32[]{:S(2)}, u32[]{:S(2)}) collective-permute-start(bf16[8,7168]{1,0:T(8,128)(2,1)S(1)} %get-tuple-element.39), channel_id=1, source_target_pairs={{0,2},{1,3},{2,0},{3,1},{4,6},{5,7},{6,4},{7,5},{8,10},{9,11},{10,... | collective-permute-start | bytes 344072 | tf_op jit(solution)/shard_map/ppermute | solution.py:59
  36.2 5.4 %collective-permute-start.17 = (bf16[2,7168]{1,0:T(2,128)(2,1)S(1)}, bf16[2,7168]{1,0:T(2,128)(2,1)S(1)}, u32[]{:S(2)}, u32[]{:S(2)}) collective-permute-start(bf16[2,7168]{1,0:T(2,128)(2,1)S(1)} %get-tuple-element.41), channel_id=1, source_target_pairs={{0,16},{1,17},{2,18},{3,19},{4,20},{5,21},{6,22},{7,23},{8,24},{9,... | collective-permute-start | bytes 86024 | tf_op jit(solution)/shard_map/ppermute | solution.py:59
  38.3 5.7 %collective-permute-start.18 = (bf16[2,7168]{1,0:T(2,128)(2,1)S(1)}, bf16[2,7168]{1,0:T(2,128)(2,1)S(1)}, u32[]{:S(2)}, u32[]{:S(2)}) collective-permute-start(bf16[2,7168]{1,0:T(2,128)(2,1)S(1)} %get-tuple-element.42), channel_id=1, source_target_pairs={{0,24},{1,25},{2,26},{3,27},{4,28},{5,29},{6,30},{7,31},{8,16},{9,... | collective-permute-start | bytes 86024 | tf_op jit(solution)/shard_map/ppermute | solution.py:59
  39.6 4.3 %collective-permute-start.19 = (bf16[2,7168]{1,0:T(2,128)(2,1)S(1)}, bf16[2,7168]{1,0:T(2,128)(2,1)S(1)}, u32[]{:S(2)}, u32[]{:S(2)}) collective-permute-start(bf16[2,7168]{1,0:T(2,128)(2,1)S(1)} %get-tuple-element.43), channel_id=1, source_target_pairs={{0,8},{1,9},{2,10},{3,11},{4,12},{5,13},{6,14},{7,15},{8,0},{9,1},... | collective-permute-start | bytes 86024 | tf_op jit(solution)/shard_map/ppermute | solution.py:59

commit v11 on v10

--- a/solution.py
+++ b/solution.py
@@ -295,28 +295,22 @@
     )(*operands, *after)
 
 
-def pages_kernel(
-    dp_count, page_hbm, dest_hbm, pool_ref, after_ref, low_ref, high_ref, page_ref, dest_ref, sems
-):
+def pages_kernel(dp_count, page_ref, dest_ref, pool_ref, after_ref, low_ref, high_ref):
     own, width = pool_ref.shape
-    page_copy = pltpu.make_async_copy(page_hbm, page_ref, sems.at[0])
-    dest_copy = pltpu.make_async_copy(dest_hbm, dest_ref, sems.at[1])
-    page_copy.start()
-    dest_copy.start()
-    page_copy.wait()
-    dest_copy.wait()
     me = lax.axis_index("dp")
     slots = dp_count * MCAP
     row = lax.broadcasted_iota(jnp.int32, (slots, own), 0)
     column = lax.broadcasted_iota(jnp.int32, (slots, own), 1)
     pick = jnp.zeros((slots, own), f32)
     entries = page_ref.shape[1]
+    pages = [page_ref[:, m : m + 1] for m in range(entries)]
+    dests = [dest_ref[:, m : m + 1] for m in range(entries)]
     for m in range(entries):
-        rank = jnp.int32(0)
+        rank = jnp.zeros((1, 1), jnp.int32)
         for n in range(m):
-            rank += jnp.where(dest_ref[0, n] == dest_ref[0, m], 1, 0)
-        bucket = jnp.bitwise_xor(dest_ref[0, m], me) * MCAP + rank
-        pick = jnp.where((row == bucket) & (column == page_ref[0, m]), 1.0, pick)
+            rank += jnp.where(dests[n] == dests[m], 1, 0)
+        bucket = jnp.bitwise_xor(dests[m], me) * MCAP + rank
+        pick = jnp.where((row == bucket) & (column == pages[m]), 1.0, pick)
     pick = pick.astype(bf16)
     step = 2048
     for i in range(width // step):
@@ -332,16 +326,11 @@
     return pl.pallas_call(
         functools.partial(pages_kernel, dp_count),
         out_shape=(half, half),
-        in_specs=[in_hbm()] * 2 + [in_vmem(), anywhere()],
+        in_specs=[in_vmem()] * 3 + [anywhere()],
         out_specs=(in_vmem(),) * 2,
-        scratch_shapes=[
-            pltpu.SMEM(moved_page.shape, jnp.int32),
-            pltpu.SMEM(moved_dest.shape, jnp.int32),
-            pltpu.SemaphoreType.DMA((2,)),
-        ],
         compiler_params=pltpu.CompilerParams(vmem_limit_bytes=4 * MIB),
         cost_estimate=pl.CostEstimate(flops=0, bytes_accessed=4 * latent_pool.size, transcendentals=0),
-    )(hbm(moved_page), hbm(moved_dest), vmem(latent_pool), after)
+    )(vmem(moved_page), vmem(moved_dest), vmem(latent_pool), after)
 
 
 def rows_kernel(places, *refs):
@@ -494,7 +483,7 @@
 
     mine = (hidden, routes, route_weight)
     got = [trade(x, 1) for x in mine]
-    *mine, pool = fetch(*mine, latent_pool)
+    *mine, pool, moved_page, moved_dest = fetch(*mine, latent_pool, moved_page, moved_dest)
     near = make_payload(mine, got, ep_count)
     for number, partners in enumerate(stages):
         got = [trade(near, bit) for bit in partners]

time: 44.8 us -> 44.4 us (level)
  transfers between devices with their start and end apart: 20 -> 20, of which waited for: 10 -> 10; matrix products, arithmetic and copies ran while one was open for 0% -> 0% of each run, Pallas kernels for 15% -> 14%
where the time goes in v11:
time: 44.4 us; the launch traced here: 44.3 us
  starting transfers between devices  19.9 us (45%)
  waiting for transfers between devices  14.5 us (33%)
  Pallas kernels  9.05 us (20%)
  between operations  0.87 us (2%)
    ppermute x20, starting transfers between devices, swap(): return lax.ppermute(x, axes, pairs)  19.9 us
    ppermute x20, waiting for transfers between devices, swap(): return lax.ppermute(x, axes, pairs)  14.5 us
    pallas_call x1, Pallas kernels, attend(): pl.pallas_call(functools.partial(attend_kernel, senders), out_shape=jax.S...  2.35 us
    pallas_call x1, Pallas kernels, far_products(): pl.pallas_call(functools.partial(far_kernel, ep_count), out_shape=(pltpu....  1.74 us
    pallas_call x1, Pallas kernels, fetch(): pl.pallas_call(fetch_kernel, out_shape=tuple((pltpu.VMEM(x.shape, x.dtype...  1.27 us
    pallas_call x1, Pallas kernels, near_products(): pl.pallas_call(near_kernel, out_shape=(acc, acc), in_specs=[in_vmem()] *...  1.13 us
  transfers between devices with their start and end apart: 20, of which 10 were waited for; matrix products, arithmetic and copies ran while one was open for 0% of the time, Pallas kernels for 14%

profile of v11, /device:TPU:0, one launch (start us, length us, event | category | flops | bytes accessed | tf_op | source)
XLA Modules:
  0.0 44.3 jit_solution(12021567667613827367)
XLA Ops:
  0.6 0.5 %collective-permute-start.1 = (s32[2,4]{1,0:T(2,128)}, s32[2,4]{1,0:T(2,128)S(1)}, u32[]{:S(2)}, u32[]{:S(2)}) collective-permute-start(s32[2,4]{1,0:T(2,128)} %refs_1_.1), channel_id=1, source_target_pairs={{0,1},{1,0},{2,3},{3,2},{4,5},{5,4},{6,7},{7,6},{8,9},{9,8},{10,11... | collective-permute-start | bytes 104 | tf_op jit(solution)/shard_map/ppermute | solution.py:59
  1.2 0.4 collective-permute-start
  1.7 1.3 %shard_map.131 = (bf16[2,7168]{1,0:T(2,128)(2,1)S(1)}, s32[2,4]{1,0:T(2,128)S(1)}, f32[2,4]{1,0:T(2,128)S(1)}, bf16[24,18432]{1,0:T(8,128)(2,1)S(1)}, s32[1,6]{1,0:T(1,128)S(1)}, /*index=5*/s32[1,6]{1,0:T(1,128)S(1)}) custom-call(bf16[2,7168]{1,0:T(2,128)(2,1)} %refs_0_.2, s32[2,4]{1,0:T(2,128)} %refs_1_.1, f32[2,4]{1,0:T(2,128)} %refs_2_.1, ...), custom_call_target="tpu_custom_call" | custom-call | flops 1250000000 | bytes 1048576 | tf_op jit(solution)/shard_map/pallas_call | solution.py:86
  3.1 3.7 %collective-permute-start.5 = (bf16[4,3712]{1,0:T(4,128)(2,1)S(1)}, bf16[4,3712]{1,0:T(4,128)(2,1)S(1)}, u32[]{:S(2)}, u32[]{:S(2)}) collective-permute-start(bf16[4,3712]{1,0:T(4,128)(2,1)S(1)} %shard_map.132.after_ref.refs_0_), channel_id=1, source_target_pairs={{0,16},{1,17},{2,18},{3,19},{4,20},{5,21},{6,22},{7,23},{8,24},{9,... | collective-permute-start | bytes 89096 | tf_op jit(solution)/shard_map/ppermute | solution.py:59
  6.8 1.3 %collective-permute-start.4 = (bf16[4,3712]{1,0:T(4,128)(2,1)S(1)}, bf16[4,3712]{1,0:T(4,128)(2,1)S(1)}, u32[]{:S(2)}, u32[]{:S(2)}) collective-permute-start(bf16[4,3712]{1,0:T(4,128)(2,1)S(1)} %shard_map.132.after_ref.refs_0_), channel_id=1, source_target_pairs={{0,24},{1,25},{2,26},{3,27},{4,28},{5,29},{6,30},{7,31},{8,16},{9,... | collective-permute-start | bytes 89096 | tf_op jit(solution)/shard_map/ppermute | solution.py:59
  8.4 0.6 %shard_map.133 = (bf16[4,18432]{1,0:T(4,128)(2,1)S(1)}, bf16[4,18432]{1,0:T(4,128)(2,1)S(1)}) custom-call(s32[1,6]{1,0:T(1,128)S(1)} %get-tuple-element.28.page_ref, s32[1,6]{1,0:T(1,128)S(1)} %get-tuple-element.29.dest_ref, bf16[24,18432]{1,0:T(8,128)(2,1)S(1)} %get-tuple-element.30.pool_ref, bf16[4,3712]{1,0:T(4,128)(2,1)S(1)} %shard_map.132.after_ref.refs_0_), custom_call_target="tpu_custom_call" | custom-call | bytes 1769472 | tf_op jit(solution)/shard_map/pallas_call | solution.py:326
  9.1 1.6 %collective-permute-start.9 = (bf16[4,18432]{1,0:T(4,128)(2,1)S(1)}, bf16[4,18432]{1,0:T(4,128)(2,1)S(1)}, u32[]{:S(2)}, u32[]{:S(2)}) collective-permute-start(bf16[4,18432]{1,0:T(4,128)(2,1)S(1)} %get-tuple-element.31.refs_4_), channel_id=1, source_target_pairs={{0,2},{1,3},{2,0},{3,1},{4,6},{5,7},{6,4},{7,5},{8,10},{9,11},{10,... | collective-permute-start | bytes 442376 | tf_op jit(solution)/shard_map/ppermute | solution.py:59
  10.6 1.9 %collective-permute-done.4.refs_2_ = bf16[4,3712]{1,0:T(4,128)(2,1)S(1)} collective-permute-done((bf16[4,3712]{1,0:T(4,128)(2,1)S(1)}, bf16[4,3712]{1,0:T(4,128)(2,1)S(1)}, u32[]{:S(2)}, u32[]{:S(2)}) %collective-permute-start.4) | collective-permute-done | bytes 29728 | tf_op jit(solution)/shard_map/ppermute | solution.py:59
  12.6 2.5 %collective-permute-start.8 = (bf16[16,3712]{1,0:T(8,128)(2,1)S(1)}, bf16[16,3712]{1,0:T(8,128)(2,1)S(1)}, u32[]{:S(2)}, u32[]{:S(2)}) collective-permute-start(bf16[16,3712]{1,0:T(8,128)(2,1)S(1)} %shard_map.134.refs_0_), channel_id=1, source_target_pairs={{0,6},{1,7},{2,4},{3,5},{4,2},{5,3},{6,0},{7,1},{8,14},{9,15},{10,... | collective-permute-start | bytes 356360 | tf_op jit(solution)/shard_map/ppermute | solution.py:59
  15.1 0.5 %collective-permute-start.7 = (bf16[16,3712]{1,0:T(8,128)(2,1)S(1)}, bf16[16,3712]{1,0:T(8,128)(2,1)S(1)}, u32[]{:S(2)}, u32[]{:S(2)}) collective-permute-start(bf16[16,3712]{1,0:T(8,128)(2,1)S(1)} %shard_map.134.refs_0_), channel_id=1, source_target_pairs={{0,4},{1,5},{2,6},{3,7},{4,0},{5,1},{6,2},{7,3},{8,12},{9,13},{10,... | collective-permute-start | bytes 356360 | tf_op jit(solution)/shard_map/ppermute | solution.py:59
  15.6 0.5 %collective-permute-start.6 = (bf16[16,3712]{1,0:T(8,128)(2,1)S(1)}, bf16[16,3712]{1,0:T(8,128)(2,1)S(1)}, u32[]{:S(2)}, u32[]{:S(2)}) collective-permute-start(bf16[16,3712]{1,0:T(8,128)(2,1)S(1)} %shard_map.134.refs_0_), channel_id=1, source_target_pairs={{0,2},{1,3},{2,0},{3,1},{4,6},{5,7},{6,4},{7,5},{8,10},{9,11},{10,... | collective-permute-start | bytes 356360 | tf_op jit(solution)/shard_map/ppermute | solution.py:59
  16.1 3.1 %collective-permute-done.8.refs_3_ = bf16[16,3712]{1,0:T(8,128)(2,1)S(1)} collective-permute-done((bf16[16,3712]{1,0:T(8,128)(2,1)S(1)}, bf16[16,3712]{1,0:T(8,128)(2,1)S(1)}, u32[]{:S(2)}, u32[]{:S(2)}) %collective-permute-start.8) | collective-permute-done | bytes 118816 | tf_op jit(solution)/shard_map/ppermute | solution.py:59
  19.2 1.6 %collective-permute-done.7.refs_2_ = bf16[16,3712]{1,0:T(8,128)(2,1)S(1)} collective-permute-done((bf16[16,3712]{1,0:T(8,128)(2,1)S(1)}, bf16[16,3712]{1,0:T(8,128)(2,1)S(1)}, u32[]{:S(2)}, u32[]{:S(2)}) %collective-permute-start.7) | collective-permute-done | bytes 118816 | tf_op jit(solution)/shard_map/ppermute | solution.py:59
  21.0 0.6 %collective-permute-start.11 = (bf16[4,18432]{1,0:T(4,128)(2,1)S(1)}, bf16[4,18432]{1,0:T(4,128)(2,1)S(1)}, u32[]{:S(2)}, u32[]{:S(2)}) collective-permute-start(bf16[4,18432]{1,0:T(4,128)(2,1)S(1)} %shard_map.136.refs_1_), channel_id=1, source_target_pairs={{0,1},{1,0},{2,3},{3,2},{4,5},{5,4},{6,7},{7,6},{8,9},{9,8},{10,11... | collective-permute-start | bytes 442376 | tf_op jit(solution)/shard_map/ppermute | solution.py:59
  21.6 1.1 %shard_map.137 = (f32[64,512]{1,0:T(8,128)S(1)}, f32[64,512]{1,0:T(8,128)S(1)}) custom-call(bf16[64,3712]{1,0:T(8,128)(2,1)S(1)} %shard_map.135.refs_2_.near_ref, bf16[1,7168,512]{2,1,0:T(8,128)(2,1)S(1)} %bitcast.3, bf16[1,7168,512]{2,1,0:T(8,128)(2,1)S(1)} %bitcast.5, bf16[1,512,7168]{2,1,0:T(8,128)(2,1)S(1)} %bitcast.1, ...), custom_call_target="tpu_custom_call" | custom-call | flops 469762048 | bytes 7340032 | tf_op jit(solution)/shard_map/pallas_call | solution.py:224
  23.0 1.7 %shard_map.138 = (bf16[64,512]{1,0:T(8,128)(2,1)S(1)}, f32[32,3584]{1,0:T(8,128)S(1)}, bf16[32,3584]{1,0:T(8,128)(2,1)S(1)}) custom-call(bf16[64,3712]{1,0:T(8,128)(2,1)S(1)} %shard_map.135.refs_2_.near_ref, bf16[64,3712]{1,0:T(8,128)(2,1)S(1)} %collective-permute-done.10.far_ref, bf16[1,7168,512]{2,1,0:T(8,128)(2,1)S(1)} %bitcast.3, ...), custom_call_target="tpu_custom_call" | custom-call | flops 704643072 | bytes 11010048 | tf_op jit(solution)/shard_map/pallas_call | solution.py:238
  24.9 0.7 %shard_map.140 = (f32[32,3584]{1,0:T(8,128)S(1)}, bf16[32,3584]{1,0:T(8,128)(2,1)S(1)}) custom-call(bf16[64,3712]{1,0:T(8,128)(2,1)S(1)} %shard_map.135.refs_2_.near_ref, bf16[64,512]{1,0:T(8,128)(2,1)S(1)} %get-tuple-element.37.inner_ref, bf16[1,512,7168]{2,1,0:T(8,128)(2,1)S(1)} %bitcast.1), custom_call_target="tpu_custom_call" | custom-call | flops 234881024 | bytes 3670016 | tf_op jit(solution)/shard_map/pallas_call | solution.py:256
  25.6 0.4 collective-permute-start.13
  26.0 0.2 collective-permute-done.12.refs_1_
  26.3 0.8 %collective-permute-done.13.refs_2_ = bf16[32,3584]{1,0:T(8,128)(2,1)S(1)} collective-permute-done((bf16[32,3584]{1,0:T(8,128)(2,1)S(1)}, bf16[32,3584]{1,0:T(8,128)(2,1)S(1)}, u32[]{:S(2)}, u32[]{:S(2)}) %collective-permute-start.13) | collective-permute-done | bytes 229408 | tf_op jit(solution)/shard_map/ppermute | solution.py:59
  27.2 1.6 %collective-permute-start.14 = (bf16[8,7168]{1,0:T(8,128)(2,1)S(1)}, bf16[8,7168]{1,0:T(8,128)(2,1)S(1)}, u32[]{:S(2)}, u32[]{:S(2)}) collective-permute-start(bf16[8,7168]{1,0:T(8,128)(2,1)S(1)} %get-tuple-element.41), channel_id=1, source_target_pairs={{0,6},{1,7},{2,4},{3,5},{4,2},{5,3},{6,0},{7,1},{8,14},{9,15},{10,... | collective-permute-start | bytes 344072 | tf_op jit(solution)/shard_map/ppermute | solution.py:59
  28.8 1.1 %collective-permute-start.15 = (bf16[8,7168]{1,0:T(8,128)(2,1)S(1)}, bf16[8,7168]{1,0:T(8,128)(2,1)S(1)}, u32[]{:S(2)}, u32[]{:S(2)}) collective-permute-start(bf16[8,7168]{1,0:T(8,128)(2,1)S(1)} %get-tuple-element.42), channel_id=1, source_target_pairs={{0,4},{1,5},{2,6},{3,7},{4,0},{5,1},{6,2},{7,3},{8,12},{9,13},{10,... | collective-permute-start | bytes 344072 | tf_op jit(solution)/shard_map/ppermute | solution.py:59
  29.9 0.9 %collective-permute-start.16 = (bf16[8,7168]{1,0:T(8,128)(2,1)S(1)}, bf16[8,7168]{1,0:T(8,128)(2,1)S(1)}, u32[]{:S(2)}, u32[]{:S(2)}) collective-permute-start(bf16[8,7168]{1,0:T(8,128)(2,1)S(1)} %get-tuple-element.43), channel_id=1, source_target_pairs={{0,2},{1,3},{2,0},{3,1},{4,6},{5,7},{6,4},{7,5},{8,10},{9,11},{10,... | collective-permute-start | bytes 344072 | tf_op jit(solution)/shard_map/ppermute | solution.py:59
  31.0 2.3 %shard_map.143.refs_4_ = bf16[2,32768]{1,0:T(2,128)(2,1)} custom-call(s32[2]{0:T(128)S(1)} %copy-done.2, s32[2,12]{1,0:T(2,128)S(1)} %copy-done.1, bf16[2,36864]{1,0:T(2,128)(2,1)S(1)} %copy-done, bf16[24,18432]{1,0:T(8,128)(2,1)S(1)} %get-tuple-element.30.pool_ref, bf16[8,18432]{1,0:T(8,128)(2,1)S(1)} %shard_map.142.arrived_ref), custom_call_target="tpu_custom_call" | custom-call | flops 1073741824 | bytes 4194304 | tf_op jit(solution)/shard_map/pallas_call | solution.py:451
  33.3 0.8 %collective-permute-done.14.refs_1_ = bf16[8,7168]{1,0:T(8,128)(2,1)S(1)} collective-permute-done((bf16[8,7168]{1,0:T(8,128)(2,1)S(1)}, bf16[8,7168]{1,0:T(8,128)(2,1)S(1)}, u32[]{:S(2)}, u32[]{:S(2)}) %collective-permute-start.14) | collective-permute-done | bytes 114720 | tf_op jit(solution)/shard_map/ppermute | solution.py:59
  34.2 1.9 %collective-permute-done.15.refs_2_ = bf16[8,7168]{1,0:T(8,128)(2,1)S(1)} collective-permute-done((bf16[8,7168]{1,0:T(8,128)(2,1)S(1)}, bf16[8,7168]{1,0:T(8,128)(2,1)S(1)}, u32[]{:S(2)}, u32[]{:S(2)}) %collective-permute-start.15) | collective-permute-done | bytes 114720 | tf_op jit(solution)/shard_map/ppermute | solution.py:59
  36.1 1.8 %collective-permute-start.17 = (bf16[2,7168]{1,0:T(2,128)(2,1)S(1)}, bf16[2,7168]{1,0:T(2,128)(2,1)S(1)}, u32[]{:S(2)}, u32[]{:S(2)}) collective-permute-start(bf16[2,7168]{1,0:T(2,128)(2,1)S(1)} %get-tuple-element.45), channel_id=1, source_target_pairs={{0,16},{1,17},{2,18},{3,19},{4,20},{5,21},{6,22},{7,23},{8,24},{9,... | collective-permute-start | bytes 86024 | tf_op jit(solution)/shard_map/ppermute | solution.py:59
  37.9 1.2 %collective-permute-start.18 = (bf16[2,7168]{1,0:T(2,128)(2,1)S(1)}, bf16[2,7168]{1,0:T(2,128)(2,1)S(1)}, u32[]{:S(2)}, u32[]{:S(2)}) collective-permute-start(bf16[2,7168]{1,0:T(2,128)(2,1)S(1)} %get-tuple-element.46), channel_id=1, source_target_pairs={{0,24},{1,25},{2,26},{3,27},{4,28},{5,29},{6,30},{7,31},{8,16},{9,... | collective-permute-start | bytes 86024 | tf_op jit(solution)/shard_map/ppermute | solution.py:59
  39.2 0.5 %collective-permute-start.19 = (bf16[2,7168]{1,0:T(2,128)(2,1)S(1)}, bf16[2,7168]{1,0:T(2,128)(2,1)S(1)}, u32[]{:S(2)}, u32[]{:S(2)}) collective-permute-start(bf16[2,7168]{1,0:T(2,128)(2,1)S(1)} %get-tuple-element.47), channel_id=1, source_target_pairs={{0,8},{1,9},{2,10},{3,11},{4,12},{5,13},{6,14},{7,15},{8,0},{9,1},... | collective-permute-start | bytes 86024 | tf_op jit(solution)/shard_map/ppermute | solution.py:59
  39.7 1.8 %collective-permute-done.17.refs_1_ = bf16[2,7168]{1,0:T(2,128)(2,1)S(1)} collective-permute-done((bf16[2,7168]{1,0:T(2,128)(2,1)S(1)}, bf16[2,7168]{1,0:T(2,128)(2,1)S(1)}, u32[]{:S(2)}, u32[]{:S(2)}) %collective-permute-start.17) | collective-permute-done | bytes 28704 | tf_op jit(solution)/shard_map/ppermute | solution.py:59
  41.4 2.2 %collective-permute-done.18.refs_2_ = bf16[2,7168]{1,0:T(2,128)(2,1)S(1)} collective-permute-done((bf16[2,7168]{1,0:T(2,128)(2,1)S(1)}, bf16[2,7168]{1,0:T(2,128)(2,1)S(1)}, u32[]{:S(2)}, u32[]{:S(2)}) %collective-permute-start.18) | collective-permute-done | bytes 28704 | tf_op jit(solution)/shard_map/ppermute | solution.py:59
  43.6 0.7 %shard_map.145 = bf16[2,7168]{1,0:T(2,128)(2,1)} custom-call(f32[2,7168]{1,0:T(2,128)S(1)} %get-tuple-element.44.refs_0_, bf16[2,7168]{1,0:T(2,128)(2,1)S(1)} %collective-permute-done.17.refs_1_, bf16[2,7168]{1,0:T(2,128)(2,1)S(1)} %collective-permute-done.18.refs_2_, bf16[2,7168]{1,0:T(2,128)(2,1)S(1)} %collective-permute-done.19.refs_3_), custom_call_target="tpu_custom_call" | custom-call | bytes 114688 | tf_op jit(solution)/shard_map/pallas_call | solution.py:288
  (44 shorter events, 1.5 us)
Async XLA Ops:
  0.6 2.3 %collective-permute-start.1 = (s32[2,4]{1,0:T(2,128)}, s32[2,4]{1,0:T(2,128)S(1)}, u32[]{:S(2)}, u32[]{:S(2)}) collective-permute-start(s32[2,4]{1,0:T(2,128)} %refs_1_.1), channel_id=1, source_target_pairs={{0,1},{1,0},{2,3},{3,2},{4,5},{5,4},{6,7},{7,6},{8,9},{9,8},{10,11... | collective-permute-start | bytes 104 | tf_op jit(solution)/shard_map/ppermute | solution.py:59
  1.1 1.8 %collective-permute-start.2 = (f32[2,4]{1,0:T(2,128)}, f32[2,4]{1,0:T(2,128)S(1)}, u32[]{:S(2)}, u32[]{:S(2)}) collective-permute-start(f32[2,4]{1,0:T(2,128)} %refs_2_.1), channel_id=1, source_target_pairs={{0,1},{1,0},{2,3},{3,2},{4,5},{5,4},{6,7},{7,6},{8,9},{9,8},{10,11... | collective-permute-start | bytes 104 | tf_op jit(solution)/shard_map/ppermute | solution.py:59
  1.2 1.7 %collective-permute-start = (bf16[2,7168]{1,0:T(2,128)(2,1)}, bf16[2,7168]{1,0:T(2,128)(2,1)S(1)}, u32[]{:S(2)}, u32[]{:S(2)}) collective-permute-start(bf16[2,7168]{1,0:T(2,128)(2,1)} %refs_0_.2), channel_id=1, source_target_pairs={{0,1},{1,0},{2,3},{3,2},{4,5},{5,4},{6,7},{7,6},{8,9},{9,8},{10,11... | collective-permute-start | bytes 86024 | tf_op jit(solution)/shard_map/ppermute | solution.py:59
  3.1 7.5 %collective-permute-start.5 = (bf16[4,3712]{1,0:T(4,128)(2,1)S(1)}, bf16[4,3712]{1,0:T(4,128)(2,1)S(1)}, u32[]{:S(2)}, u32[]{:S(2)}) collective-permute-start(bf16[4,3712]{1,0:T(4,128)(2,1)S(1)} %shard_map.132.after_ref.refs_0_), channel_id=1, source_target_pairs={{0,16},{1,17},{2,18},{3,19},{4,20},{5,21},{6,22},{7,23},{8,24},{9,... | collective-permute-start | bytes 89096 | tf_op jit(solution)/shard_map/ppermute | solution.py:59
  6.8 5.7 %collective-permute-start.4 = (bf16[4,3712]{1,0:T(4,128)(2,1)S(1)}, bf16[4,3712]{1,0:T(4,128)(2,1)S(1)}, u32[]{:S(2)}, u32[]{:S(2)}) collective-permute-start(bf16[4,3712]{1,0:T(4,128)(2,1)S(1)} %shard_map.132.after_ref.refs_0_), channel_id=1, source_target_pairs={{0,24},{1,25},{2,26},{3,27},{4,28},{5,29},{6,30},{7,31},{8,16},{9,... | collective-permute-start | bytes 89096 | tf_op jit(solution)/shard_map/ppermute | solution.py:59
  8.2 4.3 %collective-permute-start.3 = (bf16[4,3712]{1,0:T(4,128)(2,1)S(1)}, bf16[4,3712]{1,0:T(4,128)(2,1)S(1)}, u32[]{:S(2)}, u32[]{:S(2)}) collective-permute-start(bf16[4,3712]{1,0:T(4,128)(2,1)S(1)} %shard_map.132.after_ref.refs_0_), channel_id=1, source_target_pairs={{0,8},{1,9},{2,10},{3,11},{4,12},{5,13},{6,14},{7,15},{8,0},{9,1},... | collective-permute-start | bytes 89096 | tf_op jit(solution)/shard_map/ppermute | solution.py:59
  9.0 12.6 %slice-start = ((s8[7340032]{0:T(1024)(128)(4,1)}), s8[4194304]{0:T(1024)(128)(4,1)S(1)}, s32[]{:S(2)}) async-start(s8[7340032]{0:T(1024)(128)(4,1)} %bitcast), calls=%async_computation | async-start | bytes 8388608
  9.0 12.6 %slice-start.2 = ((s8[7340032]{0:T(1024)(128)(4,1)}), s8[4194304]{0:T(1024)(128)(4,1)S(1)}, s32[]{:S(2)}) async-start(s8[7340032]{0:T(1024)(128)(4,1)} %bitcast.2), calls=%async_computation.2 | async-start | bytes 8388608
  9.0 12.6 %slice-start.4 = ((s8[7340032]{0:T(1024)(128)(4,1)}), s8[4194304]{0:T(1024)(128)(4,1)S(1)}, s32[]{:S(2)}) async-start(s8[7340032]{0:T(1024)(128)(4,1)} %bitcast.4), calls=%async_computation.4 | async-start | bytes 8388608
  9.0 12.6 %slice-start.1 = ((s8[7340032]{0:T(1024)(128)(4,1)}), s8[3145728]{0:T(1024)(128)(4,1)S(1)}, s32[]{:S(2)}) async-start(s8[7340032]{0:T(1024)(128)(4,1)} %bitcast), calls=%async_computation.1 | async-start | bytes 6291456
  9.0 12.6 %slice-start.3 = ((s8[7340032]{0:T(1024)(128)(4,1)}), s8[3145728]{0:T(1024)(128)(4,1)S(1)}, s32[]{:S(2)}) async-start(s8[7340032]{0:T(1024)(128)(4,1)} %bitcast.2), calls=%async_computation.3 | async-start | bytes 6291456
  9.0 12.6 %slice-start.5 = ((s8[7340032]{0:T(1024)(128)(4,1)}), s8[3145728]{0:T(1024)(128)(4,1)S(1)}, s32[]{:S(2)}) async-start(s8[7340032]{0:T(1024)(128)(4,1)} %bitcast.4), calls=%async_computation.5 | async-start | bytes 6291456
  9.1 7.1 %collective-permute-start.9 = (bf16[4,18432]{1,0:T(4,128)(2,1)S(1)}, bf16[4,18432]{1,0:T(4,128)(2,1)S(1)}, u32[]{:S(2)}, u32[]{:S(2)}) collective-permute-start(bf16[4,18432]{1,0:T(4,128)(2,1)S(1)} %get-tuple-element.31.refs_4_), channel_id=1, source_target_pairs={{0,2},{1,3},{2,0},{3,1},{4,6},{5,7},{6,4},{7,5},{8,10},{9,11},{10,... | collective-permute-start | bytes 442376 | tf_op jit(solution)/shard_map/ppermute | solution.py:59
  12.6 6.6 %collective-permute-start.8 = (bf16[16,3712]{1,0:T(8,128)(2,1)S(1)}, bf16[16,3712]{1,0:T(8,128)(2,1)S(1)}, u32[]{:S(2)}, u32[]{:S(2)}) collective-permute-start(bf16[16,3712]{1,0:T(8,128)(2,1)S(1)} %shard_map.134.refs_0_), channel_id=1, source_target_pairs={{0,6},{1,7},{2,4},{3,5},{4,2},{5,3},{6,0},{7,1},{8,14},{9,15},{10,... | collective-permute-start | bytes 356360 | tf_op jit(solution)/shard_map/ppermute | solution.py:59
  15.1 5.7 %collective-permute-start.7 = (bf16[16,3712]{1,0:T(8,128)(2,1)S(1)}, bf16[16,3712]{1,0:T(8,128)(2,1)S(1)}, u32[]{:S(2)}, u32[]{:S(2)}) collective-permute-start(bf16[16,3712]{1,0:T(8,128)(2,1)S(1)} %shard_map.134.refs_0_), channel_id=1, source_target_pairs={{0,4},{1,5},{2,6},{3,7},{4,0},{5,1},{6,2},{7,3},{8,12},{9,13},{10,... | collective-permute-start | bytes 356360 | tf_op jit(solution)/shard_map/ppermute | solution.py:59
  15.6 5.2 %collective-permute-start.6 = (bf16[16,3712]{1,0:T(8,128)(2,1)S(1)}, bf16[16,3712]{1,0:T(8,128)(2,1)S(1)}, u32[]{:S(2)}, u32[]{:S(2)}) collective-permute-start(bf16[16,3712]{1,0:T(8,128)(2,1)S(1)} %shard_map.134.refs_0_), channel_id=1, source_target_pairs={{0,2},{1,3},{2,0},{3,1},{4,6},{5,7},{6,4},{7,5},{8,10},{9,11},{10,... | collective-permute-start | bytes 356360 | tf_op jit(solution)/shard_map/ppermute | solution.py:59
  20.8 2.1 %collective-permute-start.10 = (bf16[64,3712]{1,0:T(8,128)(2,1)S(1)}, bf16[64,3712]{1,0:T(8,128)(2,1)S(1)}, u32[]{:S(2)}, u32[]{:S(2)}) collective-permute-start(bf16[64,3712]{1,0:T(8,128)(2,1)S(1)} %shard_map.135.refs_2_.near_ref), channel_id=1, source_target_pairs={{0,1},{1,0},{2,3},{3,2},{4,5},{5,4},{6,7},{7,6},{8,9},{9,8},{10,11... | collective-permute-start | bytes 1425416 | tf_op jit(solution)/shard_map/ppermute | solution.py:59
  21.0 1.9 %collective-permute-start.11 = (bf16[4,18432]{1,0:T(4,128)(2,1)S(1)}, bf16[4,18432]{1,0:T(4,128)(2,1)S(1)}, u32[]{:S(2)}, u32[]{:S(2)}) collective-permute-start(bf16[4,18432]{1,0:T(4,128)(2,1)S(1)} %shard_map.136.refs_1_), channel_id=1, source_target_pairs={{0,1},{1,0},{2,3},{3,2},{4,5},{5,4},{6,7},{7,6},{8,9},{9,8},{10,11... | collective-permute-start | bytes 442376 | tf_op jit(solution)/shard_map/ppermute | solution.py:59
  24.7 1.6 %collective-permute-start.12 = (bf16[32,3584]{1,0:T(8,128)(2,1)S(1)}, bf16[32,3584]{1,0:T(8,128)(2,1)S(1)}, u32[]{:S(2)}, u32[]{:S(2)}) collective-permute-start(bf16[32,3584]{1,0:T(8,128)(2,1)S(1)} %get-tuple-element.36), channel_id=1, source_target_pairs={{0,1},{1,0},{2,3},{3,2},{4,5},{5,4},{6,7},{7,6},{8,9},{9,8},{10,11... | collective-permute-start | bytes 688136 | tf_op jit(solution)/shard_map/ppermute | solution.py:59
  25.6 1.6 %collective-permute-start.13 = (bf16[32,3584]{1,0:T(8,128)(2,1)S(1)}, bf16[32,3584]{1,0:T(8,128)(2,1)S(1)}, u32[]{:S(2)}, u32[]{:S(2)}) collective-permute-start(bf16[32,3584]{1,0:T(8,128)(2,1)S(1)} %get-tuple-element.39), channel_id=1, source_target_pairs={{0,1},{1,0},{2,3},{3,2},{4,5},{5,4},{6,7},{7,6},{8,9},{9,8},{10,11... | collective-permute-start | bytes 688136 | tf_op jit(solution)/shard_map/ppermute | solution.py:59
  26.3 4.7 %copy-start = (bf16[2,36864]{1,0:T(2,128)(2,1)S(1)}, bf16[2,36864]{1,0:T(2,128)(2,1)}, u32[]{:S(2)}) copy-start(bf16[2,36864]{1,0:T(2,128)(2,1)} %query_ref.1) | copy-start | bytes 442372
  26.3 4.7 %copy-start.1 = (s32[2,12]{1,0:T(2,128)S(1)}, s32[2,12]{1,0:T(2,128)}, u32[]{:S(2)}) copy-start(s32[2,12]{1,0:T(2,128)} %table_ref.1) | copy-start | bytes 292
  26.3 4.7 %copy-start.2 = (s32[2]{0:T(128)S(1)}, s32[2]{0:T(128)}, u32[]{:S(2)}) copy-start(s32[2]{0:T(128)} %length_ref.1) | copy-start | bytes 28
  27.2 7.0 %collective-permute-start.14 = (bf16[8,7168]{1,0:T(8,128)(2,1)S(1)}, bf16[8,7168]{1,0:T(8,128)(2,1)S(1)}, u32[]{:S(2)}, u32[]{:S(2)}) collective-permute-start(bf16[8,7168]{1,0:T(8,128)(2,1)S(1)} %get-tuple-element.41), channel_id=1, source_target_pairs={{0,6},{1,7},{2,4},{3,5},{4,2},{5,3},{6,0},{7,1},{8,14},{9,15},{10,... | collective-permute-start | bytes 344072 | tf_op jit(solution)/shard_map/ppermute | solution.py:59
  28.8 7.3 %collective-permute-start.15 = (bf16[8,7168]{1,0:T(8,128)(2,1)S(1)}, bf16[8,7168]{1,0:T(8,128)(2,1)S(1)}, u32[]{:S(2)}, u32[]{:S(2)}) collective-permute-start(bf16[8,7168]{1,0:T(8,128)(2,1)S(1)} %get-tuple-element.42), channel_id=1, source_target_pairs={{0,4},{1,5},{2,6},{3,7},{4,0},{5,1},{6,2},{7,3},{8,12},{9,13},{10,... | collective-permute-start | bytes 344072 | tf_op jit(solution)/shard_map/ppermute | solution.py:59
  29.9 6.2 %collective-permute-start.16 = (bf16[8,7168]{1,0:T(8,128)(2,1)S(1)}, bf16[8,7168]{1,0:T(8,128)(2,1)S(1)}, u32[]{:S(2)}, u32[]{:S(2)}) collective-permute-start(bf16[8,7168]{1,0:T(8,128)(2,1)S(1)} %get-tuple-element.43), channel_id=1, source_target_pairs={{0,2},{1,3},{2,0},{3,1},{4,6},{5,7},{6,4},{7,5},{8,10},{9,11},{10,... | collective-permute-start | bytes 344072 | tf_op jit(solution)/shard_map/ppermute | solution.py:59
  36.1 5.3 %collective-permute-start.17 = (bf16[2,7168]{1,0:T(2,128)(2,1)S(1)}, bf16[2,7168]{1,0:T(2,128)(2,1)S(1)}, u32[]{:S(2)}, u32[]{:S(2)}) collective-permute-start(bf16[2,7168]{1,0:T(2,128)(2,1)S(1)} %get-tuple-element.45), channel_id=1, source_target_pairs={{0,16},{1,17},{2,18},{3,19},{4,20},{5,21},{6,22},{7,23},{8,24},{9,... | collective-permute-start | bytes 86024 | tf_op jit(solution)/shard_map/ppermute | solution.py:59
  37.9 5.7 %collective-permute-start.18 = (bf16[2,7168]{1,0:T(2,128)(2,1)S(1)}, bf16[2,7168]{1,0:T(2,128)(2,1)S(1)}, u32[]{:S(2)}, u32[]{:S(2)}) collective-permute-start(bf16[2,7168]{1,0:T(2,128)(2,1)S(1)} %get-tuple-element.46), channel_id=1, source_target_pairs={{0,24},{1,25},{2,26},{3,27},{4,28},{5,29},{6,30},{7,31},{8,16},{9,... | collective-permute-start | bytes 86024 | tf_op jit(solution)/shard_map/ppermute | solution.py:59
  39.2 4.4 %collective-permute-start.19 = (bf16[2,7168]{1,0:T(2,128)(2,1)S(1)}, bf16[2,7168]{1,0:T(2,128)(2,1)S(1)}, u32[]{:S(2)}, u32[]{:S(2)}) collective-permute-start(bf16[2,7168]{1,0:T(2,128)(2,1)S(1)} %get-tuple-element.47), channel_id=1, source_target_pairs={{0,8},{1,9},{2,10},{3,11},{4,12},{5,13},{6,14},{7,15},{8,0},{9,1},... | collective-permute-start | bytes 86024 | tf_op jit(solution)/shard_map/ppermute | solution.py:59

commit v12 on v11

--- a/solution.py
+++ b/solution.py
@@ -161,8 +161,9 @@
     return x if rows >= 128 else jnp.concatenate([x] * (128 // rows), axis=0)
 
 
-def near_kernel(near_ref, gate_ref, up_ref, *refs):
-    gate_out, up_out = refs[-2:]
+def near_kernel(ep_count, near_ref, gate_ref, up_ref, *refs):
+    gate_out, up_out, weight_out = refs[-3:]
+    weight_out[...] = jnp.broadcast_to(row_weights(near_ref, gate_ref.shape[1] // 2, ep_count), weight_out.shape)
     rows, width = near_ref.shape[0], gate_ref.shape[1]
     at = pl.ds(half_start(width, True), width // 2)
     x = padded(near_ref[:, : width // 2])
@@ -194,12 +195,12 @@
         send_ref[:, columns] = jnp.where(first, out[rows:], out[:rows]).astype(bf16)
 
 
-def far_kernel(ep_count, near_ref, far_ref, gate_ref, up_ref, gate_in, up_in, down_ref, *refs):
+def far_kernel(weight_ref, far_ref, gate_ref, up_ref, gate_in, up_in, down_ref, *refs):
     inner_ref, keep_ref, send_ref = refs[-3:]
-    rows, width = near_ref.shape[0], gate_ref.shape[1]
+    rows, width = weight_ref.shape[0], gate_ref.shape[1]
     half = width // 2
     at = pl.ds(half_start(width, False), half)
-    row_weight = row_weights(near_ref, half, ep_count)
+    row_weight = weight_ref[:, :1]
     x = padded(far_ref[:, :half])
     gate = gate_in[...] + jnp.dot(x, gate_ref[0, at, :], preferred_element_type=f32)[:rows]
     up = up_in[...] + jnp.dot(x, up_ref[0, at, :], preferred_element_type=f32)[:rows]
@@ -208,35 +209,35 @@
     down_half(inner, row_weight, down_ref, 0, keep_ref, send_ref)
 
 
-def rest_kernel(ep_count, near_ref, inner_ref, down_ref, keep_ref, send_ref):
+def rest_kernel(weight_ref, inner_ref, down_ref, keep_ref, send_ref):
     half = keep_ref.shape[1]
-    down_half(inner_ref[...], row_weights(near_ref, half, ep_count), down_ref, half, keep_ref, send_ref)
+    down_half(inner_ref[...], weight_ref[:, :1], down_ref, half, keep_ref, send_ref)
 
 
 def estimate(rows, weights):
     return pl.CostEstimate(flops=2 * rows * weights, bytes_accessed=2 * weights, transcendentals=0)
 
 
-def near_products(near, gate, up, down, *after):
+def near_products(near, gate, up, down, ep_count, *after):
     rows = near.shape[0]
     width, units = gate.shape[1:]
     acc = pltpu.VMEM((rows, units), f32)
     return pl.pallas_call(
-        near_kernel,
-        out_shape=(acc, acc),
+        functools.partial(near_kernel, ep_count),
+        out_shape=(acc, acc, pltpu.VMEM((rows, LANES), f32)),
         in_specs=[in_vmem()] * 4 + [anywhere()] * len(after),
-        out_specs=(in_vmem(),) * 2,
+        out_specs=(in_vmem(),) * 3,
         compiler_params=pltpu.CompilerParams(vmem_limit_bytes=8 * MIB),
         cost_estimate=estimate(rows, width * units),
     )(vmem(near), gate, up, down, *after)
 
 
-def far_products(near, far, gate, up, gate_acc, up_acc, down, ep_count, *after):
-    rows = near.shape[0]
+def far_products(weight, far, gate, up, gate_acc, up_acc, down, *after):
+    rows = weight.shape[0]
     units, width = down.shape[1:]
     half = width // 2
     return pl.pallas_call(
-        functools.partial(far_kernel, ep_count),
+        far_kernel,
         out_shape=(
             pltpu.VMEM((rows, units), bf16),
             pltpu.VMEM((rows // 2, half), f32),
@@ -246,21 +247,21 @@
         out_specs=(in_vmem(),) * 3,
         compiler_params=pltpu.CompilerParams(vmem_limit_bytes=8 * MIB),
         cost_estimate=estimate(rows, 3 * half * units),
-    )(vmem(near), vmem(far), gate, up, vmem(gate_acc), vmem(up_acc), down, *after)
-
-
-def rest_products(near, inner, down, ep_count):
-    rows = near.shape[0]
+    )(vmem(weight), vmem(far), gate, up, vmem(gate_acc), vmem(up_acc), down, *after)
+
+
+def rest_products(weight, inner, down):
+    rows = weight.shape[0]
     units, width = down.shape[1:]
     half = width // 2
     return pl.pallas_call(
-        functools.partial(rest_kernel, ep_count),
+        rest_kernel,
         out_shape=(pltpu.VMEM((rows // 2, half), f32), pltpu.VMEM((rows // 2, half), bf16)),
         in_specs=[in_vmem()] * 3,
         out_specs=(in_vmem(),) * 2,
         compiler_params=pltpu.CompilerParams(vmem_limit_bytes=8 * MIB),
         cost_estimate=estimate(rows, half * units),
-    )(vmem(near), vmem(inner), down)
+    )(vmem(weight), vmem(inner), down)
 
 
 def fold_kernel(arrived, parts, *refs):
@@ -498,12 +499,12 @@
         near = merge([near] + got, MERGE_FLOPS if number < len(stages) - 1 else MERGE_FLOPS // 4, *after)
     far = trade(near, 1)
     arrived, senders, moves = exchange_pages(low, first, dp_count, near)
-    gate_acc, up_acc = near_products(near, gate_weight, up_weight, down_weight, *[sent for sent, _ in moves])
+    gate_acc, up_acc, weight = near_products(near, gate_weight, up_weight, down_weight, ep_count, *[sent for sent, _ in moves])
     inner, keep_a, send_a = far_products(
-        near, far, gate_weight, up_weight, gate_acc, up_acc, down_weight, ep_count, *[got for _, got in moves]
+        weight, far, gate_weight, up_weight, gate_acc, up_acc, down_weight, *[got for _, got in moves]
     )
     got_a = trade(send_a, 1)
-    keep_b, send_b = rest_products(near, inner, down_weight, ep_count)
+    keep_b, send_b = rest_products(weight, inner, down_weight)
     got_b = trade(send_b, 1)
     (sum_a,) = fold([(keep_a, [got_a])], 1, out=pltpu.VMEM(keep_a.shape, f32), flops=MERGE_FLOPS // 4)
     held = [(sum_a, []), (keep_b, [got_b])]

time: 44.4 us -> 44.4 us (level)
  no operation moved by 1% of the time
where the time goes in v12:
time: 44.4 us; the launch traced here: 44.3 us
  starting transfers between devices  19.9 us (45%)
  waiting for transfers between devices  14.5 us (33%)
  Pallas kernels  9.04 us (20%)
  between operations  0.87 us (2%)
    ppermute x20, starting transfers between devices, swap(): return lax.ppermute(x, axes, pairs)  19.9 us
    ppermute x20, waiting for transfers between devices, swap(): return lax.ppermute(x, axes, pairs)  14.5 us
    pallas_call x1, Pallas kernels, attend(): pl.pallas_call(functools.partial(attend_kernel, senders), out_shape=jax.S...  2.35 us
    pallas_call x1, Pallas kernels, far_products(): pl.pallas_call(far_kernel, out_shape=(pltpu.VMEM((rows, units), bf16), pl...  1.73 us
    pallas_call x1, Pallas kernels, fetch(): pl.pallas_call(fetch_kernel, out_shape=tuple((pltpu.VMEM(x.shape, x.dtype...  1.27 us
    pallas_call x1, Pallas kernels, near_products(): pl.pallas_call(functools.partial(near_kernel, ep_count), out_shape=(acc,...  1.13 us
  transfers between devices with their start and end apart: 20, of which 10 were waited for; matrix products, arithmetic and copies ran while one was open for 0% of the time, Pallas kernels for 14%

profile of v12, /device:TPU:0, one launch (start us, length us, event | category | flops | bytes accessed | tf_op | source)
XLA Modules:
  0.0 44.3 jit_solution(38298850077985223)
XLA Ops:
  0.6 0.5 %collective-permute-start.1 = (s32[2,4]{1,0:T(2,128)}, s32[2,4]{1,0:T(2,128)S(1)}, u32[]{:S(2)}, u32[]{:S(2)}) collective-permute-start(s32[2,4]{1,0:T(2,128)} %refs_1_.1), channel_id=1, source_target_pairs={{0,1},{1,0},{2,3},{3,2},{4,5},{5,4},{6,7},{7,6},{8,9},{9,8},{10,11... | collective-permute-start | bytes 104 | tf_op jit(solution)/shard_map/ppermute | solution.py:59
  1.2 0.4 collective-permute-start
  1.7 1.3 %shard_map.131 = (bf16[2,7168]{1,0:T(2,128)(2,1)S(1)}, s32[2,4]{1,0:T(2,128)S(1)}, f32[2,4]{1,0:T(2,128)S(1)}, bf16[24,18432]{1,0:T(8,128)(2,1)S(1)}, s32[1,6]{1,0:T(1,128)S(1)}, /*index=5*/s32[1,6]{1,0:T(1,128)S(1)}) custom-call(bf16[2,7168]{1,0:T(2,128)(2,1)} %refs_0_.2, s32[2,4]{1,0:T(2,128)} %refs_1_.1, f32[2,4]{1,0:T(2,128)} %refs_2_.1, ...), custom_call_target="tpu_custom_call" | custom-call | flops 1250000000 | bytes 1048576 | tf_op jit(solution)/shard_map/pallas_call | solution.py:86
  3.1 3.7 %collective-permute-start.5 = (bf16[4,3712]{1,0:T(4,128)(2,1)S(1)}, bf16[4,3712]{1,0:T(4,128)(2,1)S(1)}, u32[]{:S(2)}, u32[]{:S(2)}) collective-permute-start(bf16[4,3712]{1,0:T(4,128)(2,1)S(1)} %shard_map.132.after_ref.refs_0_), channel_id=1, source_target_pairs={{0,16},{1,17},{2,18},{3,19},{4,20},{5,21},{6,22},{7,23},{8,24},{9,... | collective-permute-start | bytes 89096 | tf_op jit(solution)/shard_map/ppermute | solution.py:59
  6.8 1.3 %collective-permute-start.4 = (bf16[4,3712]{1,0:T(4,128)(2,1)S(1)}, bf16[4,3712]{1,0:T(4,128)(2,1)S(1)}, u32[]{:S(2)}, u32[]{:S(2)}) collective-permute-start(bf16[4,3712]{1,0:T(4,128)(2,1)S(1)} %shard_map.132.after_ref.refs_0_), channel_id=1, source_target_pairs={{0,24},{1,25},{2,26},{3,27},{4,28},{5,29},{6,30},{7,31},{8,16},{9,... | collective-permute-start | bytes 89096 | tf_op jit(solution)/shard_map/ppermute | solution.py:59
  8.4 0.6 %shard_map.133 = (bf16[4,18432]{1,0:T(4,128)(2,1)S(1)}, bf16[4,18432]{1,0:T(4,128)(2,1)S(1)}) custom-call(s32[1,6]{1,0:T(1,128)S(1)} %get-tuple-element.29.page_ref, s32[1,6]{1,0:T(1,128)S(1)} %get-tuple-element.30.dest_ref, bf16[24,18432]{1,0:T(8,128)(2,1)S(1)} %get-tuple-element.31.pool_ref, bf16[4,3712]{1,0:T(4,128)(2,1)S(1)} %shard_map.132.after_ref.refs_0_), custom_call_target="tpu_custom_call" | custom-call | bytes 1769472 | tf_op jit(solution)/shard_map/pallas_call | solution.py:327
  9.1 1.6 %collective-permute-start.9 = (bf16[4,18432]{1,0:T(4,128)(2,1)S(1)}, bf16[4,18432]{1,0:T(4,128)(2,1)S(1)}, u32[]{:S(2)}, u32[]{:S(2)}) collective-permute-start(bf16[4,18432]{1,0:T(4,128)(2,1)S(1)} %get-tuple-element.32.refs_4_), channel_id=1, source_target_pairs={{0,2},{1,3},{2,0},{3,1},{4,6},{5,7},{6,4},{7,5},{8,10},{9,11},{10,... | collective-permute-start | bytes 442376 | tf_op jit(solution)/shard_map/ppermute | solution.py:59
  10.6 1.9 %collective-permute-done.4.refs_2_ = bf16[4,3712]{1,0:T(4,128)(2,1)S(1)} collective-permute-done((bf16[4,3712]{1,0:T(4,128)(2,1)S(1)}, bf16[4,3712]{1,0:T(4,128)(2,1)S(1)}, u32[]{:S(2)}, u32[]{:S(2)}) %collective-permute-start.4) | collective-permute-done | bytes 29728 | tf_op jit(solution)/shard_map/ppermute | solution.py:59
  12.6 2.5 %collective-permute-start.8 = (bf16[16,3712]{1,0:T(8,128)(2,1)S(1)}, bf16[16,3712]{1,0:T(8,128)(2,1)S(1)}, u32[]{:S(2)}, u32[]{:S(2)}) collective-permute-start(bf16[16,3712]{1,0:T(8,128)(2,1)S(1)} %shard_map.134.refs_0_), channel_id=1, source_target_pairs={{0,6},{1,7},{2,4},{3,5},{4,2},{5,3},{6,0},{7,1},{8,14},{9,15},{10,... | collective-permute-start | bytes 356360 | tf_op jit(solution)/shard_map/ppermute | solution.py:59
  15.1 0.5 %collective-permute-start.7 = (bf16[16,3712]{1,0:T(8,128)(2,1)S(1)}, bf16[16,3712]{1,0:T(8,128)(2,1)S(1)}, u32[]{:S(2)}, u32[]{:S(2)}) collective-permute-start(bf16[16,3712]{1,0:T(8,128)(2,1)S(1)} %shard_map.134.refs_0_), channel_id=1, source_target_pairs={{0,4},{1,5},{2,6},{3,7},{4,0},{5,1},{6,2},{7,3},{8,12},{9,13},{10,... | collective-permute-start | bytes 356360 | tf_op jit(solution)/shard_map/ppermute | solution.py:59
  15.6 0.5 %collective-permute-start.6 = (bf16[16,3712]{1,0:T(8,128)(2,1)S(1)}, bf16[16,3712]{1,0:T(8,128)(2,1)S(1)}, u32[]{:S(2)}, u32[]{:S(2)}) collective-permute-start(bf16[16,3712]{1,0:T(8,128)(2,1)S(1)} %shard_map.134.refs_0_), channel_id=1, source_target_pairs={{0,2},{1,3},{2,0},{3,1},{4,6},{5,7},{6,4},{7,5},{8,10},{9,11},{10,... | collective-permute-start | bytes 356360 | tf_op jit(solution)/shard_map/ppermute | solution.py:59
  16.1 3.1 %collective-permute-done.8.refs_3_ = bf16[16,3712]{1,0:T(8,128)(2,1)S(1)} collective-permute-done((bf16[16,3712]{1,0:T(8,128)(2,1)S(1)}, bf16[16,3712]{1,0:T(8,128)(2,1)S(1)}, u32[]{:S(2)}, u32[]{:S(2)}) %collective-permute-start.8) | collective-permute-done | bytes 118816 | tf_op jit(solution)/shard_map/ppermute | solution.py:59
  19.2 1.6 %collective-permute-done.7.refs_2_ = bf16[16,3712]{1,0:T(8,128)(2,1)S(1)} collective-permute-done((bf16[16,3712]{1,0:T(8,128)(2,1)S(1)}, bf16[16,3712]{1,0:T(8,128)(2,1)S(1)}, u32[]{:S(2)}, u32[]{:S(2)}) %collective-permute-start.7) | collective-permute-done | bytes 118816 | tf_op jit(solution)/shard_map/ppermute | solution.py:59
  21.0 0.6 %collective-permute-start.11 = (bf16[4,18432]{1,0:T(4,128)(2,1)S(1)}, bf16[4,18432]{1,0:T(4,128)(2,1)S(1)}, u32[]{:S(2)}, u32[]{:S(2)}) collective-permute-start(bf16[4,18432]{1,0:T(4,128)(2,1)S(1)} %shard_map.136.refs_1_), channel_id=1, source_target_pairs={{0,1},{1,0},{2,3},{3,2},{4,5},{5,4},{6,7},{7,6},{8,9},{9,8},{10,11... | collective-permute-start | bytes 442376 | tf_op jit(solution)/shard_map/ppermute | solution.py:59
  21.6 1.1 %shard_map.137 = (f32[64,512]{1,0:T(8,128)S(1)}, f32[64,512]{1,0:T(8,128)S(1)}, f32[64,128]{1,0:T(8,128)S(1)}) custom-call(bf16[64,3712]{1,0:T(8,128)(2,1)S(1)} %shard_map.135.refs_2_.near_ref, bf16[1,7168,512]{2,1,0:T(8,128)(2,1)S(1)} %bitcast.3, bf16[1,7168,512]{2,1,0:T(8,128)(2,1)S(1)} %bitcast.5, bf16[1,512,7168]{2,1,0:T(8,128)(2,1)S(1)} %bitcast.1, ...), custom_call_target="tpu_custom_call" | custom-call | flops 469762048 | bytes 7340032 | tf_op jit(solution)/shard_map/pallas_call | solution.py:225
  23.0 1.7 %shard_map.138 = (bf16[64,512]{1,0:T(8,128)(2,1)S(1)}, f32[32,3584]{1,0:T(8,128)S(1)}, bf16[32,3584]{1,0:T(8,128)(2,1)S(1)}) custom-call(f32[64,128]{1,0:T(8,128)S(1)} %get-tuple-element.34.weight_ref, bf16[64,3712]{1,0:T(8,128)(2,1)S(1)} %collective-permute-done.10.far_ref, bf16[1,7168,512]{2,1,0:T(8,128)(2,1)S(1)} %bitcast.3, ...), custom_call_target="tpu_custom_call" | custom-call | flops 704643072 | bytes 11010048 | tf_op jit(solution)/shard_map/pallas_call | solution.py:239
  24.9 0.7 %shard_map.140 = (f32[32,3584]{1,0:T(8,128)S(1)}, bf16[32,3584]{1,0:T(8,128)(2,1)S(1)}) custom-call(f32[64,128]{1,0:T(8,128)S(1)} %get-tuple-element.34.weight_ref, bf16[64,512]{1,0:T(8,128)(2,1)S(1)} %get-tuple-element.39.inner_ref, bf16[1,512,7168]{2,1,0:T(8,128)(2,1)S(1)} %bitcast.1), custom_call_target="tpu_custom_call" | custom-call | flops 234881024 | bytes 3670016 | tf_op jit(solution)/shard_map/pallas_call | solution.py:257
  25.6 0.4 collective-permute-start.13
  26.0 0.2 collective-permute-done.12.refs_1_
  26.3 0.8 %collective-permute-done.13.refs_2_ = bf16[32,3584]{1,0:T(8,128)(2,1)S(1)} collective-permute-done((bf16[32,3584]{1,0:T(8,128)(2,1)S(1)}, bf16[32,3584]{1,0:T(8,128)(2,1)S(1)}, u32[]{:S(2)}, u32[]{:S(2)}) %collective-permute-start.13) | collective-permute-done | bytes 229408 | tf_op jit(solution)/shard_map/ppermute | solution.py:59
  27.2 1.6 %collective-permute-start.14 = (bf16[8,7168]{1,0:T(8,128)(2,1)S(1)}, bf16[8,7168]{1,0:T(8,128)(2,1)S(1)}, u32[]{:S(2)}, u32[]{:S(2)}) collective-permute-start(bf16[8,7168]{1,0:T(8,128)(2,1)S(1)} %get-tuple-element.43), channel_id=1, source_target_pairs={{0,6},{1,7},{2,4},{3,5},{4,2},{5,3},{6,0},{7,1},{8,14},{9,15},{10,... | collective-permute-start | bytes 344072 | tf_op jit(solution)/shard_map/ppermute | solution.py:59
  28.8 1.1 %collective-permute-start.15 = (bf16[8,7168]{1,0:T(8,128)(2,1)S(1)}, bf16[8,7168]{1,0:T(8,128)(2,1)S(1)}, u32[]{:S(2)}, u32[]{:S(2)}) collective-permute-start(bf16[8,7168]{1,0:T(8,128)(2,1)S(1)} %get-tuple-element.44), channel_id=1, source_target_pairs={{0,4},{1,5},{2,6},{3,7},{4,0},{5,1},{6,2},{7,3},{8,12},{9,13},{10,... | collective-permute-start | bytes 344072 | tf_op jit(solution)/shard_map/ppermute | solution.py:59
  29.9 0.9 %collective-permute-start.16 = (bf16[8,7168]{1,0:T(8,128)(2,1)S(1)}, bf16[8,7168]{1,0:T(8,128)(2,1)S(1)}, u32[]{:S(2)}, u32[]{:S(2)}) collective-permute-start(bf16[8,7168]{1,0:T(8,128)(2,1)S(1)} %get-tuple-element.45), channel_id=1, source_target_pairs={{0,2},{1,3},{2,0},{3,1},{4,6},{5,7},{6,4},{7,5},{8,10},{9,11},{10,... | collective-permute-start | bytes 344072 | tf_op jit(solution)/shard_map/ppermute | solution.py:59
  31.0 2.4 %shard_map.143.refs_4_ = bf16[2,32768]{1,0:T(2,128)(2,1)} custom-call(s32[2]{0:T(128)S(1)} %copy-done.2, s32[2,12]{1,0:T(2,128)S(1)} %copy-done.1, bf16[2,36864]{1,0:T(2,128)(2,1)S(1)} %copy-done, bf16[24,18432]{1,0:T(8,128)(2,1)S(1)} %get-tuple-element.31.pool_ref, bf16[8,18432]{1,0:T(8,128)(2,1)S(1)} %shard_map.142.arrived_ref), custom_call_target="tpu_custom_call" | custom-call | flops 1073741824 | bytes 4194304 | tf_op jit(solution)/shard_map/pallas_call | solution.py:452
  33.3 0.8 %collective-permute-done.14.refs_1_ = bf16[8,7168]{1,0:T(8,128)(2,1)S(1)} collective-permute-done((bf16[8,7168]{1,0:T(8,128)(2,1)S(1)}, bf16[8,7168]{1,0:T(8,128)(2,1)S(1)}, u32[]{:S(2)}, u32[]{:S(2)}) %collective-permute-start.14) | collective-permute-done | bytes 114720 | tf_op jit(solution)/shard_map/ppermute | solution.py:59
  34.1 1.9 %collective-permute-done.15.refs_2_ = bf16[8,7168]{1,0:T(8,128)(2,1)S(1)} collective-permute-done((bf16[8,7168]{1,0:T(8,128)(2,1)S(1)}, bf16[8,7168]{1,0:T(8,128)(2,1)S(1)}, u32[]{:S(2)}, u32[]{:S(2)}) %collective-permute-start.15) | collective-permute-done | bytes 114720 | tf_op jit(solution)/shard_map/ppermute | solution.py:59
  36.1 1.8 %collective-permute-start.17 = (bf16[2,7168]{1,0:T(2,128)(2,1)S(1)}, bf16[2,7168]{1,0:T(2,128)(2,1)S(1)}, u32[]{:S(2)}, u32[]{:S(2)}) collective-permute-start(bf16[2,7168]{1,0:T(2,128)(2,1)S(1)} %get-tuple-element.47), channel_id=1, source_target_pairs={{0,16},{1,17},{2,18},{3,19},{4,20},{5,21},{6,22},{7,23},{8,24},{9,... | collective-permute-start | bytes 86024 | tf_op jit(solution)/shard_map/ppermute | solution.py:59
  37.9 1.2 %collective-permute-start.18 = (bf16[2,7168]{1,0:T(2,128)(2,1)S(1)}, bf16[2,7168]{1,0:T(2,128)(2,1)S(1)}, u32[]{:S(2)}, u32[]{:S(2)}) collective-permute-start(bf16[2,7168]{1,0:T(2,128)(2,1)S(1)} %get-tuple-element.48), channel_id=1, source_target_pairs={{0,24},{1,25},{2,26},{3,27},{4,28},{5,29},{6,30},{7,31},{8,16},{9,... | collective-permute-start | bytes 86024 | tf_op jit(solution)/shard_map/ppermute | solution.py:59
  39.2 0.5 %collective-permute-start.19 = (bf16[2,7168]{1,0:T(2,128)(2,1)S(1)}, bf16[2,7168]{1,0:T(2,128)(2,1)S(1)}, u32[]{:S(2)}, u32[]{:S(2)}) collective-permute-start(bf16[2,7168]{1,0:T(2,128)(2,1)S(1)} %get-tuple-element.49), channel_id=1, source_target_pairs={{0,8},{1,9},{2,10},{3,11},{4,12},{5,13},{6,14},{7,15},{8,0},{9,1},... | collective-permute-start | bytes 86024 | tf_op jit(solution)/shard_map/ppermute | solution.py:59
  39.7 1.8 %collective-permute-done.17.refs_1_ = bf16[2,7168]{1,0:T(2,128)(2,1)S(1)} collective-permute-done((bf16[2,7168]{1,0:T(2,128)(2,1)S(1)}, bf16[2,7168]{1,0:T(2,128)(2,1)S(1)}, u32[]{:S(2)}, u32[]{:S(2)}) %collective-permute-start.17) | collective-permute-done | bytes 28704 | tf_op jit(solution)/shard_map/ppermute | solution.py:59
  41.4 2.2 %collective-permute-done.18.refs_2_ = bf16[2,7168]{1,0:T(2,128)(2,1)S(1)} collective-permute-done((bf16[2,7168]{1,0:T(2,128)(2,1)S(1)}, bf16[2,7168]{1,0:T(2,128)(2,1)S(1)}, u32[]{:S(2)}, u32[]{:S(2)}) %collective-permute-start.18) | collective-permute-done | bytes 28704 | tf_op jit(solution)/shard_map/ppermute | solution.py:59
  43.6 0.7 %shard_map.145 = bf16[2,7168]{1,0:T(2,128)(2,1)} custom-call(f32[2,7168]{1,0:T(2,128)S(1)} %get-tuple-element.46.refs_0_, bf16[2,7168]{1,0:T(2,128)(2,1)S(1)} %collective-permute-done.17.refs_1_, bf16[2,7168]{1,0:T(2,128)(2,1)S(1)} %collective-permute-done.18.refs_2_, bf16[2,7168]{1,0:T(2,128)(2,1)S(1)} %collective-permute-done.19.refs_3_), custom_call_target="tpu_custom_call" | custom-call | bytes 114688 | tf_op jit(solution)/shard_map/pallas_call | solution.py:289
  (44 shorter events, 1.5 us)
Async XLA Ops:
  0.6 2.3 %collective-permute-start.1 = (s32[2,4]{1,0:T(2,128)}, s32[2,4]{1,0:T(2,128)S(1)}, u32[]{:S(2)}, u32[]{:S(2)}) collective-permute-start(s32[2,4]{1,0:T(2,128)} %refs_1_.1), channel_id=1, source_target_pairs={{0,1},{1,0},{2,3},{3,2},{4,5},{5,4},{6,7},{7,6},{8,9},{9,8},{10,11... | collective-permute-start | bytes 104 | tf_op jit(solution)/shard_map/ppermute | solution.py:59
  1.1 1.8 %collective-permute-start.2 = (f32[2,4]{1,0:T(2,128)}, f32[2,4]{1,0:T(2,128)S(1)}, u32[]{:S(2)}, u32[]{:S(2)}) collective-permute-start(f32[2,4]{1,0:T(2,128)} %refs_2_.1), channel_id=1, source_target_pairs={{0,1},{1,0},{2,3},{3,2},{4,5},{5,4},{6,7},{7,6},{8,9},{9,8},{10,11... | collective-permute-start | bytes 104 | tf_op jit(solution)/shard_map/ppermute | solution.py:59
  1.2 1.7 %collective-permute-start = (bf16[2,7168]{1,0:T(2,128)(2,1)}, bf16[2,7168]{1,0:T(2,128)(2,1)S(1)}, u32[]{:S(2)}, u32[]{:S(2)}) collective-permute-start(bf16[2,7168]{1,0:T(2,128)(2,1)} %refs_0_.2), channel_id=1, source_target_pairs={{0,1},{1,0},{2,3},{3,2},{4,5},{5,4},{6,7},{7,6},{8,9},{9,8},{10,11... | collective-permute-start | bytes 86024 | tf_op jit(solution)/shard_map/ppermute | solution.py:59
  3.1 7.5 %collective-permute-start.5 = (bf16[4,3712]{1,0:T(4,128)(2,1)S(1)}, bf16[4,3712]{1,0:T(4,128)(2,1)S(1)}, u32[]{:S(2)}, u32[]{:S(2)}) collective-permute-start(bf16[4,3712]{1,0:T(4,128)(2,1)S(1)} %shard_map.132.after_ref.refs_0_), channel_id=1, source_target_pairs={{0,16},{1,17},{2,18},{3,19},{4,20},{5,21},{6,22},{7,23},{8,24},{9,... | collective-permute-start | bytes 89096 | tf_op jit(solution)/shard_map/ppermute | solution.py:59
  6.8 5.7 %collective-permute-start.4 = (bf16[4,3712]{1,0:T(4,128)(2,1)S(1)}, bf16[4,3712]{1,0:T(4,128)(2,1)S(1)}, u32[]{:S(2)}, u32[]{:S(2)}) collective-permute-start(bf16[4,3712]{1,0:T(4,128)(2,1)S(1)} %shard_map.132.after_ref.refs_0_), channel_id=1, source_target_pairs={{0,24},{1,25},{2,26},{3,27},{4,28},{5,29},{6,30},{7,31},{8,16},{9,... | collective-permute-start | bytes 89096 | tf_op jit(solution)/shard_map/ppermute | solution.py:59
  8.2 4.3 %collective-permute-start.3 = (bf16[4,3712]{1,0:T(4,128)(2,1)S(1)}, bf16[4,3712]{1,0:T(4,128)(2,1)S(1)}, u32[]{:S(2)}, u32[]{:S(2)}) collective-permute-start(bf16[4,3712]{1,0:T(4,128)(2,1)S(1)} %shard_map.132.after_ref.refs_0_), channel_id=1, source_target_pairs={{0,8},{1,9},{2,10},{3,11},{4,12},{5,13},{6,14},{7,15},{8,0},{9,1},... | collective-permute-start | bytes 89096 | tf_op jit(solution)/shard_map/ppermute | solution.py:59
  9.0 12.6 %slice-start = ((s8[7340032]{0:T(1024)(128)(4,1)}), s8[4194304]{0:T(1024)(128)(4,1)S(1)}, s32[]{:S(2)}) async-start(s8[7340032]{0:T(1024)(128)(4,1)} %bitcast), calls=%async_computation | async-start | bytes 8388608
  9.0 12.6 %slice-start.2 = ((s8[7340032]{0:T(1024)(128)(4,1)}), s8[4194304]{0:T(1024)(128)(4,1)S(1)}, s32[]{:S(2)}) async-start(s8[7340032]{0:T(1024)(128)(4,1)} %bitcast.2), calls=%async_computation.2 | async-start | bytes 8388608
  9.0 12.6 %slice-start.4 = ((s8[7340032]{0:T(1024)(128)(4,1)}), s8[4194304]{0:T(1024)(128)(4,1)S(1)}, s32[]{:S(2)}) async-start(s8[7340032]{0:T(1024)(128)(4,1)} %bitcast.4), calls=%async_computation.4 | async-start | bytes 8388608
  9.0 12.6 %slice-start.1 = ((s8[7340032]{0:T(1024)(128)(4,1)}), s8[3145728]{0:T(1024)(128)(4,1)S(1)}, s32[]{:S(2)}) async-start(s8[7340032]{0:T(1024)(128)(4,1)} %bitcast), calls=%async_computation.1 | async-start | bytes 6291456
  9.0 12.6 %slice-start.3 = ((s8[7340032]{0:T(1024)(128)(4,1)}), s8[3145728]{0:T(1024)(128)(4,1)S(1)}, s32[]{:S(2)}) async-start(s8[7340032]{0:T(1024)(128)(4,1)} %bitcast.2), calls=%async_computation.3 | async-start | bytes 6291456
  9.0 12.6 %slice-start.5 = ((s8[7340032]{0:T(1024)(128)(4,1)}), s8[3145728]{0:T(1024)(128)(4,1)S(1)}, s32[]{:S(2)}) async-start(s8[7340032]{0:T(1024)(128)(4,1)} %bitcast.4), calls=%async_computation.5 | async-start | bytes 6291456
  9.1 7.1 %collective-permute-start.9 = (bf16[4,18432]{1,0:T(4,128)(2,1)S(1)}, bf16[4,18432]{1,0:T(4,128)(2,1)S(1)}, u32[]{:S(2)}, u32[]{:S(2)}) collective-permute-start(bf16[4,18432]{1,0:T(4,128)(2,1)S(1)} %get-tuple-element.32.refs_4_), channel_id=1, source_target_pairs={{0,2},{1,3},{2,0},{3,1},{4,6},{5,7},{6,4},{7,5},{8,10},{9,11},{10,... | collective-permute-start | bytes 442376 | tf_op jit(solution)/shard_map/ppermute | solution.py:59
  12.6 6.6 %collective-permute-start.8 = (bf16[16,3712]{1,0:T(8,128)(2,1)S(1)}, bf16[16,3712]{1,0:T(8,128)(2,1)S(1)}, u32[]{:S(2)}, u32[]{:S(2)}) collective-permute-start(bf16[16,3712]{1,0:T(8,128)(2,1)S(1)} %shard_map.134.refs_0_), channel_id=1, source_target_pairs={{0,6},{1,7},{2,4},{3,5},{4,2},{5,3},{6,0},{7,1},{8,14},{9,15},{10,... | collective-permute-start | bytes 356360 | tf_op jit(solution)/shard_map/ppermute | solution.py:59
  15.1 5.7 %collective-permute-start.7 = (bf16[16,3712]{1,0:T(8,128)(2,1)S(1)}, bf16[16,3712]{1,0:T(8,128)(2,1)S(1)}, u32[]{:S(2)}, u32[]{:S(2)}) collective-permute-start(bf16[16,3712]{1,0:T(8,128)(2,1)S(1)} %shard_map.134.refs_0_), channel_id=1, source_target_pairs={{0,4},{1,5},{2,6},{3,7},{4,0},{5,1},{6,2},{7,3},{8,12},{9,13},{10,... | collective-permute-start | bytes 356360 | tf_op jit(solution)/shard_map/ppermute | solution.py:59
  15.6 5.2 %collective-permute-start.6 = (bf16[16,3712]{1,0:T(8,128)(2,1)S(1)}, bf16[16,3712]{1,0:T(8,128)(2,1)S(1)}, u32[]{:S(2)}, u32[]{:S(2)}) collective-permute-start(bf16[16,3712]{1,0:T(8,128)(2,1)S(1)} %shard_map.134.refs_0_), channel_id=1, source_target_pairs={{0,2},{1,3},{2,0},{3,1},{4,6},{5,7},{6,4},{7,5},{8,10},{9,11},{10,... | collective-permute-start | bytes 356360 | tf_op jit(solution)/shard_map/ppermute | solution.py:59
  20.8 2.1 %collective-permute-start.10 = (bf16[64,3712]{1,0:T(8,128)(2,1)S(1)}, bf16[64,3712]{1,0:T(8,128)(2,1)S(1)}, u32[]{:S(2)}, u32[]{:S(2)}) collective-permute-start(bf16[64,3712]{1,0:T(8,128)(2,1)S(1)} %shard_map.135.refs_2_.near_ref), channel_id=1, source_target_pairs={{0,1},{1,0},{2,3},{3,2},{4,5},{5,4},{6,7},{7,6},{8,9},{9,8},{10,11... | collective-permute-start | bytes 1425416 | tf_op jit(solution)/shard_map/ppermute | solution.py:59
  21.0 1.9 %collective-permute-start.11 = (bf16[4,18432]{1,0:T(4,128)(2,1)S(1)}, bf16[4,18432]{1,0:T(4,128)(2,1)S(1)}, u32[]{:S(2)}, u32[]{:S(2)}) collective-permute-start(bf16[4,18432]{1,0:T(4,128)(2,1)S(1)} %shard_map.136.refs_1_), channel_id=1, source_target_pairs={{0,1},{1,0},{2,3},{3,2},{4,5},{5,4},{6,7},{7,6},{8,9},{9,8},{10,11... | collective-permute-start | bytes 442376 | tf_op jit(solution)/shard_map/ppermute | solution.py:59
  24.7 1.6 %collective-permute-start.12 = (bf16[32,3584]{1,0:T(8,128)(2,1)S(1)}, bf16[32,3584]{1,0:T(8,128)(2,1)S(1)}, u32[]{:S(2)}, u32[]{:S(2)}) collective-permute-start(bf16[32,3584]{1,0:T(8,128)(2,1)S(1)} %get-tuple-element.38), channel_id=1, source_target_pairs={{0,1},{1,0},{2,3},{3,2},{4,5},{5,4},{6,7},{7,6},{8,9},{9,8},{10,11... | collective-permute-start | bytes 688136 | tf_op jit(solution)/shard_map/ppermute | solution.py:59
  25.6 1.6 %collective-permute-start.13 = (bf16[32,3584]{1,0:T(8,128)(2,1)S(1)}, bf16[32,3584]{1,0:T(8,128)(2,1)S(1)}, u32[]{:S(2)}, u32[]{:S(2)}) collective-permute-start(bf16[32,3584]{1,0:T(8,128)(2,1)S(1)} %get-tuple-element.41), channel_id=1, source_target_pairs={{0,1},{1,0},{2,3},{3,2},{4,5},{5,4},{6,7},{7,6},{8,9},{9,8},{10,11... | collective-permute-start | bytes 688136 | tf_op jit(solution)/shard_map/ppermute | solution.py:59
  26.2 4.7 %copy-start = (bf16[2,36864]{1,0:T(2,128)(2,1)S(1)}, bf16[2,36864]{1,0:T(2,128)(2,1)}, u32[]{:S(2)}) copy-start(bf16[2,36864]{1,0:T(2,128)(2,1)} %query_ref.1) | copy-start | bytes 442372
  26.2 4.7 %copy-start.1 = (s32[2,12]{1,0:T(2,128)S(1)}, s32[2,12]{1,0:T(2,128)}, u32[]{:S(2)}) copy-start(s32[2,12]{1,0:T(2,128)} %table_ref.1) | copy-start | bytes 292
  26.3 4.7 %copy-start.2 = (s32[2]{0:T(128)S(1)}, s32[2]{0:T(128)}, u32[]{:S(2)}) copy-start(s32[2]{0:T(128)} %length_ref.1) | copy-start | bytes 28
  27.2 7.0 %collective-permute-start.14 = (bf16[8,7168]{1,0:T(8,128)(2,1)S(1)}, bf16[8,7168]{1,0:T(8,128)(2,1)S(1)}, u32[]{:S(2)}, u32[]{:S(2)}) collective-permute-start(bf16[8,7168]{1,0:T(8,128)(2,1)S(1)} %get-tuple-element.43), channel_id=1, source_target_pairs={{0,6},{1,7},{2,4},{3,5},{4,2},{5,3},{6,0},{7,1},{8,14},{9,15},{10,... | collective-permute-start | bytes 344072 | tf_op jit(solution)/shard_map/ppermute | solution.py:59
  28.8 7.3 %collective-permute-start.15 = (bf16[8,7168]{1,0:T(8,128)(2,1)S(1)}, bf16[8,7168]{1,0:T(8,128)(2,1)S(1)}, u32[]{:S(2)}, u32[]{:S(2)}) collective-permute-start(bf16[8,7168]{1,0:T(8,128)(2,1)S(1)} %get-tuple-element.44), channel_id=1, source_target_pairs={{0,4},{1,5},{2,6},{3,7},{4,0},{5,1},{6,2},{7,3},{8,12},{9,13},{10,... | collective-permute-start | bytes 344072 | tf_op jit(solution)/shard_map/ppermute | solution.py:59
  29.9 6.2 %collective-permute-start.16 = (bf16[8,7168]{1,0:T(8,128)(2,1)S(1)}, bf16[8,7168]{1,0:T(8,128)(2,1)S(1)}, u32[]{:S(2)}, u32[]{:S(2)}) collective-permute-start(bf16[8,7168]{1,0:T(8,128)(2,1)S(1)} %get-tuple-element.45), channel_id=1, source_target_pairs={{0,2},{1,3},{2,0},{3,1},{4,6},{5,7},{6,4},{7,5},{8,10},{9,11},{10,... | collective-permute-start | bytes 344072 | tf_op jit(solution)/shard_map/ppermute | solution.py:59
  36.1 5.3 %collective-permute-start.17 = (bf16[2,7168]{1,0:T(2,128)(2,1)S(1)}, bf16[2,7168]{1,0:T(2,128)(2,1)S(1)}, u32[]{:S(2)}, u32[]{:S(2)}) collective-permute-start(bf16[2,7168]{1,0:T(2,128)(2,1)S(1)} %get-tuple-element.47), channel_id=1, source_target_pairs={{0,16},{1,17},{2,18},{3,19},{4,20},{5,21},{6,22},{7,23},{8,24},{9,... | collective-permute-start | bytes 86024 | tf_op jit(solution)/shard_map/ppermute | solution.py:59
  37.9 5.7 %collective-permute-start.18 = (bf16[2,7168]{1,0:T(2,128)(2,1)S(1)}, bf16[2,7168]{1,0:T(2,128)(2,1)S(1)}, u32[]{:S(2)}, u32[]{:S(2)}) collective-permute-start(bf16[2,7168]{1,0:T(2,128)(2,1)S(1)} %get-tuple-element.48), channel_id=1, source_target_pairs={{0,24},{1,25},{2,26},{3,27},{4,28},{5,29},{6,30},{7,31},{8,16},{9,... | collective-permute-start | bytes 86024 | tf_op jit(solution)/shard_map/ppermute | solution.py:59
  39.2 4.4 %collective-permute-start.19 = (bf16[2,7168]{1,0:T(2,128)(2,1)S(1)}, bf16[2,7168]{1,0:T(2,128)(2,1)S(1)}, u32[]{:S(2)}, u32[]{:S(2)}) collective-permute-start(bf16[2,7168]{1,0:T(2,128)(2,1)S(1)} %get-tuple-element.49), channel_id=1, source_target_pairs={{0,8},{1,9},{2,10},{3,11},{4,12},{5,13},{6,14},{7,15},{8,0},{9,1},... | collective-permute-start | bytes 86024 | tf_op jit(solution)/shard_map/ppermute | solution.py:59
